TPU v7x, 32 devices: a whole 2x2x4 slice. The times are simulated.
32 devices in a mesh: ctx: 4 (over x, core), grp: 2 (over y), rep: 4 (over z).
Axes of the slice: x: 2, y: 2, z: 4, core: 2. Of those that a mesh axis runs over, the one named last changes fastest.
Arguments:
- tokens: bfloat16 [16, 1024, 1024], P(('grp', 'rep'), 'ctx'), may hold values from -6 to 6
- segment_ids: int32 [16, 1024], P(('grp', 'rep'), 'ctx'), may hold values from 0 to 2, as said below
- positions: int32 [16, 1024], P(('grp', 'rep'), 'ctx'), may hold values from 0 to 5119, as said below
- cotangent: bfloat16 [16, 1024, 1024], P(('grp', 'rep'), 'ctx'), may hold values from -6 to 6
- qkv_weight: float32 [1024, 4096], P(('ctx', 'grp')), may hold values from -0.1875 to 0.1875
- qkv_first: float32 [1024, 4096], P(('ctx', 'grp')), may hold values from -40 to 40
- qkv_second: float32 [1024, 4096], P(('ctx', 'grp')), may hold values from 212.992 to 868.352
- out_weight: float32 [2048, 1024], P(('ctx', 'grp')), may hold values from -1 to 1
- out_first: float32 [2048, 1024], P(('ctx', 'grp')), may hold values from -8 to 8
- out_second: float32 [2048, 1024], P(('ctx', 'grp')), may hold values from 8.68352 to 34.4064
- expand_weight: float32 [1024, 6144], P(('ctx', 'grp')), may hold values from -0.1875 to 0.1875
- expand_first: float32 [1024, 6144], P(('ctx', 'grp')), may hold values from -24 to 24
- expand_second: float32 [1024, 6144], P(('ctx', 'grp')), may hold values from 77.0048 to 311.296
- shrink_weight: float32 [3072, 1024], P(('ctx', 'grp')), may hold values from -0.109375 to 0.109375
- shrink_first: float32 [3072, 1024], P(('ctx', 'grp')), may hold values from -40 to 40
- shrink_second: float32 [3072, 1024], P(('ctx', 'grp')), may hold values from 212.992 to 868.352
- norm_gains: float32 [2304], P(('ctx', 'grp')), may hold values from 0.5 to 1.5
- gains_first: float32 [2304], P(('ctx', 'grp')), may hold values from -128 to 128
- gains_second: float32 [2304], P(('ctx', 'grp')), may hold values from 1966.08 to 7700.48
Outputs:
- block_output: bfloat16 [16, 1024, 1024], P(('grp', 'rep'), 'ctx')
- input_grad: bfloat16 [16, 1024, 1024], P(('grp', 'rep'), 'ctx')
- qkv_moment: float32 [1024, 4096], P(('ctx', 'grp'))
- qkv_square: float32 [1024, 4096], P(('ctx', 'grp'))
- qkv_updated: float32 [1024, 4096], P(('ctx', 'grp'))
- out_moment: float32 [2048, 1024], P(('ctx', 'grp'))
- out_square: float32 [2048, 1024], P(('ctx', 'grp'))
- out_updated: float32 [2048, 1024], P(('ctx', 'grp'))
- expand_moment: float32 [1024, 6144], P(('ctx', 'grp'))
- expand_square: float32 [1024, 6144], P(('ctx', 'grp'))
- expand_updated: float32 [1024, 6144], P(('ctx', 'grp'))
- shrink_moment: float32 [3072, 1024], P(('ctx', 'grp'))
- shrink_square: float32 [3072, 1024], P(('ctx', 'grp'))
- shrink_updated: float32 [3072, 1024], P(('ctx', 'grp'))
- gains_moment: float32 [2304], P(('ctx', 'grp'))
- gains_square: float32 [2304], P(('ctx', 'grp'))
- gains_updated: float32 [2304], P(('ctx', 'grp'))
Inputs may be any that keep to these rules, and one draw needn't show every extreme that they name: `segment_ids`: along each sequence segment ids start at 0 and never fall. Within a document the positions rise by one from token to token.
All inputs are finite; a program needn't handle non-finite values.
Results may differ from a plain program's by a relative error of at most 0.025.
Values may be sent and summed in bfloat16 or wider, within the bound.
No kernel may reach another device: no remote copies, remote signals or barrier semaphores. Data moves between devices by JAX's collectives and lax.ppermute only.
A program may use at most 320 MiB of HBM per device.

v0:
```python
import math

import jax
import jax.numpy as jnp
from jax import lax
from jax.sharding import PartitionSpec as P

D = 1024
QUERY_HEADS = 16
KEY_VALUE_HEADS = 8
HEAD_SIZE = 128
FF = 3072
STEP = 10
QUERY_FEATURES = 2048
KEY_FEATURES = 1024


EPS_NORM = 1e-06
ROPE_BASE = 1000000.0
MASKED_SCORE = -1e30
BETA_ONE = 0.9
BETA_TWO = 0.95
ADAM_EPS = 1e-08
WEIGHT_DECAY = 0.1
RATE_QKV = 0.1
RATE_OUT = 0.5
RATE_EXPAND = 0.1
RATE_SHRINK = 0.06
RATE_GAINS = 0.6


def rms_scale(values, gain_vec):
    return (
        values * lax.rsqrt(jnp.mean(values * values, axis=-1, keepdims=True) + EPS_NORM) * gain_vec
    )


def rotate(values, places):
    half_size = values.shape[-1] // 2
    ladder = jnp.arange(half_size, dtype=jnp.float32)
    frequency = jnp.exp(ladder * (-2.0 * math.log(ROPE_BASE) / values.shape[-1]))
    angles = places.astype(jnp.float32)[:, None] * frequency[None, :]
    cosine = jnp.cos(angles)[:, None, :]
    sine_part = jnp.sin(angles)[:, None, :]
    first_half = values[..., :half_size]
    second_half = values[..., half_size:]
    return jnp.concatenate(
        [
            first_half * cosine - second_half * sine_part,
            second_half * cosine + first_half * sine_part,
        ],
        axis=-1,
    )


def split_heads(projected_output, g_query, g_key, places):
    token_row_list = projected_output.shape[0]
    query_rows = projected_output[:, :QUERY_FEATURES].reshape(
        token_row_list, QUERY_HEADS, HEAD_SIZE
    )
    key_entries = projected_output[:, QUERY_FEATURES : QUERY_FEATURES + KEY_FEATURES].reshape(
        token_row_list, KEY_VALUE_HEADS, HEAD_SIZE
    )
    value_entries = projected_output[:, QUERY_FEATURES + KEY_FEATURES :].reshape(
        token_row_list, KEY_VALUE_HEADS, HEAD_SIZE
    )
    return (
        rotate(rms_scale(query_rows, g_query), places),
        rotate(rms_scale(key_entries, g_key), places),
        value_entries,
    )


def swiglu(gate_up):
    return jax.nn.silu(gate_up[:, :FF]) * gate_up[:, FF:]


def adam_step(weight, first_moment, second_moment, gradient, step_rate):
    first_moment = BETA_ONE * first_moment + (1.0 - BETA_ONE) * gradient
    second_moment = BETA_TWO * second_moment + (1.0 - BETA_TWO) * gradient * gradient
    fix_one = 1.0 - BETA_ONE**STEP
    fix_two = 1.0 - BETA_TWO**STEP
    step_dir = first_moment / fix_one / (jnp.sqrt(second_moment / fix_two) + ADAM_EPS)
    return (first_moment, second_moment, weight - step_rate * (step_dir + WEIGHT_DECAY * weight))


def on_device(
    tokens,
    segment_ids,
    positions,
    cotangent,
    qkv_weight,
    qkv_first,
    qkv_second,
    out_weight,
    out_first,
    out_second,
    expand_weight,
    expand_first,
    expand_second,
    shrink_weight,
    shrink_first,
    shrink_second,
    norm_gains,
    gains_first,
    gains_second,
):
    sequence_count, token_length, model_width = tokens.shape
    token_row_list = sequence_count * token_length
    head_groups = QUERY_HEADS // KEY_VALUE_HEADS
    score_scale = HEAD_SIZE ** (-0.5)
    qkv_full, out_full, expand_full, shrink_full, gain_low = (
        lax.all_gather(qkv_weight.astype(jnp.bfloat16), ("ctx", "grp"), axis=0, tiled=True),
        lax.all_gather(out_weight.astype(jnp.bfloat16), ("ctx", "grp"), axis=0, tiled=True),
        lax.all_gather(expand_weight.astype(jnp.bfloat16), ("ctx", "grp"), axis=0, tiled=True),
        lax.all_gather(shrink_weight.astype(jnp.bfloat16), ("ctx", "grp"), axis=0, tiled=True),
        lax.all_gather(norm_gains.astype(jnp.bfloat16), ("ctx", "grp"), axis=0, tiled=True),
    )
    gain_full = gain_low.astype(jnp.float32)
    gain_one = gain_full[:D]
    gain_two = gain_full[D : 2 * D]
    gain_query = gain_full[2 * D : 2 * D + HEAD_SIZE]
    gain_key = gain_full[2 * D + HEAD_SIZE :]
    inputs = tokens.reshape(token_row_list, model_width).astype(jnp.float32)
    normed_one, pull_one = jax.vjp(rms_scale, inputs, gain_one)
    normed_low = normed_one.astype(jnp.bfloat16)
    projected_output = jnp.dot(normed_low, qkv_full, preferred_element_type=jnp.float32)
    places = positions.reshape(token_row_list)

    def head_split(qkv_in, g_query, g_key):
        return split_heads(qkv_in, g_query, g_key, places)

    (query_rows, key_entries, value_entries), pull_heads = jax.vjp(
        head_split, projected_output, gain_query, gain_key
    )
    query_head_split = query_rows.astype(jnp.bfloat16).reshape(
        sequence_count, token_length, KEY_VALUE_HEADS, head_groups, HEAD_SIZE
    )
    key_local = key_entries.astype(jnp.bfloat16).reshape(sequence_count, token_length, KEY_FEATURES)
    value_local = value_entries.astype(jnp.bfloat16).reshape(
        sequence_count, token_length, KEY_FEATURES
    )
    seg_query = segment_ids.astype(jnp.float32)
    key_everything, value_everything, seg_all = (
        lax.all_gather(key_local, "ctx", axis=1, tiled=True),
        lax.all_gather(value_local, "ctx", axis=1, tiled=True),
        lax.all_gather(seg_query.astype(jnp.bfloat16), "ctx", axis=1, tiled=True),
    )
    key_total_count = key_everything.shape[1]
    block_len = min(512, key_total_count)
    key_head_split = key_everything.reshape(
        sequence_count, key_total_count, KEY_VALUE_HEADS, HEAD_SIZE
    )
    value_head_split = value_everything.reshape(
        sequence_count, key_total_count, KEY_VALUE_HEADS, HEAD_SIZE
    )
    seg_keys = seg_all.astype(jnp.float32)
    first_query = lax.axis_index("ctx") * token_length
    query_place = first_query + jnp.arange(token_length, dtype=jnp.int32)
    block_limit = (first_query + token_length + block_len - 1) // block_len

    def block_scores(first_key):
        key_block = lax.dynamic_slice_in_dim(key_head_split, first_key, block_len, 1)
        seg_block = lax.dynamic_slice_in_dim(seg_keys, first_key, block_len, 1)
        raw_scores = (
            jnp.einsum(
                "sqkgd,sjkd->skgqj", query_head_split, key_block, preferred_element_type=jnp.float32
            )
            * score_scale
        )
        key_place = first_key + jnp.arange(block_len, dtype=jnp.int32)
        allowed = (seg_query[:, :, None] == seg_block[:, None, :]) & (
            query_place[None, :, None] >= key_place[None, None, :]
        )
        return jnp.where(allowed[:, None, None], raw_scores, MASKED_SCORE)

    statistic_shape = (sequence_count, KEY_VALUE_HEADS, head_groups, token_length)

    def top_step(block_index, carried):
        running_top, running_sum = carried
        scores = block_scores(block_index * block_len)
        new_top = jnp.maximum(running_top, jnp.max(scores, axis=-1))
        running_sum = running_sum * jnp.exp(running_top - new_top) + jnp.sum(
            jnp.exp(scores - new_top[..., None]), axis=-1
        )
        return (new_top, running_sum)

    start_top = jnp.full(statistic_shape, MASKED_SCORE, jnp.float32)
    final_top, final_sum = lax.fori_loop(
        0, block_limit, top_step, (start_top, jnp.zeros(statistic_shape, jnp.float32))
    )
    log_total = final_top + jnp.log(final_sum)
    per_head_shape = (sequence_count, token_length, KEY_VALUE_HEADS, head_groups, HEAD_SIZE)

    def value_step(block_index, out_sum):
        first_key = block_index * block_len
        probabilities = jnp.exp(block_scores(first_key) - log_total[..., None])
        value_block = lax.dynamic_slice_in_dim(value_head_split, first_key, block_len, 1)
        return out_sum + jnp.einsum(
            "skgqj,sjkd->sqkgd",
            probabilities.astype(jnp.bfloat16),
            value_block,
            preferred_element_type=jnp.float32,
        )

    zero_heads = jnp.zeros(per_head_shape, jnp.float32)
    out_sum = lax.fori_loop(0, block_limit, value_step, zero_heads)
    attended_low = out_sum.astype(jnp.bfloat16).reshape(token_row_list, QUERY_FEATURES)
    hidden_state = inputs + jnp.dot(attended_low, out_full, preferred_element_type=jnp.float32)
    normed_two, pull_two = jax.vjp(rms_scale, hidden_state, gain_two)
    normed_two_low = normed_two.astype(jnp.bfloat16)
    gate_up = jnp.dot(normed_two_low, expand_full, preferred_element_type=jnp.float32)
    active, pull_active = jax.vjp(swiglu, gate_up)
    active_low = active.astype(jnp.bfloat16)
    block_output = (
        (hidden_state + jnp.dot(active_low, shrink_full, preferred_element_type=jnp.float32))
        .astype(jnp.bfloat16)
        .reshape(sequence_count, token_length, model_width)
    )
    qkv_full, out_full, expand_full, shrink_full = (
        lax.all_gather(qkv_weight.astype(jnp.bfloat16), ("ctx", "grp"), axis=0, tiled=True),
        lax.all_gather(out_weight.astype(jnp.bfloat16), ("ctx", "grp"), axis=0, tiled=True),
        lax.all_gather(expand_weight.astype(jnp.bfloat16), ("ctx", "grp"), axis=0, tiled=True),
        lax.all_gather(shrink_weight.astype(jnp.bfloat16), ("ctx", "grp"), axis=0, tiled=True),
    )
    incoming = cotangent.reshape(token_row_list, model_width)
    active_grad = jnp.dot(incoming, shrink_full.T, preferred_element_type=jnp.float32)
    grad_shrink = jnp.dot(active_low.T, incoming, preferred_element_type=jnp.float32)
    active_grad = lax.optimization_barrier(active_grad.astype(jnp.bfloat16)).astype(jnp.float32)
    (gate_up_grad,) = pull_active(active_grad)
    gate_up_low = gate_up_grad.astype(jnp.bfloat16)
    normed_two_grad = jnp.dot(gate_up_low, expand_full.T, preferred_element_type=jnp.float32)
    grad_expand = jnp.dot(normed_two_low.T, gate_up_low, preferred_element_type=jnp.float32)
    hidden_grad, gain_two_grad = pull_two(normed_two_grad)
    hidden_grad = hidden_grad + incoming.astype(jnp.float32)
    hidden_low = hidden_grad.astype(jnp.bfloat16)
    attended_grad = jnp.dot(hidden_low, out_full.T, preferred_element_type=jnp.float32).astype(
        jnp.bfloat16
    )
    grad_out = jnp.dot(attended_low.T, hidden_low, preferred_element_type=jnp.float32)
    grad_heads = attended_grad.reshape(per_head_shape)
    row_terms = jnp.sum(grad_heads.astype(jnp.float32) * out_sum, axis=-1)
    row_terms = jnp.transpose(row_terms, (0, 2, 3, 1))

    def grad_step(block_index, carried):
        query_grad, key_grad_all, value_grad_all = carried
        first_key = block_index * block_len
        probabilities = jnp.exp(block_scores(first_key) - log_total[..., None])
        key_block = lax.dynamic_slice_in_dim(key_head_split, first_key, block_len, 1)
        value_block = lax.dynamic_slice_in_dim(value_head_split, first_key, block_len, 1)
        prob_grad = jnp.einsum(
            "sqkgd,sjkd->skgqj", grad_heads, value_block, preferred_element_type=jnp.float32
        )
        score_grad = (probabilities * (prob_grad - row_terms[..., None])).astype(jnp.bfloat16)
        query_grad = (
            query_grad
            + jnp.einsum(
                "skgqj,sjkd->sqkgd", score_grad, key_block, preferred_element_type=jnp.float32
            )
            * score_scale
        )
        key_grad = (
            jnp.einsum(
                "skgqj,sqkgd->sjkd",
                score_grad,
                query_head_split,
                preferred_element_type=jnp.float32,
            )
            * score_scale
        )
        value_grad = jnp.einsum(
            "skgqj,sqkgd->sjkd",
            probabilities.astype(jnp.bfloat16),
            grad_heads,
            preferred_element_type=jnp.float32,
        )
        key_grad_all = lax.dynamic_update_slice_in_dim(key_grad_all, key_grad, first_key, 1)
        value_grad_all = lax.dynamic_update_slice_in_dim(value_grad_all, value_grad, first_key, 1)
        return (query_grad, key_grad_all, value_grad_all)

    empty_key_rows = jnp.zeros(
        (sequence_count, key_total_count, KEY_VALUE_HEADS, HEAD_SIZE), jnp.float32
    )
    query_grad, key_grad_all, value_grad_all = lax.fori_loop(
        0, block_limit, grad_step, (zero_heads, empty_key_rows, empty_key_rows)
    )
    key_portion, value_portion = (
        lax.psum_scatter(
            key_grad_all.astype(jnp.bfloat16), "ctx", scatter_dimension=1, tiled=True
        ).astype(jnp.float32),
        lax.psum_scatter(
            value_grad_all.astype(jnp.bfloat16), "ctx", scatter_dimension=1, tiled=True
        ).astype(jnp.float32),
    )
    qkv_grad, gain_query_grad, gain_key_grad = pull_heads(
        (
            query_grad.reshape(token_row_list, QUERY_HEADS, HEAD_SIZE),
            key_portion.reshape(token_row_list, KEY_VALUE_HEADS, HEAD_SIZE),
            value_portion.reshape(token_row_list, KEY_VALUE_HEADS, HEAD_SIZE),
        )
    )
    qkv_low = qkv_grad.astype(jnp.bfloat16)
    normed_one_grad = jnp.dot(qkv_low, qkv_full.T, preferred_element_type=jnp.float32)
    grad_qkv = jnp.dot(normed_low.T, qkv_low, preferred_element_type=jnp.float32)
    input_part, gain_one_grad = pull_one(normed_one_grad)
    input_grad = (
        (input_part + hidden_grad)
        .astype(jnp.bfloat16)
        .reshape(sequence_count, token_length, model_width)
    )
    grad_gains = jnp.concatenate([gain_one_grad, gain_two_grad, gain_query_grad, gain_key_grad])
    shard_qkv, shard_out, shard_expand, shard_shrink, shard_gains = (
        lax.psum_scatter(
            grad_qkv.astype(jnp.bfloat16), ("ctx", "grp"), scatter_dimension=0, tiled=True
        ).astype(jnp.float32),
        lax.psum_scatter(
            grad_out.astype(jnp.bfloat16), ("ctx", "grp"), scatter_dimension=0, tiled=True
        ).astype(jnp.float32),
        lax.psum_scatter(
            grad_expand.astype(jnp.bfloat16), ("ctx", "grp"), scatter_dimension=0, tiled=True
        ).astype(jnp.float32),
        lax.psum_scatter(
            grad_shrink.astype(jnp.bfloat16), ("ctx", "grp"), scatter_dimension=0, tiled=True
        ).astype(jnp.float32),
        lax.psum_scatter(
            grad_gains.astype(jnp.bfloat16), ("ctx", "grp"), scatter_dimension=0, tiled=True
        ).astype(jnp.float32),
    )
    total_qkv, total_out, total_expand, total_shrink, total_gains = (
        lax.psum(shard_qkv.astype(jnp.bfloat16), "rep").astype(jnp.float32),
        lax.psum(shard_out.astype(jnp.bfloat16), "rep").astype(jnp.float32),
        lax.psum(shard_expand.astype(jnp.bfloat16), "rep").astype(jnp.float32),
        lax.psum(shard_shrink.astype(jnp.bfloat16), "rep").astype(jnp.float32),
        lax.psum(shard_gains.astype(jnp.bfloat16), "rep").astype(jnp.float32),
    )
    qkv_m, qkv_v, qkv_w = adam_step(qkv_weight, qkv_first, qkv_second, total_qkv, RATE_QKV)
    out_m, out_v, out_w = adam_step(out_weight, out_first, out_second, total_out, RATE_OUT)
    expand_m, expand_v, expand_w = adam_step(
        expand_weight, expand_first, expand_second, total_expand, RATE_EXPAND
    )
    shrink_m, shrink_v, shrink_w = adam_step(
        shrink_weight, shrink_first, shrink_second, total_shrink, RATE_SHRINK
    )
    gains_m, gains_v, gains_w = adam_step(
        norm_gains, gains_first, gains_second, total_gains, RATE_GAINS
    )
    return (
        block_output,
        input_grad,
        qkv_m,
        qkv_v,
        qkv_w,
        out_m,
        out_v,
        out_w,
        expand_m,
        expand_v,
        expand_w,
        shrink_m,
        shrink_v,
        shrink_w,
        gains_m,
        gains_v,
        gains_w,
    )


def solution(mesh):
    placed = (
        P(("grp", "rep"), "ctx", None),
        P(("grp", "rep"), "ctx"),
        P(("grp", "rep"), "ctx"),
        P(("grp", "rep"), "ctx", None),
        P(("ctx", "grp"), None),
        P(("ctx", "grp"), None),
        P(("ctx", "grp"), None),
        P(("ctx", "grp"), None),
        P(("ctx", "grp"), None),
        P(("ctx", "grp"), None),
        P(("ctx", "grp"), None),
        P(("ctx", "grp"), None),
        P(("ctx", "grp"), None),
        P(("ctx", "grp"), None),
        P(("ctx", "grp"), None),
        P(("ctx", "grp"), None),
        P(("ctx", "grp")),
        P(("ctx", "grp")),
        P(("ctx", "grp")),
    )
    return jax.shard_map(
        on_device,
        mesh=mesh,
        in_specs=placed,
        out_specs=(
            P(("grp", "rep"), "ctx", None),
            P(("grp", "rep"), "ctx", None),
            P(("ctx", "grp"), None),
            P(("ctx", "grp"), None),
            P(("ctx", "grp"), None),
            P(("ctx", "grp"), None),
            P(("ctx", "grp"), None),
            P(("ctx", "grp"), None),
            P(("ctx", "grp"), None),
            P(("ctx", "grp"), None),
            P(("ctx", "grp"), None),
            P(("ctx", "grp"), None),
            P(("ctx", "grp"), None),
            P(("ctx", "grp"), None),
            P(("ctx", "grp")),
            P(("ctx", "grp")),
            P(("ctx", "grp")),
        ),
        check_vma=False,
    )
```

profile of v0, /device:TPU:0, one launch (start us, length us, event | category | flops | bytes accessed | tf_op | source)
XLA Modules:
  0.0 1022.4 jit_solution(3379943549523420783)
XLA Ops:
  13.3 15.8 %all-reduce.9 = bf16[2304]{0:T(1024)(128)(2,1)S(1)} all-reduce(bf16[2304]{0:T(1024)(128)(2,1)S(1)} %dynamic-update-slice), channel_id=1, replica_groups=mesh['ctx'=4,'grp'=2,'rep'=4] {'ctx','grp'}, use_global_device_ids=true, to_apply=%add.9 | all-reduce | flops 2304 | bytes 9216
  31.1 37.0 %all-gather.7.cloned.1.call-done = bf16[1024,4096]{1,0:T(8,128)(2,1)} async-done(((bf16[128,4096]{1,0:T(8,128)(2,1)}), bf16[1024,4096]{1,0:T(8,128)(2,1)}) %all-gather.7.cloned.1.call-update) | async-done | bytes 8388624 | tf_op jit(solution)/shard_map/all_gather | solution.py:113
  68.2 6.9 fusion.112
  91.9 5.3 all_gather.31
  97.2 19.0 %all-gather.17.cloned.1.call-done = bf16[3072,1024]{1,0:T(8,128)(2,1)} async-done(((bf16[384,1024]{1,0:T(8,128)(2,1)}), bf16[3072,1024]{1,0:T(8,128)(2,1)}) %all-gather.17.cloned.1.call-update) | async-done | bytes 6291472 | tf_op jit(solution)/shard_map/all_gather | solution.py:116
  116.2 8.2 convolution_convert_fusion.3
  124.4 5.2 slice_bitcast_fusion.1
  143.4 5.3 pad_maximum_fusion
  148.7 4.9 copy.183
  153.6 6.2 copy.175
  159.8 6.4 copy.182
  166.2 19.3 %while.39 = (s32[]{:T(128)}, f32[2,8,2,256]{3,2,1,0:T(2,128)S(1)}, f32[2,8,2,256]{3,2,1,0:T(2,128)S(1)}, s32[]{:T(128)}, f32[2,256]{1,0:T(2,128)S(1)}, /*index=5...) while((s32[]{:T(128)}, f32[2,8,2,256]{3,2,1,0:T(2,128)S(1)}, ...), condition=%wide.region_6.7_spmd.clone, body=%wide.region_3.6_spmd.clone.sunk | while | flops 1103774464 | bytes 39243968 | solution.py:189
  167.1 8.9 fusion.158
  176.0 9.5 exponential_reduce_fusion.2
  192.4 11.6 %while.40 = (s32[]{:T(128)}, f32[2,256,8,2,128]{1,4,3,2,0:T(8,128)}, s32[]{:T(128)}, bf16[2,1024,8,128]{1,3,2,0:T(8,128)(2,1)}, f32[2,256]{1,0:T(2,128)S(1)}, /*...) while((s32[]{:T(128)}, ...), condition=%wide.region_8.9_spmd.clone, body=%wide.region_7.8_spmd.clone.sunk | while | flops 2165965568 | bytes 15520967 | solution.py:207
  192.8 11.2 %bitcast_add_fusion.5 = f32[2,256,8,2,128]{1,4,3,2,0:T(8,128)} fusion(f32[2,256,8,2,128]{1,4,3,2,0:T(8,128)} %get-tuple-element.884, f32[2,8,2,256]{3,2,1,0:T(2,128)S(1)} %get-tuple-element.905, pred[2,256,512]{1,2,0:T(8,128)(4,1)S(1)} %compare_and_fusion.7, bf16[2,256,8,2,128]{4,1,3,2,0:T(8,128)(2,1)S(1)} %get-tuple-element.904, ...), kind=kOutput, calls=%fused_computation.26.clone.1 | convolution fusion | flops 2165309440 | bytes 14976000 | tf_op jit(solution)/shard_map/while/body/skgqj,sjkd->sqkgd/dot_general | solution.py:199
  207.8 6.3 copy.184
  218.6 10.3 %all-gather.13.cloned.1.call-done = bf16[2048,1024]{1,0:T(8,128)(2,1)} async-done(((bf16[256,1024]{1,0:T(8,128)(2,1)}), bf16[2048,1024]{1,0:T(8,128)(2,1)}) %all-gather.13.cloned.1.call-update) | async-done | bytes 4194320 | tf_op jit(solution)/shard_map/all_gather | solution.py:114
  228.9 6.8 multiply_reduce_fusion.7
  235.7 67.7 %all-gather.15.cloned.1.call-done = bf16[1024,6144]{1,0:T(8,128)(2,1)} async-done(((bf16[128,6144]{1,0:T(8,128)(2,1)}), bf16[1024,6144]{1,0:T(8,128)(2,1)}) %all-gather.15.cloned.1.call-update) | async-done | bytes 12582928 | tf_op jit(solution)/shard_map/all_gather | solution.py:115
  303.4 10.2 fusion.98
  313.7 7.0 convert_multiply_fusion.1
  320.6 15.4 %multiply_reduce_fusion.4 = (bf16[1024]{0:T(1024)(128)(2,1)}, f32[512]{0:T(512)S(1)}, f32[512,1024]{1,0:T(8,128)}) fusion(f32[512,1024]{1,0:T(8,128)} %get-tuple-element.619, f32[512]{0:T(512)S(1)} %fusion.91, f32[1024]{0:T(1024)S(1)} %copy-done.46, bf16[1024,6144]{1,0:T(8,128)(2,1)} %all-gather.15.cloned.1.call-done, f32[512,3072]{1,0:T(8,128)} %get-tuple-element.596, ...), kind=kOutput, calls=%fused_computation.140 | convolution fusion | flops 6451886592 | bytes 29370368 | tf_op jit(solution)/shard_map/dot_general | solution.py:232
  352.5 6.1 copy.185
  369.6 43.6 %while.41 = (s32[]{:T(128)}, f32[2,256,8,2,128]{1,4,3,2,0:T(8,128)}, bf16[2,1024,8,128]{3,2,1,0:T(8,128)(2,1)}, bf16[2,1024,8,128]{3,1,2,0:T(8,128)(2,1)}, s32[]...) while((s32[]{:T(128)}, ...), condition=%wide.region_13.14_spmd.clone, body=%wide.region_12.13_spmd.clone.sunk | while | flops 5415502848 | bytes 143774016 | solution.py:284
  369.6 9.7 fusion.173
  379.8 9.7 fusion.174
  389.5 6.4 bitcast_add_fusion.6
  401.7 11.4 %bitcast_dynamic-update-slice_fusion.2 = bf16[2,1024,8,128]{3,1,2,0:T(8,128)(2,1)} fusion(bf16[2,1024,8,128]{3,1,2,0:T(8,128)(2,1)} %get-tuple-element.932, s32[]{:T(128)S(6)} %select_n.81, bf16[2,256,8,2,128]{4,1,3,2,0:T(8,128)(2,1)} %get-tuple-element.958, f32[2,8,512,256,2]{3,2,4,1,0:T(8,128)} %fusion.173, ...), kind=kOutput, calls=%fused_computation.52.clone.1 | convolution fusion | flops 1090519040 | bytes 23363588 | tf_op jit(solution)/shard_map/while/body/skgqj,sqkgd->sjkd/dot_general | solution.py:271
  421.8 6.0 convolution_convert_fusion.4
  429.7 6.5 convolution_convert_fusion.2
  437.9 14.3 %convolution_convert_fusion = bf16[1024,6144]{1,0:T(8,128)(2,1)} fusion(f32[512,3072]{1,0:T(8,128)} %get-tuple-element.596, f32[512,3072]{1,0:T(8,128)} %get-tuple-element.595, f32[512,1024]{1,0:T(8,128)S(1)} %copy-done.11, f32[1024]{0:T(1024)S(1)} %copy-done.47, f32[512]{0:T(512)S(1)} %copy-done.51), kind=kOutput, calls=%fused_computation.74 | convolution fusion | flops 6456606720 | bytes 27269120 | tf_op jit(solution)/shard_map/dot_general | solution.py:233
  452.5 5.4 copy.194
  458.0 4.9 multiply_add_fusion.2
  466.6 5.6 copy_bitcast_fusion.1
  472.2 36.1 %reduce-scatter.20.cloned.1.call-done = bf16[256,2048]{1,0:T(8,128)(2,1)} async-done(((bf16[1024,2048]{1,0:T(8,128)(2,1)}), bf16[256,2048]{1,0:T(8,128)(2,1)}) %reduce-scatter.20.cloned.1.call-update) | async-done | bytes 1048592
  518.7 36.8 %reduce-scatter.10.cloned.1.call-done = bf16[2,256,8,128]{3,1,2,0:T(8,128)(2,1)} async-done(((bf16[2,1024,8,128]{3,1,2,0:T(8,128)(2,1)}), bf16[2,256,8,128]{3,1,2,0:T(8,128)(2,1)}) %reduce-scatter.10.cloned.1.call-update) | async-done | bytes 1048592 | tf_op jit(solution)/shard_map/reduce_scatter | solution.py:291
  558.8 7.1 convolution_convert_fusion.1
  566.2 44.0 %reduce-scatter.14.cloned.1.call-done = bf16[256,1024]{1,0:T(8,128)(2,1)} async-done(((bf16[2048,1024]{1,0:T(8,128)(2,1)}), bf16[256,1024]{1,0:T(8,128)(2,1)}) %reduce-scatter.14.cloned.1.call-update) | async-done | bytes 524304 | tf_op jit(solution)/shard_map/reduce_scatter | solution.py:316
  610.2 65.4 %reduce-scatter.18.cloned.1.call-done = bf16[384,1024]{1,0:T(8,128)(2,1)} async-done(((bf16[3072,1024]{1,0:T(8,128)(2,1)}), bf16[384,1024]{1,0:T(8,128)(2,1)}) %reduce-scatter.18.cloned.1.call-update) | async-done | bytes 786448 | tf_op jit(solution)/shard_map/reduce_scatter | solution.py:322
  675.6 95.9 %reduce-scatter.16.cloned.1.call-done = bf16[128,6144]{1,0:T(8,128)(2,1)} async-done(((bf16[1024,6144]{1,0:T(8,128)(2,1)}), bf16[128,6144]{1,0:T(8,128)(2,1)}) %reduce-scatter.16.cloned.1.call-update) | async-done | bytes 1572880 | tf_op jit(solution)/shard_map/reduce_scatter | solution.py:319
  771.5 74.6 %reduce-scatter.12.cloned.1.call-done = bf16[128,4096]{1,0:T(8,128)(2,1)} async-done(((bf16[1024,4096]{1,0:T(8,128)(2,1)}), bf16[128,4096]{1,0:T(8,128)(2,1)}) %reduce-scatter.12.cloned.1.call-update) | async-done | bytes 1048592 | tf_op jit(solution)/shard_map/reduce_scatter | solution.py:313
  846.9 8.3 add_convert_fusion.3
  855.2 10.5 %fusion.76 = (bf16[1024]{0:T(1024)(128)(2,1)S(1)}, f32[512]{0:T(512)S(1)}, f32[512,1024]{1,0:T(8,128)}) fusion(bf16[2,256,1024]{2,1,0:T(8,128)(2,1)S(1)} %copy-done.10, f32[512]{0:T(512)S(1)} %copy-done.57, f32[1024]{0:T(1024)S(1)} %copy-done.55, bf16[1024,4096]{1,0:T(8,128)(2,1)} %all-gather.7.cloned.1.call-done, f32[512,2048]{1,0:T(8,128)S(1)} %copy-done.25, ...), kind=kOutput, calls=%fused_computation.136 | convolution fusion | flops 4307024384 | bytes 18884608 | tf_op jit(solution)/shard_map/dot_general | solution.py:303
  865.7 14.4 %all-reduce.10 = bf16[2304]{0:T(1024)(128)(2,1)S(1)} all-reduce(bf16[2304]{0:T(1024)(128)(2,1)S(1)} %pad_maximum_fusion.2), channel_id=8, replica_groups=mesh['ctx'=4,'grp'=2,'rep'=4] {'ctx','grp'}, use_global_device_ids=true, to_apply=%region_31.32.clone | all-reduce | flops 2304 | bytes 9216
  880.2 12.9 %psum.39 = bf16[288]{0:T(512)(128)(2,1)S(1)} all-reduce(bf16[288]{0:T(512)(128)(2,1)S(1)} %dynamic-slice.2), channel_id=1, replica_groups=mesh['ctx'=4,'grp'=2,'rep'=4] {'rep'}, use_global_device_ids=true, to_apply=%region_32.33 | all-reduce | flops 288 | bytes 1152 | tf_op jit(solution)/shard_map/psum | solution.py:334
  897.7 99.1 %all-reduce.14.cloned.1.call-done = (bf16[128,4096]{1,0:T(8,128)(2,1)}, bf16[256,1024]{1,0:T(8,128)(2,1)}, bf16[128,6144]{1,0:T(8,128)(2,1)}, bf16[384,1024]{1,0:T(8,128)(2,1)}) async-done(((bf16[128,4096]{1,0:T(8,128)(2,1)}, bf16[256,1024]{1,0:T(8,128)(2,1)}, bf16[128,6144]{1,0:T(8,128)(2,1)}, bf16[384,1024]{1,0:T(8,128)(2,1)}), (bf16[128,4096]{1,0:T(8,128)(2,1)}, bf16[256,1024]{1,0:T(8,128)(2,1)}, ...) | async-done | bytes 3932176 | tf_op jit(solution)/shard_map/psum | solution.py:330
  996.8 6.5 multiply_subtract_fusion.1
  (275 shorter events, 133.9 us)
Async XLA Ops:
  7.2 60.9 %all-gather.7.cloned.1.call-start = ((), (), s32[]{:S(2)}) async-start(), calls=%async_computation.6 | async-start | bytes 9437184 | tf_op jit(solution)/shard_map/all_gather | solution.py:113
  10.1 106.0 %all-gather.17.cloned.1.call-start = ((), (), s32[]{:S(2)}) async-start(), calls=%async_computation.11 | async-start | bytes 7077888 | tf_op jit(solution)/shard_map/all_gather | solution.py:116
  11.2 142.4 %all-gather.11.cloned.1.call-start = ((), (), s32[]{:S(2)}) async-start(), calls=%async_computation.8 | async-start | bytes 5242880 | tf_op jit(solution)/shard_map/all_gather | solution.py:145
  11.7 63.4 %copy-start.56 = (f32[512]{0:T(512)}, f32[512]{0:T(512)S(1)}, u32[]{:S(2)}) copy-start(f32[512]{0:T(512)S(1)} %rsqrt.40) | copy-start | bytes 6148
  29.2 50.1 %copy-start.62 = (f32[128]{0:T(128)}, f32[128]{0:T(128)S(1)}, u32[]{:S(2)}) copy-start(f32[128]{0:T(128)S(1)} %get-tuple-element.611) | copy-start | bytes 1540
  29.2 102.6 %copy-start.60 = (f32[128]{0:T(128)}, f32[128]{0:T(128)S(1)}, u32[]{:S(2)}) copy-start(f32[128]{0:T(128)S(1)} %get-tuple-element.610) | copy-start | bytes 1540
  29.8 45.3 %copy-start.54 = (f32[1024]{0:T(1024)}, f32[1024]{0:T(1024)S(1)}, u32[]{:S(2)}) copy-start(f32[1024]{0:T(1024)S(1)} %get-tuple-element.609) | copy-start | bytes 12292
  30.8 49.4 %copy-start.18 = (f32[512,64]{1,0:T(8,128)}, f32[512,64]{1,0:T(8,128)S(1)}, u32[]{:S(2)}) copy-start(f32[512,64]{1,0:T(8,128)S(1)} %get-tuple-element.613) | copy-start | bytes 393220
  30.8 104.8 %copy-start.16 = (f32[512,64]{1,0:T(8,128)}, f32[512,64]{1,0:T(8,128)S(1)}, u32[]{:S(2)}) copy-start(f32[512,64]{1,0:T(8,128)S(1)} %get-tuple-element.612) | copy-start | bytes 393220
  31.1 44.0 %copy-start.37 = (bf16[512,1024]{1,0:T(8,128)(2,1)}, bf16[512,1024]{1,0:T(8,128)(2,1)S(1)}, u32[]{:S(2)}) copy-start(bf16[512,1024]{1,0:T(8,128)(2,1)S(1)} %fusion.75) | copy-start | bytes 3145732
  83.0 106.9 %all-gather.9.cloned.1.call-start = ((), (), s32[]{:S(2)}) async-start(), calls=%async_computation.7 | async-start | bytes 5242880 | tf_op jit(solution)/shard_map/all_gather | solution.py:146
  88.2 140.7 %all-gather.13.cloned.1.call-start = ((), (), s32[]{:S(2)}) async-start(), calls=%async_computation.9 | async-start | bytes 4718592 | tf_op jit(solution)/shard_map/all_gather | solution.py:114
  90.4 213.0 %all-gather.15.cloned.1.call-start = ((), (), s32[]{:S(2)}) async-start(), calls=%async_computation.10 | async-start | bytes 14155776 | tf_op jit(solution)/shard_map/all_gather | solution.py:115
  91.8 416.5 %reduce-scatter.20.cloned.1.call-start = ((), (), s32[]{:S(2)}) async-start(), calls=%async_computation.17 | async-start | bytes 5242880
  218.6 84.8 %copy-start.46 = (f32[1024]{0:T(1024)S(1)}, f32[1024]{0:T(1024)}, u32[]{:S(2)}) copy-start(f32[1024]{0:T(1024)} %get-tuple-element.608) | copy-start | bytes 12292
  235.7 100.3 %copy-start.50 = (f32[512]{0:T(512)}, f32[512]{0:T(512)S(1)}, u32[]{:S(2)}) copy-start(f32[512]{0:T(512)S(1)} %fusion.91) | copy-start | bytes 6148
  303.4 10.2 %copy-start.32 = (bf16[512,3072]{1,0:T(8,128)(2,1)S(1)}, bf16[512,3072]{1,0:T(8,128)(2,1)}, u32[]{:S(2)}) copy-start(bf16[512,3072]{1,0:T(8,128)(2,1)} %convolution_convert_fusion.3) | copy-start | bytes 9437188
  420.2 135.3 %reduce-scatter.10.cloned.1.call-start = ((), (), s32[]{:S(2)}) async-start(), calls=%async_computation.12 | async-start | bytes 5242880 | tf_op jit(solution)/shard_map/reduce_scatter | solution.py:291
  421.0 189.3 %reduce-scatter.14.cloned.1.call-start = ((), (), s32[]{:S(2)}) async-start(), calls=%async_computation.14 | async-start | bytes 4718592 | tf_op jit(solution)/shard_map/reduce_scatter | solution.py:316
  427.9 247.8 %reduce-scatter.18.cloned.1.call-start = ((), (), s32[]{:S(2)}) async-start(), calls=%async_computation.16 | async-start | bytes 7077888 | tf_op jit(solution)/shard_map/reduce_scatter | solution.py:322
  436.3 335.2 %reduce-scatter.16.cloned.1.call-start = ((), (), s32[]{:S(2)}) async-start(), calls=%async_computation.15 | async-start | bytes 14155776 | tf_op jit(solution)/shard_map/reduce_scatter | solution.py:319
  452.3 393.9 %reduce-scatter.12.cloned.1.call-start = ((), (), s32[]{:S(2)}) async-start(), calls=%async_computation.13 | async-start | bytes 9437184 | tf_op jit(solution)/shard_map/reduce_scatter | solution.py:313
  452.5 5.4 copy-start.17
  452.5 5.4 copy-start.20
  457.9 4.9 copy-start.2
  457.9 4.9 copy-start.44
  457.9 4.9 copy-start.61
  518.2 40.6 %copy-start.38 = (bf16[512,1024]{1,0:T(8,128)(2,1)S(1)}, bf16[512,1024]{1,0:T(8,128)(2,1)}, u32[]{:S(2)}) copy-start(bf16[512,1024]{1,0:T(8,128)(2,1)} %copy-done.37) | copy-start | bytes 3145732
  518.7 47.2 %copy-start.33 = (f32[64,8,8,128]{3,1,2,0:T(8,128)}, f32[64,8,8,128]{3,1,2,0:T(8,128)S(1)}, u32[]{:S(2)}) copy-start(f32[64,8,8,128]{3,1,2,0:T(8,128)S(1)} %copy.259) | copy-start | bytes 6291460
  565.9 280.9 %copy-start.12 = (f32[512,1024]{1,0:T(8,128)S(1)}, f32[512,1024]{1,0:T(8,128)}, u32[]{:S(2)}) copy-start(f32[512,1024]{1,0:T(8,128)} %get-tuple-element.619) | copy-start | bytes 6291460
  565.9 430.9 %all-reduce.14.cloned.1.call-start = ((), (), s32[]{:S(2)}) async-start(), calls=%async_computation.18 | async-start | bytes 7864320 | tf_op jit(solution)/shard_map/psum | solution.py:330
  846.8 8.3 copy-start.10
  846.8 8.3 copy-start.25
  846.9 8.3 copy-start.55
  846.9 8.3 copy-start.57
  855.2 10.5 %copy-start.71 = (bf16[1024]{0:T(1024)(128)(2,1)S(1)}, bf16[1024]{0:T(1024)(128)(2,1)}, u32[]{:S(2)}) copy-start(bf16[1024]{0:T(1024)(128)(2,1)} %get-tuple-element.502) | copy-start | bytes 6148
  855.2 38.0 %copy-start.59 = (f32[1,2,2,128]{3,1,2,0:T(2,128)S(1)}, f32[1,2,2,128]{3,1,2,0:T(2,128)}, u32[]{:S(2)}) copy-start(f32[1,2,2,128]{3,1,2,0:T(2,128)} %copy-done.58) | copy-start | bytes 6148
  855.2 38.0 %copy-start.65 = (f32[288]{0:T(512)S(1)}, f32[288]{0:T(512)}, u32[]{:S(2)}) copy-start(f32[288]{0:T(512)} %param.41) | copy-start | bytes 3460
  855.2 38.0 %copy-start.69 = (f32[288]{0:T(512)S(1)}, f32[288]{0:T(512)}, u32[]{:S(2)}) copy-start(f32[288]{0:T(512)} %param.43) | copy-start | bytes 3460
  855.2 38.0 %copy-start.70 = (f32[288]{0:T(512)S(1)}, f32[288]{0:T(512)}, u32[]{:S(2)}) copy-start(f32[288]{0:T(512)} %param.42) | copy-start | bytes 3460
  893.8 103.0 %copy-start.13 = (f32[128,4096]{1,0:T(8,128)S(1)}, f32[128,4096]{1,0:T(8,128)}, u32[]{:S(2)}) copy-start(f32[128,4096]{1,0:T(8,128)} %param.29) | copy-start | bytes 6291460
  996.8 6.5 copy-start.28
  996.8 6.5 copy-start.40
  996.8 6.5 copy-start.41
  996.8 6.5 copy-start.45
  996.8 8.8 copy-start.30
  996.8 8.8 copy-start.36
  1007.3 5.0 copy-start.42
  (38 other events, 102.4 us)
Sparse Core Ops, SparseCore 0:
  10.5 57.6 all-gather.6
  70.6 45.5 all-gather.16
  118.3 34.4 all-gather.10
  154.8 35.0 all-gather.8
  192.2 36.7 all-gather.12
  231.3 72.1 all-gather.14
  420.3 87.8 reduce-scatter.19
  511.0 44.4 reduce-scatter.9
  558.9 51.3 reduce-scatter.13
  613.8 61.7 reduce-scatter.17
  679.1 92.3 reduce-scatter.15
  774.9 71.2 reduce-scatter.11
  849.0 147.7 all-reduce.13
where the time goes:
time: 1030 us; the launch traced here: 1020 us
  waiting for transfers between devices  591 us (57%)
  matrix products  164 us (16%)
  local copies, waits for them, and re-layouts  105 us (10%)
  other arithmetic  96.2 us (9%)
  blocking collectives  48.4 us (5%)
  between operations  16.8 us (2%)
    psum x1, waiting for transfers between devices, on_device(): lax.psum(shard_qkv.astype(jnp.bfloat16), 'rep').astype(jnp.float32)  99.1 us
    reduce_scatter x1, waiting for transfers between devices, on_device(): lax.psum_scatter(grad_expand.astype(jnp.bfloat16), ('ctx', 'grp'), scatte...  95.9 us
    reduce_scatter x1, waiting for transfers between devices, on_device(): lax.psum_scatter(grad_qkv.astype(jnp.bfloat16), ('ctx', 'grp'), scatter_d...  74.6 us
    all_gather x1, waiting for transfers between devices, on_device(): lax.all_gather(expand_weight.astype(jnp.bfloat16), ('ctx', 'grp'), axis=0...  67.7 us
    reduce_scatter x1, waiting for transfers between devices, on_device(): lax.psum_scatter(grad_shrink.astype(jnp.bfloat16), ('ctx', 'grp'), scatte...  65.4 us
    reduce_scatter x1, waiting for transfers between devices, on_device(): lax.psum_scatter(grad_out.astype(jnp.bfloat16), ('ctx', 'grp'), scatter_d...  44 us
    unnamed x161, local copies, waits for them, and re-layouts  43.2 us
    all_gather x1, waiting for transfers between devices, on_device(): lax.all_gather(qkv_weight.astype(jnp.bfloat16), ('ctx', 'grp'), axis=0, t...  37 us
  transfers between devices with their start and end apart: 13, of which 12 were waited for; matrix products, arithmetic and copies ran while one was open for 21% of the time, Pallas kernels for 0%

commit v1 on v0

v1 whole, which is shorter than its diff:
```python
import functools
import math

import jax
import jax.numpy as jnp
from jax import lax
from jax.experimental import pallas as pl
from jax.experimental.pallas import tpu as pltpu
from jax.sharding import PartitionSpec as P

D = 1024
QUERY_HEADS = 16
KEY_VALUE_HEADS = 8
HEAD_SIZE = 128
FF = 3072
STEP = 10
QUERY_FEATURES = 2048
KEY_FEATURES = 1024
GROUP = QUERY_HEADS // KEY_VALUE_HEADS

EPS_NORM = 1e-06
ROPE_BASE = 1000000.0
MASKED_SCORE = -1e30
BETA_ONE = 0.9
BETA_TWO = 0.95
ADAM_EPS = 1e-08
WEIGHT_DECAY = 0.1
RATE_QKV = 0.1
RATE_OUT = 0.5
RATE_EXPAND = 0.1
RATE_SHRINK = 0.06
RATE_GAINS = 0.6

SCALE = HEAD_SIZE**-0.5
EXP_SCALE = SCALE * math.log2(math.e)
LOW = jnp.bfloat16
FULL = jnp.float32
MIB = 1 << 20
HALVES = 2


def dot_nn(a, b):
    return jnp.dot(a, b, preferred_element_type=FULL)


def dot_nt(a, b):
    return lax.dot_general(a, b, (((1,), (1,)), ((), ())), preferred_element_type=FULL)


def dot_tn(a, b):
    return lax.dot_general(a, b, (((0,), (0,)), ((), ())), preferred_element_type=FULL)


def inverse_rms(values):
    return lax.rsqrt(jnp.mean(values * values, axis=-1, keepdims=True) + EPS_NORM)


def norm_back(values, gain, incoming):
    scale = inverse_rms(values)
    normed = values * scale
    scaled = incoming * gain
    grad = scale * (scaled - normed * jnp.mean(scaled * normed, axis=-1, keepdims=True))
    return grad, incoming * normed


def adam_step(weight, first_moment, second_moment, gradient, step_rate):
    first_moment = BETA_ONE * first_moment + (1.0 - BETA_ONE) * gradient
    second_moment = BETA_TWO * second_moment + (1.0 - BETA_TWO) * gradient * gradient
    fix_one = 1.0 - BETA_ONE**STEP
    fix_two = 1.0 - BETA_TWO**STEP
    step_dir = first_moment / fix_one / (jnp.sqrt(second_moment / fix_two) + ADAM_EPS)
    return (first_moment, second_moment, weight - step_rate * (step_dir + WEIGHT_DECAY * weight))


def assemble(parts, whole, blocks):
    rows = whole.shape[0] // len(parts)
    for part, block in zip(parts, blocks):
        whole[pl.ds(pl.multiple_of(block * rows, rows), rows), :] = part[...]


def all_rows(place_ref, n, inner):
    return [(place_ref[0] ^ s) * inner + (place_ref[1] ^ t) for s in range(n) for t in range(inner)]


def chip_rows(place_ref, inner):
    return [
        ((place_ref[0] & 1) ^ k) * inner + (place_ref[1] ^ t) for k in range(2) for t in range(inner)
    ]


ANYWHERE = pl.BlockSpec(memory_space=pl.ANY)


def resident(shape, column=0):
    return pl.BlockSpec(shape, lambda *_: (0, column), pipeline_mode=pl.Buffered(1))


def project_kernel(n, inner, place_ref, *refs):
    parts = refs[: n * inner]
    pieces = refs[n * inner : n * inner + n]
    gain_ref, gain_q_ref, gain_k_ref, cos_ref, sin_ref = refs[n * inner + n : n * inner + n + 5]
    normed_ref, q_ref, k_ref, v_ref, raw_ref = refs[n * inner + n + 5 : n * inner + n + 10]
    weight, token = refs[n * inner + n + 10 :]
    step = pl.program_id(0)

    @pl.when(step == 0)
    def _():
        assemble(parts, weight, all_rows(place_ref, n, inner))

    for s in range(n):

        @pl.when((place_ref[0] ^ step) == s)
        def _():
            token[...] = pieces[s][...]

    x = token[...].astype(FULL)
    normed = (x * inverse_rms(x) * gain_ref[...]).astype(LOW)
    normed_ref[...] = normed
    projected = dot_nn(normed, weight[...])
    q_half, k_half = q_ref.shape[1] // HALVES, k_ref.shape[1] // HALVES
    raw_half = q_half + k_half
    half = raw_half + k_half
    cos, sin = cos_ref[...], sin_ref[...]

    def turn(values, gain):
        values = values * inverse_rms(values) * gain
        return (values * cos + pltpu.roll(values, HEAD_SIZE // 2, 1) * sin).astype(LOW)

    for i in range(HALVES):
        first = i * half
        raw_ref[:, i * raw_half : (i + 1) * raw_half] = projected[:, first : first + raw_half].astype(LOW)
        v_ref[:, i * k_half : (i + 1) * k_half] = projected[:, first + raw_half : first + half].astype(LOW)
        for h in range(0, q_half, HEAD_SIZE):
            values = projected[:, first + h : first + h + HEAD_SIZE]
            q_ref[:, i * q_half + h : i * q_half + h + HEAD_SIZE] = turn(values, gain_q_ref[...])
        for h in range(0, k_half, HEAD_SIZE):
            values = projected[:, first + q_half + h : first + q_half + h + HEAD_SIZE]
            k_ref[:, i * k_half + h : i * k_half + h + HEAD_SIZE] = turn(values, gain_k_ref[...])


def project(place, parts, pieces, gain, gain_q, gain_k, cos, sin):
    n = len(pieces)
    inner = len(parts) // n
    block = pieces[0].shape[0]
    length = n * block
    width = parts[0].shape[1]
    q_width, k_width = width // 2, width // 4
    whole = lambda j, p: (0, 0)
    natural = lambda j, p: (j, 0)
    return pl.pallas_call(
        functools.partial(project_kernel, n, inner),
        out_shape=(
            jax.ShapeDtypeStruct((length, D), LOW),
            jax.ShapeDtypeStruct((length, q_width), LOW),
            jax.ShapeDtypeStruct((length, k_width), LOW),
            jax.ShapeDtypeStruct((length, k_width), LOW),
            jax.ShapeDtypeStruct((length, q_width + k_width), LOW),
        ),
        grid_spec=pltpu.PrefetchScalarGridSpec(
            num_scalar_prefetch=1,
            grid=(n,),
            in_specs=[resident(p.shape) for p in parts]
            + [resident((block, D))] * n
            + [
                pl.BlockSpec((1, D), whole),
                pl.BlockSpec((1, HEAD_SIZE), whole),
                pl.BlockSpec((1, HEAD_SIZE), whole),
                pl.BlockSpec((block, HEAD_SIZE), natural),
                pl.BlockSpec((block, HEAD_SIZE), natural),
            ],
            out_specs=(
                pl.BlockSpec((block, D), natural),
                pl.BlockSpec((block, q_width), natural),
                pl.BlockSpec((block, k_width), natural),
                pl.BlockSpec((block, k_width), natural),
                pl.BlockSpec((block, q_width + k_width), natural),
            ),
            scratch_shapes=[
                pltpu.VMEM((D, width), LOW),
                pltpu.VMEM((block, D), LOW),
            ],
        ),
        compiler_params=pltpu.CompilerParams(vmem_limit_bytes=40 * MIB),
        cost_estimate=pl.CostEstimate(
            flops=2 * length * D * width, bytes_accessed=16 * MIB, transcendentals=0
        ),
        name="project",
    )(place, *parts, *pieces, gain, gain_q, gain_k, cos, sin)


def attend_kernel(n, inner, first, has_base, place_ref, *refs):
    parts = refs[: 2 * inner]
    q_ref, k_ref, v_ref, seg_col_ref, seg_row_ref = refs[2 * inner : 2 * inner + 5]
    rest = refs[2 * inner + 5 + (2 if has_base else 0) :]
    attended_ref, total_ref, share_ref, weight = rest
    block = q_ref.shape[0]
    heads = k_ref.shape[1] // HEAD_SIZE
    step = pl.program_id(0)

    @pl.when(step == 0)
    def _():
        assemble(parts, weight, chip_rows(place_ref, inner))

    def work(j):
        size = (j + 1) * block
        same = seg_col_ref[...] == seg_row_ref[:, :size]
        own = lax.broadcasted_iota(jnp.int32, (block, size), 0) + j * block
        key = lax.broadcasted_iota(jnp.int32, (block, size), 1)
        allowed = same & (own >= key)
        allowed = jnp.concatenate([allowed] * GROUP, axis=0)
        outs, totals = [], []
        for h in range(heads):
            lanes = slice(h * HEAD_SIZE, (h + 1) * HEAD_SIZE)
            q = jnp.concatenate(
                [
                    q_ref[:, (h * GROUP + g) * HEAD_SIZE : (h * GROUP + g + 1) * HEAD_SIZE]
                    for g in range(GROUP)
                ],
                axis=0,
            )
            scores = jnp.where(allowed, dot_nt(q, k_ref[:size, lanes]), MASKED_SCORE)
            top = jnp.max(scores, axis=-1, keepdims=True)
            weights = jnp.exp2((scores - top) * EXP_SCALE)
            total = jnp.sum(weights, axis=-1, keepdims=True)
            out = dot_nn(weights.astype(LOW), v_ref[:size, lanes]) / total
            log_total = top * EXP_SCALE + jnp.log2(total)
            for g in range(GROUP):
                outs.append(out[g * block : (g + 1) * block].astype(LOW))
                totals.append(log_total[g * block : (g + 1) * block])
        attended = jnp.concatenate(outs, axis=1)
        attended_ref[...] = attended
        share_ref[...] = dot_nn(attended, weight[...]).astype(LOW)
        lane = lax.broadcasted_iota(jnp.int32, (block, HEAD_SIZE), 1)
        packed = jnp.zeros((block, HEAD_SIZE), FULL)
        for i, column in enumerate(totals):
            packed = jnp.where(lane == i, column, packed)
        total_ref[...] = packed

    place = place_ref[0] ^ (first + step)
    for j in range(n):
        pl.when(place == j)(functools.partial(work, j))


def attend(place, parts, q, k, v, seg_col, seg_row, n, chip, base):
    inner = len(parts) // 2
    length, q_width = q.shape
    k_width = k.shape[1]
    block = length // n
    first = 2 * chip
    whole = lambda i, p: (0, 0)
    natural = lambda i, p: (p[0] ^ (first + i), 0)
    slot = lambda i, p: (first + i, 0)
    plain = lambda i, p: (i, 0)
    base = list(base or ())
    before = 1 + len(parts) + 5
    return pl.pallas_call(
        functools.partial(attend_kernel, n, inner, first, bool(base)),
        out_shape=(
            jax.ShapeDtypeStruct((length, q_width), LOW),
            jax.ShapeDtypeStruct((length, HEAD_SIZE), FULL),
            jax.ShapeDtypeStruct((2 * block, D), LOW),
        ),
        grid_spec=pltpu.PrefetchScalarGridSpec(
            num_scalar_prefetch=1,
            grid=(2,),
            in_specs=[resident(p.shape) for p in parts]
            + [
                pl.BlockSpec((block, q_width), natural),
                resident((length, k_width)),
                resident((length, k_width)),
                pl.BlockSpec((block, 1), natural),
                pl.BlockSpec((1, length), whole),
            ]
            + [ANYWHERE] * len(base),
            out_specs=(
                pl.BlockSpec((block, q_width), slot),
                pl.BlockSpec((block, HEAD_SIZE), slot),
                pl.BlockSpec((block, D), plain),
            ),
            scratch_shapes=[pltpu.VMEM((q_width, D), LOW)],
        ),
        input_output_aliases={before: 0, before + 1: 1} if base else {},
        compiler_params=pltpu.CompilerParams(vmem_limit_bytes=48 * MIB),
        cost_estimate=pl.CostEstimate(
            flops=4 * block * q_width * (D + 2 * length), bytes_accessed=8 * MIB, transcendentals=0
        ),
        name="attend",
    )(place, *parts, q, k, v, seg_col, seg_row, *base)


def feed_kernel(chips, place_ref, *refs):
    gates, ups, shrinks = refs[:chips], refs[chips : 2 * chips], refs[2 * chips : 3 * chips]
    own_ref, other_ref, c_ref, c_other_ref = refs[3 * chips : 3 * chips + 4]
    x_out, c_out, active_ref, grad_ref, share_ref, share_other, back_ref, back_other = refs[3 * chips + 4 :]
    mine = pl.program_id(0) == 0
    x = jnp.where(mine, own_ref[...], other_ref[...])
    c_near, c_far = c_ref[0], c_other_ref[0]
    c = jnp.concatenate([jnp.where(mine, c_near, c_far), jnp.where(mine, c_far, c_near)], axis=0)
    x_out[...] = x
    c_out[...] = c
    size = gates[0].shape[1]
    share, back = 0.0, 0.0
    for s in range(chips):
        here = slice(s * size, (s + 1) * size)
        there = slice((chips + s) * size, (chips + s + 1) * size)
        gate = dot_nn(x, gates[s][...])
        up = dot_nn(x, ups[s][...])
        grad_active = dot_nt(c, shrinks[s][...]).astype(LOW).astype(FULL)
        gated = jax.nn.sigmoid(gate)
        silu = gate * gated
        active = (silu * up).astype(LOW)
        grad_gate = (grad_active * up * gated * (1.0 + gate * (1.0 - gated))).astype(LOW)
        grad_up = (grad_active * silu).astype(LOW)
        active_ref[:, here] = active
        grad_ref[:, here] = grad_gate
        grad_ref[:, there] = grad_up
        share = share + dot_nn(active, shrinks[s][...])
        back = back + dot_nt(grad_gate, gates[s][...]) + dot_nt(grad_up, ups[s][...])
    share = share.astype(LOW)
    back = back.astype(LOW)

    @pl.when(mine)
    def _():
        share_ref[...] = share
        back_ref[...] = back

    @pl.when(jnp.logical_not(mine))
    def _():
        share_other[...] = share
        back_other[...] = back


def feed(place, n, expand, shrink, own, other, c, c_other):
    chips = n // 2
    rows = own.shape[0]
    size = FF // n
    whole = lambda i, p: (0, 0)
    flat = lambda i, p: (i, 0)
    core = lambda i, p: ((p[0] & 1) ^ i, 0, 0)
    once = pl.Buffered(1)
    gates = [
        pl.BlockSpec((D, size), lambda i, p, s=s: (0, 2 * s + (p[0] & 1)), pipeline_mode=once)
        for s in range(chips)
    ]
    ups = [
        pl.BlockSpec((D, size), lambda i, p, s=s: (0, n + 2 * s + (p[0] & 1)), pipeline_mode=once)
        for s in range(chips)
    ]
    shrinks = [
        pl.BlockSpec((size, D), lambda i, p, s=s: (2 * s + (p[0] & 1), 0), pipeline_mode=once)
        for s in range(chips)
    ]
    wide = lambda w: jax.ShapeDtypeStruct((2 * rows, w), LOW)
    part = jax.ShapeDtypeStruct((rows, D), LOW)
    return pl.pallas_call(
        functools.partial(feed_kernel, chips),
        out_shape=(wide(D), wide(D), wide(FF // 2), wide(FF), part, part, part, part),
        grid_spec=pltpu.PrefetchScalarGridSpec(
            num_scalar_prefetch=1,
            grid=(2,),
            in_specs=gates
            + ups
            + shrinks
            + [
                resident((rows, D)),
                resident((rows, D)),
                pl.BlockSpec((1, rows // 2, D), core),
                pl.BlockSpec((1, rows // 2, D), core),
            ],
            out_specs=(
                pl.BlockSpec((rows, D), flat),
                pl.BlockSpec((rows, D), flat),
                pl.BlockSpec((rows, FF // 2), flat),
                pl.BlockSpec((rows, FF), flat),
                pl.BlockSpec((rows, D), whole),
                pl.BlockSpec((rows, D), whole),
                pl.BlockSpec((rows, D), whole),
                pl.BlockSpec((rows, D), whole),
            ),
        ),
        compiler_params=pltpu.CompilerParams(vmem_limit_bytes=56 * MIB),
        cost_estimate=pl.CostEstimate(
            flops=12 * rows * D * FF, bytes_accessed=30 * MIB, transcendentals=0
        ),
        name="feed",
    )(place, *[expand] * (2 * chips), *[shrink] * chips, own, other, c, c_other)


def back_kernel(n, inner, half, place_ref, *refs):
    qkv_parts = refs[: n * inner]
    out_parts = refs[n * inner : (n + 2) * inner]
    refs = refs[(n + 2) * inner :]
    (
        h_ref,
        attended_ref,
        total_ref,
        q_ref,
        k_ref,
        v_ref,
        raw_ref,
        cos_ref,
        sin_ref,
        seg_col_ref,
        seg_row_ref,
        gain_q_ref,
        gain_k_ref,
    ) = refs[:13]
    refs = refs[13:]
    if half:
        base_ref, refs = refs[0], refs[1:]
    grad_ref, share_ref, gains_ref, qkv, out, key_sum, value_sum = refs
    block = q_ref.shape[0]
    heads = k_ref.shape[1] // HEAD_SIZE
    step = pl.program_id(0)

    @pl.when(step == 0)
    def _():
        assemble(qkv_parts, qkv, all_rows(place_ref, n, inner))
        rows = out_parts[0].shape[0]
        size = out.shape[0] // rows
        for part, spot in zip(out_parts, chip_rows(place_ref, inner)):

            @pl.when(spot // size == half)
            def _():
                out[pl.ds(pl.multiple_of((spot % size) * rows, rows), rows), :] = part[...]

        key_sum[...] = jnp.zeros_like(key_sum)
        value_sum[...] = jnp.zeros_like(value_sum)
        gains_ref[...] = jnp.zeros_like(gains_ref)

    def work(j):
        size = (j + 1) * block
        grad_attended = dot_nt(h_ref[...], out[...]).astype(LOW)
        attended = attended_ref[...]
        totals = total_ref[...].T
        same = seg_col_ref[:size, :] == seg_row_ref[:, j * block : size]
        key = lax.broadcasted_iota(jnp.int32, (size, block), 0)
        own = lax.broadcasted_iota(jnp.int32, (size, block), 1) + j * block
        allowed = same & (own >= key)
        allowed = jnp.concatenate([allowed] * GROUP, axis=1)
        cos, sin = cos_ref[...], sin_ref[...]
        gains = gains_ref[...]
        kind = lax.broadcasted_iota(jnp.int32, gains.shape, 0)

        def head_back(grad, values, gain):
            grad = grad * cos + pltpu.roll(grad * sin, HEAD_SIZE // 2, 1)
            grad, gain_part = norm_back(values.astype(FULL), gain, grad)
            return grad.astype(LOW), jnp.sum(gain_part, axis=0, keepdims=True)

        query_grads, key_grads, value_grads = [], [], []
        for h in range(heads):
            lanes = slice(h * HEAD_SIZE, (h + 1) * HEAD_SIZE)
            k, v = k_ref[:size, lanes], v_ref[:size, lanes]
            head_lanes = [
                slice((h * GROUP + g) * HEAD_SIZE, (h * GROUP + g + 1) * HEAD_SIZE)
                for g in range(GROUP)
            ]
            q = jnp.concatenate([q_ref[:, s] for s in head_lanes], axis=0)
            up = jnp.concatenate([grad_attended[:, s] for s in head_lanes], axis=0)
            seen = jnp.concatenate([attended[:, s] for s in head_lanes], axis=0)
            log_total = jnp.concatenate(
                [totals[(half * heads + h) * GROUP + g : (half * heads + h) * GROUP + g + 1, :] for g in range(GROUP)], axis=1
            )
            row = jnp.sum(up.astype(FULL) * seen.astype(FULL), axis=1, keepdims=True)
            row = jnp.broadcast_to(row, (GROUP * block, HEAD_SIZE)).T[:1, :]
            probs = jnp.where(allowed, jnp.exp2(dot_nt(k, q) * EXP_SCALE - log_total), 0.0)
            grad_probs = dot_nt(v, up)
            grad_scores = (probs * (grad_probs - row)).astype(LOW)
            value_sum[:size, lanes] += dot_nn(probs.astype(LOW), up)
            key_sum[:size, lanes] += dot_nn(grad_scores, q)
            query_grad = dot_tn(grad_scores, k) * SCALE
            for g in range(GROUP):
                grad, gain_part = head_back(
                    query_grad[g * block : (g + 1) * block], raw_ref[:, head_lanes[g]], gain_q_ref[...]
                )
                query_grads.append(grad)
                gains = jnp.where(kind == 0, gains + gain_part, gains)
        own_rows = slice(j * block, size)
        for h in range(heads):
            lanes = slice(h * HEAD_SIZE, (h + 1) * HEAD_SIZE)
            first = (heads * GROUP + h) * HEAD_SIZE
            grad, gain_part = head_back(
                key_sum[own_rows, lanes] * SCALE, raw_ref[:, first : first + HEAD_SIZE], gain_k_ref[...]
            )
            key_grads.append(grad)
            gains = jnp.where(kind == 1, gains + gain_part, gains)
            value_grads.append(value_sum[own_rows, lanes].astype(LOW))
        gains_ref[...] = gains
        grad = jnp.concatenate(query_grads + key_grads + value_grads, axis=1)
        grad_ref[...] = grad
        share = dot_nt(grad, qkv[...])
        if half:
            share = share + base_ref[...].astype(FULL)
        share_ref[...] = share.astype(LOW)

    for j in range(n):
        pl.when(step == n - 1 - j)(functools.partial(work, j))


def back(
    place, qkv_parts, out_parts, hidden_grad, attended, totals, q, k, v, raw, cos, sin, seg_col,
    seg_row, gain_q, gain_k, half, base,
):
    inner = len(out_parts) // 2
    n = len(qkv_parts) // inner
    length = q.shape[0]
    q_width, k_width = q.shape[1] // HALVES, k.shape[1] // HALVES
    block = length // n
    width = q_width + 2 * k_width
    whole = lambda i, p: (0, 0)
    natural = lambda i, p: (n - 1 - i, 0)
    slot = lambda i, p: (p[0] ^ (n - 1 - i), 0)
    natural_half = lambda i, p: (n - 1 - i, half)
    slot_half = lambda i, p: (p[0] ^ (n - 1 - i), half)
    base = [] if base is None else [base]
    return pl.pallas_call(
        functools.partial(back_kernel, n, inner, half),
        out_shape=(
            jax.ShapeDtypeStruct((length, width), LOW),
            jax.ShapeDtypeStruct((length, D), LOW),
            jax.ShapeDtypeStruct((8, HEAD_SIZE), FULL),
        ),
        grid_spec=pltpu.PrefetchScalarGridSpec(
            num_scalar_prefetch=1,
            grid=(n,),
            in_specs=[resident((p.shape[0], width), half) for p in qkv_parts]
            + [resident(p.shape) for p in out_parts]
            + [
                pl.BlockSpec((block, D), slot),
                pl.BlockSpec((block, q_width), slot_half),
                pl.BlockSpec((block, HEAD_SIZE), slot),
                pl.BlockSpec((block, q_width), natural_half),
                resident((length, k_width), half),
                resident((length, k_width), half),
                pl.BlockSpec((block, q_width + k_width), natural_half),
                pl.BlockSpec((block, HEAD_SIZE), natural),
                pl.BlockSpec((block, HEAD_SIZE), natural),
                pl.BlockSpec((length, 1), whole),
                pl.BlockSpec((1, length), whole),
                pl.BlockSpec((1, HEAD_SIZE), whole),
                pl.BlockSpec((1, HEAD_SIZE), whole),
            ]
            + [pl.BlockSpec((block, D), slot)] * len(base),
            out_specs=(
                pl.BlockSpec((block, width), natural),
                pl.BlockSpec((block, D), slot),
                pl.BlockSpec((8, HEAD_SIZE), whole),
            ),
            scratch_shapes=[
                pltpu.VMEM((D, width), LOW),
                pltpu.VMEM((q_width, D), LOW),
                pltpu.VMEM((length, k_width), FULL),
                pltpu.VMEM((length, k_width), FULL),
            ],
        ),
        compiler_params=pltpu.CompilerParams(vmem_limit_bytes=56 * MIB),
        cost_estimate=pl.CostEstimate(
            flops=2 * length * D * (q_width + width) + 5 * length * length * q_width,
            bytes_accessed=30 * MIB,
            transcendentals=0,
        ),
        name="back",
    )(
        place, *qkv_parts, *out_parts, hidden_grad, attended, totals, q, k, v, raw, cos, sin,
        seg_col, seg_row, gain_q, gain_k, *base,
    )


def adam_kernel(rate, blocks, key_ref, *refs):
    cuts = refs[:HALVES]
    weight_ref, first_ref, second_ref, new_first, new_second, new_weight, grad = refs[HALVES:]
    for i in range(HALVES):

        @pl.when(pl.program_id(0) // blocks == i)
        def _():
            grad[...] = cuts[i][0].astype(FULL)

    results = adam_step(weight_ref[...], first_ref[...], second_ref[...], grad[...], rate)
    new_first[...], new_second[...], new_weight[...] = results


def adam_cuts(key, cuts, weight, first, second, rate, size, column):
    chips, rows, columns = cuts[0].shape
    blocks = columns // size
    place = lambda i, s, p: (0, column(i, s))
    slot = lambda i, s, p: (p[0] ^ s, 0, i % blocks)
    spec = pl.BlockSpec((rows, size), place)
    shape = jax.ShapeDtypeStruct(weight.shape, FULL)
    return pl.pallas_call(
        functools.partial(adam_kernel, rate, blocks),
        out_shape=(shape, shape, shape),
        grid_spec=pltpu.PrefetchScalarGridSpec(
            num_scalar_prefetch=1,
            grid=(HALVES * blocks, chips),
            in_specs=[pl.BlockSpec((1, rows, size), slot)] * HALVES + [spec] * 3,
            out_specs=(spec,) * 3,
            scratch_shapes=[pltpu.VMEM((rows, size), FULL)],
        ),
        cost_estimate=pl.CostEstimate(
            flops=20 * weight.size, bytes_accessed=26 * weight.size, transcendentals=weight.size
        ),
        compiler_params=pltpu.CompilerParams(vmem_limit_bytes=24 * MIB),
        name="adam_cuts",
    )(key, *cuts, weight, first, second)


def adam_pair_kernel(rate, place_ref, own_ref, other_ref, weight_ref, first_ref, second_ref, *outs):
    mine = pl.program_id(1) == (place_ref[0] & 1)
    grad = jnp.where(mine, own_ref[...].astype(FULL), other_ref[...].astype(FULL))
    results = adam_step(weight_ref[...], first_ref[...], second_ref[...], grad, rate)
    outs[0][...], outs[1][...], outs[2][...] = results


def adam_pair(place, own, other, weight, first, second, rate, size):
    rows, width = own.shape
    cut = pl.BlockSpec((rows, size), lambda i, c, p: (0, i))
    spec = pl.BlockSpec((rows, size), lambda i, c, p: (0, 2 * i + c))
    shape = jax.ShapeDtypeStruct(weight.shape, FULL)
    return pl.pallas_call(
        functools.partial(adam_pair_kernel, rate),
        out_shape=(shape, shape, shape),
        grid_spec=pltpu.PrefetchScalarGridSpec(
            num_scalar_prefetch=1,
            grid=(width // size, 2),
            in_specs=[cut, cut] + [spec] * 3,
            out_specs=(spec,) * 3,
        ),
        cost_estimate=pl.CostEstimate(
            flops=20 * weight.size, bytes_accessed=26 * weight.size, transcendentals=weight.size
        ),
        compiler_params=pltpu.CompilerParams(vmem_limit_bytes=24 * MIB),
        name="adam_pair",
    )(place, own, other, weight, first, second)


def sum_kernel(lead, take, key_ref, kept_ref, landed_ref, *outs):
    size = outs[0].shape
    kept, landed = kept_ref[...].reshape(size), landed_ref[...].reshape(size)
    if take:
        total = jnp.where(key_ref[0] > 0, landed, kept)
    else:
        total = (kept.astype(FULL) + landed.astype(FULL)).astype(LOW)
    for s in range(lead):

        @pl.when(pl.program_id(0) == s)
        def _():
            outs[s][...] = total


def sum_parts(key, kept, kept_map, landed, landed_map, lead, steps, rows, take=False):
    columns = kept.shape[-1]

    def spec(array, place):
        ones = (1,) * (array.ndim - 2)
        return pl.BlockSpec(ones + (rows, columns), lambda i, j, p: (*place(i, j, p), 0))

    def out(s):
        spot = lambda i, j: jnp.where(i == s, j, jnp.where(i < s, 0, steps - 1))
        return pl.BlockSpec((1, rows, columns), lambda i, j, p: (spot(i, j), 0, 0))

    return pl.pallas_call(
        functools.partial(sum_kernel, lead, take),
        out_shape=(jax.ShapeDtypeStruct((steps, rows, columns), LOW),) * lead,
        grid_spec=pltpu.PrefetchScalarGridSpec(
            num_scalar_prefetch=1,
            grid=(lead, steps),
            in_specs=[spec(kept, kept_map), spec(landed, landed_map)],
            out_specs=tuple(out(s) for s in range(lead)),
        ),
        cost_estimate=pl.CostEstimate(flops=0, bytes_accessed=0, transcendentals=0),
        name="sum_parts",
    )(key, kept, landed)


def stack_kernel(*refs):
    for s, ref in enumerate(refs[:-1]):
        refs[-1][s] = ref[...]


def stack_parts(parts):
    rows, columns = parts[0].shape
    return pl.pallas_call(
        stack_kernel,
        out_shape=jax.ShapeDtypeStruct((len(parts), rows, columns), LOW),
        cost_estimate=pl.CostEstimate(flops=0, bytes_accessed=0, transcendentals=0),
        name="stack_parts",
    )(*parts)


def after(value, *others):
    return lax.optimization_barrier((value, *others))[0]


def make(n, inner, reps):
    chips = n // 2

    def swap_ctx(value, s):
        return lax.ppermute(value, "ctx", [(i, i ^ s) for i in range(n)])

    def swap_core(value):
        return swap_ctx(value, 1)

    def swap_chip(value, s):
        return swap_ctx(value, 2 * s)

    def swap_grp(value, t):
        return lax.ppermute(value, "grp", [(i, i ^ t) for i in range(inner)])

    def swap_rep(value, r):
        return lax.ppermute(value, "rep", [(i, i ^ r) for i in range(reps)])

    def over_chips(value):
        return [value] + [swap_chip(value, s) for s in range(1, chips)]

    def over_grp(value):
        return [value] + [swap_grp(value, t) for t in range(1, inner)]

    def sum_of(parts):
        total = parts[0].astype(FULL)
        for part in parts[1:]:
            total = total + part.astype(FULL)
        return total

    def swap_plane(value, s, t):
        pairs = [(c * inner + g, (c ^ s) * inner + (g ^ t)) for c in range(n) for g in range(inner)]
        return lax.ppermute(value, ("ctx", "grp"), pairs)

    def pick(value, axis, index):
        return lax.dynamic_index_in_dim(value, index, axis, False)

    middle = reps // 2
    hops = [([(k, k + 1), (reps - 1 - k, reps - 2 - k)], None) for k in range(middle - 1)]
    hops.append(([(middle - 1, middle), (middle, middle - 1)], None))
    hops += [
        ([(k, k - 1), (reps - 1 - k, reps - k)], (k - 1, reps - k)) for k in range(middle - 1, 0, -1)
    ]

    def gather_reps(value):
        return [value] + [swap_rep(value, r) for r in range(1, reps)]

    def on_device(
        tokens,
        segment_ids,
        positions,
        cotangent,
        qkv_weight,
        qkv_first,
        qkv_second,
        out_weight,
        out_first,
        out_second,
        expand_weight,
        expand_first,
        expand_second,
        shrink_weight,
        shrink_first,
        shrink_second,
        norm_gains,
        gains_first,
        gains_second,
    ):
        seqs, block, _ = tokens.shape
        length = n * block
        me = lax.axis_index("ctx")
        core = me & 1
        chip = me >> 1
        mine = lax.axis_index("grp")
        place = jnp.stack([me, mine]).astype(jnp.int32)
        order = me ^ jnp.arange(n)
        q_width = QUERY_FEATURES // chips
        k_width = KEY_FEATURES // chips
        width = q_width + 2 * k_width
        rows = qkv_weight.shape[0]

        rep = lax.axis_index("rep")

        def qkv_piece(s):
            to = chip ^ s
            parts = []
            for i in range(HALVES):
                for first, size in ((0, q_width), (QUERY_FEATURES, k_width), (QUERY_FEATURES + KEY_FEATURES, k_width)):
                    start = first + to * size + i * (size // HALVES)
                    parts.append(lax.dynamic_slice_in_dim(qkv_weight, start, size // HALVES, 1))
            return jnp.concatenate(parts, axis=1).astype(LOW)

        small = jnp.concatenate(
            [
                segment_ids.reshape(-1).astype(FULL),
                positions.reshape(-1).astype(FULL),
                norm_gains.astype(LOW).astype(FULL),
            ]
        ).reshape(1, -1)
        small = [
            swap_plane(small, s, t) if s or t else small for s in range(n) for t in range(inner)
        ]
        tokens, qkv_low, out_low, expand_low, shrink_low, other_tokens, *small = lax.optimization_barrier(
            (
                tokens,
                [qkv_piece(s) for s in range(chips)],
                out_weight.astype(LOW),
                expand_weight.astype(LOW),
                shrink_weight.astype(LOW),
                pick(tokens, 0, core ^ 1),
                *small,
            )
        )
        small = jnp.stack(small)
        small = small.reshape(n, inner, -1)[order]
        notes = small[:, 0, : 2 * seqs * block].reshape(n, 2, seqs, block)
        notes = pick(notes, 2, core)
        notes = jnp.moveaxis(notes, 0, 1).reshape(2, length)
        gains = small[:, mine ^ jnp.arange(inner), 2 * seqs * block :].reshape(1, -1)
        gain_one, gain_two = gains[:, :D], gains[:, D : 2 * D]
        gain_query = gains[:, 2 * D : 2 * D + HEAD_SIZE]
        gain_key = gains[:, 2 * D + HEAD_SIZE :]

        token_slots = [pick(tokens, 0, core), swap_core(other_tokens)]
        for s in range(1, chips):
            token_slots += [swap_chip(part, s) for part in token_slots[:2]]

        landed = [qkv_low[0]] + [swap_chip(qkv_low[s], s) for s in range(1, chips)]
        qkv_parts = []
        for part in landed:
            near = over_grp(part)
            qkv_parts += near + [swap_core(p) for p in near]

        near = over_grp(out_low)
        out_parts = near + [swap_core(p) for p in near]
        expand_full = lax.all_gather(expand_low, ("ctx", "grp"), axis=0, tiled=True)
        shrink_full = lax.all_gather(shrink_low, ("ctx", "grp"), axis=0, tiled=True)
        other_cotangent = swap_core(cotangent)

        ladder = jnp.arange(HEAD_SIZE) % (HEAD_SIZE // 2)
        frequency = jnp.exp(ladder.astype(FULL) * (-2.0 * math.log(ROPE_BASE) / HEAD_SIZE))
        angles = notes[1][:, None] * frequency[None, :]
        sign = jnp.where(jnp.arange(HEAD_SIZE) < HEAD_SIZE // 2, -1.0, 1.0)
        cos, sin = jnp.cos(angles), jnp.sin(angles) * sign
        seg_col, seg_row = notes[0][:, None], notes[0][None, :]

        normed, q, k, v, raw = project(
            place, qkv_parts, token_slots, gain_one, gain_query, gain_key, cos, sin
        )
        base, shares = None, []
        for s in range(chips - 1, -1, -1):
            *base, share = attend(place, out_parts, q, k, v, seg_col, seg_row, n, s, base)
            shares.append(swap_chip(share, s) if s else share)
        attended, totals = base
        inputs = jnp.concatenate(token_slots[:2]).astype(FULL)
        hidden = inputs + sum_of(shares)
        normed_two = (hidden * inverse_rms(hidden) * gain_two).astype(LOW)

        x_all, c_all, active, grad_gate_up, share, share_other, back_share, back_other = feed(
            place, n, expand_full, shrink_full, normed_two, swap_core(normed_two), cotangent,
            other_cotangent,
        )
        normed_grad = sum_of([back_share, swap_core(back_other)])
        hidden_grad, gain_part = norm_back(hidden, gain_two, normed_grad)
        gain_two_grad = jnp.sum(gain_part, axis=0)
        hidden_grad = hidden_grad + c_all[: 2 * block].astype(FULL)
        hidden_low = hidden_grad.astype(LOW)
        grad_slots = over_chips(hidden_low)
        grad_all = jnp.concatenate(grad_slots)

        def by_sequence(kept, landed):
            return jnp.where(core == 0, jnp.stack([kept, landed]), jnp.stack([landed, kept]))

        output = (hidden + sum_of([share, swap_core(share_other)])).astype(LOW)
        output = by_sequence(output[:block], swap_core(output[block:]))

        where = jnp.stack([chip, core, mine]).astype(jnp.int32)
        ends = {}
        for _, takes in hops:
            if takes:
                ends[takes] = ((rep == takes[0]) | (rep == takes[1])).astype(jnp.int32).reshape(1)
        line = []

        def next_sums(kept, kept_map, sent, sent_map, lead, steps, block_rows):
            for i, value in enumerate(sent):
                value = after(value, *line)
                totals = sum_parts(where, kept, kept_map, value, sent_map, lead, steps, block_rows)
                if i + 1 < len(sent):
                    kept, kept_map = jnp.stack(totals), lambda i, j, p: (i, j, 0)
            line[:] = [totals[0]]
            return totals

        def next_sum(kept, sent):
            plain = lambda i, j, p: (j, 0)
            for value in sent:
                value = after(value, *line)
                steps, block_rows = kept.shape[:2]
                (kept,) = sum_parts(where, kept, plain, value, plain, 1, steps, block_rows)
            line[:] = [kept]
            return kept

        def go(value, step=0):
            return [value, lax.ppermute(value, "rep", hops[step][0]), step]

        def step_on(trip):
            value, landed, step = trip
            if step == len(hops):
                return
            landed = after(landed, *line)
            takes = hops[step][1]
            plain = lambda i, j, p: (j, 0)
            (value,) = sum_parts(
                where if takes is None else ends[takes], value, plain, landed, plain, 1,
                value.shape[0], value.shape[1], takes is not None,
            )
            line[:] = [value]
            step += 1
            trip[:] = go(value, step) if step < len(hops) else [value, None, step]

        def send_x(parts):
            return parts[0], [swap_chip(parts[s], s) for s in range(1, chips)]

        def send_y(parts):
            return parts[0], [swap_grp(parts[t], t) for t in range(1, inner)]

        def back_part(half, attended, back_all):
            return back(
                place, qkv_parts, out_parts, grad_all, attended, totals, q, k, v, raw, cos, sin,
                seg_col, seg_row, gain_query, gain_key, half, back_all,
            )

        def cut_qkv(grad):
            grad_qkv = dot_tn(normed, grad).astype(LOW)
            cuts = grad_qkv.reshape(chips, 2, inner, rows, width // HALVES)
            return cuts, swap_core(pick(cuts, 1, core ^ 1))

        def sum_qkv_core(cuts, landed):
            return next_sums(
                cuts, lambda i, j, p: (j, p[1], p[2] ^ i, 0), [landed], lambda i, j, p: (j, p[2] ^ i, 0),
                inner, chips, rows,
            )

        def sum_by_chip(kept, sent, block_rows):
            place_of = lambda i, j, p: (p[0] ^ i, 0)
            return next_sums(kept, place_of, sent, place_of, chips, 1, block_rows)

        x_late, active_late = lax.optimization_barrier((x_all, active, hidden_low))[:2]
        grad_expand = dot_tn(x_late, grad_gate_up).astype(LOW)
        expand_cuts = grad_expand.reshape(chips, 2, inner, rows, FF)
        cut = pick(expand_cuts, 1, core ^ 1)
        other_sent = [swap_grp(pick(cut, 1, mine ^ t), t) for t in range(1, inner)]
        grad_shrink = dot_tn(active_late, c_all).astype(LOW)
        ff_rows = FF // (n * inner)
        shrink_cuts = grad_shrink.reshape(chips, inner, ff_rows, D)
        shrink_sent = [swap_grp(pick(shrink_cuts, 1, mine ^ t), t) for t in range(1, inner)]
        cut = pick(expand_cuts, 1, core)

        def own_rows(t, s):
            return pick(pick(cut, 0, chip ^ s), 0, mine ^ t)

        far_sent = [
            [swap_chip(after(own_rows(t, s), grad_slots[-1]), s) for s in range(1, chips)]
            for t in range(1, inner)
        ]

        grad_out = dot_tn(attended, grad_all).astype(LOW)
        out_rows = out_weight.shape[0]
        out_cuts = grad_out.reshape(2, inner, out_rows, D)
        out_sent = swap_core(pick(out_cuts, 0, core ^ 1))
        attended = after(attended, out_cuts)
        grad_one, back_all, gains_one = back_part(0, attended, None)

        line[:] = [gains_one]
        first_cuts, first_landed = cut_qkv(grad_one)
        other_cut = send_x(
            next_sums(
                expand_cuts, lambda i, j, p: (p[0] ^ i, p[1] ^ 1, p[2], 0), other_sent,
                lambda i, j, p: (p[0] ^ i, 0), chips, 1, rows,
            )
        )
        own_sent = []
        for t in range(1, inner):
            sent = [value[None] for value in far_sent[t - 1]]
            (total,) = next_sums(
                expand_cuts, lambda i, j, p, t=t: (p[0], p[1], p[2] ^ t, 0), sent,
                lambda i, j, p: (j, 0), 1, 1, rows,
            )
            own_sent.append(swap_grp(total, t))
        near_sent = [swap_chip(after(own_rows(0, s), *line), s)[None] for s in range(1, chips)]
        out_cut = send_y(
            next_sums(
                out_cuts, lambda i, j, p: (p[1], p[2] ^ i, 0), [out_sent],
                lambda i, j, p: (p[2] ^ i, 0), inner, 1, out_rows,
            )
        )
        attended, back_all = lax.optimization_barrier((attended, back_all, first_cuts, *line))[:2]
        grad_two, back_all, gains_two = back_part(1, attended, back_all)

        line[:] = [gains_two]
        (own_cut,) = next_sums(
            expand_cuts, lambda i, j, p: (p[0], p[1], p[2], 0), near_sent, lambda i, j, p: (j, 0), 1, 1, rows
        )
        shrink_cut = send_x(
            next_sums(
                shrink_cuts, lambda i, j, p: (p[0] ^ i, p[2], 0), shrink_sent,
                lambda i, j, p: (p[0] ^ i, 0), chips, 1, ff_rows,
            )
        )
        other_cut = swap_core(next_sum(*other_cut))
        own = go(next_sum(own_cut, own_sent))
        first_cut = send_y(sum_qkv_core(first_cuts, first_landed))
        second_cuts, second_landed = cut_qkv(after(grad_two, *line))
        other_cut = after(other_cut, *line)
        line[:] = [other_cut]
        other = go(other_cut)
        second_cut = send_y(sum_qkv_core(second_cuts, second_landed))
        shares = []
        for s in range(1, chips):
            share = after(back_all[2 * s * block : 2 * (s + 1) * block], *line)
            shares.append(swap_chip(share, s))
        out = go(next_sum(*out_cut))
        shrink = go(next_sum(*shrink_cut))

        def stacked(on_the_way):
            kept, sent = on_the_way
            total = stack_parts([kept[0]] + [after(value, *line)[0] for value in sent])
            line[:] = [total]
            return total

        step_on(own)
        first_cut = send_x(sum_by_chip(*first_cut, rows))
        step_on(other)
        second_cut = send_x(sum_by_chip(*second_cut, rows))
        first = go(stacked(first_cut))
        step_on(own)

        shares = [back_all[: 2 * block]] + [after(value, *line) for value in shares]
        input_part, gain_part = norm_back(inputs, gain_one, sum_of(shares))
        gain_one_grad = jnp.sum(gain_part, axis=0)
        input_grad = (input_part + hidden_grad).astype(LOW)
        input_landed = swap_core(input_grad[block:])
        head_gains = gains_one + gains_two
        grad_gains = jnp.concatenate([gain_one_grad, gain_two_grad, head_gains[0], head_gains[1]])
        grad_gains = grad_gains.reshape(n, inner, 1, -1)
        gains_sent = [
            swap_plane(pick(pick(grad_gains, 0, me ^ s), 0, mine ^ t), s, t)
            for s in range(n)
            for t in range(inner)
            if s or t
        ]
        line[:] = [gain_one_grad]

        step_on(out)
        second = go(stacked(second_cut))
        step_on(other)
        step_on(own)
        gains_sent = lax.optimization_barrier((*gains_sent, *line))[:-1]
        total_gains = sum_of([pick(pick(grad_gains, 0, me), 0, mine), *gains_sent])
        gains_sent = gather_reps(total_gains)
        step_on(shrink)
        step_on(out)
        step_on(other)
        step_on(first)
        step_on(shrink)
        step_on(out)
        step_on(second)
        step_on(first)
        step_on(shrink)
        step_on(second)
        step_on(first)
        step_on(second)
        trips = (own, other, out, shrink, first, second)
        for _ in hops:
            for trip in trips:
                step_on(trip)
        own_cut, other_cut, total_out, total_shrink, *qkv_cuts = [trip[0] for trip in trips]
        total_shrink, total_out, other_cut, own_cut = (
            value[0] for value in (total_shrink, total_out, other_cut, own_cut)
        )
        total_gains = sum_of(lax.optimization_barrier((*gains_sent, *line))[:-1])[0]
        input_grad = by_sequence(input_grad[:block], input_landed)

        size = k_width // HALVES

        def qkv_column(i, s):
            per_half = width // HALVES // size
            half, i = i // per_half, i % per_half
            q_blocks = q_width // HALVES // size
            q_place = (s * HALVES + half) * q_blocks + i
            k_place = QUERY_FEATURES // size + s * HALVES + half
            v_place = k_place + KEY_FEATURES // size
            return jnp.where(i < q_blocks, q_place, jnp.where(i == q_blocks, k_place, v_place))

        key = chip.reshape(1).astype(jnp.int32)
        return (
            output,
            input_grad,
            *adam_cuts(key, qkv_cuts, qkv_weight, qkv_first, qkv_second, RATE_QKV, size, qkv_column),
            *adam_step(out_weight, out_first, out_second, total_out.astype(FULL), RATE_OUT),
            *adam_pair(
                place, own_cut, other_cut, expand_weight, expand_first, expand_second, RATE_EXPAND,
                FF // n,
            ),
            *adam_step(
                shrink_weight, shrink_first, shrink_second, total_shrink.astype(FULL), RATE_SHRINK
            ),
            *adam_step(norm_gains, gains_first, gains_second, total_gains, RATE_GAINS),
        )

    return on_device


def solution(mesh):
    token_rows = P(("grp", "rep"), "ctx", None)
    token_notes = P(("grp", "rep"), "ctx")
    weight_rows = P(("ctx", "grp"), None)
    gain_rows = P(("ctx", "grp"))
    states = (weight_rows,) * 12 + (gain_rows,) * 3
    return jax.shard_map(
        make(mesh.shape["ctx"], mesh.shape["grp"], mesh.shape["rep"]),
        mesh=mesh,
        in_specs=(token_rows, token_notes, token_notes, token_rows) + states,
        out_specs=(token_rows, token_rows) + states,
        check_vma=False,
    )
```

time: 1030 us -> 584 us (0.57)
  waiting for transfers between devices: 591 us -> 128 us
  Pallas kernels: 0 us -> 226 us
  matrix products: 164 us -> 23.7 us
  starting transfers between devices: 1 us -> 89.3 us
  other arithmetic: 96.2 us -> 42.2 us
  local copies, waits for them, and re-layouts: 105 us -> 51.2 us
  blocking collectives: 48.4 us -> 0 us
    reduce_scatter x5 -> x0, waiting for transfers between devices: 317 us -> none  [the longest x1 95.9 us: on_device(): lax.psum_scatter(grad_expand.astype(jnp.bfloat16), ('ctx', 'grp'), scatte...]
    pallas_call x0 -> x41, Pallas kernels: none -> 226 us  [the longest x31 92.4 us: sum_parts(): pl.pallas_call(functools.partial(sum_kernel, lead, take), out_shape=(jax....]
    dot_general x19 -> x5, matrix products: 164 us -> 23.7 us  [dot_tn(): lax.dot_general(a, b, (((0,), (0,)), ((), ())), preferred_element_type=FULL)]
    all_gather x6 -> x2, waiting for transfers between devices: 138 us -> 18.2 us  [the longest x1 18.2 us: on_device(): expand_full = lax.all_gather(expand_low, ('ctx', 'grp'), axis=0, tiled=True)]
    ppermute x0 -> x73, waiting for transfers between devices: none -> 109 us  [the longest x29 63.5 us: swap_ctx(): return lax.ppermute(value, 'ctx', [(i, i ^ s) for i in range(n)])]
    psum x1 -> x0, waiting for transfers between devices: 99.1 us -> none  [on_device(): lax.psum(shard_qkv.astype(jnp.bfloat16), 'rep').astype(jnp.float32)]
    ppermute x0 -> x73, starting transfers between devices: none -> 89.3 us  [the longest x18 45.1 us: go(): return [value, lax.ppermute(value, 'rep', hops[step][0]), step]]
    unnamed x14 -> x2, waiting for transfers between devices: 37 us -> 0.71 us
  transfers between devices with their start and end apart: 13 -> 75, of which waited for: 12 -> 15; matrix products, arithmetic and copies ran while one was open for 21% -> 13% of each run, Pallas kernels for 0% -> 31%
where the time goes in v1:
time: 584 us; the launch traced here: 575 us
  Pallas kernels  226 us (39%)
  waiting for transfers between devices  128 us (22%)
  starting transfers between devices  89.3 us (15%)
  local copies, waits for them, and re-layouts  51.2 us (9%)
  other arithmetic  42.2 us (7%)
  matrix products  23.7 us (4%)
  between operations  15.2 us (3%)
    pallas_call x31, Pallas kernels, sum_parts(): pl.pallas_call(functools.partial(sum_kernel, lead, take), out_shape=(jax....  92.4 us
    ppermute x29, waiting for transfers between devices, swap_ctx(): return lax.ppermute(value, 'ctx', [(i, i ^ s) for i in range(n)])  63.5 us
    pallas_call x2, Pallas kernels, back(): pl.pallas_call(functools.partial(back_kernel, n, inner, half), out_shape=...  47.6 us
    ppermute x18, starting transfers between devices, go(): return [value, lax.ppermute(value, 'rep', hops[step][0]), step]  45.1 us
    pallas_call x1, Pallas kernels, feed(): pl.pallas_call(functools.partial(feed_kernel, chips), out_shape=(wide(D),...  36.9 us
    unnamed x153, local copies, waits for them, and re-layouts  34.8 us
    ppermute x9, waiting for transfers between devices, swap_grp(): return lax.ppermute(value, 'grp', [(i, i ^ t) for i in range(inner)])  24.3 us
    dot_general x5, matrix products, dot_tn(): lax.dot_general(a, b, (((0,), (0,)), ((), ())), preferred_element_type=FULL)  23.7 us
  transfers between devices with their start and end apart: 75, of which 15 were waited for; matrix products, arithmetic and copies ran while one was open for 13% of the time, Pallas kernels for 31%

profile of v1, /device:TPU:0, one launch (start us, length us, event | category | flops | bytes accessed | tf_op | source)
XLA Modules:
  0.0 575.1 jit_solution(6889337256904563800)
XLA Ops:
  28.0 3.4 convert_element_type.107
  40.8 15.1 %collective-permute-done.14.refs_4_ = bf16[128,2048]{1,0:T(8,128)(2,1)} collective-permute-done((bf16[128,2048]{1,0:T(8,128)(2,1)}, bf16[128,2048]{1,0:T(8,128)(2,1)}, u32[]{:S(2)}, u32[]{:S(2)}) %collective-permute-start.14) | collective-permute-done | bytes 524320 | tf_op jit(solution)/shard_map/ppermute | solution.py:698
  62.9 7.2 %collective-permute-done.18.refs_10_ = bf16[256,1024]{1,0:T(8,128)(2,1)S(1)} collective-permute-done((bf16[256,1024]{1,0:T(8,128)(2,1)S(1)}, bf16[256,1024]{1,0:T(8,128)(2,1)S(1)}, u32[]{:S(2)}, u32[]{:S(2)}) %collective-permute-start.18) | collective-permute-done | bytes 524320 | tf_op jit(solution)/shard_map/ppermute | solution.py:698
  76.3 20.2 %collective-permute-done.8.refs_1_.refs_9_ = bf16[256,1024]{1,0:T(8,128)(2,1)} collective-permute-done((bf16[256,1024]{1,0:T(8,128)(2,1)S(1)}, bf16[256,1024]{1,0:T(8,128)(2,1)}, u32[]{:S(2)}, u32[]{:S(2)}) %collective-permute-start.8) | collective-permute-done | bytes 524320 | tf_op jit(solution)/shard_map/ppermute | solution.py:707
  102.0 10.3 %project.1 = (bf16[1024,1024]{1,0:T(8,128)(2,1)S(1)}, bf16[1024,1024]{1,0:T(8,128)(2,1)S(1)}, bf16[1024,512]{1,0:T(8,128)(2,1)S(1)}, bf16[1024,512]{1,0:T(8,128)(2,1)S(1)}, bf16[1024,1536]{1,0:T(8,128)(2,1)}) custom-call(s32[2]{0:T(128)S(1)} %pad_add_fusion.place_ref, bf16[128,2048]{1,0:T(8,128)(2,1)S(1)} %copy-done.20, ...), custom_call_target="tpu_custom_call" | custom-call | flops 4294967296 | bytes 16777216 | tf_op jit(solution)/shard_map/project/pallas_call | solution.py:150
  114.7 12.2 %attend.2 = (bf16[1024,1024]{1,0:T(8,128)(2,1)}, f32[1024,128]{1,0:T(8,128)S(1)}, bf16[512,1024]{1,0:T(8,128)(2,1)S(1)}) custom-call(s32[2]{0:T(128)S(1)} %pad_add_fusion.place_ref, bf16[256,1024]{1,0:T(8,128)(2,1)S(1)} %convert_element_type.106.refs_0_.refs_8_, bf16[256,1024]{1,0:T(8,128)(2,1)} %collective-permute-done.8.refs_1_.refs_9_, ...), custom_call_target="tpu_custom_call" | custom-call | flops 3221225472 | bytes 8388608 | tf_op jit(solution)/shard_map/attend/pallas_call | solution.py:256
  127.0 8.7 %attend.3 = (bf16[1024,1024]{1,0:T(8,128)(2,1)}, f32[1024,128]{1,0:T(8,128)S(1)}, bf16[512,1024]{1,0:T(8,128)(2,1)S(1)}) custom-call(s32[2]{0:T(128)S(1)} %pad_add_fusion.place_ref, bf16[256,1024]{1,0:T(8,128)(2,1)S(1)} %convert_element_type.106.refs_0_.refs_8_, ...), custom_call_target="tpu_custom_call", output_to_operand_aliasing={{0}: (10, {}), {1}: (11, {})} | custom-call | flops 3221225472 | bytes 8388608 | tf_op jit(solution)/shard_map/attend/pallas_call | solution.py:256
  135.8 30.0 %collective-permute-done.20 = bf16[512,1024]{1,0:T(8,128)(2,1)S(1)} collective-permute-done((bf16[512,1024]{1,0:T(8,128)(2,1)S(1)}, bf16[512,1024]{1,0:T(8,128)(2,1)S(1)}, u32[]{:S(2)}, u32[]{:S(2)}) %collective-permute-start.20) | collective-permute-done | bytes 1048608 | tf_op jit(solution)/shard_map/ppermute | solution.py:698
  172.4 18.2 %all-gather.3.cloned.1.call-done.refs_0_.refs_1_.refs_2_.refs_3_ = bf16[1024,6144]{1,0:T(8,128)(2,1)} async-done(((bf16[128,6144]{1,0:T(8,128)(2,1)}), bf16[1024,6144]{1,0:T(8,128)(2,1)}) %all-gather.3.cloned.1.call-update) | async-done | bytes 12582928 | tf_op jit(solution)/shard_map/all_gather | solution.py:829
  190.6 36.9 %feed.1 = (bf16[1024,1024]{1,0:T(8,128)(2,1)}, bf16[1024,1024]{1,0:T(8,128)(2,1)}, bf16[1024,1536]{1,0:T(8,128)(2,1)}, bf16[1024,3072]{1,0:T(8,128)(2,1)}, bf16[...) custom-call(s32[2]{0:T(128)} %copy-done.27, ...), custom_call_target="tpu_custom_call" | custom-call | flops 19327352832 | bytes 31457280 | tf_op jit(solution)/shard_map/feed/pallas_call | solution.py:355
  230.6 3.1 multiply_reduce_fusion
  237.5 8.9 %convolution_convert_fusion = bf16[1024,3072]{1,0:T(8,128)(2,1)S(1)} fusion(bf16[1024,1024]{1,0:T(8,128)(2,1)} %get-tuple-element.168, bf16[1024,3072]{1,0:T(8,128)(2,1)S(1)} %copy-done.69), kind=kOutput, calls=%fused_computation.2 | convolution fusion | flops 6445596672 | bytes 14680064 | tf_op jit(solution)/shard_map/dot_general | solution.py:51
  250.6 3.7 convolution_convert_fusion.1
  258.5 3.4 collective-permute-done.26
  268.6 23.6 %back.2 = (bf16[1024,1024]{1,0:T(8,128)(2,1)}, bf16[1024,1024]{1,0:T(8,128)(2,1)}, f32[8,128]{1,0:T(8,128)}) custom-call(s32[2]{0:T(128)} %copy-done.27, bf16[128,2048]{1,0:T(8,128)(2,1)} %copy-done.19, bf16[128,2048]{1,0:T(8,128)(2,1)} %collective-permute-done.11.refs_1_, bf16[128,2048]{1,0:T(8,128)(2,1)} %copy-done.21, ...), custom_call_target="tpu_custom_call" | custom-call | flops 5905580032 | bytes 31457280 | tf_op jit(solution)/shard_map/back/pallas_call | solution.py:516
  292.2 4.0 convolution_convert_fusion.3
  299.6 4.1 sum_parts.31
  303.7 3.1 sum_parts.32
  310.6 3.5 sum_parts.33
  314.0 24.1 %back.3 = (bf16[1024,1024]{1,0:T(8,128)(2,1)}, bf16[1024,1024]{1,0:T(8,128)(2,1)}, f32[8,128]{1,0:T(8,128)}) custom-call(s32[2]{0:T(128)} %copy-done.27, bf16[128,2048]{1,0:T(8,128)(2,1)} %copy-done.19, bf16[128,2048]{1,0:T(8,128)(2,1)} %collective-permute-done.11.refs_1_, bf16[128,2048]{1,0:T(8,128)(2,1)} %copy-done.21, ...), custom_call_target="tpu_custom_call" | custom-call | flops 5905580032 | bytes 31457280 | tf_op jit(solution)/shard_map/back/pallas_call | solution.py:516
  338.1 3.1 sum_parts.34.kept_ref
  341.2 4.1 sum_parts.35
  345.3 3.1 sum_parts.36
  348.4 3.1 sum_parts.37.kept_ref
  351.5 4.5 sum_parts.38
  356.0 4.7 convolution_convert_fusion.2
  362.9 4.3 collective-permute-start.38
  373.4 4.5 sum_parts.39
  377.9 4.1 collective-permute-done.40.landed_ref
  385.6 3.2 sum_parts.41.kept_ref
  388.8 3.1 sum_parts.42.kept_ref
  394.0 3.1 collective-permute-start.50
  402.1 3.1 sum_parts.44.kept_ref
  412.7 4.8 collective-permute-start.53
  417.5 3.1 sum_parts.46.kept_ref
  423.4 5.5 collective-permute-start.47
  436.6 6.3 %collective-permute-done.54.landed_ref = bf16[1,128,3072]{2,1,0:T(8,128)(2,1)} collective-permute-done((bf16[1,128,3072]{2,1,0:T(8,128)(2,1)}, bf16[1,128,3072]{2,1,0:T(8,128)(2,1)}, u32[]{:S(2)}, u32[]{:S(2)}) %collective-permute-start.54) | collective-permute-done | bytes 786464 | tf_op jit(solution)/shard_map/ppermute | solution.py:896
  442.9 3.1 sum_parts.48.kept_ref
  449.8 3.1 sum_parts.50.kept_ref
  457.3 5.2 fusion.7
  469.2 8.1 %collective-permute-start.56 = (bf16[2,128,1024]{2,1,0:T(8,128)(2,1)}, bf16[2,128,1024]{2,1,0:T(8,128)(2,1)}, u32[]{:S(2)}, u32[]{:S(2)}) collective-permute-start(bf16[2,128,1024]{2,1,0:T(8,128)(2,1)} %stack_parts.3.kept_ref), channel_id=1, source_target_pairs={{0,1},{3,2},{4,5},{7,6},{8,9},{11,10},{12,13},{15,14},{16,17},{19,... | collective-permute-start | bytes 1572872 | tf_op jit(solution)/shard_map/ppermute | solution.py:896
  485.1 3.1 sum_parts.54.kept_ref
  489.7 3.6 collective-permute-start.70
  511.8 6.5 %adam_pair.1 = (f32[128,6144]{1,0:T(8,128)}, f32[128,6144]{1,0:T(8,128)}, f32[128,6144]{1,0:T(8,128)}) custom-call(s32[2]{0:T(128)S(1)} %copy-done.28, bf16[128,3072]{1,0:T(8,128)(2,1)S(1)} %bitcast.128, bf16[128,3072]{1,0:T(8,128)(2,1)S(1)} %bitcast.129, f32[128,6144]{1,0:T(8,128)S(1)} %copy-done.2, f32[128,6144]{1,0:T(8,128)S(1)} %copy-done.4, ...), custom_call_target="tpu_custom_call" | custom-call | flops 15728640 | bytes 20447232 | tf_op jit(solution)/shard_map/adam_pair/pallas_call | solution.py:619
  532.6 5.0 multiply_subtract_fusion
  537.6 5.9 %collective-permute-done.59.landed_ref = bf16[2,128,1024]{2,1,0:T(8,128)(2,1)} collective-permute-done((bf16[2,128,1024]{2,1,0:T(8,128)(2,1)}, bf16[2,128,1024]{2,1,0:T(8,128)(2,1)}, u32[]{:S(2)}, u32[]{:S(2)}) %collective-permute-start.59) | collective-permute-done | bytes 524320 | tf_op jit(solution)/shard_map/ppermute | solution.py:896
  545.5 7.2 %collective-permute-done.62.landed_ref = bf16[2,128,1024]{2,1,0:T(8,128)(2,1)} collective-permute-done((bf16[2,128,1024]{2,1,0:T(8,128)(2,1)}, bf16[2,128,1024]{2,1,0:T(8,128)(2,1)}, u32[]{:S(2)}, u32[]{:S(2)}) %collective-permute-start.62) | collective-permute-done | bytes 524320 | tf_op jit(solution)/shard_map/ppermute | solution.py:896
  560.0 7.3 %adam_cuts.1 = (f32[128,4096]{1,0:T(8,128)}, f32[128,4096]{1,0:T(8,128)}, f32[128,4096]{1,0:T(8,128)}) custom-call(s32[1]{0:T(128)} %bitcast.23.key_ref, bf16[2,128,1024]{2,1,0:T(8,128)(2,1)S(1)} %copy-done.14, bf16[2,128,1024]{2,1,0:T(8,128)(2,1)S(1)} %copy-done.15, f32[128,4096]{1,0:T(8,128)S(1)} %copy-done.3, f32[128,4096]{1,0:T(8,128)S(1)} %copy-done.12, ...), custom_call_target="tpu_custom_call" | custom-call | flops 10485760 | bytes 13631488 | tf_op jit(solution)/shard_map/adam_cuts/pallas_call | solution.py:589
  (366 shorter events, 190.3 us)
Async XLA Ops:
  7.2 165.2 %all-gather.5.cloned.1.call-start = ((), (), s32[]{:S(2)}) async-start(), calls=%async_computation.1 | async-start | bytes 7077888 | tf_op jit(solution)/shard_map/all_gather | solution.py:830
  12.4 22.7 %collective-permute-start.2 = (f32[1,1312]{1,0:T(1,128)S(1)}, f32[1,1312]{1,0:T(1,128)S(1)}, u32[]{:S(2)}, u32[]{:S(2)}) collective-permute-start(f32[1,1312]{1,0:T(1,128)S(1)} %reshape.178), channel_id=1, source_target_pairs={{0,12},{4,8},{8,4},{12,0},{16,28},{20,24},{24,20},{28,16},{1,13},{... | collective-permute-start | bytes 15752 | tf_op jit(solution)/shard_map/ppermute | solution.py:726
  12.6 22.5 %collective-permute-start.3 = (f32[1,1312]{1,0:T(1,128)S(1)}, f32[1,1312]{1,0:T(1,128)S(1)}, u32[]{:S(2)}, u32[]{:S(2)}) collective-permute-start(f32[1,1312]{1,0:T(1,128)S(1)} %reshape.178), channel_id=1, source_target_pairs={{0,16},{4,20},{8,24},{12,28},{16,0},{20,4},{24,8},{28,12},{1,17},{... | collective-permute-start | bytes 15752 | tf_op jit(solution)/shard_map/ppermute | solution.py:726
  14.6 20.6 %collective-permute-start.4 = (f32[1,1312]{1,0:T(1,128)S(1)}, f32[1,1312]{1,0:T(1,128)S(1)}, u32[]{:S(2)}, u32[]{:S(2)}) collective-permute-start(f32[1,1312]{1,0:T(1,128)S(1)} %reshape.178), channel_id=1, source_target_pairs={{0,20},{4,16},{8,28},{12,24},{16,4},{20,0},{24,12},{28,8},{1,21},{... | collective-permute-start | bytes 15752 | tf_op jit(solution)/shard_map/ppermute | solution.py:726
  35.3 155.4 %all-gather.3.cloned.1.call-start = ((), (), s32[]{:S(2)}) async-start(), calls=%async_computation | async-start | bytes 14155776 | tf_op jit(solution)/shard_map/all_gather | solution.py:829
  36.0 19.9 %collective-permute-start.14 = (bf16[128,2048]{1,0:T(8,128)(2,1)}, bf16[128,2048]{1,0:T(8,128)(2,1)}, u32[]{:S(2)}, u32[]{:S(2)}) collective-permute-start(bf16[128,2048]{1,0:T(8,128)(2,1)} %get-tuple-element.136), channel_id=1, source_target_pairs={{0,16},{8,24},{16,0},{24,8},{1,17},{9,25},{17,1},{25,9},{2,18},{10... | collective-permute-start | bytes 1572872 | tf_op jit(solution)/shard_map/ppermute | solution.py:698
  38.1 32.1 %collective-permute-start.18 = (bf16[256,1024]{1,0:T(8,128)(2,1)S(1)}, bf16[256,1024]{1,0:T(8,128)(2,1)S(1)}, u32[]{:S(2)}, u32[]{:S(2)}) collective-permute-start(bf16[256,1024]{1,0:T(8,128)(2,1)S(1)} %dynamic-slice_bitcast_fusion.7.refs_8_), channel_id=1, source_target_pairs={{0,16},{8,24},{16,0},{24,8},{1,17},{9,25},{17,1},{25,9},{2,18},{10... | collective-permute-start | bytes 1572872 | tf_op jit(solution)/shard_map/ppermute | solution.py:698
  38.2 34.2 %collective-permute-start.11 = (bf16[128,2048]{1,0:T(8,128)(2,1)S(1)}, bf16[128,2048]{1,0:T(8,128)(2,1)}, u32[]{:S(2)}, u32[]{:S(2)}) collective-permute-start(bf16[128,2048]{1,0:T(8,128)(2,1)S(1)} %get-tuple-element.135.refs_0_), channel_id=1, source_target_pairs={{0,4},{4,0},{1,5},{5,1},{2,6},{6,2},{3,7},{7,3},{8,12},{12,8},{9,1... | collective-permute-start | bytes 1572872 | tf_op jit(solution)/shard_map/ppermute | solution.py:707
  40.2 32.9 %collective-permute-start.12 = (bf16[128,2048]{1,0:T(8,128)(2,1)S(1)}, bf16[128,2048]{1,0:T(8,128)(2,1)S(1)}, u32[]{:S(2)}, u32[]{:S(2)}) collective-permute-start(bf16[128,2048]{1,0:T(8,128)(2,1)S(1)} %get-tuple-element.135.refs_0_), channel_id=1, source_target_pairs={{0,8},{8,0},{16,24},{24,16},{1,9},{9,1},{17,25},{25,17},{2,10},{10... | collective-permute-start | bytes 1572872 | tf_op jit(solution)/shard_map/ppermute | solution.py:698
  40.3 32.2 %collective-permute-start.7 = (bf16[256,1024]{1,0:T(8,128)(2,1)}, bf16[256,1024]{1,0:T(8,128)(2,1)S(1)}, u32[]{:S(2)}, u32[]{:S(2)}) collective-permute-start(bf16[256,1024]{1,0:T(8,128)(2,1)} %dynamic-slice_bitcast_fusion.8), channel_id=1, source_target_pairs={{0,8},{8,0},{16,24},{24,16},{1,9},{9,1},{17,25},{25,17},{2,10},{10... | collective-permute-start | bytes 1572872 | tf_op jit(solution)/shard_map/ppermute | solution.py:698
  70.9 25.6 %collective-permute-start.8 = (bf16[256,1024]{1,0:T(8,128)(2,1)S(1)}, bf16[256,1024]{1,0:T(8,128)(2,1)}, u32[]{:S(2)}, u32[]{:S(2)}) collective-permute-start(bf16[256,1024]{1,0:T(8,128)(2,1)S(1)} %convert_element_type.106.refs_0_.refs_8_), channel_id=1, source_target_pairs={{0,4},{4,0},{1,5},{5,1},{2,6},{6,2},{3,7},{7,3},{8,12},{12,8},{9,1... | collective-permute-start | bytes 1572872 | tf_op jit(solution)/shard_map/ppermute | solution.py:707
  72.4 24.1 %collective-permute-start.13 = (bf16[128,2048]{1,0:T(8,128)(2,1)}, bf16[128,2048]{1,0:T(8,128)(2,1)}, u32[]{:S(2)}, u32[]{:S(2)}) collective-permute-start(bf16[128,2048]{1,0:T(8,128)(2,1)} %collective-permute-done.11.refs_1_), channel_id=1, source_target_pairs={{0,8},{8,0},{16,24},{24,16},{1,9},{9,1},{17,25},{25,17},{2,10},{10... | collective-permute-start | bytes 1572872 | tf_op jit(solution)/shard_map/ppermute | solution.py:698
  72.5 24.5 %collective-permute-start.16 = (bf16[128,2048]{1,0:T(8,128)(2,1)}, bf16[128,2048]{1,0:T(8,128)(2,1)}, u32[]{:S(2)}, u32[]{:S(2)}) collective-permute-start(bf16[128,2048]{1,0:T(8,128)(2,1)} %collective-permute-done.14.refs_4_), channel_id=1, source_target_pairs={{0,8},{8,0},{16,24},{24,16},{1,9},{9,1},{17,25},{25,17},{2,10},{10... | collective-permute-start | bytes 1572872 | tf_op jit(solution)/shard_map/ppermute | solution.py:698
  73.1 25.8 %collective-permute-start.19 = (bf16[256,1024]{1,0:T(8,128)(2,1)S(1)}, bf16[256,1024]{1,0:T(8,128)(2,1)}, u32[]{:S(2)}, u32[]{:S(2)}) collective-permute-start(bf16[256,1024]{1,0:T(8,128)(2,1)S(1)} %collective-permute-done.7.refs_9_), channel_id=1, source_target_pairs={{0,16},{8,24},{16,0},{24,8},{1,17},{9,25},{17,1},{25,9},{2,18},{10... | collective-permute-start | bytes 1572872 | tf_op jit(solution)/shard_map/ppermute | solution.py:698
  74.1 24.8 %collective-permute-start.17 = (bf16[128,2048]{1,0:T(8,128)(2,1)}, bf16[128,2048]{1,0:T(8,128)(2,1)}, u32[]{:S(2)}, u32[]{:S(2)}) collective-permute-start(bf16[128,2048]{1,0:T(8,128)(2,1)} %collective-permute-done.15.refs_5_), channel_id=1, source_target_pairs={{0,8},{8,0},{16,24},{24,16},{1,9},{9,1},{17,25},{25,17},{2,10},{10... | collective-permute-start | bytes 1572872 | tf_op jit(solution)/shard_map/ppermute | solution.py:698
  126.9 38.9 %collective-permute-start.20 = (bf16[512,1024]{1,0:T(8,128)(2,1)S(1)}, bf16[512,1024]{1,0:T(8,128)(2,1)S(1)}, u32[]{:S(2)}, u32[]{:S(2)}) collective-permute-start(bf16[512,1024]{1,0:T(8,128)(2,1)S(1)} %get-tuple-element.148), channel_id=1, source_target_pairs={{0,16},{8,24},{16,0},{24,8},{1,17},{9,25},{17,1},{25,9},{2,18},{10... | collective-permute-start | bytes 3145736 | tf_op jit(solution)/shard_map/ppermute | solution.py:698
  126.9 42.7 %collective-permute-start.22 = (bf16[2,256,1024]{2,1,0:T(8,128)(2,1)S(1)}, bf16[2,256,1024]{2,1,0:T(8,128)(2,1)S(1)}, u32[]{:S(2)}, u32[]{:S(2)}) collective-permute-start(bf16[2,256,1024]{2,1,0:T(8,128)(2,1)S(1)} %copy-done.66), channel_id=1, source_target_pairs={{0,8},{8,0},{16,24},{24,16},{1,9},{9,1},{17,25},{25,17},{2,10},{10... | collective-permute-start | bytes 3145736 | tf_op jit(solution)/shard_map/ppermute | solution.py:698
  236.5 25.4 %collective-permute-start.26 = (bf16[512,1024]{1,0:T(8,128)(2,1)S(1)}, bf16[512,1024]{1,0:T(8,128)(2,1)S(1)}, u32[]{:S(2)}, u32[]{:S(2)}) collective-permute-start(bf16[512,1024]{1,0:T(8,128)(2,1)S(1)} %fusion.49), channel_id=1, source_target_pairs={{0,16},{8,24},{16,0},{24,8},{1,17},{9,25},{17,1},{25,9},{2,18},{10... | collective-permute-start | bytes 3145736 | tf_op jit(solution)/shard_map/ppermute | solution.py:698
  247.6 52.0 %collective-permute-start.29 = (bf16[2,128,3072]{2,1,0:T(8,128)(2,1)}, bf16[2,128,3072]{2,1,0:T(8,128)(2,1)}, u32[]{:S(2)}, u32[]{:S(2)}) collective-permute-start(bf16[2,128,3072]{2,1,0:T(8,128)(2,1)} %dynamic-slice_bitcast_fusion.1), channel_id=1, source_target_pairs={{0,4},{4,0},{1,5},{5,1},{2,6},{6,2},{3,7},{7,3},{8,12},{12,8},{9,1... | collective-permute-start | bytes 4718600 | tf_op jit(solution)/shard_map/ppermute | solution.py:707
  255.7 85.5 %collective-permute-start.34 = (bf16[2,384,1024]{2,1,0:T(8,128)(2,1)}, bf16[2,384,1024]{2,1,0:T(8,128)(2,1)}, u32[]{:S(2)}, u32[]{:S(2)}) collective-permute-start(bf16[2,384,1024]{2,1,0:T(8,128)(2,1)} %dynamic-slice_bitcast_fusion), channel_id=1, source_target_pairs={{0,4},{4,0},{1,5},{5,1},{2,6},{6,2},{3,7},{7,3},{8,12},{12,8},{9,1... | collective-permute-start | bytes 4718600 | tf_op jit(solution)/shard_map/ppermute | solution.py:707
  261.9 41.8 %collective-permute-start.28 = (bf16[128,3072]{1,0:T(8,128)(2,1)}, bf16[128,3072]{1,0:T(8,128)(2,1)}, u32[]{:S(2)}, u32[]{:S(2)}) collective-permute-start(bf16[128,3072]{1,0:T(8,128)(2,1)} %get-tuple-element.170), channel_id=1, source_target_pairs={{0,16},{8,24},{16,0},{24,8},{1,17},{9,25},{17,1},{25,9},{2,18},{10... | collective-permute-start | bytes 2359304 | tf_op jit(solution)/shard_map/ppermute | solution.py:698
  267.1 41.8 %collective-permute-start.27 = (bf16[2,256,1024]{2,1,0:T(8,128)(2,1)}, bf16[2,256,1024]{2,1,0:T(8,128)(2,1)}, u32[]{:S(2)}, u32[]{:S(2)}) collective-permute-start(bf16[2,256,1024]{2,1,0:T(8,128)(2,1)} %dynamic-slice_bitcast_fusion.4), channel_id=1, source_target_pairs={{0,8},{8,0},{16,24},{24,16},{1,9},{9,1},{17,25},{25,17},{2,10},{10... | collective-permute-start | bytes 3145736 | tf_op jit(solution)/shard_map/ppermute | solution.py:698
  298.6 52.9 %collective-permute-start.30 = (bf16[2,2,128,1024]{3,2,1,0:T(8,128)(2,1)}, bf16[2,2,128,1024]{3,2,1,0:T(8,128)(2,1)}, u32[]{:S(2)}, u32[]{:S(2)}) collective-permute-start(bf16[2,2,128,1024]{3,2,1,0:T(8,128)(2,1)} %dynamic-slice_bitcast_fusion.3), channel_id=1, source_target_pairs={{0,8},{8,0},{16,24},{24,16},{1,9},{9,1},{17,25},{25,17},{2,10},{10... | collective-permute-start | bytes 3145736 | tf_op jit(solution)/shard_map/ppermute | solution.py:698
  306.8 31.3 %collective-permute-start.31 = (bf16[128,3072]{1,0:T(8,128)(2,1)}, bf16[128,3072]{1,0:T(8,128)(2,1)}, u32[]{:S(2)}, u32[]{:S(2)}) collective-permute-start(bf16[128,3072]{1,0:T(8,128)(2,1)} %get-tuple-element.181), channel_id=1, source_target_pairs={{0,16},{8,24},{16,0},{24,8},{1,17},{9,25},{17,1},{25,9},{2,18},{10... | collective-permute-start | bytes 2359304 | tf_op jit(solution)/shard_map/ppermute | solution.py:698
  308.6 36.7 %collective-permute-start.33 = (bf16[1,128,3072]{2,1,0:T(8,128)(2,1)}, bf16[1,128,3072]{2,1,0:T(8,128)(2,1)}, u32[]{:S(2)}, u32[]{:S(2)}) collective-permute-start(bf16[1,128,3072]{2,1,0:T(8,128)(2,1)} %get-tuple-element.184), channel_id=1, source_target_pairs={{0,16},{8,24},{16,0},{24,8},{1,17},{9,25},{17,1},{25,9},{2,18},{10... | collective-permute-start | bytes 2359304 | tf_op jit(solution)/shard_map/ppermute | solution.py:698
  308.9 39.5 %collective-permute-start.32 = (bf16[1,128,3072]{2,1,0:T(8,128)(2,1)}, bf16[1,128,3072]{2,1,0:T(8,128)(2,1)}, u32[]{:S(2)}, u32[]{:S(2)}) collective-permute-start(bf16[1,128,3072]{2,1,0:T(8,128)(2,1)} %sum_parts.32), channel_id=1, source_target_pairs={{0,4},{4,0},{1,5},{5,1},{2,6},{6,2},{3,7},{7,3},{8,12},{12,8},{9,1... | collective-permute-start | bytes 2359304 | tf_op jit(solution)/shard_map/ppermute | solution.py:707
  361.4 24.2 %collective-permute-start.39 = (bf16[1,384,1024]{2,1,0:T(8,128)(2,1)}, bf16[1,384,1024]{2,1,0:T(8,128)(2,1)}, u32[]{:S(2)}, u32[]{:S(2)}) collective-permute-start(bf16[1,384,1024]{2,1,0:T(8,128)(2,1)} %get-tuple-element.197), channel_id=1, source_target_pairs={{0,16},{8,24},{16,0},{24,8},{1,17},{9,25},{17,1},{25,9},{2,18},{10... | collective-permute-start | bytes 2359304 | tf_op jit(solution)/shard_map/ppermute | solution.py:698
  362.9 25.9 %collective-permute-start.38 = (bf16[1,128,3072]{2,1,0:T(8,128)(2,1)}, bf16[1,128,3072]{2,1,0:T(8,128)(2,1)}, u32[]{:S(2)}, u32[]{:S(2)}) collective-permute-start(bf16[1,128,3072]{2,1,0:T(8,128)(2,1)} %sum_parts.37.kept_ref), channel_id=1, source_target_pairs={{0,1},{3,2},{4,5},{7,6},{8,9},{11,10},{12,13},{15,14},{16,17},{19,... | collective-permute-start | bytes 2359304 | tf_op jit(solution)/shard_map/ppermute | solution.py:896
  367.7 33.7 %collective-permute-start.45 = (bf16[1,128,3072]{2,1,0:T(8,128)(2,1)}, bf16[1,128,3072]{2,1,0:T(8,128)(2,1)}, u32[]{:S(2)}, u32[]{:S(2)}) collective-permute-start(bf16[1,128,3072]{2,1,0:T(8,128)(2,1)} %collective-permute-done.36.kept_ref), channel_id=1, source_target_pairs={{0,1},{3,2},{4,5},{7,6},{8,9},{11,10},{12,13},{15,14},{16,17},{19,... | collective-permute-start | bytes 2359304 | tf_op jit(solution)/shard_map/ppermute | solution.py:896
  371.9 22.1 %collective-permute-start.42 = (bf16[2,128,1024]{2,1,0:T(8,128)(2,1)}, bf16[2,128,1024]{2,1,0:T(8,128)(2,1)}, u32[]{:S(2)}, u32[]{:S(2)}) collective-permute-start(bf16[2,128,1024]{2,1,0:T(8,128)(2,1)} %get-tuple-element.202), channel_id=1, source_target_pairs={{0,4},{4,0},{1,5},{5,1},{2,6},{6,2},{3,7},{7,3},{8,12},{12,8},{9,1... | collective-permute-start | bytes 1572872 | tf_op jit(solution)/shard_map/ppermute | solution.py:707
  382.0 40.1 %collective-permute-start.37 = (bf16[512,1024]{1,0:T(8,128)(2,1)}, bf16[512,1024]{1,0:T(8,128)(2,1)}, u32[]{:S(2)}, u32[]{:S(2)}) collective-permute-start(bf16[512,1024]{1,0:T(8,128)(2,1)} %slice.65), channel_id=1, source_target_pairs={{0,16},{8,24},{16,0},{24,8},{1,17},{9,25},{17,1},{25,9},{2,18},{10... | collective-permute-start | bytes 3145736 | tf_op jit(solution)/shard_map/ppermute | solution.py:698
  391.9 20.8 %collective-permute-start.41 = (bf16[1,128,3072]{2,1,0:T(8,128)(2,1)}, bf16[1,128,3072]{2,1,0:T(8,128)(2,1)}, u32[]{:S(2)}, u32[]{:S(2)}) collective-permute-start(bf16[1,128,3072]{2,1,0:T(8,128)(2,1)} %sum_parts.42.kept_ref), channel_id=1, source_target_pairs={{1,2},{2,1},{5,6},{6,5},{9,10},{10,9},{13,14},{14,13},{17,18},{18,... | collective-permute-start | bytes 2359304 | tf_op jit(solution)/shard_map/ppermute | solution.py:896
  394.0 26.5 %collective-permute-start.50 = (bf16[1,256,1024]{2,1,0:T(8,128)(2,1)S(1)}, bf16[1,256,1024]{2,1,0:T(8,128)(2,1)}, u32[]{:S(2)}, u32[]{:S(2)}) collective-permute-start(bf16[1,256,1024]{2,1,0:T(8,128)(2,1)S(1)} %copy-done.48), channel_id=1, source_target_pairs={{0,1},{3,2},{4,5},{7,6},{8,9},{11,10},{12,13},{15,14},{16,17},{19,... | collective-permute-start | bytes 1572872 | tf_op jit(solution)/shard_map/ppermute | solution.py:896
  405.2 47.7 %collective-permute-start.23 = (bf16[512,1024]{1,0:T(8,128)(2,1)}, bf16[512,1024]{1,0:T(8,128)(2,1)}, u32[]{:S(2)}, u32[]{:S(2)}) collective-permute-start(bf16[512,1024]{1,0:T(8,128)(2,1)} %get-tuple-element.155), channel_id=1, source_target_pairs={{0,8},{8,0},{16,24},{24,16},{1,9},{9,1},{17,25},{25,17},{2,10},{10... | collective-permute-start | bytes 3145736 | tf_op jit(solution)/shard_map/ppermute | solution.py:698
  412.7 35.6 %collective-permute-start.53 = (bf16[1,384,1024]{2,1,0:T(8,128)(2,1)}, bf16[1,384,1024]{2,1,0:T(8,128)(2,1)}, u32[]{:S(2)}, u32[]{:S(2)}) collective-permute-start(bf16[1,384,1024]{2,1,0:T(8,128)(2,1)} %sum_parts.41.kept_ref), channel_id=1, source_target_pairs={{0,1},{3,2},{4,5},{7,6},{8,9},{11,10},{12,13},{15,14},{16,17},{19,... | collective-permute-start | bytes 2359304 | tf_op jit(solution)/shard_map/ppermute | solution.py:896
  422.1 20.8 %collective-permute-start.54 = (bf16[1,128,3072]{2,1,0:T(8,128)(2,1)}, bf16[1,128,3072]{2,1,0:T(8,128)(2,1)}, u32[]{:S(2)}, u32[]{:S(2)}) collective-permute-start(bf16[1,128,3072]{2,1,0:T(8,128)(2,1)} %sum_parts.46.kept_ref), channel_id=1, source_target_pairs={{1,0},{2,3},{5,4},{6,7},{9,8},{10,11},{13,12},{14,15},{17,16},{18,... | collective-permute-start | bytes 2359304 | tf_op jit(solution)/shard_map/ppermute | solution.py:896
  423.4 30.1 %collective-permute-start.47 = (bf16[2,128,1024]{2,1,0:T(8,128)(2,1)S(1)}, bf16[2,128,1024]{2,1,0:T(8,128)(2,1)S(1)}, u32[]{:S(2)}, u32[]{:S(2)}) collective-permute-start(bf16[2,128,1024]{2,1,0:T(8,128)(2,1)S(1)} %copy-done.47), channel_id=1, source_target_pairs={{0,1},{3,2},{4,5},{7,6},{8,9},{11,10},{12,13},{15,14},{16,17},{19,... | collective-permute-start | bytes 1572872 | tf_op jit(solution)/shard_map/ppermute | solution.py:896
  454.4 25.2 %collective-permute-start.51 = (bf16[1,128,3072]{2,1,0:T(8,128)(2,1)}, bf16[1,128,3072]{2,1,0:T(8,128)(2,1)}, u32[]{:S(2)}, u32[]{:S(2)}) collective-permute-start(bf16[1,128,3072]{2,1,0:T(8,128)(2,1)} %sum_parts.48.kept_ref), channel_id=1, source_target_pairs={{1,0},{2,3},{5,4},{6,7},{9,8},{10,11},{13,12},{14,15},{17,16},{18,... | collective-permute-start | bytes 2359304 | tf_op jit(solution)/shard_map/ppermute | solution.py:896
  455.7 29.4 %collective-permute-start.58 = (bf16[1,384,1024]{2,1,0:T(8,128)(2,1)}, bf16[1,384,1024]{2,1,0:T(8,128)(2,1)}, u32[]{:S(2)}, u32[]{:S(2)}) collective-permute-start(bf16[1,384,1024]{2,1,0:T(8,128)(2,1)} %sum_parts.50.kept_ref), channel_id=1, source_target_pairs={{1,2},{2,1},{5,6},{6,5},{9,10},{10,9},{13,14},{14,13},{17,18},{18,... | collective-permute-start | bytes 2359304 | tf_op jit(solution)/shard_map/ppermute | solution.py:896
  469.2 28.1 %collective-permute-start.56 = (bf16[2,128,1024]{2,1,0:T(8,128)(2,1)}, bf16[2,128,1024]{2,1,0:T(8,128)(2,1)}, u32[]{:S(2)}, u32[]{:S(2)}) collective-permute-start(bf16[2,128,1024]{2,1,0:T(8,128)(2,1)} %stack_parts.3.kept_ref), channel_id=1, source_target_pairs={{0,1},{3,2},{4,5},{7,6},{8,9},{11,10},{12,13},{15,14},{16,17},{19,... | collective-permute-start | bytes 1572872 | tf_op jit(solution)/shard_map/ppermute | solution.py:896
  479.7 21.9 %collective-permute-start.24 = (bf16[256,1024]{1,0:T(8,128)(2,1)}, bf16[256,1024]{1,0:T(8,128)(2,1)}, u32[]{:S(2)}, u32[]{:S(2)}) collective-permute-start(bf16[256,1024]{1,0:T(8,128)(2,1)} %get-tuple-element.282), channel_id=1, source_target_pairs={{0,8},{8,0},{16,24},{24,16},{1,9},{9,1},{17,25},{25,17},{2,10},{10... | collective-permute-start | bytes 1572872 | tf_op jit(solution)/shard_map/ppermute | solution.py:698
  488.2 36.6 %collective-permute-start.61 = (bf16[1,384,1024]{2,1,0:T(8,128)(2,1)}, bf16[1,384,1024]{2,1,0:T(8,128)(2,1)}, u32[]{:S(2)}, u32[]{:S(2)}) collective-permute-start(bf16[1,384,1024]{2,1,0:T(8,128)(2,1)} %sum_parts.54.kept_ref), channel_id=1, source_target_pairs={{1,0},{2,3},{5,4},{6,7},{9,8},{10,11},{13,12},{14,15},{17,16},{18,... | collective-permute-start | bytes 2359304 | tf_op jit(solution)/shard_map/ppermute | solution.py:896
  489.7 65.0 %collective-permute-start.70 = (f32[1,288]{1,0:T(1,128)S(1)}, f32[1,288]{1,0:T(1,128)S(1)}, u32[]{:S(2)}, u32[]{:S(2)}) collective-permute-start(f32[1,288]{1,0:T(1,128)S(1)} %add_add_fusion), channel_id=1, source_target_pairs={{0,1},{1,0},{2,3},{3,2},{4,5},{5,4},{6,7},{7,6},{8,9},{9,8},{10,11... | collective-permute-start | bytes 3464 | tf_op jit(solution)/shard_map/ppermute | solution.py:710
  494.5 60.2 %collective-permute-start.71 = (f32[1,288]{1,0:T(1,128)S(1)}, f32[1,288]{1,0:T(1,128)S(1)}, u32[]{:S(2)}, u32[]{:S(2)}) collective-permute-start(f32[1,288]{1,0:T(1,128)S(1)} %add_add_fusion), channel_id=1, source_target_pairs={{0,2},{1,3},{2,0},{3,1},{4,6},{5,7},{6,4},{7,5},{8,10},{9,11},{10,... | collective-permute-start | bytes 3464 | tf_op jit(solution)/shard_map/ppermute | solution.py:710
  497.3 23.3 %collective-permute-start.55 = (bf16[2,128,1024]{2,1,0:T(8,128)(2,1)}, bf16[2,128,1024]{2,1,0:T(8,128)(2,1)}, u32[]{:S(2)}, u32[]{:S(2)}) collective-permute-start(bf16[2,128,1024]{2,1,0:T(8,128)(2,1)} %sum_parts.53.kept_ref), channel_id=1, source_target_pairs={{1,2},{2,1},{5,6},{6,5},{9,10},{10,9},{13,14},{14,13},{17,18},{18,... | collective-permute-start | bytes 1572872 | tf_op jit(solution)/shard_map/ppermute | solution.py:896
  501.6 27.0 %collective-permute-start.60 = (bf16[2,128,1024]{2,1,0:T(8,128)(2,1)}, bf16[2,128,1024]{2,1,0:T(8,128)(2,1)}, u32[]{:S(2)}, u32[]{:S(2)}) collective-permute-start(bf16[2,128,1024]{2,1,0:T(8,128)(2,1)} %sum_parts.56.kept_ref), channel_id=1, source_target_pairs={{1,2},{2,1},{5,6},{6,5},{9,10},{10,9},{13,14},{14,13},{17,18},{18,... | collective-permute-start | bytes 1572872 | tf_op jit(solution)/shard_map/ppermute | solution.py:896
  520.6 34.1 %collective-permute-start.72 = (f32[1,288]{1,0:T(1,128)S(1)}, f32[1,288]{1,0:T(1,128)S(1)}, u32[]{:S(2)}, u32[]{:S(2)}) collective-permute-start(f32[1,288]{1,0:T(1,128)S(1)} %add_add_fusion), channel_id=1, source_target_pairs={{0,3},{1,2},{2,1},{3,0},{4,7},{5,6},{6,5},{7,4},{8,11},{9,10},{10,... | collective-permute-start | bytes 3464 | tf_op jit(solution)/shard_map/ppermute | solution.py:710
  531.3 21.3 %collective-permute-start.62 = (bf16[2,128,1024]{2,1,0:T(8,128)(2,1)}, bf16[2,128,1024]{2,1,0:T(8,128)(2,1)}, u32[]{:S(2)}, u32[]{:S(2)}) collective-permute-start(bf16[2,128,1024]{2,1,0:T(8,128)(2,1)} %sum_parts.59.kept_ref), channel_id=1, source_target_pairs={{1,0},{2,3},{5,4},{6,7},{9,8},{10,11},{13,12},{14,15},{17,16},{18,... | collective-permute-start | bytes 1572872 | tf_op jit(solution)/shard_map/ppermute | solution.py:896
  (98 other events, 1170.5 us)
Sparse Core Ops, SparseCore 0:
  35.4 66.5 all-gather.4
  104.5 86.1 all-gather.2

commit v2 on v1

--- a/solution.py
+++ b/solution.py
@@ -633,60 +633,6 @@
     )(place, own, other, weight, first, second)
 
 
-def sum_kernel(lead, take, key_ref, kept_ref, landed_ref, *outs):
-    size = outs[0].shape
-    kept, landed = kept_ref[...].reshape(size), landed_ref[...].reshape(size)
-    if take:
-        total = jnp.where(key_ref[0] > 0, landed, kept)
-    else:
-        total = (kept.astype(FULL) + landed.astype(FULL)).astype(LOW)
-    for s in range(lead):
-
-        @pl.when(pl.program_id(0) == s)
-        def _():
-            outs[s][...] = total
-
-
-def sum_parts(key, kept, kept_map, landed, landed_map, lead, steps, rows, take=False):
-    columns = kept.shape[-1]
-
-    def spec(array, place):
-        ones = (1,) * (array.ndim - 2)
-        return pl.BlockSpec(ones + (rows, columns), lambda i, j, p: (*place(i, j, p), 0))
-
-    def out(s):
-        spot = lambda i, j: jnp.where(i == s, j, jnp.where(i < s, 0, steps - 1))
-        return pl.BlockSpec((1, rows, columns), lambda i, j, p: (spot(i, j), 0, 0))
-
-    return pl.pallas_call(
-        functools.partial(sum_kernel, lead, take),
-        out_shape=(jax.ShapeDtypeStruct((steps, rows, columns), LOW),) * lead,
-        grid_spec=pltpu.PrefetchScalarGridSpec(
-            num_scalar_prefetch=1,
-            grid=(lead, steps),
-            in_specs=[spec(kept, kept_map), spec(landed, landed_map)],
-            out_specs=tuple(out(s) for s in range(lead)),
-        ),
-        cost_estimate=pl.CostEstimate(flops=0, bytes_accessed=0, transcendentals=0),
-        name="sum_parts",
-    )(key, kept, landed)
-
-
-def stack_kernel(*refs):
-    for s, ref in enumerate(refs[:-1]):
-        refs[-1][s] = ref[...]
-
-
-def stack_parts(parts):
-    rows, columns = parts[0].shape
-    return pl.pallas_call(
-        stack_kernel,
-        out_shape=jax.ShapeDtypeStruct((len(parts), rows, columns), LOW),
-        cost_estimate=pl.CostEstimate(flops=0, bytes_accessed=0, transcendentals=0),
-        name="stack_parts",
-    )(*parts)
-
-
 def after(value, *others):
     return lax.optimization_barrier((value, *others))[0]
 
@@ -793,16 +739,8 @@
         small = [
             swap_plane(small, s, t) if s or t else small for s in range(n) for t in range(inner)
         ]
-        tokens, qkv_low, out_low, expand_low, shrink_low, other_tokens, *small = lax.optimization_barrier(
-            (
-                tokens,
-                [qkv_piece(s) for s in range(chips)],
-                out_weight.astype(LOW),
-                expand_weight.astype(LOW),
-                shrink_weight.astype(LOW),
-                pick(tokens, 0, core ^ 1),
-                *small,
-            )
+        tokens, qkv_low, other_tokens, *small = lax.optimization_barrier(
+            (tokens, [qkv_piece(s) for s in range(chips)], pick(tokens, 0, core ^ 1), *small)
         )
         small = jnp.stack(small)
         small = small.reshape(n, inner, -1)[order]
@@ -824,10 +762,15 @@
             near = over_grp(part)
             qkv_parts += near + [swap_core(p) for p in near]
 
-        near = over_grp(out_low)
+        near = over_grp(out_weight.astype(LOW))
         out_parts = near + [swap_core(p) for p in near]
-        expand_full = lax.all_gather(expand_low, ("ctx", "grp"), axis=0, tiled=True)
-        shrink_full = lax.all_gather(shrink_low, ("ctx", "grp"), axis=0, tiled=True)
+        def gather_all(weight):
+            share = weight.shape[0] // reps
+            low = lax.dynamic_slice_in_dim(weight, rep * share, share, 0).astype(LOW)
+            return lax.all_gather(low, ("ctx", "grp", "rep"), axis=0, tiled=True)
+
+        expand_full = gather_all(expand_weight)
+        shrink_full = gather_all(shrink_weight)
         other_cotangent = swap_core(cotangent)
 
         ladder = jnp.arange(HEAD_SIZE) % (HEAD_SIZE // 2)
@@ -867,30 +810,23 @@
         output = (hidden + sum_of([share, swap_core(share_other)])).astype(LOW)
         output = by_sequence(output[:block], swap_core(output[block:]))
 
-        where = jnp.stack([chip, core, mine]).astype(jnp.int32)
-        ends = {}
-        for _, takes in hops:
-            if takes:
-                ends[takes] = ((rep == takes[0]) | (rep == takes[1])).astype(jnp.int32).reshape(1)
         line = []
 
-        def next_sums(kept, kept_map, sent, sent_map, lead, steps, block_rows):
-            for i, value in enumerate(sent):
-                value = after(value, *line)
-                totals = sum_parts(where, kept, kept_map, value, sent_map, lead, steps, block_rows)
-                if i + 1 < len(sent):
-                    kept, kept_map = jnp.stack(totals), lambda i, j, p: (i, j, 0)
-            line[:] = [totals[0]]
-            return totals
-
         def next_sum(kept, sent):
-            plain = lambda i, j, p: (j, 0)
-            for value in sent:
-                value = after(value, *line)
-                steps, block_rows = kept.shape[:2]
-                (kept,) = sum_parts(where, kept, plain, value, plain, 1, steps, block_rows)
-            line[:] = [kept]
-            return kept
+            if line:
+                sent = lax.optimization_barrier((*sent, *line))[: len(sent)]
+            total = sum_of([kept, *sent]).astype(LOW)
+            line[:] = [total]
+            return total
+
+        def next_cut(kept, sent, axis, place, count):
+            sent = lax.optimization_barrier((*sent, *line))[: len(sent)]
+            pieces = [
+                sum_of([pick(value, axis, place ^ s) for value in (kept, *sent)]).astype(LOW)
+                for s in range(count)
+            ]
+            line[:] = pieces
+            return pieces
 
         def go(value, step=0):
             return [value, lax.ppermute(value, "rep", hops[step][0]), step]
@@ -899,14 +835,13 @@
             value, landed, step = trip
             if step == len(hops):
                 return
-            landed = after(landed, *line)
             takes = hops[step][1]
-            plain = lambda i, j, p: (j, 0)
-            (value,) = sum_parts(
-                where if takes is None else ends[takes], value, plain, landed, plain, 1,
-                value.shape[0], value.shape[1], takes is not None,
-            )
-            line[:] = [value]
+            if takes is None:
+                value = next_sum(value, [landed])
+            else:
+                landed = after(landed, *line)
+                value = jnp.where((rep == takes[0]) | (rep == takes[1]), landed, value)
+                line[:] = [value]
             step += 1
             trip[:] = go(value, step) if step < len(hops) else [value, None, step]
 
@@ -925,108 +860,71 @@
         def cut_qkv(grad):
             grad_qkv = dot_tn(normed, grad).astype(LOW)
             cuts = grad_qkv.reshape(chips, 2, inner, rows, width // HALVES)
-            return cuts, swap_core(pick(cuts, 1, core ^ 1))
-
-        def sum_qkv_core(cuts, landed):
-            return next_sums(
-                cuts, lambda i, j, p: (j, p[1], p[2] ^ i, 0), [landed], lambda i, j, p: (j, p[2] ^ i, 0),
-                inner, chips, rows,
-            )
-
-        def sum_by_chip(kept, sent, block_rows):
-            place_of = lambda i, j, p: (p[0] ^ i, 0)
-            return next_sums(kept, place_of, sent, place_of, chips, 1, block_rows)
+            return pick(cuts, 1, core), [swap_core(pick(cuts, 1, core ^ 1))]
 
         x_late, active_late = lax.optimization_barrier((x_all, active, hidden_low))[:2]
         grad_expand = dot_tn(x_late, grad_gate_up).astype(LOW)
         expand_cuts = grad_expand.reshape(chips, 2, inner, rows, FF)
-        cut = pick(expand_cuts, 1, core ^ 1)
-        other_sent = [swap_grp(pick(cut, 1, mine ^ t), t) for t in range(1, inner)]
+        other_rows = pick(expand_cuts, 1, core ^ 1)
+        other_sent = [swap_grp(pick(other_rows, 1, mine ^ t), t) for t in range(1, inner)]
         grad_shrink = dot_tn(active_late, c_all).astype(LOW)
-        ff_rows = FF // (n * inner)
-        shrink_cuts = grad_shrink.reshape(chips, inner, ff_rows, D)
-        shrink_sent = [swap_grp(pick(shrink_cuts, 1, mine ^ t), t) for t in range(1, inner)]
-        cut = pick(expand_cuts, 1, core)
-
-        def own_rows(t, s):
-            return pick(pick(cut, 0, chip ^ s), 0, mine ^ t)
-
-        far_sent = [
-            [swap_chip(after(own_rows(t, s), grad_slots[-1]), s) for s in range(1, chips)]
-            for t in range(1, inner)
-        ]
+        shrink_cuts = grad_shrink.reshape(chips, inner, FF // (n * inner), D)
+        own_cuts = pick(expand_cuts, 1, core)
+
+        def first_over_x(cuts, t, *gates):
+            cut = after(cuts, *gates)
+            sent = [swap_chip(pick(pick(cut, 0, chip ^ s), 0, mine ^ t), s) for s in range(1, chips)]
+            return pick(pick(cuts, 0, chip), 0, mine ^ t), sent
+
+        own_far = [first_over_x(own_cuts, t, grad_slots[-1]) for t in range(1, inner)]
+        own_near = first_over_x(own_cuts, 0, grad_slots[-1])
 
         grad_out = dot_tn(attended, grad_all).astype(LOW)
-        out_rows = out_weight.shape[0]
-        out_cuts = grad_out.reshape(2, inner, out_rows, D)
+        out_cuts = grad_out.reshape(2, inner, out_weight.shape[0], D)
         out_sent = swap_core(pick(out_cuts, 0, core ^ 1))
         attended = after(attended, out_cuts)
         grad_one, back_all, gains_one = back_part(0, attended, None)
 
         line[:] = [gains_one]
-        first_cuts, first_landed = cut_qkv(grad_one)
-        other_cut = send_x(
-            next_sums(
-                expand_cuts, lambda i, j, p: (p[0] ^ i, p[1] ^ 1, p[2], 0), other_sent,
-                lambda i, j, p: (p[0] ^ i, 0), chips, 1, rows,
-            )
-        )
-        own_sent = []
-        for t in range(1, inner):
-            sent = [value[None] for value in far_sent[t - 1]]
-            (total,) = next_sums(
-                expand_cuts, lambda i, j, p, t=t: (p[0], p[1], p[2] ^ t, 0), sent,
-                lambda i, j, p: (j, 0), 1, 1, rows,
-            )
-            own_sent.append(swap_grp(total, t))
-        near_sent = [swap_chip(after(own_rows(0, s), *line), s)[None] for s in range(1, chips)]
-        out_cut = send_y(
-            next_sums(
-                out_cuts, lambda i, j, p: (p[1], p[2] ^ i, 0), [out_sent],
-                lambda i, j, p: (p[2] ^ i, 0), inner, 1, out_rows,
-            )
-        )
+        own_sent = [swap_grp(next_sum(*own_far[t - 1]), t) for t in range(1, inner)]
+        other_cut = send_x(next_cut(pick(other_rows, 1, mine), other_sent, 0, chip, chips))
+        own_cut = next_sum(*own_near)
+        first_cuts, first_sent = cut_qkv(grad_one)
+        shrink_far = [first_over_x(shrink_cuts, t, *line) for t in range(1, inner)]
+        shrink_near = first_over_x(shrink_cuts, 0, *line)
+        out_cut = send_y(next_cut(pick(out_cuts, 0, core), [out_sent], 0, mine, inner))
         attended, back_all = lax.optimization_barrier((attended, back_all, first_cuts, *line))[:2]
         grad_two, back_all, gains_two = back_part(1, attended, back_all)
 
         line[:] = [gains_two]
-        (own_cut,) = next_sums(
-            expand_cuts, lambda i, j, p: (p[0], p[1], p[2], 0), near_sent, lambda i, j, p: (j, 0), 1, 1, rows
-        )
-        shrink_cut = send_x(
-            next_sums(
-                shrink_cuts, lambda i, j, p: (p[0] ^ i, p[2], 0), shrink_sent,
-                lambda i, j, p: (p[0] ^ i, 0), chips, 1, ff_rows,
-            )
-        )
+        shrink_sent = [swap_grp(next_sum(*shrink_far[t - 1]), t) for t in range(1, inner)]
+        shrink_cut = next_sum(*shrink_near)
+        own_cut = next_sum(own_cut, own_sent)
+        first_cut = send_y(next_cut(first_cuts, first_sent, 1, mine, inner))
+        second_cuts, second_sent = cut_qkv(after(grad_two, *line))
         other_cut = swap_core(next_sum(*other_cut))
-        own = go(next_sum(own_cut, own_sent))
-        first_cut = send_y(sum_qkv_core(first_cuts, first_landed))
-        second_cuts, second_landed = cut_qkv(after(grad_two, *line))
-        other_cut = after(other_cut, *line)
-        line[:] = [other_cut]
-        other = go(other_cut)
-        second_cut = send_y(sum_qkv_core(second_cuts, second_landed))
+        second_cut = send_y(next_cut(second_cuts, second_sent, 1, mine, inner))
         shares = []
         for s in range(1, chips):
             share = after(back_all[2 * s * block : 2 * (s + 1) * block], *line)
             shares.append(swap_chip(share, s))
         out = go(next_sum(*out_cut))
-        shrink = go(next_sum(*shrink_cut))
+        shrink_cut = next_sum(shrink_cut, shrink_sent)
+        own_cut, other_cut, shrink_cut = lax.optimization_barrier((own_cut, other_cut, shrink_cut, *line))[:3]
+        line[:] = [own_cut]
+        own_cut, other_cut, total_shrink = lax.psum((own_cut, other_cut, shrink_cut), "rep")
+        first_cut = send_x(next_cut(*first_cut, 0, chip, chips))
+        second_cut = send_x(next_cut(*second_cut, 0, chip, chips))
 
         def stacked(on_the_way):
             kept, sent = on_the_way
-            total = stack_parts([kept[0]] + [after(value, *line)[0] for value in sent])
+            total = jnp.stack([kept, *lax.optimization_barrier((*sent, *line))[: len(sent)]])
             line[:] = [total]
             return total
 
-        step_on(own)
-        first_cut = send_x(sum_by_chip(*first_cut, rows))
-        step_on(other)
-        second_cut = send_x(sum_by_chip(*second_cut, rows))
+        step_on(out)
         first = go(stacked(first_cut))
-        step_on(own)
-
+        second = go(stacked(second_cut))
         shares = [back_all[: 2 * block]] + [after(value, *line) for value in shares]
         input_part, gain_part = norm_back(inputs, gain_one, sum_of(shares))
         gain_one_grad = jnp.sum(gain_part, axis=0)
@@ -1044,32 +942,19 @@
         line[:] = [gain_one_grad]
 
         step_on(out)
-        second = go(stacked(second_cut))
-        step_on(other)
-        step_on(own)
+        step_on(first)
+        step_on(second)
         gains_sent = lax.optimization_barrier((*gains_sent, *line))[:-1]
         total_gains = sum_of([pick(pick(grad_gains, 0, me), 0, mine), *gains_sent])
         gains_sent = gather_reps(total_gains)
-        step_on(shrink)
-        step_on(out)
-        step_on(other)
         step_on(first)
-        step_on(shrink)
         step_on(out)
         step_on(second)
-        step_on(first)
-        step_on(shrink)
-        step_on(second)
-        step_on(first)
-        step_on(second)
-        trips = (own, other, out, shrink, first, second)
+        trips = (out, first, second)
         for _ in hops:
             for trip in trips:
                 step_on(trip)
-        own_cut, other_cut, total_out, total_shrink, *qkv_cuts = [trip[0] for trip in trips]
-        total_shrink, total_out, other_cut, own_cut = (
-            value[0] for value in (total_shrink, total_out, other_cut, own_cut)
-        )
+        total_out, *qkv_cuts = [trip[0] for trip in trips]
         total_gains = sum_of(lax.optimization_barrier((*gains_sent, *line))[:-1])[0]
         input_grad = by_sequence(input_grad[:block], input_landed)
 

time: 584 us -> 620 us (1.062)
  waiting for transfers between devices: 128 us -> 243 us
  Pallas kernels: 226 us -> 129 us
  other arithmetic: 42.2 us -> 70.4 us
  local copies, waits for them, and re-layouts: 51.2 us -> 42.9 us
    pallas_call x33 -> x0, Pallas kernels: 96.1 us -> none  [the longest x31 92.4 us: sum_parts(): pl.pallas_call(functools.partial(sum_kernel, lead, take), out_shape=(jax....]
    ppermute x18 -> x9, waiting for transfers between devices: 20.8 us -> 60.7 us  [go(): return [value, lax.ppermute(value, 'rep', hops[step][0]), step]]
    all_gather x2, waiting for transfers between devices: 18.2 us -> 47.7 us  [gather_all(): return lax.all_gather(low, ('ctx', 'grp', 'rep'), axis=0, tiled=True)]
    convert_element_type x3 -> x21, other arithmetic: 7.11 us -> 36.4 us  [the longest x14 23.4 us: next_sum(): total = sum_of([kept, *sent]).astype(LOW)]
    ppermute x18 -> x9, starting transfers between devices: 45.1 us -> 17.5 us  [go(): return [value, lax.ppermute(value, 'rep', hops[step][0]), step]]
    ppermute x3, starting transfers between devices: 5.18 us -> 32.3 us  [swap_rep(): return lax.ppermute(value, 'rep', [(i, i ^ r) for i in range(reps)])]
    ppermute x29 -> x30, waiting for transfers between devices: 63.5 us -> 89.4 us  [swap_ctx(): return lax.ppermute(value, 'ctx', [(i, i ^ s) for i in range(n)])]
    ppermute x9, waiting for transfers between devices: 24.3 us -> 44.7 us  [swap_grp(): return lax.ppermute(value, 'grp', [(i, i ^ t) for i in range(inner)])]
  transfers between devices with their start and end apart: 75 -> 68, of which waited for: 15 -> 21; matrix products, arithmetic and copies ran while one was open for 13% -> 18% of each run, Pallas kernels for 31% -> 13%
where the time goes in v2:
time: 620 us; the launch traced here: 613 us
  waiting for transfers between devices  243 us (39%)
  Pallas kernels  129 us (21%)
  starting transfers between devices  90 us (15%)
  other arithmetic  70.4 us (11%)
  local copies, waits for them, and re-layouts  42.9 us (7%)
  matrix products  22.5 us (4%)
  between operations  15.1 us (2%)
    ppermute x30, waiting for transfers between devices, swap_ctx(): return lax.ppermute(value, 'ctx', [(i, i ^ s) for i in range(n)])  89.4 us
    ppermute x9, waiting for transfers between devices, go(): return [value, lax.ppermute(value, 'rep', hops[step][0]), step]  60.7 us
    all_gather x2, waiting for transfers between devices, gather_all(): return lax.all_gather(low, ('ctx', 'grp', 'rep'), axis=0, tiled=True)  47.7 us
    pallas_call x2, Pallas kernels, back(): pl.pallas_call(functools.partial(back_kernel, n, inner, half), out_shape=...  47.6 us
    ppermute x9, waiting for transfers between devices, swap_grp(): return lax.ppermute(value, 'grp', [(i, i ^ t) for i in range(inner)])  44.7 us
    pallas_call x1, Pallas kernels, feed(): pl.pallas_call(functools.partial(feed_kernel, chips), out_shape=(wide(D),...  37 us
    ppermute x3, starting transfers between devices, swap_rep(): return lax.ppermute(value, 'rep', [(i, i ^ r) for i in range(reps)])  32.3 us
    convert_element_type x14, other arithmetic, next_sum(): total = sum_of([kept, *sent]).astype(LOW)  23.4 us
  transfers between devices with their start and end apart: 68, of which 21 were waited for; matrix products, arithmetic and copies ran while one was open for 18% of the time, Pallas kernels for 13%

profile of v2, /device:TPU:0, one launch (start us, length us, event | category | flops | bytes accessed | tf_op | source)
XLA Modules:
  0.0 613.0 jit_solution(16063853304011962087)
XLA Ops:
  13.3 3.0 collective-permute-start
  36.8 18.1 %collective-permute-done.14.refs_4_ = bf16[128,2048]{1,0:T(8,128)(2,1)S(1)} collective-permute-done((bf16[128,2048]{1,0:T(8,128)(2,1)}, bf16[128,2048]{1,0:T(8,128)(2,1)S(1)}, u32[]{:S(2)}, u32[]{:S(2)}) %collective-permute-start.14) | collective-permute-done | bytes 524320 | tf_op jit(solution)/shard_map/ppermute | solution.py:644
  57.9 2.6 gather_fusion.1
  61.5 4.5 collective-permute-done.18.refs_10_
  67.1 11.4 %collective-permute-done.15.refs_5_ = bf16[128,2048]{1,0:T(8,128)(2,1)} collective-permute-done((bf16[128,2048]{1,0:T(8,128)(2,1)S(1)}, bf16[128,2048]{1,0:T(8,128)(2,1)}, u32[]{:S(2)}, u32[]{:S(2)}) %collective-permute-start.15) | collective-permute-done | bytes 524320 | tf_op jit(solution)/shard_map/ppermute | solution.py:653
  82.2 6.6 %collective-permute-done.19.refs_11_ = bf16[256,1024]{1,0:T(8,128)(2,1)} collective-permute-done((bf16[256,1024]{1,0:T(8,128)(2,1)S(1)}, bf16[256,1024]{1,0:T(8,128)(2,1)}, u32[]{:S(2)}, u32[]{:S(2)}) %collective-permute-start.19) | collective-permute-done | bytes 524320 | tf_op jit(solution)/shard_map/ppermute | solution.py:644
  89.8 10.6 %project.1 = (bf16[1024,1024]{1,0:T(8,128)(2,1)S(1)}, bf16[1024,1024]{1,0:T(8,128)(2,1)S(1)}, bf16[1024,512]{1,0:T(8,128)(2,1)S(1)}, bf16[1024,512]{1,0:T(8,128)(2,1)S(1)}, bf16[1024,1536]{1,0:T(8,128)(2,1)}) custom-call(s32[2]{0:T(128)S(1)} %pad_add_fusion.place_ref, bf16[128,2048]{1,0:T(8,128)(2,1)} %get-tuple-element.111.refs_0_, ...), custom_call_target="tpu_custom_call" | custom-call | flops 4294967296 | bytes 16777216 | tf_op jit(solution)/shard_map/project/pallas_call | solution.py:150
  104.1 11.4 %attend.2 = (bf16[1024,1024]{1,0:T(8,128)(2,1)}, f32[1024,128]{1,0:T(8,128)S(1)}, bf16[512,1024]{1,0:T(8,128)(2,1)S(1)}) custom-call(s32[2]{0:T(128)S(1)} %pad_add_fusion.place_ref, bf16[256,1024]{1,0:T(8,128)(2,1)S(1)} %convert_element_type.416.refs_0_.refs_8_, bf16[256,1024]{1,0:T(8,128)(2,1)S(1)} %collective-permute-done.8.refs_1_.refs_9_, ...), custom_call_target="tpu_custom_call" | custom-call | flops 3221225472 | bytes 8388608 | tf_op jit(solution)/shard_map/attend/pallas_call | solution.py:256
  115.6 8.5 %attend.3 = (bf16[1024,1024]{1,0:T(8,128)(2,1)}, f32[1024,128]{1,0:T(8,128)S(1)}, bf16[512,1024]{1,0:T(8,128)(2,1)S(1)}) custom-call(s32[2]{0:T(128)S(1)} %pad_add_fusion.place_ref, bf16[256,1024]{1,0:T(8,128)(2,1)S(1)} %convert_element_type.416.refs_0_.refs_8_, ...), custom_call_target="tpu_custom_call", output_to_operand_aliasing={{0}: (10, {}), {1}: (11, {})} | custom-call | flops 3221225472 | bytes 8388608 | tf_op jit(solution)/shard_map/attend/pallas_call | solution.py:256
  124.2 27.5 %collective-permute-done.20 = bf16[512,1024]{1,0:T(8,128)(2,1)S(1)} collective-permute-done((bf16[512,1024]{1,0:T(8,128)(2,1)S(1)}, bf16[512,1024]{1,0:T(8,128)(2,1)S(1)}, u32[]{:S(2)}, u32[]{:S(2)}) %collective-permute-start.20) | collective-permute-done | bytes 1048608 | tf_op jit(solution)/shard_map/ppermute | solution.py:644
  158.2 47.7 %all-gather.3.cloned.1.call-done.refs_0_.refs_1_.refs_2_.refs_3_ = bf16[1024,6144]{1,0:T(8,128)(2,1)} async-done(((bf16[32,6144]{1,0:T(8,128)(2,1)}), bf16[1024,6144]{1,0:T(8,128)(2,1)}) %all-gather.3.cloned.1.call-update) | async-done | bytes 12582928 | tf_op jit(solution)/shard_map/all_gather | solution.py:770
  206.0 37.0 %feed.1 = (bf16[1024,1024]{1,0:T(8,128)(2,1)}, bf16[1024,1024]{1,0:T(8,128)(2,1)}, bf16[1024,1536]{1,0:T(8,128)(2,1)}, bf16[1024,3072]{1,0:T(8,128)(2,1)}, bf16[...) custom-call(s32[2]{0:T(128)} %copy-done.23, ...), custom_call_target="tpu_custom_call" | custom-call | flops 19327352832 | bytes 31457280 | tf_op jit(solution)/shard_map/feed/pallas_call | solution.py:355
  243.2 2.6 collective-permute-done.25
  246.9 3.1 multiply_reduce_fusion
  250.4 2.5 fusion.63
  254.4 8.9 %convolution_convert_fusion = bf16[1024,3072]{1,0:T(8,128)(2,1)S(1)} fusion(bf16[1024,1024]{1,0:T(8,128)(2,1)} %get-tuple-element.140, bf16[1024,3072]{1,0:T(8,128)(2,1)S(1)} %copy-done.62), kind=kOutput, calls=%fused_computation.2 | convolution fusion | flops 6445596672 | bytes 14680064 | tf_op jit(solution)/shard_map/dot_general | solution.py:51
  267.8 4.9 convolution_convert_fusion.1
  272.7 5.6 collective-permute-done.26
  278.2 2.4 convolution_convert_fusion.4
  285.9 23.6 %back.2 = (bf16[1024,1024]{1,0:T(8,128)(2,1)}, bf16[1024,1024]{1,0:T(8,128)(2,1)}, f32[8,128]{1,0:T(8,128)}) custom-call(s32[2]{0:T(128)} %copy-done.23, bf16[128,2048]{1,0:T(8,128)(2,1)} %get-tuple-element.111.refs_0_, bf16[128,2048]{1,0:T(8,128)(2,1)} %collective-permute-done.11.refs_1_, bf16[128,2048]{1,0:T(8,128)(2,1)} %collective-permute-done.12.refs_2_, ...), custom_call_target="tpu_custom_call" | custom-call | flops 5905580032 | bytes 31457280 | tf_op jit(solution)/shard_map/back/pallas_call | solution.py:516
  309.5 4.0 convolution_convert_fusion.3
  315.8 3.8 fusion.16
  327.5 2.4 fusion.26
  329.9 24.0 %back.3 = (bf16[1024,1024]{1,0:T(8,128)(2,1)}, bf16[1024,1024]{1,0:T(8,128)(2,1)}, f32[8,128]{1,0:T(8,128)}) custom-call(s32[2]{0:T(128)} %copy-done.23, bf16[128,2048]{1,0:T(8,128)(2,1)} %get-tuple-element.111.refs_0_, bf16[128,2048]{1,0:T(8,128)(2,1)} %collective-permute-done.11.refs_1_, bf16[128,2048]{1,0:T(8,128)(2,1)} %collective-permute-done.12.refs_2_, ...), custom_call_target="tpu_custom_call" | custom-call | flops 5905580032 | bytes 31457280 | tf_op jit(solution)/shard_map/back/pallas_call | solution.py:516
  354.0 2.6 fusion.14
  356.5 19.6 %collective-permute-done.33 = bf16[384,1024]{1,0:T(8,128)(2,1)} collective-permute-done((bf16[384,1024]{1,0:T(8,128)(2,1)}, bf16[384,1024]{1,0:T(8,128)(2,1)}, u32[]{:S(2)}, u32[]{:S(2)}) %collective-permute-start.33) | collective-permute-done | bytes 786464 | tf_op jit(solution)/shard_map/ppermute | solution.py:644
  376.1 2.6 fusion.15
  382.8 2.4 convolution_convert_fusion.2
  389.2 2.4 slice.65
  395.3 2.6 fusion.22
  398.5 4.1 collective-permute-done.42
  403.6 3.6 collective-permute-start.45
  407.3 12.3 %collective-permute-done.41 = bf16[384,1024]{1,0:T(8,128)(2,1)S(1)} collective-permute-done((bf16[384,1024]{1,0:T(8,128)(2,1)}, bf16[384,1024]{1,0:T(8,128)(2,1)S(1)}, u32[]{:S(2)}, u32[]{:S(2)}) %collective-permute-start.41) | collective-permute-done | bytes 786464 | tf_op jit(solution)/shard_map/ppermute | solution.py:653
  422.2 8.7 %collective-permute-done.39 = bf16[2,128,1024]{2,1,0:T(8,128)(2,1)} collective-permute-done((bf16[2,128,1024]{2,1,0:T(8,128)(2,1)}, bf16[2,128,1024]{2,1,0:T(8,128)(2,1)}, u32[]{:S(2)}, u32[]{:S(2)}) %collective-permute-start.39) | collective-permute-done | bytes 524320 | tf_op jit(solution)/shard_map/ppermute | solution.py:653
  433.8 7.9 %collective-permute-done.38 = bf16[2,128,1024]{2,1,0:T(8,128)(2,1)} collective-permute-done((bf16[2,128,1024]{2,1,0:T(8,128)(2,1)}, bf16[2,128,1024]{2,1,0:T(8,128)(2,1)}, u32[]{:S(2)}, u32[]{:S(2)}) %collective-permute-start.38) | collective-permute-done | bytes 524320 | tf_op jit(solution)/shard_map/ppermute | solution.py:653
  448.3 3.2 collective-permute-done.44
  452.3 3.6 collective-permute-start.47
  456.7 3.2 collective-permute-start.50
  463.7 4.6 fusion.7
  470.3 8.8 %collective-permute-done.47 = bf16[2,128,1024]{2,1,0:T(8,128)(2,1)} collective-permute-done((bf16[2,128,1024]{2,1,0:T(8,128)(2,1)}, bf16[2,128,1024]{2,1,0:T(8,128)(2,1)}, u32[]{:S(2)}, u32[]{:S(2)}) %collective-permute-start.47) | collective-permute-done | bytes 524320 | tf_op jit(solution)/shard_map/ppermute | solution.py:832
  481.9 16.3 %collective-permute-done.50 = bf16[2,128,1024]{2,1,0:T(8,128)(2,1)} collective-permute-done((bf16[2,128,1024]{2,1,0:T(8,128)(2,1)}, bf16[2,128,1024]{2,1,0:T(8,128)(2,1)}, u32[]{:S(2)}, u32[]{:S(2)}) %collective-permute-start.50) | collective-permute-done | bytes 524320 | tf_op jit(solution)/shard_map/ppermute | solution.py:832
  500.6 2.7 collective-permute-start.59
  508.2 28.8 %collective-permute-start.62 = (f32[1,288]{1,0:T(1,128)S(1)}, f32[1,288]{1,0:T(1,128)S(1)}, u32[]{:S(2)}, u32[]{:S(2)}) collective-permute-start(f32[1,288]{1,0:T(1,128)S(1)} %add_add_fusion), channel_id=1, source_target_pairs={{0,1},{1,0},{2,3},{3,2},{4,5},{5,4},{6,7},{7,6},{8,9},{9,8},{10,11... | collective-permute-start | bytes 3464 | tf_op jit(solution)/shard_map/ppermute | solution.py:656
  550.5 27.0 %collective-permute-done.51 = bf16[2,128,1024]{2,1,0:T(8,128)(2,1)S(1)} collective-permute-done((bf16[2,128,1024]{2,1,0:T(8,128)(2,1)S(1)}, bf16[2,128,1024]{2,1,0:T(8,128)(2,1)S(1)}, u32[]{:S(2)}, u32[]{:S(2)}) %collective-permute-start.51) | collective-permute-done | bytes 524320 | tf_op jit(solution)/shard_map/ppermute | solution.py:832
  577.5 8.6 %collective-permute-done.54 = bf16[2,128,1024]{2,1,0:T(8,128)(2,1)S(1)} collective-permute-done((bf16[2,128,1024]{2,1,0:T(8,128)(2,1)S(1)}, bf16[2,128,1024]{2,1,0:T(8,128)(2,1)S(1)}, u32[]{:S(2)}, u32[]{:S(2)}) %collective-permute-start.54) | collective-permute-done | bytes 524320 | tf_op jit(solution)/shard_map/ppermute | solution.py:832
  586.9 5.4 multiply_subtract_fusion
  592.3 7.4 %adam_cuts.1 = (f32[128,4096]{1,0:T(8,128)}, f32[128,4096]{1,0:T(8,128)}, f32[128,4096]{1,0:T(8,128)}) custom-call(s32[1]{0:T(128)} %bitcast.62.key_ref, bf16[2,128,1024]{2,1,0:T(8,128)(2,1)S(1)} %broadcast_select_fusion.2.refs_0_, bf16[2,128,1024]{2,1,0:T(8,128)(2,1)S(1)} %broadcast_select_fusion.1.refs_1_, f32[128,4096]{1,0:T(8,128)S(1)} %copy-done.2, ...), custom_call_target="tpu_custom_call" | custom-call | flops 10485760 | bytes 13631488 | tf_op jit(solution)/shard_map/adam_cuts/pallas_call | solution.py:589
  599.8 6.5 %adam_pair.1 = (f32[128,6144]{1,0:T(8,128)}, f32[128,6144]{1,0:T(8,128)}, f32[128,6144]{1,0:T(8,128)}) custom-call(s32[2]{0:T(128)S(1)} %copy-done.24, bf16[128,3072]{1,0:T(8,128)(2,1)S(1)} %copy-done.15, bf16[128,3072]{1,0:T(8,128)(2,1)S(1)} %copy-done.16, f32[128,6144]{1,0:T(8,128)S(1)} %copy-done.3, f32[128,6144]{1,0:T(8,128)S(1)} %copy-done.4, ...), custom_call_target="tpu_custom_call" | custom-call | flops 15728640 | bytes 20447232 | tf_op jit(solution)/shard_map/adam_pair/pallas_call | solution.py:619
  (330 shorter events, 126.4 us)
Async XLA Ops:
  7.2 151.0 %all-gather.5.cloned.1.call-start = ((), (), s32[]{:S(2)}) async-start(), calls=%async_computation.1 | async-start | bytes 6488064 | tf_op jit(solution)/shard_map/all_gather | solution.py:770
  9.1 196.9 %all-gather.3.cloned.1.call-start = ((), (), s32[]{:S(2)}) async-start(), calls=%async_computation | async-start | bytes 12976128 | tf_op jit(solution)/shard_map/all_gather | solution.py:770
  11.2 575.7 %all-reduce.4.cloned.1.call-start = ((), (), s32[]{:S(2)}) async-start(), calls=%async_computation.2 | async-start | bytes 4718592 | tf_op jit(solution)/shard_map/psum | solution.py:915
  32.3 28.6 %collective-permute-start.8 = (bf16[256,1024]{1,0:T(8,128)(2,1)S(1)}, bf16[256,1024]{1,0:T(8,128)(2,1)S(1)}, u32[]{:S(2)}, u32[]{:S(2)}) collective-permute-start(bf16[256,1024]{1,0:T(8,128)(2,1)S(1)} %convert_element_type.416.refs_0_.refs_8_), channel_id=1, source_target_pairs={{0,4},{4,0},{1,5},{5,1},{2,6},{6,2},{3,7},{7,3},{8,12},{12,8},{9,1... | collective-permute-start | bytes 1572872 | tf_op jit(solution)/shard_map/ppermute | solution.py:653
  34.3 20.7 %collective-permute-start.14 = (bf16[128,2048]{1,0:T(8,128)(2,1)}, bf16[128,2048]{1,0:T(8,128)(2,1)S(1)}, u32[]{:S(2)}, u32[]{:S(2)}) collective-permute-start(bf16[128,2048]{1,0:T(8,128)(2,1)} %get-tuple-element.112), channel_id=1, source_target_pairs={{0,16},{8,24},{16,0},{24,8},{1,17},{9,25},{17,1},{25,9},{2,18},{10... | collective-permute-start | bytes 1572872 | tf_op jit(solution)/shard_map/ppermute | solution.py:644
  35.9 25.3 %collective-permute-start.11 = (bf16[128,2048]{1,0:T(8,128)(2,1)}, bf16[128,2048]{1,0:T(8,128)(2,1)}, u32[]{:S(2)}, u32[]{:S(2)}) collective-permute-start(bf16[128,2048]{1,0:T(8,128)(2,1)} %get-tuple-element.111.refs_0_), channel_id=1, source_target_pairs={{0,4},{4,0},{1,5},{5,1},{2,6},{6,2},{3,7},{7,3},{8,12},{12,8},{9,1... | collective-permute-start | bytes 1572872 | tf_op jit(solution)/shard_map/ppermute | solution.py:653
  36.5 29.5 %collective-permute-start.18 = (bf16[256,1024]{1,0:T(8,128)(2,1)S(1)}, bf16[256,1024]{1,0:T(8,128)(2,1)S(1)}, u32[]{:S(2)}, u32[]{:S(2)}) collective-permute-start(bf16[256,1024]{1,0:T(8,128)(2,1)S(1)} %dynamic-slice_bitcast_fusion.7.refs_8_), channel_id=1, source_target_pairs={{0,16},{8,24},{16,0},{24,8},{1,17},{9,25},{17,1},{25,9},{2,18},{10... | collective-permute-start | bytes 1572872 | tf_op jit(solution)/shard_map/ppermute | solution.py:644
  36.7 30.2 %collective-permute-start.7 = (bf16[256,1024]{1,0:T(8,128)(2,1)}, bf16[256,1024]{1,0:T(8,128)(2,1)S(1)}, u32[]{:S(2)}, u32[]{:S(2)}) collective-permute-start(bf16[256,1024]{1,0:T(8,128)(2,1)} %dynamic-slice_bitcast_fusion.8), channel_id=1, source_target_pairs={{0,8},{8,0},{16,24},{24,16},{1,9},{9,1},{17,25},{25,17},{2,10},{10... | collective-permute-start | bytes 1572872 | tf_op jit(solution)/shard_map/ppermute | solution.py:644
  55.0 23.5 %collective-permute-start.15 = (bf16[128,2048]{1,0:T(8,128)(2,1)S(1)}, bf16[128,2048]{1,0:T(8,128)(2,1)}, u32[]{:S(2)}, u32[]{:S(2)}) collective-permute-start(bf16[128,2048]{1,0:T(8,128)(2,1)S(1)} %collective-permute-done.14.refs_4_), channel_id=1, source_target_pairs={{0,4},{4,0},{1,5},{5,1},{2,6},{6,2},{3,7},{7,3},{8,12},{12,8},{9,1... | collective-permute-start | bytes 1572872 | tf_op jit(solution)/shard_map/ppermute | solution.py:653
  61.2 20.9 %collective-permute-start.13 = (bf16[128,2048]{1,0:T(8,128)(2,1)}, bf16[128,2048]{1,0:T(8,128)(2,1)}, u32[]{:S(2)}, u32[]{:S(2)}) collective-permute-start(bf16[128,2048]{1,0:T(8,128)(2,1)} %collective-permute-done.11.refs_1_), channel_id=1, source_target_pairs={{0,8},{8,0},{16,24},{24,16},{1,9},{9,1},{17,25},{25,17},{2,10},{10... | collective-permute-start | bytes 1572872 | tf_op jit(solution)/shard_map/ppermute | solution.py:644
  66.9 21.9 %collective-permute-start.19 = (bf16[256,1024]{1,0:T(8,128)(2,1)S(1)}, bf16[256,1024]{1,0:T(8,128)(2,1)}, u32[]{:S(2)}, u32[]{:S(2)}) collective-permute-start(bf16[256,1024]{1,0:T(8,128)(2,1)S(1)} %collective-permute-done.7.refs_9_), channel_id=1, source_target_pairs={{0,16},{8,24},{16,0},{24,8},{1,17},{9,25},{17,1},{25,9},{2,18},{10... | collective-permute-start | bytes 1572872 | tf_op jit(solution)/shard_map/ppermute | solution.py:644
  81.5 22.6 %collective-permute-start.9 = (bf16[256,1024]{1,0:T(8,128)(2,1)S(1)}, bf16[256,1024]{1,0:T(8,128)(2,1)S(1)}, u32[]{:S(2)}, u32[]{:S(2)}) collective-permute-start(bf16[256,1024]{1,0:T(8,128)(2,1)S(1)} %convert_element_type.416.refs_0_.refs_8_), channel_id=1, source_target_pairs={{0,8},{8,0},{16,24},{24,16},{1,9},{9,1},{17,25},{25,17},{2,10},{10... | collective-permute-start | bytes 1572872 | tf_op jit(solution)/shard_map/ppermute | solution.py:644
  82.1 22.0 %collective-permute-start.10 = (bf16[256,1024]{1,0:T(8,128)(2,1)S(1)}, bf16[256,1024]{1,0:T(8,128)(2,1)S(1)}, u32[]{:S(2)}, u32[]{:S(2)}) collective-permute-start(bf16[256,1024]{1,0:T(8,128)(2,1)S(1)} %collective-permute-done.8.refs_1_.refs_9_), channel_id=1, source_target_pairs={{0,8},{8,0},{16,24},{24,16},{1,9},{9,1},{17,25},{25,17},{2,10},{10... | collective-permute-start | bytes 1572872 | tf_op jit(solution)/shard_map/ppermute | solution.py:644
  115.5 36.2 %collective-permute-start.20 = (bf16[512,1024]{1,0:T(8,128)(2,1)S(1)}, bf16[512,1024]{1,0:T(8,128)(2,1)S(1)}, u32[]{:S(2)}, u32[]{:S(2)}) collective-permute-start(bf16[512,1024]{1,0:T(8,128)(2,1)S(1)} %get-tuple-element.124), channel_id=1, source_target_pairs={{0,16},{8,24},{16,0},{24,8},{1,17},{9,25},{17,1},{25,9},{2,18},{10... | collective-permute-start | bytes 3145736 | tf_op jit(solution)/shard_map/ppermute | solution.py:644
  115.5 39.9 %collective-permute-start.22 = (bf16[2,256,1024]{2,1,0:T(8,128)(2,1)S(1)}, bf16[2,256,1024]{2,1,0:T(8,128)(2,1)S(1)}, u32[]{:S(2)}, u32[]{:S(2)}) collective-permute-start(bf16[2,256,1024]{2,1,0:T(8,128)(2,1)S(1)} %copy-done.60), channel_id=1, source_target_pairs={{0,8},{8,0},{16,24},{24,16},{1,9},{9,1},{17,25},{25,17},{2,10},{10... | collective-permute-start | bytes 3145736 | tf_op jit(solution)/shard_map/ppermute | solution.py:644
  252.9 25.4 %collective-permute-start.26 = (bf16[512,1024]{1,0:T(8,128)(2,1)S(1)}, bf16[512,1024]{1,0:T(8,128)(2,1)S(1)}, u32[]{:S(2)}, u32[]{:S(2)}) collective-permute-start(bf16[512,1024]{1,0:T(8,128)(2,1)S(1)} %fusion.63), channel_id=1, source_target_pairs={{0,16},{8,24},{16,0},{24,8},{1,17},{9,25},{17,1},{25,9},{2,18},{10... | collective-permute-start | bytes 3145736 | tf_op jit(solution)/shard_map/ppermute | solution.py:644
  264.6 51.2 %collective-permute-start.29 = (bf16[2,128,3072]{2,1,0:T(8,128)(2,1)}, bf16[2,128,3072]{2,1,0:T(8,128)(2,1)}, u32[]{:S(2)}, u32[]{:S(2)}) collective-permute-start(bf16[2,128,3072]{2,1,0:T(8,128)(2,1)} %dynamic-slice_bitcast_fusion.1), channel_id=1, source_target_pairs={{0,4},{4,0},{1,5},{5,1},{2,6},{6,2},{3,7},{7,3},{8,12},{12,8},{9,1... | collective-permute-start | bytes 4718600 | tf_op jit(solution)/shard_map/ppermute | solution.py:653
  282.3 31.1 %collective-permute-start.30 = (bf16[128,3072]{1,0:T(8,128)(2,1)S(1)}, bf16[128,3072]{1,0:T(8,128)(2,1)}, u32[]{:S(2)}, u32[]{:S(2)}) collective-permute-start(bf16[128,3072]{1,0:T(8,128)(2,1)S(1)} %get-tuple-element.230), channel_id=1, source_target_pairs={{0,16},{8,24},{16,0},{24,8},{1,17},{9,25},{17,1},{25,9},{2,18},{10... | collective-permute-start | bytes 2359304 | tf_op jit(solution)/shard_map/ppermute | solution.py:644
  283.8 35.8 %collective-permute-start.28 = (bf16[128,3072]{1,0:T(8,128)(2,1)S(1)}, bf16[128,3072]{1,0:T(8,128)(2,1)S(1)}, u32[]{:S(2)}, u32[]{:S(2)}) collective-permute-start(bf16[128,3072]{1,0:T(8,128)(2,1)S(1)} %get-tuple-element.231), channel_id=1, source_target_pairs={{0,16},{8,24},{16,0},{24,8},{1,17},{9,25},{17,1},{25,9},{2,18},{10... | collective-permute-start | bytes 2359304 | tf_op jit(solution)/shard_map/ppermute | solution.py:644
  284.4 42.5 %collective-permute-start.27 = (bf16[2,256,1024]{2,1,0:T(8,128)(2,1)}, bf16[2,256,1024]{2,1,0:T(8,128)(2,1)}, u32[]{:S(2)}, u32[]{:S(2)}) collective-permute-start(bf16[2,256,1024]{2,1,0:T(8,128)(2,1)} %dynamic-slice_bitcast_fusion.2), channel_id=1, source_target_pairs={{0,8},{8,0},{16,24},{24,16},{1,9},{9,1},{17,25},{25,17},{2,10},{10... | collective-permute-start | bytes 3145736 | tf_op jit(solution)/shard_map/ppermute | solution.py:644
  322.2 31.8 %collective-permute-start.34 = (bf16[384,1024]{1,0:T(8,128)(2,1)}, bf16[384,1024]{1,0:T(8,128)(2,1)}, u32[]{:S(2)}, u32[]{:S(2)}) collective-permute-start(bf16[384,1024]{1,0:T(8,128)(2,1)} %get-tuple-element.226), channel_id=1, source_target_pairs={{0,16},{8,24},{16,0},{24,8},{1,17},{9,25},{17,1},{25,9},{2,18},{10... | collective-permute-start | bytes 2359304 | tf_op jit(solution)/shard_map/ppermute | solution.py:644
  324.6 56.3 %collective-permute-start.31 = (bf16[2,2,128,1024]{3,2,0,1:T(8,128)(2,1)}, bf16[2,2,128,1024]{3,2,0,1:T(8,128)(2,1)S(1)}, u32[]{:S(2)}, u32[]{:S(2)}) collective-permute-start(bf16[2,2,128,1024]{3,2,0,1:T(8,128)(2,1)} %copy_bitcast_fusion.1), channel_id=1, source_target_pairs={{0,8},{8,0},{16,24},{24,16},{1,9},{9,1},{17,25},{25,17},{2,10},{10... | collective-permute-start | bytes 3145736 | tf_op jit(solution)/shard_map/ppermute | solution.py:644
  324.9 53.8 %collective-permute-start.32 = (bf16[128,3072]{1,0:T(8,128)(2,1)S(1)}, bf16[128,3072]{1,0:T(8,128)(2,1)}, u32[]{:S(2)}, u32[]{:S(2)}) collective-permute-start(bf16[128,3072]{1,0:T(8,128)(2,1)S(1)} %fusion.18), channel_id=1, source_target_pairs={{0,4},{4,0},{1,5},{5,1},{2,6},{6,2},{3,7},{7,3},{8,12},{12,8},{9,1... | collective-permute-start | bytes 2359304 | tf_op jit(solution)/shard_map/ppermute | solution.py:653
  325.4 68.2 %collective-permute-start.36 = (bf16[128,3072]{1,0:T(8,128)(2,1)}, bf16[128,3072]{1,0:T(8,128)(2,1)}, u32[]{:S(2)}, u32[]{:S(2)}) collective-permute-start(bf16[128,3072]{1,0:T(8,128)(2,1)} %get-tuple-element.220), channel_id=1, source_target_pairs={{0,16},{8,24},{16,0},{24,8},{1,17},{9,25},{17,1},{25,9},{2,18},{10... | collective-permute-start | bytes 2359304 | tf_op jit(solution)/shard_map/ppermute | solution.py:644
  326.9 49.2 %collective-permute-start.33 = (bf16[384,1024]{1,0:T(8,128)(2,1)}, bf16[384,1024]{1,0:T(8,128)(2,1)}, u32[]{:S(2)}, u32[]{:S(2)}) collective-permute-start(bf16[384,1024]{1,0:T(8,128)(2,1)} %get-tuple-element.227), channel_id=1, source_target_pairs={{0,16},{8,24},{16,0},{24,8},{1,17},{9,25},{17,1},{25,9},{2,18},{10... | collective-permute-start | bytes 2359304 | tf_op jit(solution)/shard_map/ppermute | solution.py:644
  391.6 27.9 %collective-permute-start.41 = (bf16[384,1024]{1,0:T(8,128)(2,1)}, bf16[384,1024]{1,0:T(8,128)(2,1)S(1)}, u32[]{:S(2)}, u32[]{:S(2)}) collective-permute-start(bf16[384,1024]{1,0:T(8,128)(2,1)} %fusion.14), channel_id=1, source_target_pairs={{0,4},{4,0},{1,5},{5,1},{2,6},{6,2},{3,7},{7,3},{8,12},{12,8},{9,1... | collective-permute-start | bytes 2359304 | tf_op jit(solution)/shard_map/ppermute | solution.py:653
  392.2 38.7 %collective-permute-start.39 = (bf16[2,128,1024]{2,1,0:T(8,128)(2,1)}, bf16[2,128,1024]{2,1,0:T(8,128)(2,1)}, u32[]{:S(2)}, u32[]{:S(2)}) collective-permute-start(bf16[2,128,1024]{2,1,0:T(8,128)(2,1)} %get-tuple-element.224), channel_id=1, source_target_pairs={{0,4},{4,0},{1,5},{5,1},{2,6},{6,2},{3,7},{7,3},{8,12},{12,8},{9,1... | collective-permute-start | bytes 1572872 | tf_op jit(solution)/shard_map/ppermute | solution.py:653
  395.2 26.9 %collective-permute-start.40 = (bf16[128,3072]{1,0:T(8,128)(2,1)S(1)}, bf16[128,3072]{1,0:T(8,128)(2,1)}, u32[]{:S(2)}, u32[]{:S(2)}) collective-permute-start(bf16[128,3072]{1,0:T(8,128)(2,1)S(1)} %add_convert_fusion.2), channel_id=1, source_target_pairs={{0,8},{8,0},{16,24},{24,16},{1,9},{9,1},{17,25},{25,17},{2,10},{10... | collective-permute-start | bytes 2359304 | tf_op jit(solution)/shard_map/ppermute | solution.py:644
  398.0 43.7 %collective-permute-start.38 = (bf16[2,128,1024]{2,1,0:T(8,128)(2,1)}, bf16[2,128,1024]{2,1,0:T(8,128)(2,1)}, u32[]{:S(2)}, u32[]{:S(2)}) collective-permute-start(bf16[2,128,1024]{2,1,0:T(8,128)(2,1)} %get-tuple-element.222), channel_id=1, source_target_pairs={{0,4},{4,0},{1,5},{5,1},{2,6},{6,2},{3,7},{7,3},{8,12},{12,8},{9,1... | collective-permute-start | bytes 1572872 | tf_op jit(solution)/shard_map/ppermute | solution.py:653
  403.6 41.0 %collective-permute-start.45 = (bf16[256,1024]{1,0:T(8,128)(2,1)}, bf16[256,1024]{1,0:T(8,128)(2,1)}, u32[]{:S(2)}, u32[]{:S(2)}) collective-permute-start(bf16[256,1024]{1,0:T(8,128)(2,1)} %add_convert_fusion.10), channel_id=1, source_target_pairs={{0,1},{3,2},{4,5},{7,6},{8,9},{11,10},{12,13},{15,14},{16,17},{19,... | collective-permute-start | bytes 1572872 | tf_op jit(solution)/shard_map/ppermute | solution.py:832
  419.5 40.4 %collective-permute-start.37 = (bf16[512,1024]{1,0:T(8,128)(2,1)}, bf16[512,1024]{1,0:T(8,128)(2,1)}, u32[]{:S(2)}, u32[]{:S(2)}) collective-permute-start(bf16[512,1024]{1,0:T(8,128)(2,1)} %slice.65), channel_id=1, source_target_pairs={{0,16},{8,24},{16,0},{24,8},{1,17},{9,25},{17,1},{25,9},{2,18},{10... | collective-permute-start | bytes 3145736 | tf_op jit(solution)/shard_map/ppermute | solution.py:644
  422.1 41.5 %collective-permute-start.23 = (bf16[512,1024]{1,0:T(8,128)(2,1)}, bf16[512,1024]{1,0:T(8,128)(2,1)}, u32[]{:S(2)}, u32[]{:S(2)}) collective-permute-start(bf16[512,1024]{1,0:T(8,128)(2,1)} %get-tuple-element.129), channel_id=1, source_target_pairs={{0,8},{8,0},{16,24},{24,16},{1,9},{9,1},{17,25},{25,17},{2,10},{10... | collective-permute-start | bytes 3145736 | tf_op jit(solution)/shard_map/ppermute | solution.py:644
  446.8 21.4 %collective-permute-start.48 = (bf16[256,1024]{1,0:T(8,128)(2,1)}, bf16[256,1024]{1,0:T(8,128)(2,1)}, u32[]{:S(2)}, u32[]{:S(2)}) collective-permute-start(bf16[256,1024]{1,0:T(8,128)(2,1)} %add_convert_fusion.9), channel_id=1, source_target_pairs={{1,2},{2,1},{5,6},{6,5},{9,10},{10,9},{13,14},{14,13},{17,18},{18,... | collective-permute-start | bytes 1572872 | tf_op jit(solution)/shard_map/ppermute | solution.py:832
  452.3 26.8 %collective-permute-start.47 = (bf16[2,128,1024]{2,1,0:T(8,128)(2,1)}, bf16[2,128,1024]{2,1,0:T(8,128)(2,1)}, u32[]{:S(2)}, u32[]{:S(2)}) collective-permute-start(bf16[2,128,1024]{2,1,0:T(8,128)(2,1)} %pad_maximum_fusion.2), channel_id=1, source_target_pairs={{0,1},{3,2},{4,5},{7,6},{8,9},{11,10},{12,13},{15,14},{16,17},{19,... | collective-permute-start | bytes 1572872 | tf_op jit(solution)/shard_map/ppermute | solution.py:832
  456.7 41.5 %collective-permute-start.50 = (bf16[2,128,1024]{2,1,0:T(8,128)(2,1)}, bf16[2,128,1024]{2,1,0:T(8,128)(2,1)}, u32[]{:S(2)}, u32[]{:S(2)}) collective-permute-start(bf16[2,128,1024]{2,1,0:T(8,128)(2,1)} %pad_maximum_fusion.3), channel_id=1, source_target_pairs={{0,1},{3,2},{4,5},{7,6},{8,9},{11,10},{12,13},{15,14},{16,17},{19,... | collective-permute-start | bytes 1572872 | tf_op jit(solution)/shard_map/ppermute | solution.py:832
  462.1 36.9 %collective-permute-start.55 = (f32[1,288]{1,0:T(1,128)S(1)}, f32[1,288]{1,0:T(1,128)S(1)}, u32[]{:S(2)}, u32[]{:S(2)}) collective-permute-start(f32[1,288]{1,0:T(1,128)S(1)} %get-tuple-element.261), channel_id=1, source_target_pairs={{0,4},{4,0},{8,12},{12,8},{16,20},{20,16},{24,28},{28,24},{1,5},{5... | collective-permute-start | bytes 3464 | tf_op jit(solution)/shard_map/ppermute | solution.py:672
  463.6 37.0 %collective-permute-start.56 = (f32[1,288]{1,0:T(1,128)S(1)}, f32[1,288]{1,0:T(1,128)S(1)}, u32[]{:S(2)}, u32[]{:S(2)}) collective-permute-start(f32[1,288]{1,0:T(1,128)S(1)} %get-tuple-element.260), channel_id=1, source_target_pairs={{0,8},{4,12},{8,0},{12,4},{16,24},{20,28},{24,16},{28,20},{1,9},{5... | collective-permute-start | bytes 3464 | tf_op jit(solution)/shard_map/ppermute | solution.py:672
  468.2 35.1 %collective-permute-start.57 = (f32[1,288]{1,0:T(1,128)S(1)}, f32[1,288]{1,0:T(1,128)S(1)}, u32[]{:S(2)}, u32[]{:S(2)}) collective-permute-start(f32[1,288]{1,0:T(1,128)S(1)} %get-tuple-element.259), channel_id=1, source_target_pairs={{0,12},{4,8},{8,4},{12,0},{16,28},{20,24},{24,20},{28,16},{1,13},{... | collective-permute-start | bytes 3464 | tf_op jit(solution)/shard_map/ppermute | solution.py:672
  479.1 24.2 %collective-permute-start.58 = (f32[1,288]{1,0:T(1,128)S(1)}, f32[1,288]{1,0:T(1,128)S(1)}, u32[]{:S(2)}, u32[]{:S(2)}) collective-permute-start(f32[1,288]{1,0:T(1,128)S(1)} %get-tuple-element.258), channel_id=1, source_target_pairs={{0,16},{4,20},{8,24},{12,28},{16,0},{20,4},{24,8},{28,12},{1,17},{... | collective-permute-start | bytes 3464 | tf_op jit(solution)/shard_map/ppermute | solution.py:672
  499.1 39.3 %collective-permute-start.53 = (bf16[256,1024]{1,0:T(8,128)(2,1)S(1)}, bf16[256,1024]{1,0:T(8,128)(2,1)S(1)}, u32[]{:S(2)}, u32[]{:S(2)}) collective-permute-start(bf16[256,1024]{1,0:T(8,128)(2,1)S(1)} %add_convert_fusion.8), channel_id=1, source_target_pairs={{1,0},{2,3},{5,4},{6,7},{9,8},{10,11},{13,12},{14,15},{17,16},{18,... | collective-permute-start | bytes 1572872 | tf_op jit(solution)/shard_map/ppermute | solution.py:832
  506.3 39.1 %collective-permute-start.46 = (bf16[256,1024]{1,0:T(8,128)(2,1)S(1)}, bf16[256,1024]{1,0:T(8,128)(2,1)S(1)}, u32[]{:S(2)}, u32[]{:S(2)}) collective-permute-start(bf16[256,1024]{1,0:T(8,128)(2,1)S(1)} %get-tuple-element.247), channel_id=1, source_target_pairs={{0,8},{8,0},{16,24},{24,16},{1,9},{9,1},{17,25},{25,17},{2,10},{10... | collective-permute-start | bytes 1572872 | tf_op jit(solution)/shard_map/ppermute | solution.py:644
  506.4 41.4 %collective-permute-start.24 = (bf16[256,1024]{1,0:T(8,128)(2,1)S(1)}, bf16[256,1024]{1,0:T(8,128)(2,1)S(1)}, u32[]{:S(2)}, u32[]{:S(2)}) collective-permute-start(bf16[256,1024]{1,0:T(8,128)(2,1)S(1)} %get-tuple-element.254), channel_id=1, source_target_pairs={{0,8},{8,0},{16,24},{24,16},{1,9},{9,1},{17,25},{25,17},{2,10},{10... | collective-permute-start | bytes 1572872 | tf_op jit(solution)/shard_map/ppermute | solution.py:644
  507.3 35.5 %collective-permute-start.52 = (bf16[2,128,1024]{2,1,0:T(8,128)(2,1)S(1)}, bf16[2,128,1024]{2,1,0:T(8,128)(2,1)S(1)}, u32[]{:S(2)}, u32[]{:S(2)}) collective-permute-start(bf16[2,128,1024]{2,1,0:T(8,128)(2,1)S(1)} %add_convert_fusion.6), channel_id=1, source_target_pairs={{1,2},{2,1},{5,6},{6,5},{9,10},{10,9},{13,14},{14,13},{17,18},{18,... | collective-permute-start | bytes 1572872 | tf_op jit(solution)/shard_map/ppermute | solution.py:832
  508.2 77.9 %collective-permute-start.62 = (f32[1,288]{1,0:T(1,128)S(1)}, f32[1,288]{1,0:T(1,128)S(1)}, u32[]{:S(2)}, u32[]{:S(2)}) collective-permute-start(f32[1,288]{1,0:T(1,128)S(1)} %add_add_fusion), channel_id=1, source_target_pairs={{0,1},{1,0},{2,3},{3,2},{4,5},{5,4},{6,7},{7,6},{8,9},{9,8},{10,11... | collective-permute-start | bytes 3464 | tf_op jit(solution)/shard_map/ppermute | solution.py:656
  538.4 47.8 %collective-permute-start.63 = (f32[1,288]{1,0:T(1,128)S(1)}, f32[1,288]{1,0:T(1,128)S(1)}, u32[]{:S(2)}, u32[]{:S(2)}) collective-permute-start(f32[1,288]{1,0:T(1,128)S(1)} %add_add_fusion), channel_id=1, source_target_pairs={{0,2},{1,3},{2,0},{3,1},{4,6},{5,7},{6,4},{7,5},{8,10},{9,11},{10,... | collective-permute-start | bytes 3464 | tf_op jit(solution)/shard_map/ppermute | solution.py:656
  542.8 34.7 %collective-permute-start.51 = (bf16[2,128,1024]{2,1,0:T(8,128)(2,1)S(1)}, bf16[2,128,1024]{2,1,0:T(8,128)(2,1)S(1)}, u32[]{:S(2)}, u32[]{:S(2)}) collective-permute-start(bf16[2,128,1024]{2,1,0:T(8,128)(2,1)S(1)} %add_convert_fusion.5), channel_id=1, source_target_pairs={{1,0},{2,3},{5,4},{6,7},{9,8},{10,11},{13,12},{14,15},{17,16},{18,... | collective-permute-start | bytes 1572872 | tf_op jit(solution)/shard_map/ppermute | solution.py:832
  545.4 40.7 %collective-permute-start.54 = (bf16[2,128,1024]{2,1,0:T(8,128)(2,1)S(1)}, bf16[2,128,1024]{2,1,0:T(8,128)(2,1)S(1)}, u32[]{:S(2)}, u32[]{:S(2)}) collective-permute-start(bf16[2,128,1024]{2,1,0:T(8,128)(2,1)S(1)} %add_convert_fusion.4), channel_id=1, source_target_pairs={{1,0},{2,3},{5,4},{6,7},{9,8},{10,11},{13,12},{14,15},{17,16},{18,... | collective-permute-start | bytes 1572872 | tf_op jit(solution)/shard_map/ppermute | solution.py:832
  547.8 38.4 %collective-permute-start.64 = (f32[1,288]{1,0:T(1,128)S(1)}, f32[1,288]{1,0:T(1,128)S(1)}, u32[]{:S(2)}, u32[]{:S(2)}) collective-permute-start(f32[1,288]{1,0:T(1,128)S(1)} %add_add_fusion), channel_id=1, source_target_pairs={{0,3},{1,2},{2,1},{3,0},{4,7},{5,6},{6,5},{7,4},{8,11},{9,10},{10,... | collective-permute-start | bytes 3464 | tf_op jit(solution)/shard_map/ppermute | solution.py:656
  (84 other events, 1358.9 us)
Sparse Core Ops, SparseCore 0:
  11.5 83.9 all-gather.4
  98.9 107.0 all-gather.2
  433.9 131.0 all-reduce.3

commit v3 on v2

--- a/solution.py
+++ b/solution.py
@@ -36,7 +36,7 @@
 LOW = jnp.bfloat16
 FULL = jnp.float32
 MIB = 1 << 20
-HALVES = 2
+HALVES = 1
 
 
 def dot_nn(a, b):
@@ -292,10 +292,10 @@
     gates, ups, shrinks = refs[:chips], refs[chips : 2 * chips], refs[2 * chips : 3 * chips]
     own_ref, other_ref, c_ref, c_other_ref = refs[3 * chips : 3 * chips + 4]
     x_out, c_out, active_ref, grad_ref, share_ref, share_other, back_ref, back_other = refs[3 * chips + 4 :]
-    mine = pl.program_id(0) == 0
+    step = pl.program_id(0)
+    mine = step < 2
     x = jnp.where(mine, own_ref[...], other_ref[...])
-    c_near, c_far = c_ref[0], c_other_ref[0]
-    c = jnp.concatenate([jnp.where(mine, c_near, c_far), jnp.where(mine, c_far, c_near)], axis=0)
+    c = jnp.where((step == 0) | (step == 3), c_ref[0], c_other_ref[0])
     x_out[...] = x
     c_out[...] = c
     size = gates[0].shape[1]
@@ -334,9 +334,11 @@
     chips = n // 2
     rows = own.shape[0]
     size = FF // n
-    whole = lambda i, p: (0, 0)
+    near = lambda i, p: (jnp.minimum(i, 1), 0)
+    far = lambda i, p: (jnp.maximum(i - 2, 0), 0)
     flat = lambda i, p: (i, 0)
-    core = lambda i, p: ((p[0] & 1) ^ i, 0, 0)
+    core = lambda i, p: ((p[0] & 1) ^ (i // 2), 0, 0)
+    block = rows // 2
     once = pl.Buffered(1)
     gates = [
         pl.BlockSpec((D, size), lambda i, p, s=s: (0, 2 * s + (p[0] & 1)), pipeline_mode=once)
@@ -357,25 +359,25 @@
         out_shape=(wide(D), wide(D), wide(FF // 2), wide(FF), part, part, part, part),
         grid_spec=pltpu.PrefetchScalarGridSpec(
             num_scalar_prefetch=1,
-            grid=(2,),
+            grid=(4,),
             in_specs=gates
             + ups
             + shrinks
             + [
-                resident((rows, D)),
-                resident((rows, D)),
-                pl.BlockSpec((1, rows // 2, D), core),
-                pl.BlockSpec((1, rows // 2, D), core),
+                pl.BlockSpec((block, D), near),
+                pl.BlockSpec((block, D), far),
+                pl.BlockSpec((1, block, D), core),
+                pl.BlockSpec((1, block, D), core),
             ],
             out_specs=(
-                pl.BlockSpec((rows, D), flat),
-                pl.BlockSpec((rows, D), flat),
-                pl.BlockSpec((rows, FF // 2), flat),
-                pl.BlockSpec((rows, FF), flat),
-                pl.BlockSpec((rows, D), whole),
-                pl.BlockSpec((rows, D), whole),
-                pl.BlockSpec((rows, D), whole),
-                pl.BlockSpec((rows, D), whole),
+                pl.BlockSpec((block, D), flat),
+                pl.BlockSpec((block, D), flat),
+                pl.BlockSpec((block, FF // 2), flat),
+                pl.BlockSpec((block, FF), flat),
+                pl.BlockSpec((block, D), near),
+                pl.BlockSpec((block, D), far),
+                pl.BlockSpec((block, D), near),
+                pl.BlockSpec((block, D), far),
             ),
         ),
         compiler_params=pltpu.CompilerParams(vmem_limit_bytes=56 * MIB),
@@ -566,33 +568,31 @@
     )
 
 
-def adam_kernel(rate, blocks, key_ref, *refs):
-    cuts = refs[:HALVES]
-    weight_ref, first_ref, second_ref, new_first, new_second, new_weight, grad = refs[HALVES:]
-    for i in range(HALVES):
-
-        @pl.when(pl.program_id(0) // blocks == i)
+def adam_kernel(rate, key_ref, *refs):
+    cuts = refs[:-7]
+    weight_ref, first_ref, second_ref, new_first, new_second, new_weight, grad = refs[-7:]
+    for s, cut in enumerate(cuts):
+
+        @pl.when((pl.program_id(1) ^ key_ref[0]) == s)
         def _():
-            grad[...] = cuts[i][0].astype(FULL)
+            grad[...] = cut[...].astype(FULL)
 
     results = adam_step(weight_ref[...], first_ref[...], second_ref[...], grad[...], rate)
     new_first[...], new_second[...], new_weight[...] = results
 
 
 def adam_cuts(key, cuts, weight, first, second, rate, size, column):
-    chips, rows, columns = cuts[0].shape
-    blocks = columns // size
-    place = lambda i, s, p: (0, column(i, s))
-    slot = lambda i, s, p: (p[0] ^ s, 0, i % blocks)
-    spec = pl.BlockSpec((rows, size), place)
+    rows, columns = cuts[0].shape
+    cut = pl.BlockSpec((rows, size), lambda i, s, p: (0, i))
+    spec = pl.BlockSpec((rows, size), lambda i, s, p: (0, column(i, s)))
     shape = jax.ShapeDtypeStruct(weight.shape, FULL)
     return pl.pallas_call(
-        functools.partial(adam_kernel, rate, blocks),
+        functools.partial(adam_kernel, rate),
         out_shape=(shape, shape, shape),
         grid_spec=pltpu.PrefetchScalarGridSpec(
             num_scalar_prefetch=1,
-            grid=(HALVES * blocks, chips),
-            in_specs=[pl.BlockSpec((1, rows, size), slot)] * HALVES + [spec] * 3,
+            grid=(columns // size, len(cuts)),
+            in_specs=[cut] * len(cuts) + [spec] * 3,
             out_specs=(spec,) * 3,
             scratch_shapes=[pltpu.VMEM((rows, size), FULL)],
         ),
@@ -652,9 +652,6 @@
     def swap_grp(value, t):
         return lax.ppermute(value, "grp", [(i, i ^ t) for i in range(inner)])
 
-    def swap_rep(value, r):
-        return lax.ppermute(value, "rep", [(i, i ^ r) for i in range(reps)])
-
     def over_chips(value):
         return [value] + [swap_chip(value, s) for s in range(1, chips)]
 
@@ -680,9 +677,6 @@
     hops += [
         ([(k, k - 1), (reps - 1 - k, reps - k)], (k - 1, reps - k)) for k in range(middle - 1, 0, -1)
     ]
-
-    def gather_reps(value):
-        return [value] + [swap_rep(value, r) for r in range(1, reps)]
 
     def on_device(
         tokens,
@@ -765,9 +759,7 @@
         near = over_grp(out_weight.astype(LOW))
         out_parts = near + [swap_core(p) for p in near]
         def gather_all(weight):
-            share = weight.shape[0] // reps
-            low = lax.dynamic_slice_in_dim(weight, rep * share, share, 0).astype(LOW)
-            return lax.all_gather(low, ("ctx", "grp", "rep"), axis=0, tiled=True)
+            return lax.all_gather(weight.astype(LOW), ("ctx", "grp"), axis=0, tiled=True)
 
         expand_full = gather_all(expand_weight)
         shrink_full = gather_all(shrink_weight)
@@ -851,12 +843,6 @@
         def send_y(parts):
             return parts[0], [swap_grp(parts[t], t) for t in range(1, inner)]
 
-        def back_part(half, attended, back_all):
-            return back(
-                place, qkv_parts, out_parts, grad_all, attended, totals, q, k, v, raw, cos, sin,
-                seg_col, seg_row, gain_query, gain_key, half, back_all,
-            )
-
         def cut_qkv(grad):
             grad_qkv = dot_tn(normed, grad).astype(LOW)
             cuts = grad_qkv.reshape(chips, 2, inner, rows, width // HALVES)
@@ -869,111 +855,93 @@
         other_sent = [swap_grp(pick(other_rows, 1, mine ^ t), t) for t in range(1, inner)]
         grad_shrink = dot_tn(active_late, c_all).astype(LOW)
         shrink_cuts = grad_shrink.reshape(chips, inner, FF // (n * inner), D)
-        own_cuts = pick(expand_cuts, 1, core)
-
-        def first_over_x(cuts, t, *gates):
-            cut = after(cuts, *gates)
-            sent = [swap_chip(pick(pick(cut, 0, chip ^ s), 0, mine ^ t), s) for s in range(1, chips)]
-            return pick(pick(cuts, 0, chip), 0, mine ^ t), sent
-
-        own_far = [first_over_x(own_cuts, t, grad_slots[-1]) for t in range(1, inner)]
-        own_near = first_over_x(own_cuts, 0, grad_slots[-1])
-
-        grad_out = dot_tn(attended, grad_all).astype(LOW)
+        shrink_sent = [swap_grp(pick(shrink_cuts, 1, mine ^ t), t) for t in range(1, inner)]
+        own_rows = pick(expand_cuts, 1, core)
+        late_rows = after(own_rows, grad_slots[-1])
+        own_sent = [swap_chip(pick(late_rows, 0, chip ^ s), s) for s in range(1, chips)]
+        grad, back_all, head_gains = back(
+            place, qkv_parts, out_parts, grad_all, attended, totals, q, k, v, raw, cos, sin, seg_col,
+            seg_row, gain_query, gain_key, 0, None,
+        )
+
+        line[:] = [head_gains]
+        own_cut = send_y(next_cut(pick(own_rows, 0, chip), own_sent, 0, mine, inner))
+        other_cut = send_x(next_cut(pick(other_rows, 1, mine), other_sent, 0, chip, chips))
+        qkv_cuts, qkv_sent = cut_qkv(after(grad, *line))
+        shrink_cut = send_x(next_cut(pick(shrink_cuts, 1, mine), shrink_sent, 0, chip, chips))
+        grad_out = dot_tn(after(attended, *line), grad_all).astype(LOW)
         out_cuts = grad_out.reshape(2, inner, out_weight.shape[0], D)
-        out_sent = swap_core(pick(out_cuts, 0, core ^ 1))
-        attended = after(attended, out_cuts)
-        grad_one, back_all, gains_one = back_part(0, attended, None)
-
-        line[:] = [gains_one]
-        own_sent = [swap_grp(next_sum(*own_far[t - 1]), t) for t in range(1, inner)]
-        other_cut = send_x(next_cut(pick(other_rows, 1, mine), other_sent, 0, chip, chips))
-        own_cut = next_sum(*own_near)
-        first_cuts, first_sent = cut_qkv(grad_one)
-        shrink_far = [first_over_x(shrink_cuts, t, *line) for t in range(1, inner)]
-        shrink_near = first_over_x(shrink_cuts, 0, *line)
-        out_cut = send_y(next_cut(pick(out_cuts, 0, core), [out_sent], 0, mine, inner))
-        attended, back_all = lax.optimization_barrier((attended, back_all, first_cuts, *line))[:2]
-        grad_two, back_all, gains_two = back_part(1, attended, back_all)
-
-        line[:] = [gains_two]
-        shrink_sent = [swap_grp(next_sum(*shrink_far[t - 1]), t) for t in range(1, inner)]
-        shrink_cut = next_sum(*shrink_near)
-        own_cut = next_sum(own_cut, own_sent)
-        first_cut = send_y(next_cut(first_cuts, first_sent, 1, mine, inner))
-        second_cuts, second_sent = cut_qkv(after(grad_two, *line))
+        out_sent = [swap_core(pick(out_cuts, 0, core ^ 1))]
+        qkv_cut = send_y(next_cut(qkv_cuts, qkv_sent, 1, mine, inner))
         other_cut = swap_core(next_sum(*other_cut))
-        second_cut = send_y(next_cut(second_cuts, second_sent, 1, mine, inner))
+        out_cut = send_y(next_cut(pick(out_cuts, 0, core), out_sent, 0, mine, inner))
         shares = []
         for s in range(1, chips):
             share = after(back_all[2 * s * block : 2 * (s + 1) * block], *line)
             shares.append(swap_chip(share, s))
+        other_cut = after(other_cut, *line)
+        line[:] = [other_cut]
+        other = go(other_cut)
+        own = go(next_sum(*own_cut))
+        shrink = go(next_sum(*shrink_cut))
+        step_on(other)
+        kept, sent = send_x(next_cut(*qkv_cut, 0, chip, chips))
+        qkv = [go(kept)]
         out = go(next_sum(*out_cut))
-        shrink_cut = next_sum(shrink_cut, shrink_sent)
-        own_cut, other_cut, shrink_cut = lax.optimization_barrier((own_cut, other_cut, shrink_cut, *line))[:3]
-        line[:] = [own_cut]
-        own_cut, other_cut, total_shrink = lax.psum((own_cut, other_cut, shrink_cut), "rep")
-        first_cut = send_x(next_cut(*first_cut, 0, chip, chips))
-        second_cut = send_x(next_cut(*second_cut, 0, chip, chips))
-
-        def stacked(on_the_way):
-            kept, sent = on_the_way
-            total = jnp.stack([kept, *lax.optimization_barrier((*sent, *line))[: len(sent)]])
-            line[:] = [total]
-            return total
-
-        step_on(out)
-        first = go(stacked(first_cut))
-        second = go(stacked(second_cut))
+        step_on(own)
+        step_on(other)
+        for value in sent:
+            value = after(value, *line)
+            line[:] = [value]
+            qkv.append(go(value))
+        step_on(shrink)
+        step_on(own)
+
         shares = [back_all[: 2 * block]] + [after(value, *line) for value in shares]
         input_part, gain_part = norm_back(inputs, gain_one, sum_of(shares))
         gain_one_grad = jnp.sum(gain_part, axis=0)
         input_grad = (input_part + hidden_grad).astype(LOW)
         input_landed = swap_core(input_grad[block:])
-        head_gains = gains_one + gains_two
+        line[:] = [gain_one_grad]
+
+        step_on(qkv[0])
+        step_on(other)
+        step_on(shrink)
+        step_on(out)
+        step_on(own)
+        step_on(qkv[0])
+        for trip in qkv[1:]:
+            step_on(trip)
+        step_on(out)
         grad_gains = jnp.concatenate([gain_one_grad, gain_two_grad, head_gains[0], head_gains[1]])
-        grad_gains = grad_gains.reshape(n, inner, 1, -1)
-        gains_sent = [
-            swap_plane(pick(pick(grad_gains, 0, me ^ s), 0, mine ^ t), s, t)
-            for s in range(n)
-            for t in range(inner)
-            if s or t
-        ]
-        line[:] = [gain_one_grad]
-
-        step_on(out)
-        step_on(first)
-        step_on(second)
-        gains_sent = lax.optimization_barrier((*gains_sent, *line))[:-1]
-        total_gains = sum_of([pick(pick(grad_gains, 0, me), 0, mine), *gains_sent])
-        gains_sent = gather_reps(total_gains)
-        step_on(first)
-        step_on(out)
-        step_on(second)
-        trips = (out, first, second)
+        total_gains = lax.psum(after(grad_gains, *line), ("ctx", "grp", "rep"))
+        line[:] = [total_gains]
+        total_gains = lax.dynamic_slice_in_dim(
+            total_gains, (me * inner + mine) * norm_gains.shape[0], norm_gains.shape[0], 0
+        )
+        step_on(shrink)
+        for trip in qkv[1:]:
+            step_on(trip)
+        trips = (other, own, shrink, out, *qkv)
         for _ in hops:
             for trip in trips:
                 step_on(trip)
-        total_out, *qkv_cuts = [trip[0] for trip in trips]
-        total_gains = sum_of(lax.optimization_barrier((*gains_sent, *line))[:-1])[0]
+        other_cut, own_cut, total_shrink, total_out, *qkv_cuts = [trip[0] for trip in trips]
         input_grad = by_sequence(input_grad[:block], input_landed)
 
-        size = k_width // HALVES
-
         def qkv_column(i, s):
-            per_half = width // HALVES // size
-            half, i = i // per_half, i % per_half
-            q_blocks = q_width // HALVES // size
-            q_place = (s * HALVES + half) * q_blocks + i
-            k_place = QUERY_FEATURES // size + s * HALVES + half
-            v_place = k_place + KEY_FEATURES // size
-            return jnp.where(i < q_blocks, q_place, jnp.where(i == q_blocks, k_place, v_place))
+            q_blocks = q_width // k_width
+            k_place = QUERY_FEATURES // k_width + s
+            v_place = k_place + chips
+            return jnp.where(i < q_blocks, s * q_blocks + i, jnp.where(i == q_blocks, k_place, v_place))
 
         key = chip.reshape(1).astype(jnp.int32)
         return (
             output,
             input_grad,
-            *adam_cuts(key, qkv_cuts, qkv_weight, qkv_first, qkv_second, RATE_QKV, size, qkv_column),
+            *adam_cuts(
+                key, qkv_cuts, qkv_weight, qkv_first, qkv_second, RATE_QKV, k_width, qkv_column
+            ),
             *adam_step(out_weight, out_first, out_second, total_out.astype(FULL), RATE_OUT),
             *adam_pair(
                 place, own_cut, other_cut, expand_weight, expand_first, expand_second, RATE_EXPAND,

time: 620 us -> 587 us (0.947)
  waiting for transfers between devices: 243 us -> 187 us
  blocking collectives: 0 us -> 45.6 us
  local copies, waits for them, and re-layouts: 42.9 us -> 24.2 us
  Pallas kernels: 129 us -> 146 us
  other arithmetic: 70.4 us -> 60.7 us
  starting transfers between devices: 90 us -> 81 us
    psum x0 -> x1, blocking collectives: none -> 45.6 us  [on_device(): total_gains = lax.psum(after(grad_gains, *line), ('ctx', 'grp', 'rep'))]
    all_gather x2, waiting for transfers between devices: 47.7 us -> 8.33 us  [gather_all(): lax.all_gather(weight.astype(LOW), ('ctx', 'grp'), axis=0, tiled=True)]
    ppermute x9 -> x18, starting transfers between devices: 17.5 us -> 50.1 us  [go(): return [value, lax.ppermute(value, 'rep', hops[step][0]), step]]
    ppermute x3 -> x0, starting transfers between devices: 32.3 us -> none  [swap_rep(): return lax.ppermute(value, 'rep', [(i, i ^ r) for i in range(reps)])]
    pallas_call x2 -> x1, Pallas kernels: 47.6 us -> 66.6 us  [back(): pl.pallas_call(functools.partial(back_kernel, n, inner, half), out_shape=...]
    convert_element_type x14 -> x16, other arithmetic: 23.4 us -> 9.95 us  [next_sum(): total = sum_of([kept, *sent]).astype(LOW)]
    unnamed x139 -> x136, local copies, waits for them, and re-layouts: 22 us -> 9.67 us
    ppermute x9 -> x18, waiting for transfers between devices: 60.7 us -> 48.6 us  [go(): return [value, lax.ppermute(value, 'rep', hops[step][0]), step]]
  transfers between devices with their start and end apart: 68 -> 61, of which waited for: 21 -> 19; matrix products, arithmetic and copies ran while one was open for 18% -> 15% of each run, Pallas kernels for 13% -> 18%
where the time goes in v3:
time: 587 us; the launch traced here: 580 us
  waiting for transfers between devices  187 us (32%)
  Pallas kernels  146 us (25%)
  starting transfers between devices  81 us (14%)
  other arithmetic  60.7 us (10%)
  blocking collectives  45.6 us (8%)
  local copies, waits for them, and re-layouts  24.2 us (4%)
  matrix products  19.9 us (3%)
  between operations  15.6 us (3%)
    ppermute x26, waiting for transfers between devices, swap_ctx(): return lax.ppermute(value, 'ctx', [(i, i ^ s) for i in range(n)])  83.7 us
    pallas_call x1, Pallas kernels, back(): pl.pallas_call(functools.partial(back_kernel, n, inner, half), out_shape=...  66.6 us
    ppermute x18, starting transfers between devices, go(): return [value, lax.ppermute(value, 'rep', hops[step][0]), step]  50.1 us
    ppermute x18, waiting for transfers between devices, go(): return [value, lax.ppermute(value, 'rep', hops[step][0]), step]  48.6 us
    ppermute x8, waiting for transfers between devices, swap_grp(): return lax.ppermute(value, 'grp', [(i, i ^ t) for i in range(inner)])  46.3 us
    psum x1, blocking collectives, on_device(): total_gains = lax.psum(after(grad_gains, *line), ('ctx', 'grp', 'rep'))  45.6 us
    pallas_call x1, Pallas kernels, feed(): pl.pallas_call(functools.partial(feed_kernel, chips), out_shape=(wide(D),...  35.6 us
    pallas_call x2, Pallas kernels, attend(): pl.pallas_call(functools.partial(attend_kernel, n, inner, first, bool(bas...  21.4 us
  transfers between devices with their start and end apart: 61, of which 19 were waited for; matrix products, arithmetic and copies ran while one was open for 15% of the time, Pallas kernels for 18%

profile of v3, /device:TPU:0, one launch (start us, length us, event | category | flops | bytes accessed | tf_op | source)
XLA Modules:
  0.0 580.3 jit_solution(1236218500093049510)
XLA Ops:
  7.3 2.5 convert_element_type.430
  9.9 3.4 convert_element_type.429
  13.4 3.0 collective-permute-start
  28.9 14.6 %collective-permute-done.14.refs_4_ = bf16[128,2048]{1,0:T(8,128)(2,1)} collective-permute-done((bf16[128,2048]{1,0:T(8,128)(2,1)}, bf16[128,2048]{1,0:T(8,128)(2,1)}, u32[]{:S(2)}, u32[]{:S(2)}) %collective-permute-start.14) | collective-permute-done | bytes 524320 | tf_op jit(solution)/shard_map/ppermute | solution.py:644
  45.6 2.0 copy.40
  47.7 2.5 gather_fusion.1
  50.6 13.6 %collective-permute-done.11.refs_1_ = bf16[128,2048]{1,0:T(8,128)(2,1)} collective-permute-done((bf16[128,2048]{1,0:T(8,128)(2,1)}, bf16[128,2048]{1,0:T(8,128)(2,1)}, u32[]{:S(2)}, u32[]{:S(2)}) %collective-permute-start.11) | collective-permute-done | bytes 524320 | tf_op jit(solution)/shard_map/ppermute | solution.py:653
  64.8 2.1 collective-permute-start.19
  66.9 16.1 %collective-permute-done.15.refs_5_ = bf16[128,2048]{1,0:T(8,128)(2,1)S(1)} collective-permute-done((bf16[128,2048]{1,0:T(8,128)(2,1)}, bf16[128,2048]{1,0:T(8,128)(2,1)S(1)}, u32[]{:S(2)}, u32[]{:S(2)}) %collective-permute-start.15) | collective-permute-done | bytes 524320 | tf_op jit(solution)/shard_map/ppermute | solution.py:653
  89.6 10.7 %project.1 = (bf16[1024,1024]{1,0:T(8,128)(2,1)S(1)}, bf16[1024,1024]{1,0:T(8,128)(2,1)S(1)}, bf16[1024,512]{1,0:T(8,128)(2,1)S(1)}, bf16[1024,512]{1,0:T(8,128)(2,1)S(1)}, bf16[1024,1536]{1,0:T(8,128)(2,1)}) custom-call(s32[2]{0:T(128)S(1)} %pad_add_fusion.place_ref, bf16[128,2048]{1,0:T(8,128)(2,1)} %get-tuple-element.97.refs_0_, ...), custom_call_target="tpu_custom_call" | custom-call | flops 4294967296 | bytes 16777216 | tf_op jit(solution)/shard_map/project/pallas_call | solution.py:150
  104.1 11.2 %attend.2 = (bf16[1024,1024]{1,0:T(8,128)(2,1)}, f32[1024,128]{1,0:T(8,128)S(1)}, bf16[512,1024]{1,0:T(8,128)(2,1)S(1)}) custom-call(s32[2]{0:T(128)S(1)} %pad_add_fusion.place_ref, bf16[256,1024]{1,0:T(8,128)(2,1)S(1)} %convert_element_type.425.refs_0_.refs_8_, bf16[256,1024]{1,0:T(8,128)(2,1)S(1)} %copy-done.19, ...), custom_call_target="tpu_custom_call" | custom-call | flops 3221225472 | bytes 8388608 | tf_op jit(solution)/shard_map/attend/pallas_call | solution.py:256
  115.9 10.1 %attend.3 = (bf16[1024,1024]{1,0:T(8,128)(2,1)}, f32[1024,128]{1,0:T(8,128)S(1)}, bf16[512,1024]{1,0:T(8,128)(2,1)S(1)}) custom-call(s32[2]{0:T(128)S(1)} %pad_add_fusion.place_ref, bf16[256,1024]{1,0:T(8,128)(2,1)S(1)} %convert_element_type.425.refs_0_.refs_8_, bf16[256,1024]{1,0:T(8,128)(2,1)S(1)} %copy-done.19, ...), custom_call_target="tpu_custom_call", output_to_operand_aliasing={{0}: (10, {}), {1}: (11, {})} | custom-call | flops 3221225472 | bytes 8388608 | tf_op jit(solution)/shard_map/attend/pallas_call | solution.py:256
  126.0 35.5 %collective-permute-done.20 = bf16[512,1024]{1,0:T(8,128)(2,1)S(1)} collective-permute-done((bf16[512,1024]{1,0:T(8,128)(2,1)S(1)}, bf16[512,1024]{1,0:T(8,128)(2,1)S(1)}, u32[]{:S(2)}, u32[]{:S(2)}) %collective-permute-start.20) | collective-permute-done | bytes 1048608 | tf_op jit(solution)/shard_map/ppermute | solution.py:644
  167.9 8.3 %all-gather.3.cloned.1.call-done.refs_0_.refs_1_.refs_2_.refs_3_ = bf16[1024,6144]{1,0:T(8,128)(2,1)} async-done(((bf16[128,6144]{1,0:T(8,128)(2,1)}), bf16[1024,6144]{1,0:T(8,128)(2,1)}) %all-gather.3.cloned.1.call-update) | async-done | bytes 12582928 | tf_op jit(solution)/shard_map/all_gather | solution.py:762
  176.3 35.6 %feed.1 = (bf16[1024,1024]{1,0:T(8,128)(2,1)}, bf16[1024,1024]{1,0:T(8,128)(2,1)}, bf16[1024,1536]{1,0:T(8,128)(2,1)}, bf16[1024,3072]{1,0:T(8,128)(2,1)}, bf16[...) custom-call(s32[2]{0:T(128)} %copy-done.14, ...), custom_call_target="tpu_custom_call" | custom-call | flops 19327352832 | bytes 31457280 | tf_op jit(solution)/shard_map/feed/pallas_call | solution.py:357
  212.2 2.6 collective-permute-done.25
  214.9 2.8 multiply_reduce_fusion
  217.7 2.5 fusion.38
  221.1 8.9 %convolution_convert_fusion = bf16[1024,3072]{1,0:T(8,128)(2,1)S(1)} fusion(bf16[1024,1024]{1,0:T(8,128)(2,1)} %get-tuple-element.126, bf16[1024,3072]{1,0:T(8,128)(2,1)S(1)} %copy-done.62), kind=kOutput, calls=%fused_computation.2 | convolution fusion | flops 6445596672 | bytes 14680064 | tf_op jit(solution)/shard_map/dot_general | solution.py:51
  231.6 14.0 %collective-permute-done.26 = bf16[512,1024]{1,0:T(8,128)(2,1)S(1)} collective-permute-done((bf16[512,1024]{1,0:T(8,128)(2,1)S(1)}, bf16[512,1024]{1,0:T(8,128)(2,1)S(1)}, u32[]{:S(2)}, u32[]{:S(2)}) %collective-permute-start.26) | collective-permute-done | bytes 1048608 | tf_op jit(solution)/shard_map/ppermute | solution.py:644
  247.2 3.7 convolution_convert_fusion.1
  253.9 66.6 %back.1 = (bf16[1024,2048]{1,0:T(8,128)(2,1)}, bf16[1024,1024]{1,0:T(8,128)(2,1)}, f32[8,128]{1,0:T(8,128)}) custom-call(s32[2]{0:T(128)} %copy-done.14, bf16[128,2048]{1,0:T(8,128)(2,1)} %get-tuple-element.97.refs_0_, bf16[128,2048]{1,0:T(8,128)(2,1)} %collective-permute-done.11.refs_1_, bf16[128,2048]{1,0:T(8,128)(2,1)} %copy-done.22, ...), custom_call_target="tpu_custom_call" | custom-call | flops 11811160064 | bytes 31457280 | tf_op jit(solution)/shard_map/back/pallas_call | solution.py:518
  320.6 3.7 fusion.20
  324.3 2.6 fusion.18
  326.9 4.9 convolution_convert_fusion.2
  334.0 3.2 fusion.16
  337.2 2.4 convolution_convert_fusion.3
  341.0 2.1 fusion.10
  343.1 9.1 %collective-permute-done.31 = bf16[128,3072]{1,0:T(8,128)(2,1)S(1)} collective-permute-done((bf16[128,3072]{1,0:T(8,128)(2,1)S(1)}, bf16[128,3072]{1,0:T(8,128)(2,1)S(1)}, u32[]{:S(2)}, u32[]{:S(2)}) %collective-permute-start.31) | collective-permute-done | bytes 786464 | tf_op jit(solution)/shard_map/ppermute | solution.py:644
  363.1 10.9 %collective-permute-done.34 = bf16[128,3072]{1,0:T(8,128)(2,1)} collective-permute-done((bf16[128,3072]{1,0:T(8,128)(2,1)}, bf16[128,3072]{1,0:T(8,128)(2,1)}, u32[]{:S(2)}, u32[]{:S(2)}) %collective-permute-start.34) | collective-permute-done | bytes 786464 | tf_op jit(solution)/shard_map/ppermute | solution.py:653
  374.0 3.7 collective-permute-start.39
  381.1 13.1 %collective-permute-done.39 = bf16[128,3072]{1,0:T(8,128)(2,1)S(1)} collective-permute-done((bf16[128,3072]{1,0:T(8,128)(2,1)}, bf16[128,3072]{1,0:T(8,128)(2,1)S(1)}, u32[]{:S(2)}, u32[]{:S(2)}) %collective-permute-start.39) | collective-permute-done | bytes 786464 | tf_op jit(solution)/shard_map/ppermute | solution.py:824
  394.2 4.3 collective-permute-start.36
  401.6 5.8 collective-permute-done.37
  408.3 8.2 %collective-permute-done.36 = bf16[128,3072]{1,0:T(8,128)(2,1)S(1)} collective-permute-done((bf16[128,3072]{1,0:T(8,128)(2,1)S(1)}, bf16[128,3072]{1,0:T(8,128)(2,1)S(1)}, u32[]{:S(2)}, u32[]{:S(2)}) %collective-permute-start.36) | collective-permute-done | bytes 786464 | tf_op jit(solution)/shard_map/ppermute | solution.py:824
  419.4 6.3 %collective-permute-done.43 = bf16[128,2048]{1,0:T(8,128)(2,1)S(1)} collective-permute-done((bf16[128,2048]{1,0:T(8,128)(2,1)S(1)}, bf16[128,2048]{1,0:T(8,128)(2,1)S(1)}, u32[]{:S(2)}, u32[]{:S(2)}) %collective-permute-start.43) | collective-permute-done | bytes 524320 | tf_op jit(solution)/shard_map/ppermute | solution.py:644
  425.6 10.0 %collective-permute-start.46 = (bf16[128,2048]{1,0:T(8,128)(2,1)S(1)}, bf16[128,2048]{1,0:T(8,128)(2,1)S(1)}, u32[]{:S(2)}, u32[]{:S(2)}) collective-permute-start(bf16[128,2048]{1,0:T(8,128)(2,1)S(1)} %get-tuple-element.203), channel_id=1, source_target_pairs={{0,1},{3,2},{4,5},{7,6},{8,9},{11,10},{12,13},{15,14},{16,17},{19,... | collective-permute-start | bytes 1572872 | tf_op jit(solution)/shard_map/ppermute | solution.py:824
  440.9 3.5 fusion.7
  444.6 3.4 collective-permute-done.46
  450.5 15.9 %collective-permute-start.54 = (bf16[128,2048]{1,0:T(8,128)(2,1)S(1)}, bf16[128,2048]{1,0:T(8,128)(2,1)S(1)}, u32[]{:S(2)}, u32[]{:S(2)}) collective-permute-start(bf16[128,2048]{1,0:T(8,128)(2,1)S(1)} %collective-permute-done.43), channel_id=1, source_target_pairs={{0,1},{3,2},{4,5},{7,6},{8,9},{11,10},{12,13},{15,14},{16,17},{19,... | collective-permute-start | bytes 1572872 | tf_op jit(solution)/shard_map/ppermute | solution.py:824
  467.6 2.1 collective-permute-done.51
  473.3 13.2 %collective-permute-done.48 = bf16[128,3072]{1,0:T(8,128)(2,1)S(1)} collective-permute-done((bf16[128,3072]{1,0:T(8,128)(2,1)S(1)}, bf16[128,3072]{1,0:T(8,128)(2,1)S(1)}, u32[]{:S(2)}, u32[]{:S(2)}) %collective-permute-start.48) | collective-permute-done | bytes 786464 | tf_op jit(solution)/shard_map/ppermute | solution.py:824
  491.5 6.5 %adam_pair.1 = (f32[128,6144]{1,0:T(8,128)}, f32[128,6144]{1,0:T(8,128)}, f32[128,6144]{1,0:T(8,128)}) custom-call(s32[2]{0:T(128)S(1)} %copy-done.15, bf16[128,3072]{1,0:T(8,128)(2,1)S(1)} %broadcast_select_fusion.1.own_ref, bf16[128,3072]{1,0:T(8,128)(2,1)S(1)} %broadcast_select_fusion.2.other_ref, f32[128,6144]{1,0:T(8,128)S(1)} %copy-done.2, ...), custom_call_target="tpu_custom_call" | custom-call | flops 15728640 | bytes 20447232 | tf_op jit(solution)/shard_map/adam_pair/pallas_call | solution.py:619
  500.3 45.6 %psum.7 = f32[2304]{0:T(1024)S(1)} all-reduce(f32[2304]{0:T(1024)S(1)} %pad_maximum_fusion.4), channel_id=1, replica_groups=mesh['ctx'=4,'grp'=2,'rep'=4] {'ctx','grp','rep'}, use_global_device_ids=true, to_apply=%region_6.7 | all-reduce | flops 2304 | bytes 18432 | tf_op jit(solution)/shard_map/psum | solution.py:917
  546.6 5.5 multiply_subtract_fusion
  554.8 3.5 multiply_subtract_fusion.1
  559.6 8.6 %collective-permute-done.58 = bf16[128,2048]{1,0:T(8,128)(2,1)S(1)} collective-permute-done((bf16[128,2048]{1,0:T(8,128)(2,1)S(1)}, bf16[128,2048]{1,0:T(8,128)(2,1)S(1)}, u32[]{:S(2)}, u32[]{:S(2)}) %collective-permute-start.58) | collective-permute-done | bytes 524320 | tf_op jit(solution)/shard_map/ppermute | solution.py:824
  568.4 4.8 adam_cuts.1
  (309 shorter events, 89.3 us)
Async XLA Ops:
  7.2 160.7 %all-gather.5.cloned.1.call-start = ((), (), s32[]{:S(2)}) async-start(), calls=%async_computation.1 | async-start | bytes 7077888 | tf_op jit(solution)/shard_map/all_gather | solution.py:762
  9.8 166.5 %all-gather.3.cloned.1.call-start = ((), (), s32[]{:S(2)}) async-start(), calls=%async_computation | async-start | bytes 14155776 | tf_op jit(solution)/shard_map/all_gather | solution.py:762
  23.5 27.1 %collective-permute-start.8 = (bf16[256,1024]{1,0:T(8,128)(2,1)S(1)}, bf16[256,1024]{1,0:T(8,128)(2,1)S(1)}, u32[]{:S(2)}, u32[]{:S(2)}) collective-permute-start(bf16[256,1024]{1,0:T(8,128)(2,1)S(1)} %convert_element_type.425.refs_0_.refs_8_), channel_id=1, source_target_pairs={{0,4},{4,0},{1,5},{5,1},{2,6},{6,2},{3,7},{7,3},{8,12},{12,8},{9,1... | collective-permute-start | bytes 1572872 | tf_op jit(solution)/shard_map/ppermute | solution.py:653
  25.9 17.6 %collective-permute-start.14 = (bf16[128,2048]{1,0:T(8,128)(2,1)}, bf16[128,2048]{1,0:T(8,128)(2,1)}, u32[]{:S(2)}, u32[]{:S(2)}) collective-permute-start(bf16[128,2048]{1,0:T(8,128)(2,1)} %get-tuple-element.98), channel_id=1, source_target_pairs={{0,16},{8,24},{16,0},{24,8},{1,17},{9,25},{17,1},{25,9},{2,18},{10... | collective-permute-start | bytes 1572872 | tf_op jit(solution)/shard_map/ppermute | solution.py:644
  27.1 37.1 %collective-permute-start.11 = (bf16[128,2048]{1,0:T(8,128)(2,1)}, bf16[128,2048]{1,0:T(8,128)(2,1)}, u32[]{:S(2)}, u32[]{:S(2)}) collective-permute-start(bf16[128,2048]{1,0:T(8,128)(2,1)} %get-tuple-element.97.refs_0_), channel_id=1, source_target_pairs={{0,4},{4,0},{1,5},{5,1},{2,6},{6,2},{3,7},{7,3},{8,12},{12,8},{9,1... | collective-permute-start | bytes 1572872 | tf_op jit(solution)/shard_map/ppermute | solution.py:653
  27.7 36.5 %collective-permute-start.18 = (bf16[256,1024]{1,0:T(8,128)(2,1)S(1)}, bf16[256,1024]{1,0:T(8,128)(2,1)}, u32[]{:S(2)}, u32[]{:S(2)}) collective-permute-start(bf16[256,1024]{1,0:T(8,128)(2,1)S(1)} %dynamic-slice_bitcast_fusion.5.refs_8_), channel_id=1, source_target_pairs={{0,16},{8,24},{16,0},{24,8},{1,17},{9,25},{17,1},{25,9},{2,18},{10... | collective-permute-start | bytes 1572872 | tf_op jit(solution)/shard_map/ppermute | solution.py:644
  28.6 36.2 %collective-permute-start.7 = (bf16[256,1024]{1,0:T(8,128)(2,1)}, bf16[256,1024]{1,0:T(8,128)(2,1)S(1)}, u32[]{:S(2)}, u32[]{:S(2)}) collective-permute-start(bf16[256,1024]{1,0:T(8,128)(2,1)} %dynamic-slice_bitcast_fusion.6), channel_id=1, source_target_pairs={{0,8},{8,0},{16,24},{24,16},{1,9},{9,1},{17,25},{25,17},{2,10},{10... | collective-permute-start | bytes 1572872 | tf_op jit(solution)/shard_map/ppermute | solution.py:644
  43.5 39.6 %collective-permute-start.15 = (bf16[128,2048]{1,0:T(8,128)(2,1)}, bf16[128,2048]{1,0:T(8,128)(2,1)S(1)}, u32[]{:S(2)}, u32[]{:S(2)}) collective-permute-start(bf16[128,2048]{1,0:T(8,128)(2,1)} %collective-permute-done.14.refs_4_), channel_id=1, source_target_pairs={{0,4},{4,0},{1,5},{5,1},{2,6},{6,2},{3,7},{7,3},{8,12},{12,8},{9,1... | collective-permute-start | bytes 1572872 | tf_op jit(solution)/shard_map/ppermute | solution.py:653
  50.5 35.5 %collective-permute-start.12 = (bf16[128,2048]{1,0:T(8,128)(2,1)}, bf16[128,2048]{1,0:T(8,128)(2,1)S(1)}, u32[]{:S(2)}, u32[]{:S(2)}) collective-permute-start(bf16[128,2048]{1,0:T(8,128)(2,1)} %get-tuple-element.97.refs_0_), channel_id=1, source_target_pairs={{0,8},{8,0},{16,24},{24,16},{1,9},{9,1},{17,25},{25,17},{2,10},{10... | collective-permute-start | bytes 1572872 | tf_op jit(solution)/shard_map/ppermute | solution.py:644
  64.2 23.3 %collective-permute-start.13 = (bf16[128,2048]{1,0:T(8,128)(2,1)}, bf16[128,2048]{1,0:T(8,128)(2,1)}, u32[]{:S(2)}, u32[]{:S(2)}) collective-permute-start(bf16[128,2048]{1,0:T(8,128)(2,1)} %collective-permute-done.11.refs_1_), channel_id=1, source_target_pairs={{0,8},{8,0},{16,24},{24,16},{1,9},{9,1},{17,25},{25,17},{2,10},{10... | collective-permute-start | bytes 1572872 | tf_op jit(solution)/shard_map/ppermute | solution.py:644
  64.2 23.3 %collective-permute-start.16 = (bf16[128,2048]{1,0:T(8,128)(2,1)}, bf16[128,2048]{1,0:T(8,128)(2,1)}, u32[]{:S(2)}, u32[]{:S(2)}) collective-permute-start(bf16[128,2048]{1,0:T(8,128)(2,1)} %collective-permute-done.14.refs_4_), channel_id=1, source_target_pairs={{0,8},{8,0},{16,24},{24,16},{1,9},{9,1},{17,25},{25,17},{2,10},{10... | collective-permute-start | bytes 1572872 | tf_op jit(solution)/shard_map/ppermute | solution.py:644
  64.8 22.7 %collective-permute-start.19 = (bf16[256,1024]{1,0:T(8,128)(2,1)S(1)}, bf16[256,1024]{1,0:T(8,128)(2,1)}, u32[]{:S(2)}, u32[]{:S(2)}) collective-permute-start(bf16[256,1024]{1,0:T(8,128)(2,1)S(1)} %collective-permute-done.7.refs_9_), channel_id=1, source_target_pairs={{0,16},{8,24},{16,0},{24,8},{1,17},{9,25},{17,1},{25,9},{2,18},{10... | collective-permute-start | bytes 1572872 | tf_op jit(solution)/shard_map/ppermute | solution.py:644
  87.0 17.1 %collective-permute-start.9 = (bf16[256,1024]{1,0:T(8,128)(2,1)S(1)}, bf16[256,1024]{1,0:T(8,128)(2,1)S(1)}, u32[]{:S(2)}, u32[]{:S(2)}) collective-permute-start(bf16[256,1024]{1,0:T(8,128)(2,1)S(1)} %convert_element_type.425.refs_0_.refs_8_), channel_id=1, source_target_pairs={{0,8},{8,0},{16,24},{24,16},{1,9},{9,1},{17,25},{25,17},{2,10},{10... | collective-permute-start | bytes 1572872 | tf_op jit(solution)/shard_map/ppermute | solution.py:644
  87.5 16.6 %collective-permute-start.10 = (bf16[256,1024]{1,0:T(8,128)(2,1)}, bf16[256,1024]{1,0:T(8,128)(2,1)S(1)}, u32[]{:S(2)}, u32[]{:S(2)}) collective-permute-start(bf16[256,1024]{1,0:T(8,128)(2,1)} %copy-done.18), channel_id=1, source_target_pairs={{0,8},{8,0},{16,24},{24,16},{1,9},{9,1},{17,25},{25,17},{2,10},{10... | collective-permute-start | bytes 1572872 | tf_op jit(solution)/shard_map/ppermute | solution.py:644
  115.3 46.3 %collective-permute-start.20 = (bf16[512,1024]{1,0:T(8,128)(2,1)S(1)}, bf16[512,1024]{1,0:T(8,128)(2,1)S(1)}, u32[]{:S(2)}, u32[]{:S(2)}) collective-permute-start(bf16[512,1024]{1,0:T(8,128)(2,1)S(1)} %get-tuple-element.110), channel_id=1, source_target_pairs={{0,16},{8,24},{16,0},{24,8},{1,17},{9,25},{17,1},{25,9},{2,18},{10... | collective-permute-start | bytes 3145736 | tf_op jit(solution)/shard_map/ppermute | solution.py:644
  115.3 50.0 %collective-permute-start.22 = (bf16[2,256,1024]{2,1,0:T(8,128)(2,1)S(1)}, bf16[2,256,1024]{2,1,0:T(8,128)(2,1)S(1)}, u32[]{:S(2)}, u32[]{:S(2)}) collective-permute-start(bf16[2,256,1024]{2,1,0:T(8,128)(2,1)S(1)} %copy-done.58), channel_id=1, source_target_pairs={{0,8},{8,0},{16,24},{24,16},{1,9},{9,1},{17,25},{25,17},{2,10},{10... | collective-permute-start | bytes 3145736 | tf_op jit(solution)/shard_map/ppermute | solution.py:644
  220.2 25.4 %collective-permute-start.26 = (bf16[512,1024]{1,0:T(8,128)(2,1)S(1)}, bf16[512,1024]{1,0:T(8,128)(2,1)S(1)}, u32[]{:S(2)}, u32[]{:S(2)}) collective-permute-start(bf16[512,1024]{1,0:T(8,128)(2,1)S(1)} %fusion.38), channel_id=1, source_target_pairs={{0,16},{8,24},{16,0},{24,8},{1,17},{9,25},{17,1},{25,9},{2,18},{10... | collective-permute-start | bytes 3145736 | tf_op jit(solution)/shard_map/ppermute | solution.py:644
  231.4 92.9 %collective-permute-start.28 = (bf16[2,128,3072]{2,1,0:T(8,128)(2,1)}, bf16[2,128,3072]{2,1,0:T(8,128)(2,1)}, u32[]{:S(2)}, u32[]{:S(2)}) collective-permute-start(bf16[2,128,3072]{2,1,0:T(8,128)(2,1)} %dynamic-slice_bitcast_fusion.2), channel_id=1, source_target_pairs={{0,4},{4,0},{1,5},{5,1},{2,6},{6,2},{3,7},{7,3},{8,12},{12,8},{9,1... | collective-permute-start | bytes 4718600 | tf_op jit(solution)/shard_map/ppermute | solution.py:653
  247.0 73.6 %collective-permute-start.29 = (bf16[2,128,3072]{2,1,0:T(8,128)(2,1)}, bf16[2,128,3072]{2,1,0:T(8,128)(2,1)}, u32[]{:S(2)}, u32[]{:S(2)}) collective-permute-start(bf16[2,128,3072]{2,1,0:T(8,128)(2,1)} %dynamic-slice_bitcast_fusion.1), channel_id=1, source_target_pairs={{0,16},{8,24},{16,0},{24,8},{1,17},{9,25},{17,1},{25,9},{2,18},{10... | collective-permute-start | bytes 4718600 | tf_op jit(solution)/shard_map/ppermute | solution.py:644
  252.4 81.6 %collective-permute-start.27 = (bf16[2,384,1024]{2,1,0:T(8,128)(2,1)}, bf16[2,384,1024]{2,1,0:T(8,128)(2,1)}, u32[]{:S(2)}, u32[]{:S(2)}) collective-permute-start(bf16[2,384,1024]{2,1,0:T(8,128)(2,1)} %dynamic-slice_bitcast_fusion.3), channel_id=1, source_target_pairs={{0,4},{4,0},{1,5},{5,1},{2,6},{6,2},{3,7},{7,3},{8,12},{12,8},{9,1... | collective-permute-start | bytes 4718600 | tf_op jit(solution)/shard_map/ppermute | solution.py:653
  332.1 8.9 %collective-permute-start.32 = (bf16[2,2,128,2048]{3,2,0,1:T(8,128)(2,1)S(1)}, bf16[2,2,128,2048]{3,2,0,1:T(8,128)(2,1)S(1)}, u32[]{:S(2)}, u32[]{:S(2)}) collective-permute-start(bf16[2,2,128,2048]{3,2,0,1:T(8,128)(2,1)S(1)} %copy_bitcast_fusion), channel_id=1, source_target_pairs={{0,8},{8,0},{16,24},{24,16},{1,9},{9,1},{17,25},{25,17},{2,10},{10... | collective-permute-start | bytes 6291464 | tf_op jit(solution)/shard_map/ppermute | solution.py:644
  332.1 20.0 %collective-permute-start.31 = (bf16[128,3072]{1,0:T(8,128)(2,1)S(1)}, bf16[128,3072]{1,0:T(8,128)(2,1)S(1)}, u32[]{:S(2)}, u32[]{:S(2)}) collective-permute-start(bf16[128,3072]{1,0:T(8,128)(2,1)S(1)} %get-tuple-element.190), channel_id=1, source_target_pairs={{0,16},{8,24},{16,0},{24,8},{1,17},{9,25},{17,1},{25,9},{2,18},{10... | collective-permute-start | bytes 2359304 | tf_op jit(solution)/shard_map/ppermute | solution.py:644
  340.8 18.6 %collective-permute-start.30 = (bf16[2,256,1024]{2,1,0:T(8,128)(2,1)}, bf16[2,256,1024]{2,1,0:T(8,128)(2,1)}, u32[]{:S(2)}, u32[]{:S(2)}) collective-permute-start(bf16[2,256,1024]{2,1,0:T(8,128)(2,1)} %dynamic-slice_bitcast_fusion.4), channel_id=1, source_target_pairs={{0,8},{8,0},{16,24},{24,16},{1,9},{9,1},{17,25},{25,17},{2,10},{10... | collective-permute-start | bytes 3145736 | tf_op jit(solution)/shard_map/ppermute | solution.py:644
  353.2 20.7 %collective-permute-start.34 = (bf16[128,3072]{1,0:T(8,128)(2,1)}, bf16[128,3072]{1,0:T(8,128)(2,1)}, u32[]{:S(2)}, u32[]{:S(2)}) collective-permute-start(bf16[128,3072]{1,0:T(8,128)(2,1)} %get-tuple-element.192), channel_id=1, source_target_pairs={{0,4},{4,0},{1,5},{5,1},{2,6},{6,2},{3,7},{7,3},{8,12},{12,8},{9,1... | collective-permute-start | bytes 2359304 | tf_op jit(solution)/shard_map/ppermute | solution.py:653
  355.2 85.5 %collective-permute-start.23 = (bf16[512,1024]{1,0:T(8,128)(2,1)}, bf16[512,1024]{1,0:T(8,128)(2,1)S(1)}, u32[]{:S(2)}, u32[]{:S(2)}) collective-permute-start(bf16[512,1024]{1,0:T(8,128)(2,1)} %get-tuple-element.115), channel_id=1, source_target_pairs={{0,8},{8,0},{16,24},{24,16},{1,9},{9,1},{17,25},{25,17},{2,10},{10... | collective-permute-start | bytes 3145736 | tf_op jit(solution)/shard_map/ppermute | solution.py:644
  357.6 21.4 %collective-permute-start.40 = (bf16[384,1024]{1,0:T(8,128)(2,1)}, bf16[384,1024]{1,0:T(8,128)(2,1)S(1)}, u32[]{:S(2)}, u32[]{:S(2)}) collective-permute-start(bf16[384,1024]{1,0:T(8,128)(2,1)} %get-tuple-element.196), channel_id=1, source_target_pairs={{0,16},{8,24},{16,0},{24,8},{1,17},{9,25},{17,1},{25,9},{2,18},{10... | collective-permute-start | bytes 2359304 | tf_op jit(solution)/shard_map/ppermute | solution.py:644
  359.4 40.5 %collective-permute-start.38 = (bf16[2,128,2048]{2,1,0:T(8,128)(2,1)}, bf16[2,128,2048]{2,1,0:T(8,128)(2,1)S(1)}, u32[]{:S(2)}, u32[]{:S(2)}) collective-permute-start(bf16[2,128,2048]{2,1,0:T(8,128)(2,1)} %get-tuple-element.194), channel_id=1, source_target_pairs={{0,4},{4,0},{1,5},{5,1},{2,6},{6,2},{3,7},{7,3},{8,12},{12,8},{9,1... | collective-permute-start | bytes 3145736 | tf_op jit(solution)/shard_map/ppermute | solution.py:653
  361.3 46.0 %collective-permute-start.37 = (bf16[256,1024]{1,0:T(8,128)(2,1)S(1)}, bf16[256,1024]{1,0:T(8,128)(2,1)S(1)}, u32[]{:S(2)}, u32[]{:S(2)}) collective-permute-start(bf16[256,1024]{1,0:T(8,128)(2,1)S(1)} %get-tuple-element.198), channel_id=1, source_target_pairs={{0,4},{4,0},{1,5},{5,1},{2,6},{6,2},{3,7},{7,3},{8,12},{12,8},{9,1... | collective-permute-start | bytes 1572872 | tf_op jit(solution)/shard_map/ppermute | solution.py:653
  374.0 20.3 %collective-permute-start.39 = (bf16[128,3072]{1,0:T(8,128)(2,1)}, bf16[128,3072]{1,0:T(8,128)(2,1)S(1)}, u32[]{:S(2)}, u32[]{:S(2)}) collective-permute-start(bf16[128,3072]{1,0:T(8,128)(2,1)} %collective-permute-done.35), channel_id=1, source_target_pairs={{0,1},{3,2},{4,5},{7,6},{8,9},{11,10},{12,13},{15,14},{16,17},{19,... | collective-permute-start | bytes 2359304 | tf_op jit(solution)/shard_map/ppermute | solution.py:824
  379.0 60.0 %collective-permute-start.33 = (bf16[512,1024]{1,0:T(8,128)(2,1)S(1)}, bf16[512,1024]{1,0:T(8,128)(2,1)S(1)}, u32[]{:S(2)}, u32[]{:S(2)}) collective-permute-start(bf16[512,1024]{1,0:T(8,128)(2,1)S(1)} %slice.65), channel_id=1, source_target_pairs={{0,16},{8,24},{16,0},{24,8},{1,17},{9,25},{17,1},{25,9},{2,18},{10... | collective-permute-start | bytes 3145736 | tf_op jit(solution)/shard_map/ppermute | solution.py:644
  394.2 22.3 %collective-permute-start.36 = (bf16[128,3072]{1,0:T(8,128)(2,1)S(1)}, bf16[128,3072]{1,0:T(8,128)(2,1)S(1)}, u32[]{:S(2)}, u32[]{:S(2)}) collective-permute-start(bf16[128,3072]{1,0:T(8,128)(2,1)S(1)} %add_convert_fusion.8), channel_id=1, source_target_pairs={{0,1},{3,2},{4,5},{7,6},{8,9},{11,10},{12,13},{15,14},{16,17},{19,... | collective-permute-start | bytes 2359304 | tf_op jit(solution)/shard_map/ppermute | solution.py:824
  399.9 35.8 %collective-permute-start.42 = (bf16[384,1024]{1,0:T(8,128)(2,1)S(1)}, bf16[384,1024]{1,0:T(8,128)(2,1)S(1)}, u32[]{:S(2)}, u32[]{:S(2)}) collective-permute-start(bf16[384,1024]{1,0:T(8,128)(2,1)S(1)} %add_convert_fusion.7), channel_id=1, source_target_pairs={{0,1},{3,2},{4,5},{7,6},{8,9},{11,10},{12,13},{15,14},{16,17},{19,... | collective-permute-start | bytes 2359304 | tf_op jit(solution)/shard_map/ppermute | solution.py:824
  407.3 11.1 %collective-permute-start.44 = (bf16[128,3072]{1,0:T(8,128)(2,1)S(1)}, bf16[128,3072]{1,0:T(8,128)(2,1)S(1)}, u32[]{:S(2)}, u32[]{:S(2)}) collective-permute-start(bf16[128,3072]{1,0:T(8,128)(2,1)S(1)} %add_convert_fusion.6), channel_id=1, source_target_pairs={{1,2},{2,1},{5,6},{6,5},{9,10},{10,9},{13,14},{14,13},{17,18},{18,... | collective-permute-start | bytes 2359304 | tf_op jit(solution)/shard_map/ppermute | solution.py:824
  416.5 9.2 %collective-permute-start.43 = (bf16[128,2048]{1,0:T(8,128)(2,1)S(1)}, bf16[128,2048]{1,0:T(8,128)(2,1)S(1)}, u32[]{:S(2)}, u32[]{:S(2)}) collective-permute-start(bf16[128,2048]{1,0:T(8,128)(2,1)S(1)} %get-tuple-element.202), channel_id=1, source_target_pairs={{0,16},{8,24},{16,0},{24,8},{1,17},{9,25},{17,1},{25,9},{2,18},{10... | collective-permute-start | bytes 1572872 | tf_op jit(solution)/shard_map/ppermute | solution.py:644
  418.4 18.9 %collective-permute-start.41 = (bf16[128,3072]{1,0:T(8,128)(2,1)S(1)}, bf16[128,3072]{1,0:T(8,128)(2,1)S(1)}, u32[]{:S(2)}, u32[]{:S(2)}) collective-permute-start(bf16[128,3072]{1,0:T(8,128)(2,1)S(1)} %add_convert_fusion.5), channel_id=1, source_target_pairs={{1,2},{2,1},{5,6},{6,5},{9,10},{10,9},{13,14},{14,13},{17,18},{18,... | collective-permute-start | bytes 2359304 | tf_op jit(solution)/shard_map/ppermute | solution.py:824
  425.6 22.3 %collective-permute-start.46 = (bf16[128,2048]{1,0:T(8,128)(2,1)S(1)}, bf16[128,2048]{1,0:T(8,128)(2,1)S(1)}, u32[]{:S(2)}, u32[]{:S(2)}) collective-permute-start(bf16[128,2048]{1,0:T(8,128)(2,1)S(1)} %get-tuple-element.203), channel_id=1, source_target_pairs={{0,1},{3,2},{4,5},{7,6},{8,9},{11,10},{12,13},{15,14},{16,17},{19,... | collective-permute-start | bytes 1572872 | tf_op jit(solution)/shard_map/ppermute | solution.py:824
  435.6 36.6 %collective-permute-start.49 = (bf16[256,1024]{1,0:T(8,128)(2,1)S(1)}, bf16[256,1024]{1,0:T(8,128)(2,1)S(1)}, u32[]{:S(2)}, u32[]{:S(2)}) collective-permute-start(bf16[256,1024]{1,0:T(8,128)(2,1)S(1)} %add_convert_fusion.16), channel_id=1, source_target_pairs={{0,1},{3,2},{4,5},{7,6},{8,9},{11,10},{12,13},{15,14},{16,17},{19,... | collective-permute-start | bytes 1572872 | tf_op jit(solution)/shard_map/ppermute | solution.py:824
  437.3 32.4 %collective-permute-start.51 = (bf16[128,3072]{1,0:T(8,128)(2,1)S(1)}, bf16[128,3072]{1,0:T(8,128)(2,1)S(1)}, u32[]{:S(2)}, u32[]{:S(2)}) collective-permute-start(bf16[128,3072]{1,0:T(8,128)(2,1)S(1)} %add_convert_fusion.4), channel_id=1, source_target_pairs={{1,0},{2,3},{5,4},{6,7},{9,8},{10,11},{13,12},{14,15},{17,16},{18,... | collective-permute-start | bytes 2359304 | tf_op jit(solution)/shard_map/ppermute | solution.py:824
  439.0 31.5 %collective-permute-start.50 = (bf16[384,1024]{1,0:T(8,128)(2,1)S(1)}, bf16[384,1024]{1,0:T(8,128)(2,1)S(1)}, u32[]{:S(2)}, u32[]{:S(2)}) collective-permute-start(bf16[384,1024]{1,0:T(8,128)(2,1)S(1)} %add_convert_fusion.3), channel_id=1, source_target_pairs={{1,2},{2,1},{5,6},{6,5},{9,10},{10,9},{13,14},{14,13},{17,18},{18,... | collective-permute-start | bytes 2359304 | tf_op jit(solution)/shard_map/ppermute | solution.py:824
  448.1 38.4 %collective-permute-start.48 = (bf16[128,3072]{1,0:T(8,128)(2,1)S(1)}, bf16[128,3072]{1,0:T(8,128)(2,1)S(1)}, u32[]{:S(2)}, u32[]{:S(2)}) collective-permute-start(bf16[128,3072]{1,0:T(8,128)(2,1)S(1)} %add_convert_fusion.2), channel_id=1, source_target_pairs={{1,0},{2,3},{5,4},{6,7},{9,8},{10,11},{13,12},{14,15},{17,16},{18,... | collective-permute-start | bytes 2359304 | tf_op jit(solution)/shard_map/ppermute | solution.py:824
  450.5 38.5 %collective-permute-start.54 = (bf16[128,2048]{1,0:T(8,128)(2,1)S(1)}, bf16[128,2048]{1,0:T(8,128)(2,1)S(1)}, u32[]{:S(2)}, u32[]{:S(2)}) collective-permute-start(bf16[128,2048]{1,0:T(8,128)(2,1)S(1)} %collective-permute-done.43), channel_id=1, source_target_pairs={{0,1},{3,2},{4,5},{7,6},{8,9},{11,10},{12,13},{15,14},{16,17},{19,... | collective-permute-start | bytes 1572872 | tf_op jit(solution)/shard_map/ppermute | solution.py:824
  469.7 16.9 %collective-permute-start.47 = (bf16[128,2048]{1,0:T(8,128)(2,1)S(1)}, bf16[128,2048]{1,0:T(8,128)(2,1)S(1)}, u32[]{:S(2)}, u32[]{:S(2)}) collective-permute-start(bf16[128,2048]{1,0:T(8,128)(2,1)S(1)} %add_convert_fusion.15), channel_id=1, source_target_pairs={{1,2},{2,1},{5,6},{6,5},{9,10},{10,9},{13,14},{14,13},{17,18},{18,... | collective-permute-start | bytes 1572872 | tf_op jit(solution)/shard_map/ppermute | solution.py:824
  470.8 75.8 %collective-permute-start.57 = (bf16[384,1024]{1,0:T(8,128)(2,1)S(1)}, bf16[384,1024]{1,0:T(8,128)(2,1)}, u32[]{:S(2)}, u32[]{:S(2)}) collective-permute-start(bf16[384,1024]{1,0:T(8,128)(2,1)S(1)} %add_convert_fusion.1), channel_id=1, source_target_pairs={{1,0},{2,3},{5,4},{6,7},{9,8},{10,11},{13,12},{14,15},{17,16},{18,... | collective-permute-start | bytes 2359304 | tf_op jit(solution)/shard_map/ppermute | solution.py:824
  472.5 25.6 %collective-permute-start.53 = (bf16[256,1024]{1,0:T(8,128)(2,1)S(1)}, bf16[256,1024]{1,0:T(8,128)(2,1)S(1)}, u32[]{:S(2)}, u32[]{:S(2)}) collective-permute-start(bf16[256,1024]{1,0:T(8,128)(2,1)S(1)} %add_convert_fusion.14), channel_id=1, source_target_pairs={{1,2},{2,1},{5,6},{6,5},{9,10},{10,9},{13,14},{14,13},{17,18},{18,... | collective-permute-start | bytes 1572872 | tf_op jit(solution)/shard_map/ppermute | solution.py:824
  487.6 70.8 %collective-permute-start.52 = (bf16[128,2048]{1,0:T(8,128)(2,1)}, bf16[128,2048]{1,0:T(8,128)(2,1)}, u32[]{:S(2)}, u32[]{:S(2)}) collective-permute-start(bf16[128,2048]{1,0:T(8,128)(2,1)} %add_convert_fusion.13), channel_id=1, source_target_pairs={{1,0},{2,3},{5,4},{6,7},{9,8},{10,11},{13,12},{14,15},{17,16},{18,... | collective-permute-start | bytes 1572872 | tf_op jit(solution)/shard_map/ppermute | solution.py:824
  489.9 62.1 %collective-permute-start.56 = (bf16[128,2048]{1,0:T(8,128)(2,1)}, bf16[128,2048]{1,0:T(8,128)(2,1)}, u32[]{:S(2)}, u32[]{:S(2)}) collective-permute-start(bf16[128,2048]{1,0:T(8,128)(2,1)} %add_convert_fusion.12), channel_id=1, source_target_pairs={{1,2},{2,1},{5,6},{6,5},{9,10},{10,9},{13,14},{14,13},{17,18},{18,... | collective-permute-start | bytes 1572872 | tf_op jit(solution)/shard_map/ppermute | solution.py:824
  499.0 55.7 %collective-permute-start.55 = (bf16[256,1024]{1,0:T(8,128)(2,1)}, bf16[256,1024]{1,0:T(8,128)(2,1)}, u32[]{:S(2)}, u32[]{:S(2)}) collective-permute-start(bf16[256,1024]{1,0:T(8,128)(2,1)} %add_convert_fusion.11), channel_id=1, source_target_pairs={{1,0},{2,3},{5,4},{6,7},{9,8},{10,11},{13,12},{14,15},{17,16},{18,... | collective-permute-start | bytes 1572872 | tf_op jit(solution)/shard_map/ppermute | solution.py:824
  553.5 14.8 %collective-permute-start.58 = (bf16[128,2048]{1,0:T(8,128)(2,1)S(1)}, bf16[128,2048]{1,0:T(8,128)(2,1)S(1)}, u32[]{:S(2)}, u32[]{:S(2)}) collective-permute-start(bf16[128,2048]{1,0:T(8,128)(2,1)S(1)} %add_convert_fusion.10), channel_id=1, source_target_pairs={{1,0},{2,3},{5,4},{6,7},{9,8},{10,11},{13,12},{14,15},{17,16},{18,... | collective-permute-start | bytes 1572872 | tf_op jit(solution)/shard_map/ppermute | solution.py:824
  (78 other events, 999.7 us)
Sparse Core Ops, SparseCore 0:
  10.5 71.2 all-gather.4
  84.2 91.9 all-gather.2

commit v4 on v3

--- a/solution.py
+++ b/solution.py
@@ -36,7 +36,7 @@
 LOW = jnp.bfloat16
 FULL = jnp.float32
 MIB = 1 << 20
-HALVES = 1
+HALVES = 2
 
 
 def dot_nn(a, b):
@@ -231,10 +231,12 @@
         attended_ref[...] = attended
         share_ref[...] = dot_nn(attended, weight[...]).astype(LOW)
         lane = lax.broadcasted_iota(jnp.int32, (block, HEAD_SIZE), 1)
-        packed = jnp.zeros((block, HEAD_SIZE), FULL)
-        for i, column in enumerate(totals):
-            packed = jnp.where(lane == i, column, packed)
-        total_ref[...] = packed
+        count = len(totals) // HALVES
+        for half in range(HALVES):
+            packed = jnp.zeros((block, HEAD_SIZE), FULL)
+            for i, column in enumerate(totals[half * count : (half + 1) * count]):
+                packed = jnp.where(lane == i, column, packed)
+            total_ref[:, half * HEAD_SIZE : (half + 1) * HEAD_SIZE] = packed
 
     place = place_ref[0] ^ (first + step)
     for j in range(n):
@@ -257,7 +259,7 @@
         functools.partial(attend_kernel, n, inner, first, bool(base)),
         out_shape=(
             jax.ShapeDtypeStruct((length, q_width), LOW),
-            jax.ShapeDtypeStruct((length, HEAD_SIZE), FULL),
+            jax.ShapeDtypeStruct((length, HALVES * HEAD_SIZE), FULL),
             jax.ShapeDtypeStruct((2 * block, D), LOW),
         ),
         grid_spec=pltpu.PrefetchScalarGridSpec(
@@ -274,7 +276,7 @@
             + [ANYWHERE] * len(base),
             out_specs=(
                 pl.BlockSpec((block, q_width), slot),
-                pl.BlockSpec((block, HEAD_SIZE), slot),
+                pl.BlockSpec((block, HALVES * HEAD_SIZE), slot),
                 pl.BlockSpec((block, D), plain),
             ),
             scratch_shapes=[pltpu.VMEM((q_width, D), LOW)],
@@ -388,7 +390,7 @@
     )(place, *[expand] * (2 * chips), *[shrink] * chips, own, other, c, c_other)
 
 
-def back_kernel(n, inner, half, place_ref, *refs):
+def back_kernel(n, inner, place_ref, *refs):
     qkv_parts = refs[: n * inner]
     out_parts = refs[n * inner : (n + 2) * inner]
     refs = refs[(n + 2) * inner :]
@@ -407,13 +409,14 @@
         gain_q_ref,
         gain_k_ref,
     ) = refs[:13]
-    refs = refs[13:]
-    if half:
-        base_ref, refs = refs[0], refs[1:]
-    grad_ref, share_ref, gains_ref, qkv, out, key_sum, value_sum = refs
+    grad_ref, share_ref, gains_ref, qkv, out, key_sum, value_sum, share_sum = refs[13:]
     block = q_ref.shape[0]
     heads = k_ref.shape[1] // HEAD_SIZE
-    step = pl.program_id(0)
+    half, step = pl.program_id(0), pl.program_id(1)
+
+    @pl.when((half == 0) & (step == 0))
+    def _():
+        gains_ref[...] = jnp.zeros_like(gains_ref)
 
     @pl.when(step == 0)
     def _():
@@ -428,7 +431,6 @@
 
         key_sum[...] = jnp.zeros_like(key_sum)
         value_sum[...] = jnp.zeros_like(value_sum)
-        gains_ref[...] = jnp.zeros_like(gains_ref)
 
     def work(j):
         size = (j + 1) * block
@@ -461,7 +463,7 @@
             up = jnp.concatenate([grad_attended[:, s] for s in head_lanes], axis=0)
             seen = jnp.concatenate([attended[:, s] for s in head_lanes], axis=0)
             log_total = jnp.concatenate(
-                [totals[(half * heads + h) * GROUP + g : (half * heads + h) * GROUP + g + 1, :] for g in range(GROUP)], axis=1
+                [totals[h * GROUP + g : h * GROUP + g + 1, :] for g in range(GROUP)], axis=1
             )
             row = jnp.sum(up.astype(FULL) * seen.astype(FULL), axis=1, keepdims=True)
             row = jnp.broadcast_to(row, (GROUP * block, HEAD_SIZE)).T[:1, :]
@@ -491,9 +493,18 @@
         grad = jnp.concatenate(query_grads + key_grads + value_grads, axis=1)
         grad_ref[...] = grad
         share = dot_nt(grad, qkv[...])
-        if half:
-            share = share + base_ref[...].astype(FULL)
-        share_ref[...] = share.astype(LOW)
+
+        @pl.when(half == 0)
+        def _():
+            share_sum[j] = share
+
+        @pl.when((half > 0) & (half < HALVES - 1))
+        def _():
+            share_sum[j] += share
+
+        @pl.when(half == HALVES - 1)
+        def _():
+            share_ref[...] = (share_sum[j] + share).astype(LOW)
 
     for j in range(n):
         pl.when(step == n - 1 - j)(functools.partial(work, j))
@@ -501,7 +512,7 @@
 
 def back(
     place, qkv_parts, out_parts, hidden_grad, attended, totals, q, k, v, raw, cos, sin, seg_col,
-    seg_row, gain_q, gain_k, half, base,
+    seg_row, gain_q, gain_k,
 ):
     inner = len(out_parts) // 2
     n = len(qkv_parts) // inner
@@ -509,31 +520,32 @@
     q_width, k_width = q.shape[1] // HALVES, k.shape[1] // HALVES
     block = length // n
     width = q_width + 2 * k_width
-    whole = lambda i, p: (0, 0)
-    natural = lambda i, p: (n - 1 - i, 0)
-    slot = lambda i, p: (p[0] ^ (n - 1 - i), 0)
-    natural_half = lambda i, p: (n - 1 - i, half)
-    slot_half = lambda i, p: (p[0] ^ (n - 1 - i), half)
-    base = [] if base is None else [base]
+    whole = lambda h, i, p: (0, 0)
+    natural = lambda h, i, p: (n - 1 - i, 0)
+    slot = lambda h, i, p: (p[0] ^ (n - 1 - i), 0)
+    last_slot = lambda h, i, p: (p[0] ^ (n - 1 - jnp.where(h == HALVES - 1, i, 0)), 0)
+    of_half = lambda h, i, p: (0, h)
+    natural_half = lambda h, i, p: (n - 1 - i, h)
+    slot_half = lambda h, i, p: (p[0] ^ (n - 1 - i), h)
     return pl.pallas_call(
-        functools.partial(back_kernel, n, inner, half),
+        functools.partial(back_kernel, n, inner),
         out_shape=(
-            jax.ShapeDtypeStruct((length, width), LOW),
+            jax.ShapeDtypeStruct((length, HALVES * width), LOW),
             jax.ShapeDtypeStruct((length, D), LOW),
             jax.ShapeDtypeStruct((8, HEAD_SIZE), FULL),
         ),
         grid_spec=pltpu.PrefetchScalarGridSpec(
             num_scalar_prefetch=1,
-            grid=(n,),
-            in_specs=[resident((p.shape[0], width), half) for p in qkv_parts]
+            grid=(HALVES, n),
+            in_specs=[pl.BlockSpec((p.shape[0], width), of_half) for p in qkv_parts]
             + [resident(p.shape) for p in out_parts]
             + [
                 pl.BlockSpec((block, D), slot),
                 pl.BlockSpec((block, q_width), slot_half),
-                pl.BlockSpec((block, HEAD_SIZE), slot),
+                pl.BlockSpec((block, HEAD_SIZE), slot_half),
                 pl.BlockSpec((block, q_width), natural_half),
-                resident((length, k_width), half),
-                resident((length, k_width), half),
+                pl.BlockSpec((length, k_width), of_half),
+                pl.BlockSpec((length, k_width), of_half),
                 pl.BlockSpec((block, q_width + k_width), natural_half),
                 pl.BlockSpec((block, HEAD_SIZE), natural),
                 pl.BlockSpec((block, HEAD_SIZE), natural),
@@ -541,11 +553,10 @@
                 pl.BlockSpec((1, length), whole),
                 pl.BlockSpec((1, HEAD_SIZE), whole),
                 pl.BlockSpec((1, HEAD_SIZE), whole),
-            ]
-            + [pl.BlockSpec((block, D), slot)] * len(base),
+            ],
             out_specs=(
-                pl.BlockSpec((block, width), natural),
-                pl.BlockSpec((block, D), slot),
+                pl.BlockSpec((block, width), natural_half),
+                pl.BlockSpec((block, D), last_slot),
                 pl.BlockSpec((8, HEAD_SIZE), whole),
             ),
             scratch_shapes=[
@@ -553,6 +564,7 @@
                 pltpu.VMEM((q_width, D), LOW),
                 pltpu.VMEM((length, k_width), FULL),
                 pltpu.VMEM((length, k_width), FULL),
+                pltpu.VMEM((n, block, D), FULL),
             ],
         ),
         compiler_params=pltpu.CompilerParams(vmem_limit_bytes=56 * MIB),
@@ -564,7 +576,7 @@
         name="back",
     )(
         place, *qkv_parts, *out_parts, hidden_grad, attended, totals, q, k, v, raw, cos, sin,
-        seg_col, seg_row, gain_q, gain_k, *base,
+        seg_col, seg_row, gain_q, gain_k,
     )
 
 
@@ -670,13 +682,6 @@
 
     def pick(value, axis, index):
         return lax.dynamic_index_in_dim(value, index, axis, False)
-
-    middle = reps // 2
-    hops = [([(k, k + 1), (reps - 1 - k, reps - 2 - k)], None) for k in range(middle - 1)]
-    hops.append(([(middle - 1, middle), (middle, middle - 1)], None))
-    hops += [
-        ([(k, k - 1), (reps - 1 - k, reps - k)], (k - 1, reps - k)) for k in range(middle - 1, 0, -1)
-    ]
 
     def on_device(
         tokens,
@@ -794,7 +799,6 @@
         hidden_grad = hidden_grad + c_all[: 2 * block].astype(FULL)
         hidden_low = hidden_grad.astype(LOW)
         grad_slots = over_chips(hidden_low)
-        grad_all = jnp.concatenate(grad_slots)
 
         def by_sequence(kept, landed):
             return jnp.where(core == 0, jnp.stack([kept, landed]), jnp.stack([landed, kept]))
@@ -820,23 +824,6 @@
             line[:] = pieces
             return pieces
 
-        def go(value, step=0):
-            return [value, lax.ppermute(value, "rep", hops[step][0]), step]
-
-        def step_on(trip):
-            value, landed, step = trip
-            if step == len(hops):
-                return
-            takes = hops[step][1]
-            if takes is None:
-                value = next_sum(value, [landed])
-            else:
-                landed = after(landed, *line)
-                value = jnp.where((rep == takes[0]) | (rep == takes[1]), landed, value)
-                line[:] = [value]
-            step += 1
-            trip[:] = go(value, step) if step < len(hops) else [value, None, step]
-
         def send_x(parts):
             return parts[0], [swap_chip(parts[s], s) for s in range(1, chips)]
 
@@ -845,7 +832,7 @@
 
         def cut_qkv(grad):
             grad_qkv = dot_tn(normed, grad).astype(LOW)
-            cuts = grad_qkv.reshape(chips, 2, inner, rows, width // HALVES)
+            cuts = grad_qkv.reshape(chips, 2, inner, rows, width)
             return pick(cuts, 1, core), [swap_core(pick(cuts, 1, core ^ 1))]
 
         x_late, active_late = lax.optimization_barrier((x_all, active, hidden_low))[:2]
@@ -859,9 +846,11 @@
         own_rows = pick(expand_cuts, 1, core)
         late_rows = after(own_rows, grad_slots[-1])
         own_sent = [swap_chip(pick(late_rows, 0, chip ^ s), s) for s in range(1, chips)]
+        grad_slots = lax.optimization_barrier((*grad_slots, grad_shrink))[:-1]
+        grad_all = jnp.concatenate(grad_slots)
         grad, back_all, head_gains = back(
             place, qkv_parts, out_parts, grad_all, attended, totals, q, k, v, raw, cos, sin, seg_col,
-            seg_row, gain_query, gain_key, 0, None,
+            seg_row, gain_query, gain_key,
         )
 
         line[:] = [head_gains]
@@ -875,72 +864,57 @@
         qkv_cut = send_y(next_cut(qkv_cuts, qkv_sent, 1, mine, inner))
         other_cut = swap_core(next_sum(*other_cut))
         out_cut = send_y(next_cut(pick(out_cuts, 0, core), out_sent, 0, mine, inner))
+        own_cut = next_sum(*own_cut)
+        own_cut, other_cut = lax.optimization_barrier((own_cut, other_cut, *line))[:2]
+        line[:] = [other_cut]
+        own_cut, other_cut = lax.psum((own_cut, other_cut), "rep")
+        shrink_cut = next_sum(*shrink_cut)
+        kept, sent = send_x(next_cut(*qkv_cut, 0, chip, chips))
         shares = []
         for s in range(1, chips):
-            share = after(back_all[2 * s * block : 2 * (s + 1) * block], *line)
+            share = after(back_all[2 * s * block : 2 * (s + 1) * block], kept)
             shares.append(swap_chip(share, s))
-        other_cut = after(other_cut, *line)
-        line[:] = [other_cut]
-        other = go(other_cut)
-        own = go(next_sum(*own_cut))
-        shrink = go(next_sum(*shrink_cut))
-        step_on(other)
-        kept, sent = send_x(next_cut(*qkv_cut, 0, chip, chips))
-        qkv = [go(kept)]
-        out = go(next_sum(*out_cut))
-        step_on(own)
-        step_on(other)
-        for value in sent:
-            value = after(value, *line)
-            line[:] = [value]
-            qkv.append(go(value))
-        step_on(shrink)
-        step_on(own)
+        out_cut = next_sum(*out_cut)
+        *qkv_cuts, shrink_cut, out_cut, own_cut, other_cut = lax.optimization_barrier(
+            (kept, *sent, shrink_cut, out_cut, own_cut, other_cut, *line)
+        )[: 4 + chips]
+        total_shrink, total_out, *qkv_cuts = lax.psum((shrink_cut, out_cut, *qkv_cuts), "rep")
 
         shares = [back_all[: 2 * block]] + [after(value, *line) for value in shares]
         input_part, gain_part = norm_back(inputs, gain_one, sum_of(shares))
         gain_one_grad = jnp.sum(gain_part, axis=0)
         input_grad = (input_part + hidden_grad).astype(LOW)
         input_landed = swap_core(input_grad[block:])
-        line[:] = [gain_one_grad]
-
-        step_on(qkv[0])
-        step_on(other)
-        step_on(shrink)
-        step_on(out)
-        step_on(own)
-        step_on(qkv[0])
-        for trip in qkv[1:]:
-            step_on(trip)
-        step_on(out)
         grad_gains = jnp.concatenate([gain_one_grad, gain_two_grad, head_gains[0], head_gains[1]])
-        total_gains = lax.psum(after(grad_gains, *line), ("ctx", "grp", "rep"))
-        line[:] = [total_gains]
-        total_gains = lax.dynamic_slice_in_dim(
-            total_gains, (me * inner + mine) * norm_gains.shape[0], norm_gains.shape[0], 0
-        )
-        step_on(shrink)
-        for trip in qkv[1:]:
-            step_on(trip)
-        trips = (other, own, shrink, out, *qkv)
-        for _ in hops:
-            for trip in trips:
-                step_on(trip)
-        other_cut, own_cut, total_shrink, total_out, *qkv_cuts = [trip[0] for trip in trips]
+        grad_gains = grad_gains.reshape(n, inner, 1, -1)
+        gains_of = lambda s, t: pick(pick(grad_gains, 0, me ^ s), 0, mine ^ t)
+        gains_sent = [
+            swap_plane(gains_of(s, t), s, t) for s in range(n) for t in range(inner) if s or t
+        ]
+        gains_sent = lax.optimization_barrier(tuple(gains_sent))
+        total_gains = sum_of([gains_of(0, 0), *gains_sent])
+        gains_sent = [
+            lax.ppermute(total_gains, "rep", [(i, i ^ r) for i in range(reps)]) for r in range(1, reps)
+        ]
+        total_gains = sum_of([total_gains, *lax.optimization_barrier(tuple(gains_sent))])[0]
         input_grad = by_sequence(input_grad[:block], input_landed)
 
+        size = k_width // HALVES
+
         def qkv_column(i, s):
-            q_blocks = q_width // k_width
-            k_place = QUERY_FEATURES // k_width + s
-            v_place = k_place + chips
-            return jnp.where(i < q_blocks, s * q_blocks + i, jnp.where(i == q_blocks, k_place, v_place))
+            q_blocks = q_width // HALVES // size
+            half, i = i // (q_blocks + 2), i % (q_blocks + 2)
+            q_place = (s * HALVES + half) * q_blocks + i
+            k_place = QUERY_FEATURES // size + s * HALVES + half
+            v_place = k_place + KEY_FEATURES // size
+            return jnp.where(i < q_blocks, q_place, jnp.where(i == q_blocks, k_place, v_place))
 
         key = chip.reshape(1).astype(jnp.int32)
         return (
             output,
             input_grad,
             *adam_cuts(
-                key, qkv_cuts, qkv_weight, qkv_first, qkv_second, RATE_QKV, k_width, qkv_column
+                key, qkv_cuts, qkv_weight, qkv_first, qkv_second, RATE_QKV, size, qkv_column
             ),
             *adam_step(out_weight, out_first, out_second, total_out.astype(FULL), RATE_OUT),
             *adam_pair(

time: 587 us -> 543 us (0.925)
  waiting for transfers between devices: 187 us -> 241 us
  blocking collectives: 45.6 us -> 0 us
  starting transfers between devices: 81 us -> 38.6 us
  Pallas kernels: 146 us -> 124 us
  local copies, waits for them, and re-layouts: 24.2 us -> 38.2 us
    psum x0 -> x2, waiting for transfers between devices: none -> 74.5 us  [the longest x1 58.5 us: on_device(): lax.psum((shrink_cut, out_cut, *qkv_cuts), 'rep')]
    ppermute x18 -> x3, starting transfers between devices: 50.1 us -> 4.45 us  [on_device(): lax.ppermute(total_gains, 'rep', [(i, i ^ r) for i in range(reps)])]
    ppermute x18 -> x3, waiting for transfers between devices: 48.6 us -> 3.02 us  [on_device(): lax.ppermute(total_gains, 'rep', [(i, i ^ r) for i in range(reps)])]
    psum x1 -> x0, blocking collectives: 45.6 us -> none  [on_device(): total_gains = lax.psum(after(grad_gains, *line), ('ctx', 'grp', 'rep'))]
    pallas_call x1, Pallas kernels: 66.6 us -> 43 us  [back(): pl.pallas_call(functools.partial(back_kernel, n, inner), out_shape=(jax.S...]
    ppermute x26, waiting for transfers between devices: 83.7 us -> 101 us  [swap_ctx(): return lax.ppermute(value, 'ctx', [(i, i ^ s) for i in range(n)])]
    unnamed x136 -> x138, local copies, waits for them, and re-layouts: 9.67 us -> 24.1 us
    ppermute x8, waiting for transfers between devices: 46.3 us -> 57.1 us  [swap_grp(): return lax.ppermute(value, 'grp', [(i, i ^ t) for i in range(inner)])]
  transfers between devices with their start and end apart: 61 -> 55, of which waited for: 19 -> 21; matrix products, arithmetic and copies ran while one was open for 15% -> 15% of each run, Pallas kernels for 18% -> 15%
where the time goes in v4:
time: 543 us; the launch traced here: 536 us
  waiting for transfers between devices  241 us (44%)
  Pallas kernels  124 us (23%)
  other arithmetic  58.7 us (11%)
  starting transfers between devices  38.6 us (7%)
  local copies, waits for them, and re-layouts  38.2 us (7%)
  matrix products  19.9 us (4%)
  between operations  15 us (3%)
    ppermute x26, waiting for transfers between devices, swap_ctx(): return lax.ppermute(value, 'ctx', [(i, i ^ s) for i in range(n)])  101 us
    psum x1, waiting for transfers between devices, on_device(): lax.psum((shrink_cut, out_cut, *qkv_cuts), 'rep')  58.5 us
    ppermute x8, waiting for transfers between devices, swap_grp(): return lax.ppermute(value, 'grp', [(i, i ^ t) for i in range(inner)])  57.1 us
    pallas_call x1, Pallas kernels, back(): pl.pallas_call(functools.partial(back_kernel, n, inner), out_shape=(jax.S...  43 us
    pallas_call x1, Pallas kernels, feed(): pl.pallas_call(functools.partial(feed_kernel, chips), out_shape=(wide(D),...  35.6 us
    unnamed x138, local copies, waits for them, and re-layouts  24.1 us
    pallas_call x2, Pallas kernels, attend(): pl.pallas_call(functools.partial(attend_kernel, n, inner, first, bool(bas...  21.4 us
    dot_general x4, matrix products, dot_tn(): lax.dot_general(a, b, (((0,), (0,)), ((), ())), preferred_element_type=FULL)  19.9 us
  transfers between devices with their start and end apart: 55, of which 21 were waited for; matrix products, arithmetic and copies ran while one was open for 15% of the time, Pallas kernels for 15%

profile of v4, /device:TPU:0, one launch (start us, length us, event | category | flops | bytes accessed | tf_op | source)
XLA Modules:
  0.0 536.2 jit_solution(5070998000015959033)
XLA Ops:
  7.3 2.5 convert_element_type.322
  9.9 3.4 convert_element_type.321
  13.4 3.0 collective-permute-start
  32.1 15.8 %collective-permute-done.14.refs_4_ = bf16[128,2048]{1,0:T(8,128)(2,1)} collective-permute-done((bf16[128,2048]{1,0:T(8,128)(2,1)}, bf16[128,2048]{1,0:T(8,128)(2,1)}, u32[]{:S(2)}, u32[]{:S(2)}) %collective-permute-start.14) | collective-permute-done | bytes 524320 | tf_op jit(solution)/shard_map/ppermute | solution.py:656
  50.8 2.6 gather_fusion.1
  53.8 14.6 %collective-permute-done.11.refs_1_ = bf16[128,2048]{1,0:T(8,128)(2,1)} collective-permute-done((bf16[128,2048]{1,0:T(8,128)(2,1)}, bf16[128,2048]{1,0:T(8,128)(2,1)}, u32[]{:S(2)}, u32[]{:S(2)}) %collective-permute-start.11) | collective-permute-done | bytes 524320 | tf_op jit(solution)/shard_map/ppermute | solution.py:665
  71.2 11.8 %collective-permute-done.15.refs_5_ = bf16[128,2048]{1,0:T(8,128)(2,1)S(1)} collective-permute-done((bf16[128,2048]{1,0:T(8,128)(2,1)}, bf16[128,2048]{1,0:T(8,128)(2,1)S(1)}, u32[]{:S(2)}, u32[]{:S(2)}) %collective-permute-start.15) | collective-permute-done | bytes 524320 | tf_op jit(solution)/shard_map/ppermute | solution.py:665
  89.7 10.6 %project.1 = (bf16[1024,1024]{1,0:T(8,128)(2,1)S(1)}, bf16[1024,1024]{1,0:T(8,128)(2,1)S(1)}, bf16[1024,512]{1,0:T(8,128)(2,1)S(1)}, bf16[1024,512]{1,0:T(8,128)(2,1)S(1)}, bf16[1024,1536]{1,0:T(8,128)(2,1)}) custom-call(s32[2]{0:T(128)S(1)} %pad_add_fusion.place_ref, bf16[128,2048]{1,0:T(8,128)(2,1)} %get-tuple-element.96.refs_0_, ...), custom_call_target="tpu_custom_call" | custom-call | flops 4294967296 | bytes 16777216 | tf_op jit(solution)/shard_map/project/pallas_call | solution.py:150
  104.0 11.3 %attend.2 = (bf16[1024,1024]{1,0:T(8,128)(2,1)}, f32[1024,256]{1,0:T(8,128)S(1)}, bf16[512,1024]{1,0:T(8,128)(2,1)S(1)}) custom-call(s32[2]{0:T(128)S(1)} %pad_add_fusion.place_ref, bf16[256,1024]{1,0:T(8,128)(2,1)S(1)} %convert_element_type.317.refs_0_.refs_8_, bf16[256,1024]{1,0:T(8,128)(2,1)S(1)} %copy-done.23, ...), custom_call_target="tpu_custom_call" | custom-call | flops 3221225472 | bytes 8388608 | tf_op jit(solution)/shard_map/attend/pallas_call | solution.py:258
  115.7 10.1 %attend.3 = (bf16[1024,1024]{1,0:T(8,128)(2,1)}, f32[1024,256]{1,0:T(8,128)S(1)}, bf16[512,1024]{1,0:T(8,128)(2,1)S(1)}) custom-call(s32[2]{0:T(128)S(1)} %pad_add_fusion.place_ref, bf16[256,1024]{1,0:T(8,128)(2,1)S(1)} %convert_element_type.317.refs_0_.refs_8_, bf16[256,1024]{1,0:T(8,128)(2,1)S(1)} %copy-done.23, ...), custom_call_target="tpu_custom_call", output_to_operand_aliasing={{0}: (10, {}), {1}: (11, {})} | custom-call | flops 3221225472 | bytes 8388608 | tf_op jit(solution)/shard_map/attend/pallas_call | solution.py:258
  125.9 37.6 %collective-permute-done.20 = bf16[512,1024]{1,0:T(8,128)(2,1)S(1)} collective-permute-done((bf16[512,1024]{1,0:T(8,128)(2,1)S(1)}, bf16[512,1024]{1,0:T(8,128)(2,1)S(1)}, u32[]{:S(2)}, u32[]{:S(2)}) %collective-permute-start.20) | collective-permute-done | bytes 1048608 | tf_op jit(solution)/shard_map/ppermute | solution.py:656
  169.9 4.3 all-gather.3.cloned.1.call-done.refs_0_.refs_1_.refs_2_.refs_3_
  174.2 35.6 %feed.1 = (bf16[1024,1024]{1,0:T(8,128)(2,1)}, bf16[1024,1024]{1,0:T(8,128)(2,1)}, bf16[1024,1536]{1,0:T(8,128)(2,1)}, bf16[1024,3072]{1,0:T(8,128)(2,1)}, bf16[...) custom-call(s32[2]{0:T(128)} %copy-done.18, ...), custom_call_target="tpu_custom_call" | custom-call | flops 19327352832 | bytes 31457280 | tf_op jit(solution)/shard_map/feed/pallas_call | solution.py:359
  210.1 2.6 collective-permute-done.25
  212.8 2.8 multiply_reduce_fusion
  215.6 2.5 fusion.61
  219.1 8.9 %convolution_convert_fusion = bf16[1024,3072]{1,0:T(8,128)(2,1)S(1)} fusion(bf16[1024,1024]{1,0:T(8,128)(2,1)} %get-tuple-element.129, bf16[1024,3072]{1,0:T(8,128)(2,1)S(1)} %copy-done.61), kind=kOutput, calls=%fused_computation.2 | convolution fusion | flops 6445596672 | bytes 14680064 | tf_op jit(solution)/shard_map/dot_general | solution.py:51
  229.8 13.7 %collective-permute-done.26 = bf16[512,1024]{1,0:T(8,128)(2,1)S(1)} collective-permute-done((bf16[512,1024]{1,0:T(8,128)(2,1)S(1)}, bf16[512,1024]{1,0:T(8,128)(2,1)S(1)}, u32[]{:S(2)}, u32[]{:S(2)}) %collective-permute-start.26) | collective-permute-done | bytes 1048608 | tf_op jit(solution)/shard_map/ppermute | solution.py:656
  245.1 3.7 convolution_convert_fusion.1
  253.3 43.0 %back.1 = (bf16[1024,2048]{1,0:T(8,128)(2,1)}, bf16[1024,1024]{1,0:T(8,128)(2,1)}, f32[8,128]{1,0:T(8,128)}) custom-call(s32[2]{0:T(128)} %copy-done.18, bf16[128,2048]{1,0:T(8,128)(2,1)} %get-tuple-element.96.refs_0_, bf16[128,2048]{1,0:T(8,128)(2,1)} %collective-permute-done.11.refs_1_, bf16[128,2048]{1,0:T(8,128)(2,1)} %copy-done.26, ...), custom_call_target="tpu_custom_call" | custom-call | flops 5905580032 | bytes 31457280 | tf_op jit(solution)/shard_map/back/pallas_call | solution.py:530
  296.3 2.6 fusion.20
  298.9 2.5 fusion.18
  301.6 4.9 convolution_convert_fusion.2
  308.3 3.2 fusion.16
  311.5 2.4 convolution_convert_fusion.3
  317.7 2.1 fusion.11
  321.6 5.5 %collective-permute-done.35 = bf16[128,3072]{1,0:T(8,128)(2,1)S(1)} collective-permute-done((bf16[128,3072]{1,0:T(8,128)(2,1)S(1)}, bf16[128,3072]{1,0:T(8,128)(2,1)S(1)}, u32[]{:S(2)}, u32[]{:S(2)}) %collective-permute-start.35) | collective-permute-done | bytes 786464 | tf_op jit(solution)/shard_map/ppermute | solution.py:656
  328.8 8.1 %collective-permute-done.33 = bf16[128,3072]{1,0:T(8,128)(2,1)S(1)} collective-permute-done((bf16[128,3072]{1,0:T(8,128)(2,1)S(1)}, bf16[128,3072]{1,0:T(8,128)(2,1)S(1)}, u32[]{:S(2)}, u32[]{:S(2)}) %collective-permute-start.33) | collective-permute-done | bytes 786464 | tf_op jit(solution)/shard_map/ppermute | solution.py:665
  338.1 5.6 %collective-permute-done.32 = bf16[384,1024]{1,0:T(8,128)(2,1)} collective-permute-done((bf16[384,1024]{1,0:T(8,128)(2,1)}, bf16[384,1024]{1,0:T(8,128)(2,1)}, u32[]{:S(2)}, u32[]{:S(2)}) %collective-permute-start.32) | collective-permute-done | bytes 786464 | tf_op jit(solution)/shard_map/ppermute | solution.py:656
  343.8 2.6 add_convert_fusion.1
  346.4 12.4 %collective-permute-done.31 = bf16[2,128,2048]{2,1,0:T(8,128)(2,1)} collective-permute-done((bf16[2,128,2048]{2,1,0:T(8,128)(2,1)}, bf16[2,128,2048]{2,1,0:T(8,128)(2,1)}, u32[]{:S(2)}, u32[]{:S(2)}) %collective-permute-start.31) | collective-permute-done | bytes 1048608 | tf_op jit(solution)/shard_map/ppermute | solution.py:665
  358.8 2.6 fusion.28
  364.7 10.1 %collective-permute-done.38 = bf16[256,1024]{1,0:T(8,128)(2,1)} collective-permute-done((bf16[256,1024]{1,0:T(8,128)(2,1)}, bf16[256,1024]{1,0:T(8,128)(2,1)}, u32[]{:S(2)}, u32[]{:S(2)}) %collective-permute-start.38) | collective-permute-done | bytes 524320 | tf_op jit(solution)/shard_map/ppermute | solution.py:665
  374.9 2.2 add_convert_fusion.4
  377.0 10.7 %collective-permute-done.37 = bf16[512,1024]{1,0:T(8,128)(2,1)} collective-permute-done((bf16[512,1024]{1,0:T(8,128)(2,1)}, bf16[512,1024]{1,0:T(8,128)(2,1)}, u32[]{:S(2)}, u32[]{:S(2)}) %collective-permute-start.37) | collective-permute-done | bytes 1048608 | tf_op jit(solution)/shard_map/ppermute | solution.py:656
  387.8 2.4 fusion.8
  390.2 7.1 %collective-permute-done.40 = bf16[128,2048]{1,0:T(8,128)(2,1)} collective-permute-done((bf16[128,2048]{1,0:T(8,128)(2,1)}, bf16[128,2048]{1,0:T(8,128)(2,1)}, u32[]{:S(2)}, u32[]{:S(2)}) %collective-permute-start.40) | collective-permute-done | bytes 524320 | tf_op jit(solution)/shard_map/ppermute | solution.py:656
  397.3 16.0 %all-reduce.8.cloned.1.call-done = (bf16[128,3072]{1,0:T(8,128)(2,1)}, bf16[128,3072]{1,0:T(8,128)(2,1)}) async-done(((bf16[128,3072]{1,0:T(8,128)(2,1)}, bf16[128,3072]{1,0:T(8,128)(2,1)}), (bf16[128,3072]{1,0:T(8,128)(2,1)}, bf16[128,3072]{1,0:T(8,128)(2,1)})) %all-reduce.8.cloned.1.call-update) | async-done | bytes 1572880 | tf_op jit(solution)/shard_map/psum | solution.py:870
  418.6 4.7 fusion.7
  430.4 2.4 collective-permute-start.50
  433.5 2.3 collective-permute-done.50
  442.2 6.5 %adam_pair.1 = (f32[128,6144]{1,0:T(8,128)}, f32[128,6144]{1,0:T(8,128)}, f32[128,6144]{1,0:T(8,128)}) custom-call(s32[2]{0:T(128)S(1)} %copy-done.19, bf16[128,3072]{1,0:T(8,128)(2,1)S(1)} %copy-done.9, bf16[128,3072]{1,0:T(8,128)(2,1)S(1)} %copy-done.10, f32[128,6144]{1,0:T(8,128)S(1)} %copy-done.2, f32[128,6144]{1,0:T(8,128)S(1)} %copy-done.5, ...), custom_call_target="tpu_custom_call" | custom-call | flops 15728640 | bytes 20447232 | tf_op jit(solution)/shard_map/adam_pair/pallas_call | solution.py:631
  449.5 2.4 maximum_select_fusion.1
  451.9 2.3 maximum_select_fusion
  454.3 58.5 %all-reduce.6.cloned.1.call-done = (bf16[128,2048]{1,0:T(8,128)(2,1)}, bf16[128,2048]{1,0:T(8,128)(2,1)}, bf16[256,1024]{1,0:T(8,128)(2,1)}, bf16[384,1024]{1,0:T(8,128)(2,1)}) async-done(((bf16[128,2048]{1,0:T(8,128)(2,1)}, bf16[128,2048]{1,0:T(8,128)(2,1)}, bf16[256,1024]{1,0:T(8,128)(2,1)}, bf16[384,1024]{1,0:T(8,128)(2,1)}), (bf16[128,2048]{1,0:T(8,128)(2,1)}, bf16[128,2048]{1,0:T(8,128)(2,1)}, ...) | async-done | bytes 2359312 | tf_op jit(solution)/shard_map/psum | solution.py:881
  512.8 5.4 %multiply_subtract_fusion = (f32[384,1024]{1,0:T(8,128)}, f32[384,1024]{1,0:T(8,128)}, f32[384,1024]{1,0:T(8,128)}) fusion(f32[384,1024]{1,0:T(8,128)S(1)} %copy-done.38, bf16[384,1024]{1,0:T(8,128)(2,1)} %get-tuple-element.178, f32[384,1024]{1,0:T(8,128)} %param.34, f32[384,1024]{1,0:T(8,128)} %param.33), kind=kLoop, calls=%fused_computation.51 | loop fusion | flops 6291456 | bytes 10223616 | tf_op jit(solution)/shard_map/sub | solution.py:72
  518.3 2.3 multiply_subtract_fusion.1
  522.3 7.2 %adam_cuts.1 = (f32[128,4096]{1,0:T(8,128)}, f32[128,4096]{1,0:T(8,128)}, f32[128,4096]{1,0:T(8,128)}) custom-call(s32[1]{0:T(128)} %bitcast.56.key_ref, bf16[128,2048]{1,0:T(8,128)(2,1)S(1)} %copy-done.15, bf16[128,2048]{1,0:T(8,128)(2,1)S(1)} %copy-done.16, f32[128,4096]{1,0:T(8,128)S(1)} %copy-done.4, f32[128,4096]{1,0:T(8,128)S(1)} %copy-done.7, ...), custom_call_target="tpu_custom_call" | custom-call | flops 10485760 | bytes 13631488 | tf_op jit(solution)/shard_map/adam_cuts/pallas_call | solution.py:601
  (286 shorter events, 83.7 us)
Async XLA Ops:
  7.2 162.7 %all-gather.5.cloned.1.call-start = ((), (), s32[]{:S(2)}) async-start(), calls=%async_computation.1 | async-start | bytes 7077888 | tf_op jit(solution)/shard_map/all_gather | solution.py:767
  9.8 164.4 %all-gather.3.cloned.1.call-start = ((), (), s32[]{:S(2)}) async-start(), calls=%async_computation | async-start | bytes 14155776 | tf_op jit(solution)/shard_map/all_gather | solution.py:767
  13.3 400.1 %all-reduce.8.cloned.1.call-start = ((), (), s32[]{:S(2)}) async-start(), calls=%async_computation.3 | async-start | bytes 3145728 | tf_op jit(solution)/shard_map/psum | solution.py:870
  13.4 11.0 %collective-permute-start = (f32[1,1312]{1,0:T(1,128)S(1)}, f32[1,1312]{1,0:T(1,128)S(1)}, u32[]{:S(2)}, u32[]{:S(2)}) collective-permute-start(f32[1,1312]{1,0:T(1,128)S(1)} %reshape.234), channel_id=1, source_target_pairs={{0,4},{4,0},{8,12},{12,8},{16,20},{20,16},{24,28},{28,24},{1,5},{5... | collective-permute-start | bytes 15752 | tf_op jit(solution)/shard_map/ppermute | solution.py:681
  16.4 8.5 %collective-permute-start.1 = (f32[1,1312]{1,0:T(1,128)S(1)}, f32[1,1312]{1,0:T(1,128)S(1)}, u32[]{:S(2)}, u32[]{:S(2)}) collective-permute-start(f32[1,1312]{1,0:T(1,128)S(1)} %reshape.234), channel_id=1, source_target_pairs={{0,8},{4,12},{8,0},{12,4},{16,24},{20,28},{24,16},{28,20},{1,9},{5... | collective-permute-start | bytes 15752 | tf_op jit(solution)/shard_map/ppermute | solution.py:681
  16.4 11.2 %collective-permute-start.2 = (f32[1,1312]{1,0:T(1,128)S(1)}, f32[1,1312]{1,0:T(1,128)S(1)}, u32[]{:S(2)}, u32[]{:S(2)}) collective-permute-start(f32[1,1312]{1,0:T(1,128)S(1)} %reshape.234), channel_id=1, source_target_pairs={{0,12},{4,8},{8,4},{12,0},{16,28},{20,24},{24,20},{28,16},{1,13},{... | collective-permute-start | bytes 15752 | tf_op jit(solution)/shard_map/ppermute | solution.py:681
  16.7 13.0 %collective-permute-start.3 = (f32[1,1312]{1,0:T(1,128)S(1)}, f32[1,1312]{1,0:T(1,128)S(1)}, u32[]{:S(2)}, u32[]{:S(2)}) collective-permute-start(f32[1,1312]{1,0:T(1,128)S(1)} %reshape.234), channel_id=1, source_target_pairs={{0,16},{4,20},{8,24},{12,28},{16,0},{20,4},{24,8},{28,12},{1,17},{... | collective-permute-start | bytes 15752 | tf_op jit(solution)/shard_map/ppermute | solution.py:681
  18.6 11.1 %collective-permute-start.4 = (f32[1,1312]{1,0:T(1,128)S(1)}, f32[1,1312]{1,0:T(1,128)S(1)}, u32[]{:S(2)}, u32[]{:S(2)}) collective-permute-start(f32[1,1312]{1,0:T(1,128)S(1)} %reshape.234), channel_id=1, source_target_pairs={{0,20},{4,16},{8,28},{12,24},{16,4},{20,0},{24,12},{28,8},{1,21},{... | collective-permute-start | bytes 15752 | tf_op jit(solution)/shard_map/ppermute | solution.py:681
  24.4 5.3 collective-permute-start.5
  24.9 4.7 collective-permute-start.6
  27.7 26.0 %collective-permute-start.8 = (bf16[256,1024]{1,0:T(8,128)(2,1)S(1)}, bf16[256,1024]{1,0:T(8,128)(2,1)S(1)}, u32[]{:S(2)}, u32[]{:S(2)}) collective-permute-start(bf16[256,1024]{1,0:T(8,128)(2,1)S(1)} %convert_element_type.317.refs_0_.refs_8_), channel_id=1, source_target_pairs={{0,4},{4,0},{1,5},{5,1},{2,6},{6,2},{3,7},{7,3},{8,12},{12,8},{9,1... | collective-permute-start | bytes 1572872 | tf_op jit(solution)/shard_map/ppermute | solution.py:665
  29.7 18.2 %collective-permute-start.14 = (bf16[128,2048]{1,0:T(8,128)(2,1)}, bf16[128,2048]{1,0:T(8,128)(2,1)}, u32[]{:S(2)}, u32[]{:S(2)}) collective-permute-start(bf16[128,2048]{1,0:T(8,128)(2,1)} %get-tuple-element.97), channel_id=1, source_target_pairs={{0,16},{8,24},{16,0},{24,8},{1,17},{9,25},{17,1},{25,9},{2,18},{10... | collective-permute-start | bytes 1572872 | tf_op jit(solution)/shard_map/ppermute | solution.py:656
  31.3 37.1 %collective-permute-start.11 = (bf16[128,2048]{1,0:T(8,128)(2,1)}, bf16[128,2048]{1,0:T(8,128)(2,1)}, u32[]{:S(2)}, u32[]{:S(2)}) collective-permute-start(bf16[128,2048]{1,0:T(8,128)(2,1)} %get-tuple-element.96.refs_0_), channel_id=1, source_target_pairs={{0,4},{4,0},{1,5},{5,1},{2,6},{6,2},{3,7},{7,3},{8,12},{12,8},{9,1... | collective-permute-start | bytes 1572872 | tf_op jit(solution)/shard_map/ppermute | solution.py:665
  31.9 37.5 %collective-permute-start.18 = (bf16[256,1024]{1,0:T(8,128)(2,1)S(1)}, bf16[256,1024]{1,0:T(8,128)(2,1)}, u32[]{:S(2)}, u32[]{:S(2)}) collective-permute-start(bf16[256,1024]{1,0:T(8,128)(2,1)S(1)} %dynamic-slice_bitcast_fusion.5.refs_8_), channel_id=1, source_target_pairs={{0,16},{8,24},{16,0},{24,8},{1,17},{9,25},{17,1},{25,9},{2,18},{10... | collective-permute-start | bytes 1572872 | tf_op jit(solution)/shard_map/ppermute | solution.py:656
  32.1 37.3 %collective-permute-start.7 = (bf16[256,1024]{1,0:T(8,128)(2,1)}, bf16[256,1024]{1,0:T(8,128)(2,1)S(1)}, u32[]{:S(2)}, u32[]{:S(2)}) collective-permute-start(bf16[256,1024]{1,0:T(8,128)(2,1)} %dynamic-slice_bitcast_fusion.6), channel_id=1, source_target_pairs={{0,8},{8,0},{16,24},{24,16},{1,9},{9,1},{17,25},{25,17},{2,10},{10... | collective-permute-start | bytes 1572872 | tf_op jit(solution)/shard_map/ppermute | solution.py:656
  47.9 35.1 %collective-permute-start.15 = (bf16[128,2048]{1,0:T(8,128)(2,1)}, bf16[128,2048]{1,0:T(8,128)(2,1)S(1)}, u32[]{:S(2)}, u32[]{:S(2)}) collective-permute-start(bf16[128,2048]{1,0:T(8,128)(2,1)} %collective-permute-done.14.refs_4_), channel_id=1, source_target_pairs={{0,4},{4,0},{1,5},{5,1},{2,6},{6,2},{3,7},{7,3},{8,12},{12,8},{9,1... | collective-permute-start | bytes 1572872 | tf_op jit(solution)/shard_map/ppermute | solution.py:665
  53.7 32.3 %collective-permute-start.12 = (bf16[128,2048]{1,0:T(8,128)(2,1)}, bf16[128,2048]{1,0:T(8,128)(2,1)S(1)}, u32[]{:S(2)}, u32[]{:S(2)}) collective-permute-start(bf16[128,2048]{1,0:T(8,128)(2,1)} %get-tuple-element.96.refs_0_), channel_id=1, source_target_pairs={{0,8},{8,0},{16,24},{24,16},{1,9},{9,1},{17,25},{25,17},{2,10},{10... | collective-permute-start | bytes 1572872 | tf_op jit(solution)/shard_map/ppermute | solution.py:656
  68.4 19.0 %collective-permute-start.13 = (bf16[128,2048]{1,0:T(8,128)(2,1)}, bf16[128,2048]{1,0:T(8,128)(2,1)}, u32[]{:S(2)}, u32[]{:S(2)}) collective-permute-start(bf16[128,2048]{1,0:T(8,128)(2,1)} %collective-permute-done.11.refs_1_), channel_id=1, source_target_pairs={{0,8},{8,0},{16,24},{24,16},{1,9},{9,1},{17,25},{25,17},{2,10},{10... | collective-permute-start | bytes 1572872 | tf_op jit(solution)/shard_map/ppermute | solution.py:656
  69.4 18.1 %collective-permute-start.16 = (bf16[128,2048]{1,0:T(8,128)(2,1)}, bf16[128,2048]{1,0:T(8,128)(2,1)}, u32[]{:S(2)}, u32[]{:S(2)}) collective-permute-start(bf16[128,2048]{1,0:T(8,128)(2,1)} %collective-permute-done.14.refs_4_), channel_id=1, source_target_pairs={{0,8},{8,0},{16,24},{24,16},{1,9},{9,1},{17,25},{25,17},{2,10},{10... | collective-permute-start | bytes 1572872 | tf_op jit(solution)/shard_map/ppermute | solution.py:656
  69.4 18.1 %collective-permute-start.19 = (bf16[256,1024]{1,0:T(8,128)(2,1)S(1)}, bf16[256,1024]{1,0:T(8,128)(2,1)}, u32[]{:S(2)}, u32[]{:S(2)}) collective-permute-start(bf16[256,1024]{1,0:T(8,128)(2,1)S(1)} %collective-permute-done.7.refs_9_), channel_id=1, source_target_pairs={{0,16},{8,24},{16,0},{24,8},{1,17},{9,25},{17,1},{25,9},{2,18},{10... | collective-permute-start | bytes 1572872 | tf_op jit(solution)/shard_map/ppermute | solution.py:656
  86.9 17.0 %collective-permute-start.9 = (bf16[256,1024]{1,0:T(8,128)(2,1)S(1)}, bf16[256,1024]{1,0:T(8,128)(2,1)S(1)}, u32[]{:S(2)}, u32[]{:S(2)}) collective-permute-start(bf16[256,1024]{1,0:T(8,128)(2,1)S(1)} %convert_element_type.317.refs_0_.refs_8_), channel_id=1, source_target_pairs={{0,8},{8,0},{16,24},{24,16},{1,9},{9,1},{17,25},{25,17},{2,10},{10... | collective-permute-start | bytes 1572872 | tf_op jit(solution)/shard_map/ppermute | solution.py:656
  87.4 16.5 %collective-permute-start.10 = (bf16[256,1024]{1,0:T(8,128)(2,1)}, bf16[256,1024]{1,0:T(8,128)(2,1)S(1)}, u32[]{:S(2)}, u32[]{:S(2)}) collective-permute-start(bf16[256,1024]{1,0:T(8,128)(2,1)} %copy-done.22), channel_id=1, source_target_pairs={{0,8},{8,0},{16,24},{24,16},{1,9},{9,1},{17,25},{25,17},{2,10},{10... | collective-permute-start | bytes 1572872 | tf_op jit(solution)/shard_map/ppermute | solution.py:656
  115.2 48.3 %collective-permute-start.20 = (bf16[512,1024]{1,0:T(8,128)(2,1)S(1)}, bf16[512,1024]{1,0:T(8,128)(2,1)S(1)}, u32[]{:S(2)}, u32[]{:S(2)}) collective-permute-start(bf16[512,1024]{1,0:T(8,128)(2,1)S(1)} %get-tuple-element.109), channel_id=1, source_target_pairs={{0,16},{8,24},{16,0},{24,8},{1,17},{9,25},{17,1},{25,9},{2,18},{10... | collective-permute-start | bytes 3145736 | tf_op jit(solution)/shard_map/ppermute | solution.py:656
  115.2 52.0 %collective-permute-start.22 = (bf16[2,256,1024]{2,1,0:T(8,128)(2,1)S(1)}, bf16[2,256,1024]{2,1,0:T(8,128)(2,1)S(1)}, u32[]{:S(2)}, u32[]{:S(2)}) collective-permute-start(bf16[2,256,1024]{2,1,0:T(8,128)(2,1)S(1)} %copy-done.56), channel_id=1, source_target_pairs={{0,8},{8,0},{16,24},{24,16},{1,9},{9,1},{17,25},{25,17},{2,10},{10... | collective-permute-start | bytes 3145736 | tf_op jit(solution)/shard_map/ppermute | solution.py:656
  218.2 25.4 %collective-permute-start.26 = (bf16[512,1024]{1,0:T(8,128)(2,1)S(1)}, bf16[512,1024]{1,0:T(8,128)(2,1)S(1)}, u32[]{:S(2)}, u32[]{:S(2)}) collective-permute-start(bf16[512,1024]{1,0:T(8,128)(2,1)S(1)} %fusion.61), channel_id=1, source_target_pairs={{0,16},{8,24},{16,0},{24,8},{1,17},{9,25},{17,1},{25,9},{2,18},{10... | collective-permute-start | bytes 3145736 | tf_op jit(solution)/shard_map/ppermute | solution.py:656
  228.1 70.9 %collective-permute-start.27 = (bf16[2,128,3072]{2,1,0:T(8,128)(2,1)S(1)}, bf16[2,128,3072]{2,1,0:T(8,128)(2,1)}, u32[]{:S(2)}, u32[]{:S(2)}) collective-permute-start(bf16[2,128,3072]{2,1,0:T(8,128)(2,1)S(1)} %dynamic-slice_bitcast_fusion.3), channel_id=1, source_target_pairs={{0,4},{4,0},{1,5},{5,1},{2,6},{6,2},{3,7},{7,3},{8,12},{12,8},{9,1... | collective-permute-start | bytes 4718600 | tf_op jit(solution)/shard_map/ppermute | solution.py:665
  244.8 51.5 %collective-permute-start.28 = (bf16[2,128,3072]{2,1,0:T(8,128)(2,1)}, bf16[2,128,3072]{2,1,0:T(8,128)(2,1)}, u32[]{:S(2)}, u32[]{:S(2)}) collective-permute-start(bf16[2,128,3072]{2,1,0:T(8,128)(2,1)} %dynamic-slice_bitcast_fusion.2), channel_id=1, source_target_pairs={{0,16},{8,24},{16,0},{24,8},{1,17},{9,25},{17,1},{25,9},{2,18},{10... | collective-permute-start | bytes 4718600 | tf_op jit(solution)/shard_map/ppermute | solution.py:656
  250.1 58.2 %collective-permute-start.30 = (bf16[2,384,1024]{2,1,0:T(8,128)(2,1)}, bf16[2,384,1024]{2,1,0:T(8,128)(2,1)}, u32[]{:S(2)}, u32[]{:S(2)}) collective-permute-start(bf16[2,384,1024]{2,1,0:T(8,128)(2,1)} %dynamic-slice_bitcast_fusion.1), channel_id=1, source_target_pairs={{0,4},{4,0},{1,5},{5,1},{2,6},{6,2},{3,7},{7,3},{8,12},{12,8},{9,1... | collective-permute-start | bytes 4718600 | tf_op jit(solution)/shard_map/ppermute | solution.py:665
  306.7 11.0 %collective-permute-start.29 = (bf16[2,2,128,2048]{3,2,0,1:T(8,128)(2,1)S(1)}, bf16[2,2,128,2048]{3,2,0,1:T(8,128)(2,1)S(1)}, u32[]{:S(2)}, u32[]{:S(2)}) collective-permute-start(bf16[2,2,128,2048]{3,2,0,1:T(8,128)(2,1)S(1)} %copy_bitcast_fusion), channel_id=1, source_target_pairs={{0,8},{8,0},{16,24},{24,16},{1,9},{9,1},{17,25},{25,17},{2,10},{10... | collective-permute-start | bytes 6291464 | tf_op jit(solution)/shard_map/ppermute | solution.py:656
  306.8 20.4 %collective-permute-start.35 = (bf16[128,3072]{1,0:T(8,128)(2,1)S(1)}, bf16[128,3072]{1,0:T(8,128)(2,1)S(1)}, u32[]{:S(2)}, u32[]{:S(2)}) collective-permute-start(bf16[128,3072]{1,0:T(8,128)(2,1)S(1)} %get-tuple-element.192), channel_id=1, source_target_pairs={{0,16},{8,24},{16,0},{24,8},{1,17},{9,25},{17,1},{25,9},{2,18},{10... | collective-permute-start | bytes 2359304 | tf_op jit(solution)/shard_map/ppermute | solution.py:656
  314.0 13.4 %collective-permute-start.34 = (bf16[2,256,1024]{2,1,0:T(8,128)(2,1)S(1)}, bf16[2,256,1024]{2,1,0:T(8,128)(2,1)S(1)}, u32[]{:S(2)}, u32[]{:S(2)}) collective-permute-start(bf16[2,256,1024]{2,1,0:T(8,128)(2,1)S(1)} %dynamic-slice_bitcast_fusion.4), channel_id=1, source_target_pairs={{0,8},{8,0},{16,24},{24,16},{1,9},{9,1},{17,25},{25,17},{2,10},{10... | collective-permute-start | bytes 3145736 | tf_op jit(solution)/shard_map/ppermute | solution.py:656
  316.6 20.4 %collective-permute-start.33 = (bf16[128,3072]{1,0:T(8,128)(2,1)S(1)}, bf16[128,3072]{1,0:T(8,128)(2,1)S(1)}, u32[]{:S(2)}, u32[]{:S(2)}) collective-permute-start(bf16[128,3072]{1,0:T(8,128)(2,1)S(1)} %get-tuple-element.194), channel_id=1, source_target_pairs={{0,4},{4,0},{1,5},{5,1},{2,6},{6,2},{3,7},{7,3},{8,12},{12,8},{9,1... | collective-permute-start | bytes 2359304 | tf_op jit(solution)/shard_map/ppermute | solution.py:665
  317.1 26.5 %collective-permute-start.32 = (bf16[384,1024]{1,0:T(8,128)(2,1)}, bf16[384,1024]{1,0:T(8,128)(2,1)}, u32[]{:S(2)}, u32[]{:S(2)}) collective-permute-start(bf16[384,1024]{1,0:T(8,128)(2,1)} %get-tuple-element.198), channel_id=1, source_target_pairs={{0,16},{8,24},{16,0},{24,8},{1,17},{9,25},{17,1},{25,9},{2,18},{10... | collective-permute-start | bytes 2359304 | tf_op jit(solution)/shard_map/ppermute | solution.py:656
  319.8 39.0 %collective-permute-start.31 = (bf16[2,128,2048]{2,1,0:T(8,128)(2,1)}, bf16[2,128,2048]{2,1,0:T(8,128)(2,1)}, u32[]{:S(2)}, u32[]{:S(2)}) collective-permute-start(bf16[2,128,2048]{2,1,0:T(8,128)(2,1)} %get-tuple-element.197), channel_id=1, source_target_pairs={{0,4},{4,0},{1,5},{5,1},{2,6},{6,2},{3,7},{7,3},{8,12},{12,8},{9,1... | collective-permute-start | bytes 3145736 | tf_op jit(solution)/shard_map/ppermute | solution.py:665
  327.4 10.7 %collective-permute-start.36 = (bf16[128,3072]{1,0:T(8,128)(2,1)S(1)}, bf16[128,3072]{1,0:T(8,128)(2,1)}, u32[]{:S(2)}, u32[]{:S(2)}) collective-permute-start(bf16[128,3072]{1,0:T(8,128)(2,1)S(1)} %add_convert_fusion.3), channel_id=1, source_target_pairs={{0,8},{8,0},{16,24},{24,16},{1,9},{9,1},{17,25},{25,17},{2,10},{10... | collective-permute-start | bytes 2359304 | tf_op jit(solution)/shard_map/ppermute | solution.py:656
  343.7 169.1 %all-reduce.6.cloned.1.call-start = ((), (), s32[]{:S(2)}) async-start(), calls=%async_computation.2 | async-start | bytes 4718592 | tf_op jit(solution)/shard_map/psum | solution.py:881
  361.4 26.4 %collective-permute-start.37 = (bf16[512,1024]{1,0:T(8,128)(2,1)}, bf16[512,1024]{1,0:T(8,128)(2,1)}, u32[]{:S(2)}, u32[]{:S(2)}) collective-permute-start(bf16[512,1024]{1,0:T(8,128)(2,1)} %slice.65), channel_id=1, source_target_pairs={{0,16},{8,24},{16,0},{24,8},{1,17},{9,25},{17,1},{25,9},{2,18},{10... | collective-permute-start | bytes 3145736 | tf_op jit(solution)/shard_map/ppermute | solution.py:656
  361.9 12.9 %collective-permute-start.38 = (bf16[256,1024]{1,0:T(8,128)(2,1)}, bf16[256,1024]{1,0:T(8,128)(2,1)}, u32[]{:S(2)}, u32[]{:S(2)}) collective-permute-start(bf16[256,1024]{1,0:T(8,128)(2,1)} %get-tuple-element.200), channel_id=1, source_target_pairs={{0,4},{4,0},{1,5},{5,1},{2,6},{6,2},{3,7},{7,3},{8,12},{12,8},{9,1... | collective-permute-start | bytes 1572872 | tf_op jit(solution)/shard_map/ppermute | solution.py:665
  362.2 54.8 %collective-permute-start.23 = (bf16[512,1024]{1,0:T(8,128)(2,1)}, bf16[512,1024]{1,0:T(8,128)(2,1)}, u32[]{:S(2)}, u32[]{:S(2)}) collective-permute-start(bf16[512,1024]{1,0:T(8,128)(2,1)} %get-tuple-element.114), channel_id=1, source_target_pairs={{0,8},{8,0},{16,24},{24,16},{1,9},{9,1},{17,25},{25,17},{2,10},{10... | collective-permute-start | bytes 3145736 | tf_op jit(solution)/shard_map/ppermute | solution.py:656
  363.0 34.3 %collective-permute-start.40 = (bf16[128,2048]{1,0:T(8,128)(2,1)}, bf16[128,2048]{1,0:T(8,128)(2,1)}, u32[]{:S(2)}, u32[]{:S(2)}) collective-permute-start(bf16[128,2048]{1,0:T(8,128)(2,1)} %get-tuple-element.204), channel_id=1, source_target_pairs={{0,16},{8,24},{16,0},{24,8},{1,17},{9,25},{17,1},{25,9},{2,18},{10... | collective-permute-start | bytes 1572872 | tf_op jit(solution)/shard_map/ppermute | solution.py:656
  413.4 10.8 %collective-permute-start.41 = (f32[1,288]{1,0:T(1,128)S(1)}, f32[1,288]{1,0:T(1,128)S(1)}, u32[]{:S(2)}, u32[]{:S(2)}) collective-permute-start(f32[1,288]{1,0:T(1,128)S(1)} %get-tuple-element.229), channel_id=1, source_target_pairs={{0,4},{4,0},{8,12},{12,8},{16,20},{20,16},{24,28},{28,24},{1,5},{5... | collective-permute-start | bytes 3464 | tf_op jit(solution)/shard_map/ppermute | solution.py:681
  414.9 9.5 %collective-permute-start.42 = (f32[1,288]{1,0:T(1,128)S(1)}, f32[1,288]{1,0:T(1,128)S(1)}, u32[]{:S(2)}, u32[]{:S(2)}) collective-permute-start(f32[1,288]{1,0:T(1,128)S(1)} %get-tuple-element.228), channel_id=1, source_target_pairs={{0,8},{4,12},{8,0},{12,4},{16,24},{20,28},{24,16},{28,20},{1,9},{5... | collective-permute-start | bytes 3464 | tf_op jit(solution)/shard_map/ppermute | solution.py:681
  414.9 11.7 %collective-permute-start.43 = (f32[1,288]{1,0:T(1,128)S(1)}, f32[1,288]{1,0:T(1,128)S(1)}, u32[]{:S(2)}, u32[]{:S(2)}) collective-permute-start(f32[1,288]{1,0:T(1,128)S(1)} %get-tuple-element.227), channel_id=1, source_target_pairs={{0,12},{4,8},{8,4},{12,0},{16,28},{20,24},{24,20},{28,16},{1,13},{... | collective-permute-start | bytes 3464 | tf_op jit(solution)/shard_map/ppermute | solution.py:681
  415.6 11.1 %collective-permute-start.44 = (f32[1,288]{1,0:T(1,128)S(1)}, f32[1,288]{1,0:T(1,128)S(1)}, u32[]{:S(2)}, u32[]{:S(2)}) collective-permute-start(f32[1,288]{1,0:T(1,128)S(1)} %get-tuple-element.226), channel_id=1, source_target_pairs={{0,16},{4,20},{8,24},{12,28},{16,0},{20,4},{24,8},{28,12},{1,17},{... | collective-permute-start | bytes 3464 | tf_op jit(solution)/shard_map/ppermute | solution.py:681
  417.1 10.1 %collective-permute-start.45 = (f32[1,288]{1,0:T(1,128)S(1)}, f32[1,288]{1,0:T(1,128)S(1)}, u32[]{:S(2)}, u32[]{:S(2)}) collective-permute-start(f32[1,288]{1,0:T(1,128)S(1)} %get-tuple-element.225), channel_id=1, source_target_pairs={{0,20},{4,16},{8,28},{12,24},{16,4},{20,0},{24,12},{28,8},{1,21},{... | collective-permute-start | bytes 3464 | tf_op jit(solution)/shard_map/ppermute | solution.py:681
  426.7 22.0 %collective-permute-start.39 = (bf16[256,1024]{1,0:T(8,128)(2,1)}, bf16[256,1024]{1,0:T(8,128)(2,1)S(1)}, u32[]{:S(2)}, u32[]{:S(2)}) collective-permute-start(bf16[256,1024]{1,0:T(8,128)(2,1)} %get-tuple-element.219), channel_id=1, source_target_pairs={{0,8},{8,0},{16,24},{24,16},{1,9},{9,1},{17,25},{25,17},{2,10},{10... | collective-permute-start | bytes 1572872 | tf_op jit(solution)/shard_map/ppermute | solution.py:656
  426.7 25.3 %collective-permute-start.24 = (bf16[256,1024]{1,0:T(8,128)(2,1)}, bf16[256,1024]{1,0:T(8,128)(2,1)}, u32[]{:S(2)}, u32[]{:S(2)}) collective-permute-start(bf16[256,1024]{1,0:T(8,128)(2,1)} %get-tuple-element.222), channel_id=1, source_target_pairs={{0,8},{8,0},{16,24},{24,16},{1,9},{9,1},{17,25},{25,17},{2,10},{10... | collective-permute-start | bytes 1572872 | tf_op jit(solution)/shard_map/ppermute | solution.py:656
  430.4 5.4 %collective-permute-start.50 = (f32[1,288]{1,0:T(1,128)S(1)}, f32[1,288]{1,0:T(1,128)S(1)}, u32[]{:S(2)}, u32[]{:S(2)}) collective-permute-start(f32[1,288]{1,0:T(1,128)S(1)} %add_add_fusion), channel_id=1, source_target_pairs={{0,3},{1,2},{2,1},{3,0},{4,7},{5,6},{6,5},{7,4},{8,11},{9,10},{10,... | collective-permute-start | bytes 3464 | tf_op jit(solution)/shard_map/ppermute | solution.py:897
  (70 other events, 739.9 us)
Sparse Core Ops, SparseCore 0:
  10.5 67.0 all-gather.4
  80.0 94.0 all-gather.2
  343.8 69.4 all-reduce.7
  417.0 95.7 all-reduce.5

commit v5 on v4

--- a/solution.py
+++ b/solution.py
@@ -293,7 +293,8 @@
 def feed_kernel(chips, place_ref, *refs):
     gates, ups, shrinks = refs[:chips], refs[chips : 2 * chips], refs[2 * chips : 3 * chips]
     own_ref, other_ref, c_ref, c_other_ref = refs[3 * chips : 3 * chips + 4]
-    x_out, c_out, active_ref, grad_ref, share_ref, share_other, back_ref, back_other = refs[3 * chips + 4 :]
+    refs = refs[3 * chips + 4 :]
+    x_out, c_out, active_ref, grad_ref, share_ref, share_other, back_ref, back_other, expand, shrink = refs
     step = pl.program_id(0)
     mine = step < 2
     x = jnp.where(mine, own_ref[...], other_ref[...])
@@ -301,25 +302,29 @@
     x_out[...] = x
     c_out[...] = c
     size = gates[0].shape[1]
-    share, back = 0.0, 0.0
-    for s in range(chips):
-        here = slice(s * size, (s + 1) * size)
-        there = slice((chips + s) * size, (chips + s + 1) * size)
-        gate = dot_nn(x, gates[s][...])
-        up = dot_nn(x, ups[s][...])
-        grad_active = dot_nt(c, shrinks[s][...]).astype(LOW).astype(FULL)
-        gated = jax.nn.sigmoid(gate)
-        silu = gate * gated
-        active = (silu * up).astype(LOW)
-        grad_gate = (grad_active * up * gated * (1.0 + gate * (1.0 - gated))).astype(LOW)
-        grad_up = (grad_active * silu).astype(LOW)
-        active_ref[:, here] = active
-        grad_ref[:, here] = grad_gate
-        grad_ref[:, there] = grad_up
-        share = share + dot_nn(active, shrinks[s][...])
-        back = back + dot_nt(grad_gate, gates[s][...]) + dot_nt(grad_up, ups[s][...])
-    share = share.astype(LOW)
-    back = back.astype(LOW)
+    half = chips * size
+
+    @pl.when(step == 0)
+    def _():
+        for s in range(chips):
+            here = slice(s * size, (s + 1) * size)
+            expand[:, here] = gates[s][...]
+            expand[:, half + s * size : half + (s + 1) * size] = ups[s][...]
+            shrink[here, :] = shrinks[s][...]
+
+    gate_up = dot_nn(x, expand[...])
+    grad_active = dot_nt(c, shrink[...]).astype(LOW).astype(FULL)
+    gate, up = gate_up[:, :half], gate_up[:, half:]
+    gated = jax.nn.sigmoid(gate)
+    silu = gate * gated
+    active = (silu * up).astype(LOW)
+    active_ref[...] = active
+    grad_gate = (grad_active * up * gated * (1.0 + gate * (1.0 - gated))).astype(LOW)
+    grad_up = (grad_active * silu).astype(LOW)
+    grad = jnp.concatenate([grad_gate, grad_up], axis=1)
+    grad_ref[...] = grad
+    share = dot_nn(active, shrink[...]).astype(LOW)
+    back = dot_nt(grad, expand[...]).astype(LOW)
 
     @pl.when(mine)
     def _():
@@ -381,6 +386,7 @@
                 pl.BlockSpec((block, D), near),
                 pl.BlockSpec((block, D), far),
             ),
+            scratch_shapes=[pltpu.VMEM((D, FF), LOW), pltpu.VMEM((FF // 2, D), LOW)],
         ),
         compiler_params=pltpu.CompilerParams(vmem_limit_bytes=56 * MIB),
         cost_estimate=pl.CostEstimate(
@@ -793,7 +799,10 @@
             place, n, expand_full, shrink_full, normed_two, swap_core(normed_two), cotangent,
             other_cotangent,
         )
-        normed_grad = sum_of([back_share, swap_core(back_other)])
+        grad_shrink = dot_tn(active, c_all).astype(LOW)
+        shrink_cuts = grad_shrink.reshape(chips, inner, FF // (n * inner), D)
+        shrink_sent = [swap_grp(pick(shrink_cuts, 1, mine ^ t), t) for t in range(1, inner)]
+        normed_grad = sum_of([after(back_share, grad_shrink), swap_core(back_other)])
         hidden_grad, gain_part = norm_back(hidden, gain_two, normed_grad)
         gain_two_grad = jnp.sum(gain_part, axis=0)
         hidden_grad = hidden_grad + c_all[: 2 * block].astype(FULL)
@@ -835,18 +844,16 @@
             cuts = grad_qkv.reshape(chips, 2, inner, rows, width)
             return pick(cuts, 1, core), [swap_core(pick(cuts, 1, core ^ 1))]
 
-        x_late, active_late = lax.optimization_barrier((x_all, active, hidden_low))[:2]
-        grad_expand = dot_tn(x_late, grad_gate_up).astype(LOW)
+        grad_expand = dot_tn(after(x_all, hidden_low), grad_gate_up).astype(LOW)
         expand_cuts = grad_expand.reshape(chips, 2, inner, rows, FF)
         other_rows = pick(expand_cuts, 1, core ^ 1)
         other_sent = [swap_grp(pick(other_rows, 1, mine ^ t), t) for t in range(1, inner)]
-        grad_shrink = dot_tn(active_late, c_all).astype(LOW)
-        shrink_cuts = grad_shrink.reshape(chips, inner, FF // (n * inner), D)
-        shrink_sent = [swap_grp(pick(shrink_cuts, 1, mine ^ t), t) for t in range(1, inner)]
         own_rows = pick(expand_cuts, 1, core)
         late_rows = after(own_rows, grad_slots[-1])
         own_sent = [swap_chip(pick(late_rows, 0, chip ^ s), s) for s in range(1, chips)]
-        grad_slots = lax.optimization_barrier((*grad_slots, grad_shrink))[:-1]
+        line[:] = [grad_expand]
+        shrink_cut = send_x(next_cut(pick(shrink_cuts, 1, mine), shrink_sent, 0, chip, chips))
+        grad_slots = lax.optimization_barrier((*grad_slots, *line))[:chips]
         grad_all = jnp.concatenate(grad_slots)
         grad, back_all, head_gains = back(
             place, qkv_parts, out_parts, grad_all, attended, totals, q, k, v, raw, cos, sin, seg_col,
@@ -854,31 +861,34 @@
         )
 
         line[:] = [head_gains]
+        shrink_cut = next_sum(*shrink_cut)
+        total_shrink = lax.psum(shrink_cut, "rep")
         own_cut = send_y(next_cut(pick(own_rows, 0, chip), own_sent, 0, mine, inner))
         other_cut = send_x(next_cut(pick(other_rows, 1, mine), other_sent, 0, chip, chips))
-        qkv_cuts, qkv_sent = cut_qkv(after(grad, *line))
-        shrink_cut = send_x(next_cut(pick(shrink_cuts, 1, mine), shrink_sent, 0, chip, chips))
         grad_out = dot_tn(after(attended, *line), grad_all).astype(LOW)
         out_cuts = grad_out.reshape(2, inner, out_weight.shape[0], D)
         out_sent = [swap_core(pick(out_cuts, 0, core ^ 1))]
+        line[:] = [grad_out]
+        qkv_cuts, qkv_sent = cut_qkv(after(grad, *line))
+        out_cut = send_y(next_cut(pick(out_cuts, 0, core), out_sent, 0, mine, inner))
         qkv_cut = send_y(next_cut(qkv_cuts, qkv_sent, 1, mine, inner))
+        own_cut = next_sum(*own_cut)
         other_cut = swap_core(next_sum(*other_cut))
-        out_cut = send_y(next_cut(pick(out_cuts, 0, core), out_sent, 0, mine, inner))
-        own_cut = next_sum(*own_cut)
-        own_cut, other_cut = lax.optimization_barrier((own_cut, other_cut, *line))[:2]
-        line[:] = [other_cut]
-        own_cut, other_cut = lax.psum((own_cut, other_cut), "rep")
-        shrink_cut = next_sum(*shrink_cut)
+        out_cut = next_sum(*out_cut)
+        own_cut, other_cut, out_cut, total_shrink = lax.optimization_barrier(
+            (own_cut, other_cut, out_cut, total_shrink, *line)
+        )[:4]
+        line[:] = [out_cut]
+        own_cut, other_cut, total_out = lax.psum((own_cut, other_cut, out_cut), "rep")
         kept, sent = send_x(next_cut(*qkv_cut, 0, chip, chips))
         shares = []
         for s in range(1, chips):
             share = after(back_all[2 * s * block : 2 * (s + 1) * block], kept)
             shares.append(swap_chip(share, s))
-        out_cut = next_sum(*out_cut)
-        *qkv_cuts, shrink_cut, out_cut, own_cut, other_cut = lax.optimization_barrier(
-            (kept, *sent, shrink_cut, out_cut, own_cut, other_cut, *line)
-        )[: 4 + chips]
-        total_shrink, total_out, *qkv_cuts = lax.psum((shrink_cut, out_cut, *qkv_cuts), "rep")
+        *qkv_cuts, own_cut, other_cut, total_out = lax.optimization_barrier(
+            (kept, *sent, own_cut, other_cut, total_out, *line)
+        )[: 3 + chips]
+        qkv_cuts = lax.psum(tuple(qkv_cuts), "rep")
 
         shares = [back_all[: 2 * block]] + [after(value, *line) for value in shares]
         input_part, gain_part = norm_back(inputs, gain_one, sum_of(shares))

time: 543 us -> 546 us (level)
    psum x2 -> x3, waiting for transfers between devices: 74.5 us -> 90.2 us  [the longest x1 42.7 us: on_device(): lax.psum((own_cut, other_cut, out_cut), 'rep')]
    ppermute x8, waiting for transfers between devices: 57.1 us -> 48 us  [swap_grp(): return lax.ppermute(value, 'grp', [(i, i ^ t) for i in range(inner)])]
    unnamed x138 -> x144, local copies, waits for them, and re-layouts: 24.1 us -> 21.1 us
  transfers between devices with their start and end apart: 55 -> 56, of which waited for: 21 -> 19; matrix products, arithmetic and copies ran while one was open for 15% -> 16% of each run, Pallas kernels for 15% -> 15%
where the time goes in v5:
time: 546 us; the launch traced here: 539 us
  waiting for transfers between devices  243 us (45%)
  Pallas kernels  122 us (22%)
  other arithmetic  61.7 us (11%)
  starting transfers between devices  39.2 us (7%)
  local copies, waits for them, and re-layouts  37.6 us (7%)
  matrix products  20.7 us (4%)
  between operations  15 us (3%)
    ppermute x26, waiting for transfers between devices, swap_ctx(): return lax.ppermute(value, 'ctx', [(i, i ^ s) for i in range(n)])  99.3 us
    ppermute x8, waiting for transfers between devices, swap_grp(): return lax.ppermute(value, 'grp', [(i, i ^ t) for i in range(inner)])  48 us
    pallas_call x1, Pallas kernels, back(): pl.pallas_call(functools.partial(back_kernel, n, inner), out_shape=(jax.S...  43 us
    psum x1, waiting for transfers between devices, on_device(): lax.psum((own_cut, other_cut, out_cut), 'rep')  42.7 us
    psum x1, waiting for transfers between devices, on_device(): qkv_cuts = lax.psum(tuple(qkv_cuts), 'rep')  34.4 us
    pallas_call x1, Pallas kernels, feed(): pl.pallas_call(functools.partial(feed_kernel, chips), out_shape=(wide(D),...  31.6 us
    pallas_call x2, Pallas kernels, attend(): pl.pallas_call(functools.partial(attend_kernel, n, inner, first, bool(bas...  23.1 us
    unnamed x144, local copies, waits for them, and re-layouts  21.1 us
  transfers between devices with their start and end apart: 56, of which 19 were waited for; matrix products, arithmetic and copies ran while one was open for 16% of the time, Pallas kernels for 15%

profile of v5, /device:TPU:0, one launch (start us, length us, event | category | flops | bytes accessed | tf_op | source)
XLA Modules:
  0.0 538.8 jit_solution(9745999271970836463)
XLA Ops:
  7.3 2.5 convert_element_type.322
  9.9 3.4 convert_element_type.321
  13.4 3.0 collective-permute-start
  27.7 2.0 collective-permute-start.8
  32.1 15.8 %collective-permute-done.14.refs_4_ = bf16[128,2048]{1,0:T(8,128)(2,1)} collective-permute-done((bf16[128,2048]{1,0:T(8,128)(2,1)}, bf16[128,2048]{1,0:T(8,128)(2,1)}, u32[]{:S(2)}, u32[]{:S(2)}) %collective-permute-start.14) | collective-permute-done | bytes 524320 | tf_op jit(solution)/shard_map/ppermute | solution.py:662
  48.7 2.0 copy.40
  50.7 2.5 gather_fusion.1
  53.7 14.8 %collective-permute-done.11.refs_1_ = bf16[128,2048]{1,0:T(8,128)(2,1)} collective-permute-done((bf16[128,2048]{1,0:T(8,128)(2,1)}, bf16[128,2048]{1,0:T(8,128)(2,1)}, u32[]{:S(2)}, u32[]{:S(2)}) %collective-permute-start.11) | collective-permute-done | bytes 524320 | tf_op jit(solution)/shard_map/ppermute | solution.py:671
  71.2 11.9 %collective-permute-done.15.refs_5_ = bf16[128,2048]{1,0:T(8,128)(2,1)S(1)} collective-permute-done((bf16[128,2048]{1,0:T(8,128)(2,1)}, bf16[128,2048]{1,0:T(8,128)(2,1)S(1)}, u32[]{:S(2)}, u32[]{:S(2)}) %collective-permute-start.15) | collective-permute-done | bytes 524320 | tf_op jit(solution)/shard_map/ppermute | solution.py:671
  89.7 10.5 %project.1 = (bf16[1024,1024]{1,0:T(8,128)(2,1)S(1)}, bf16[1024,1024]{1,0:T(8,128)(2,1)S(1)}, bf16[1024,512]{1,0:T(8,128)(2,1)S(1)}, bf16[1024,512]{1,0:T(8,128)(2,1)S(1)}, bf16[1024,1536]{1,0:T(8,128)(2,1)}) custom-call(s32[2]{0:T(128)S(1)} %pad_add_fusion.place_ref, bf16[128,2048]{1,0:T(8,128)(2,1)} %get-tuple-element.97.refs_0_, ...), custom_call_target="tpu_custom_call" | custom-call | flops 4294967296 | bytes 16777216 | tf_op jit(solution)/shard_map/project/pallas_call | solution.py:150
  104.0 11.3 %attend.2 = (bf16[1024,1024]{1,0:T(8,128)(2,1)}, f32[1024,256]{1,0:T(8,128)S(1)}, bf16[512,1024]{1,0:T(8,128)(2,1)S(1)}) custom-call(s32[2]{0:T(128)S(1)} %pad_add_fusion.place_ref, bf16[256,1024]{1,0:T(8,128)(2,1)S(1)} %convert_element_type.317.refs_0_.refs_8_, bf16[256,1024]{1,0:T(8,128)(2,1)S(1)} %copy-done.23, ...), custom_call_target="tpu_custom_call" | custom-call | flops 3221225472 | bytes 8388608 | tf_op jit(solution)/shard_map/attend/pallas_call | solution.py:258
  115.8 11.8 %attend.3 = (bf16[1024,1024]{1,0:T(8,128)(2,1)}, f32[1024,256]{1,0:T(8,128)S(1)}, bf16[512,1024]{1,0:T(8,128)(2,1)S(1)}) custom-call(s32[2]{0:T(128)S(1)} %pad_add_fusion.place_ref, bf16[256,1024]{1,0:T(8,128)(2,1)S(1)} %convert_element_type.317.refs_0_.refs_8_, bf16[256,1024]{1,0:T(8,128)(2,1)S(1)} %copy-done.23, ...), custom_call_target="tpu_custom_call", output_to_operand_aliasing={{0}: (10, {}), {1}: (11, {})} | custom-call | flops 3221225472 | bytes 8388608 | tf_op jit(solution)/shard_map/attend/pallas_call | solution.py:258
  127.6 35.9 %collective-permute-done.20 = bf16[512,1024]{1,0:T(8,128)(2,1)S(1)} collective-permute-done((bf16[512,1024]{1,0:T(8,128)(2,1)S(1)}, bf16[512,1024]{1,0:T(8,128)(2,1)S(1)}, u32[]{:S(2)}, u32[]{:S(2)}) %collective-permute-start.20) | collective-permute-done | bytes 1048608 | tf_op jit(solution)/shard_map/ppermute | solution.py:662
  169.9 4.3 all-gather.3.cloned.1.call-done.refs_0_.refs_1_.refs_2_.refs_3_
  174.2 31.6 %feed.1 = (bf16[1024,1024]{1,0:T(8,128)(2,1)}, bf16[1024,1024]{1,0:T(8,128)(2,1)}, bf16[1024,1536]{1,0:T(8,128)(2,1)}, bf16[1024,3072]{1,0:T(8,128)(2,1)}, bf16[...) custom-call(s32[2]{0:T(128)} %copy-done.18, ...), custom_call_target="tpu_custom_call" | custom-call | flops 19327352832 | bytes 31457280 | tf_op jit(solution)/shard_map/feed/pallas_call | solution.py:364
  206.1 6.0 %convolution_convert_fusion.1 = bf16[1536,1024]{1,0:T(8,128)(2,1)S(1)} fusion(bf16[1024,1536]{1,0:T(8,128)(2,1)} %get-tuple-element.117, bf16[1024,1024]{1,0:T(8,128)(2,1)} %get-tuple-element.118), kind=kOutput, calls=%fused_computation.3 | convolution fusion | flops 3222798336 | bytes 8388608 | tf_op jit(solution)/shard_map/dot_general | solution.py:51
  213.8 2.5 multiply_reduce_fusion
  216.3 2.5 fusion.61
  219.7 7.3 %convolution_convert_fusion = bf16[1024,3072]{1,0:T(8,128)(2,1)S(1)} fusion(bf16[1024,1024]{1,0:T(8,128)(2,1)S(1)} %copy-done.65, bf16[1024,3072]{1,0:T(8,128)(2,1)S(1)} %copy-done.64), kind=kOutput, calls=%fused_computation.2 | convolution fusion | flops 6445596672 | bytes 14680064 | tf_op jit(solution)/shard_map/dot_general | solution.py:51
  227.3 16.7 %collective-permute-done.26 = bf16[512,1024]{1,0:T(8,128)(2,1)S(1)} collective-permute-done((bf16[512,1024]{1,0:T(8,128)(2,1)S(1)}, bf16[512,1024]{1,0:T(8,128)(2,1)S(1)}, u32[]{:S(2)}, u32[]{:S(2)}) %collective-permute-start.26) | collective-permute-done | bytes 1048608 | tf_op jit(solution)/shard_map/ppermute | solution.py:662
  252.0 43.0 %back.1 = (bf16[1024,2048]{1,0:T(8,128)(2,1)}, bf16[1024,1024]{1,0:T(8,128)(2,1)}, f32[8,128]{1,0:T(8,128)}) custom-call(s32[2]{0:T(128)} %copy-done.18, bf16[128,2048]{1,0:T(8,128)(2,1)} %get-tuple-element.97.refs_0_, bf16[128,2048]{1,0:T(8,128)(2,1)} %collective-permute-done.11.refs_1_, bf16[128,2048]{1,0:T(8,128)(2,1)} %copy-done.26, ...), custom_call_target="tpu_custom_call" | custom-call | flops 5905580032 | bytes 31457280 | tf_op jit(solution)/shard_map/back/pallas_call | solution.py:536
  295.0 2.7 collective-permute-done.30
  298.9 3.6 fusion.18
  302.5 3.7 fusion.16
  306.3 2.4 convolution_convert_fusion.3
  309.1 4.9 convolution_convert_fusion.2
  320.6 2.2 collective-permute-done.32
  326.4 4.5 fusion.11
  331.4 7.6 %collective-permute-done.34 = bf16[128,3072]{1,0:T(8,128)(2,1)} collective-permute-done((bf16[128,3072]{1,0:T(8,128)(2,1)}, bf16[128,3072]{1,0:T(8,128)(2,1)}, u32[]{:S(2)}, u32[]{:S(2)}) %collective-permute-start.34) | collective-permute-done | bytes 786464 | tf_op jit(solution)/shard_map/ppermute | solution.py:671
  339.1 2.4 add_convert_fusion.2
  341.4 2.2 add_convert_fusion.1
  344.7 5.5 %collective-permute-done.37 = bf16[256,1024]{1,0:T(8,128)(2,1)S(1)} collective-permute-done((bf16[256,1024]{1,0:T(8,128)(2,1)S(1)}, bf16[256,1024]{1,0:T(8,128)(2,1)S(1)}, u32[]{:S(2)}, u32[]{:S(2)}) %collective-permute-start.37) | collective-permute-done | bytes 524320 | tf_op jit(solution)/shard_map/ppermute | solution.py:671
  351.2 13.1 %all-reduce.7.cloned.1.call-done = bf16[384,1024]{1,0:T(8,128)(2,1)} async-done(((bf16[384,1024]{1,0:T(8,128)(2,1)}), bf16[384,1024]{1,0:T(8,128)(2,1)}) %all-reduce.7.cloned.1.call-update) | async-done | bytes 786448 | tf_op jit(solution)/shard_map/psum | solution.py:865
  364.3 7.5 %collective-permute-done.33 = bf16[2,128,2048]{2,1,0:T(8,128)(2,1)} collective-permute-done((bf16[2,128,2048]{2,1,0:T(8,128)(2,1)}, bf16[2,128,2048]{2,1,0:T(8,128)(2,1)}, u32[]{:S(2)}, u32[]{:S(2)}) %collective-permute-start.33) | collective-permute-done | bytes 1048608 | tf_op jit(solution)/shard_map/ppermute | solution.py:671
  371.8 2.9 fusion.28
  377.5 23.5 %collective-permute-done.38 = bf16[512,1024]{1,0:T(8,128)(2,1)} collective-permute-done((bf16[512,1024]{1,0:T(8,128)(2,1)}, bf16[512,1024]{1,0:T(8,128)(2,1)}, u32[]{:S(2)}, u32[]{:S(2)}) %collective-permute-start.38) | collective-permute-done | bytes 1048608 | tf_op jit(solution)/shard_map/ppermute | solution.py:662
  401.1 2.4 fusion.8
  406.4 4.5 fusion.7
  411.7 2.5 collective-permute-start.45
  419.7 2.4 collective-permute-start.49
  422.7 42.7 %all-reduce.11.cloned.1.call-done = (bf16[128,3072]{1,0:T(8,128)(2,1)}, bf16[128,3072]{1,0:T(8,128)(2,1)}, bf16[256,1024]{1,0:T(8,128)(2,1)}) async-done(((bf16[128,3072]{1,0:T(8,128)(2,1)}, bf16[128,3072]{1,0:T(8,128)(2,1)}, bf16[256,1024]{1,0:T(8,128)(2,1)}), (bf16[128,3072]{1,0:T(8,128)(2,1)}, bf16[128,3072]{1,0:T(8,128)(2,1)}, bf16[256,1024]{1,0:T(8,128)(2,1)})) %all-reduce.11.cloned.1.call-update) | async-done | bytes 2097168 | tf_op jit(solution)/shard_map/psum | solution.py:882
  465.5 5.1 multiply_subtract_fusion
  471.3 2.5 maximum_select_fusion.1
  473.8 2.4 maximum_select_fusion
  476.3 6.5 %adam_pair.1 = (f32[128,6144]{1,0:T(8,128)}, f32[128,6144]{1,0:T(8,128)}, f32[128,6144]{1,0:T(8,128)}) custom-call(s32[2]{0:T(128)S(1)} %copy-done.19, bf16[128,3072]{1,0:T(8,128)(2,1)S(1)} %copy-done.9, bf16[128,3072]{1,0:T(8,128)(2,1)S(1)} %copy-done.10, f32[128,6144]{1,0:T(8,128)S(1)} %copy-done.2, f32[128,6144]{1,0:T(8,128)S(1)} %copy-done.5, ...), custom_call_target="tpu_custom_call" | custom-call | flops 15728640 | bytes 20447232 | tf_op jit(solution)/shard_map/adam_pair/pallas_call | solution.py:637
  482.8 2.3 multiply_subtract_fusion.1
  485.1 34.4 %all-reduce.9.cloned.1.call-done = (bf16[128,2048]{1,0:T(8,128)(2,1)}, bf16[128,2048]{1,0:T(8,128)(2,1)}) async-done(((bf16[128,2048]{1,0:T(8,128)(2,1)}, bf16[128,2048]{1,0:T(8,128)(2,1)}), (bf16[128,2048]{1,0:T(8,128)(2,1)}, bf16[128,2048]{1,0:T(8,128)(2,1)})) %all-reduce.9.cloned.1.call-update) | async-done | bytes 1048592 | tf_op jit(solution)/shard_map/psum | solution.py:891
  524.9 7.2 %adam_cuts.1 = (f32[128,4096]{1,0:T(8,128)}, f32[128,4096]{1,0:T(8,128)}, f32[128,4096]{1,0:T(8,128)}) custom-call(s32[1]{0:T(128)} %bitcast.56.key_ref, bf16[128,2048]{1,0:T(8,128)(2,1)S(1)} %copy-done.15, bf16[128,2048]{1,0:T(8,128)(2,1)S(1)} %copy-done.16, f32[128,4096]{1,0:T(8,128)S(1)} %copy-done.4, f32[128,4096]{1,0:T(8,128)S(1)} %copy-done.7, ...), custom_call_target="tpu_custom_call" | custom-call | flops 10485760 | bytes 13631488 | tf_op jit(solution)/shard_map/adam_cuts/pallas_call | solution.py:607
  (295 shorter events, 78.9 us)
Async XLA Ops:
  7.2 162.7 %all-gather.5.cloned.1.call-start = ((), (), s32[]{:S(2)}) async-start(), calls=%async_computation.1 | async-start | bytes 7077888 | tf_op jit(solution)/shard_map/all_gather | solution.py:773
  9.8 164.4 %all-gather.3.cloned.1.call-start = ((), (), s32[]{:S(2)}) async-start(), calls=%async_computation | async-start | bytes 14155776 | tf_op jit(solution)/shard_map/all_gather | solution.py:773
  13.3 351.1 %all-reduce.7.cloned.1.call-start = ((), (), s32[]{:S(2)}) async-start(), calls=%async_computation.2 | async-start | bytes 1572864 | tf_op jit(solution)/shard_map/psum | solution.py:865
  13.4 11.0 %collective-permute-start = (f32[1,1312]{1,0:T(1,128)S(1)}, f32[1,1312]{1,0:T(1,128)S(1)}, u32[]{:S(2)}, u32[]{:S(2)}) collective-permute-start(f32[1,1312]{1,0:T(1,128)S(1)} %reshape.234), channel_id=1, source_target_pairs={{0,4},{4,0},{8,12},{12,8},{16,20},{20,16},{24,28},{28,24},{1,5},{5... | collective-permute-start | bytes 15752 | tf_op jit(solution)/shard_map/ppermute | solution.py:687
  16.4 8.5 %collective-permute-start.1 = (f32[1,1312]{1,0:T(1,128)S(1)}, f32[1,1312]{1,0:T(1,128)S(1)}, u32[]{:S(2)}, u32[]{:S(2)}) collective-permute-start(f32[1,1312]{1,0:T(1,128)S(1)} %reshape.234), channel_id=1, source_target_pairs={{0,8},{4,12},{8,0},{12,4},{16,24},{20,28},{24,16},{28,20},{1,9},{5... | collective-permute-start | bytes 15752 | tf_op jit(solution)/shard_map/ppermute | solution.py:687
  16.4 11.2 %collective-permute-start.2 = (f32[1,1312]{1,0:T(1,128)S(1)}, f32[1,1312]{1,0:T(1,128)S(1)}, u32[]{:S(2)}, u32[]{:S(2)}) collective-permute-start(f32[1,1312]{1,0:T(1,128)S(1)} %reshape.234), channel_id=1, source_target_pairs={{0,12},{4,8},{8,4},{12,0},{16,28},{20,24},{24,20},{28,16},{1,13},{... | collective-permute-start | bytes 15752 | tf_op jit(solution)/shard_map/ppermute | solution.py:687
  16.7 13.0 %collective-permute-start.3 = (f32[1,1312]{1,0:T(1,128)S(1)}, f32[1,1312]{1,0:T(1,128)S(1)}, u32[]{:S(2)}, u32[]{:S(2)}) collective-permute-start(f32[1,1312]{1,0:T(1,128)S(1)} %reshape.234), channel_id=1, source_target_pairs={{0,16},{4,20},{8,24},{12,28},{16,0},{20,4},{24,8},{28,12},{1,17},{... | collective-permute-start | bytes 15752 | tf_op jit(solution)/shard_map/ppermute | solution.py:687
  18.6 11.1 %collective-permute-start.4 = (f32[1,1312]{1,0:T(1,128)S(1)}, f32[1,1312]{1,0:T(1,128)S(1)}, u32[]{:S(2)}, u32[]{:S(2)}) collective-permute-start(f32[1,1312]{1,0:T(1,128)S(1)} %reshape.234), channel_id=1, source_target_pairs={{0,20},{4,16},{8,28},{12,24},{16,4},{20,0},{24,12},{28,8},{1,21},{... | collective-permute-start | bytes 15752 | tf_op jit(solution)/shard_map/ppermute | solution.py:687
  27.7 25.9 %collective-permute-start.8 = (bf16[256,1024]{1,0:T(8,128)(2,1)S(1)}, bf16[256,1024]{1,0:T(8,128)(2,1)S(1)}, u32[]{:S(2)}, u32[]{:S(2)}) collective-permute-start(bf16[256,1024]{1,0:T(8,128)(2,1)S(1)} %convert_element_type.317.refs_0_.refs_8_), channel_id=1, source_target_pairs={{0,4},{4,0},{1,5},{5,1},{2,6},{6,2},{3,7},{7,3},{8,12},{12,8},{9,1... | collective-permute-start | bytes 1572872 | tf_op jit(solution)/shard_map/ppermute | solution.py:671
  29.7 18.2 %collective-permute-start.14 = (bf16[128,2048]{1,0:T(8,128)(2,1)}, bf16[128,2048]{1,0:T(8,128)(2,1)}, u32[]{:S(2)}, u32[]{:S(2)}) collective-permute-start(bf16[128,2048]{1,0:T(8,128)(2,1)} %get-tuple-element.98), channel_id=1, source_target_pairs={{0,16},{8,24},{16,0},{24,8},{1,17},{9,25},{17,1},{25,9},{2,18},{10... | collective-permute-start | bytes 1572872 | tf_op jit(solution)/shard_map/ppermute | solution.py:662
  31.3 37.1 %collective-permute-start.11 = (bf16[128,2048]{1,0:T(8,128)(2,1)}, bf16[128,2048]{1,0:T(8,128)(2,1)}, u32[]{:S(2)}, u32[]{:S(2)}) collective-permute-start(bf16[128,2048]{1,0:T(8,128)(2,1)} %get-tuple-element.97.refs_0_), channel_id=1, source_target_pairs={{0,4},{4,0},{1,5},{5,1},{2,6},{6,2},{3,7},{7,3},{8,12},{12,8},{9,1... | collective-permute-start | bytes 1572872 | tf_op jit(solution)/shard_map/ppermute | solution.py:671
  31.9 37.5 %collective-permute-start.18 = (bf16[256,1024]{1,0:T(8,128)(2,1)S(1)}, bf16[256,1024]{1,0:T(8,128)(2,1)}, u32[]{:S(2)}, u32[]{:S(2)}) collective-permute-start(bf16[256,1024]{1,0:T(8,128)(2,1)S(1)} %dynamic-slice_bitcast_fusion.5.refs_8_), channel_id=1, source_target_pairs={{0,16},{8,24},{16,0},{24,8},{1,17},{9,25},{17,1},{25,9},{2,18},{10... | collective-permute-start | bytes 1572872 | tf_op jit(solution)/shard_map/ppermute | solution.py:662
  32.1 37.3 %collective-permute-start.7 = (bf16[256,1024]{1,0:T(8,128)(2,1)}, bf16[256,1024]{1,0:T(8,128)(2,1)S(1)}, u32[]{:S(2)}, u32[]{:S(2)}) collective-permute-start(bf16[256,1024]{1,0:T(8,128)(2,1)} %dynamic-slice_bitcast_fusion.6), channel_id=1, source_target_pairs={{0,8},{8,0},{16,24},{24,16},{1,9},{9,1},{17,25},{25,17},{2,10},{10... | collective-permute-start | bytes 1572872 | tf_op jit(solution)/shard_map/ppermute | solution.py:662
  47.9 35.2 %collective-permute-start.15 = (bf16[128,2048]{1,0:T(8,128)(2,1)}, bf16[128,2048]{1,0:T(8,128)(2,1)S(1)}, u32[]{:S(2)}, u32[]{:S(2)}) collective-permute-start(bf16[128,2048]{1,0:T(8,128)(2,1)} %collective-permute-done.14.refs_4_), channel_id=1, source_target_pairs={{0,4},{4,0},{1,5},{5,1},{2,6},{6,2},{3,7},{7,3},{8,12},{12,8},{9,1... | collective-permute-start | bytes 1572872 | tf_op jit(solution)/shard_map/ppermute | solution.py:671
  53.6 32.5 %collective-permute-start.12 = (bf16[128,2048]{1,0:T(8,128)(2,1)}, bf16[128,2048]{1,0:T(8,128)(2,1)S(1)}, u32[]{:S(2)}, u32[]{:S(2)}) collective-permute-start(bf16[128,2048]{1,0:T(8,128)(2,1)} %get-tuple-element.97.refs_0_), channel_id=1, source_target_pairs={{0,8},{8,0},{16,24},{24,16},{1,9},{9,1},{17,25},{25,17},{2,10},{10... | collective-permute-start | bytes 1572872 | tf_op jit(solution)/shard_map/ppermute | solution.py:662
  68.4 19.0 %collective-permute-start.13 = (bf16[128,2048]{1,0:T(8,128)(2,1)}, bf16[128,2048]{1,0:T(8,128)(2,1)}, u32[]{:S(2)}, u32[]{:S(2)}) collective-permute-start(bf16[128,2048]{1,0:T(8,128)(2,1)} %collective-permute-done.11.refs_1_), channel_id=1, source_target_pairs={{0,8},{8,0},{16,24},{24,16},{1,9},{9,1},{17,25},{25,17},{2,10},{10... | collective-permute-start | bytes 1572872 | tf_op jit(solution)/shard_map/ppermute | solution.py:662
  69.3 18.1 %collective-permute-start.16 = (bf16[128,2048]{1,0:T(8,128)(2,1)}, bf16[128,2048]{1,0:T(8,128)(2,1)}, u32[]{:S(2)}, u32[]{:S(2)}) collective-permute-start(bf16[128,2048]{1,0:T(8,128)(2,1)} %collective-permute-done.14.refs_4_), channel_id=1, source_target_pairs={{0,8},{8,0},{16,24},{24,16},{1,9},{9,1},{17,25},{25,17},{2,10},{10... | collective-permute-start | bytes 1572872 | tf_op jit(solution)/shard_map/ppermute | solution.py:662
  69.3 18.1 %collective-permute-start.19 = (bf16[256,1024]{1,0:T(8,128)(2,1)S(1)}, bf16[256,1024]{1,0:T(8,128)(2,1)}, u32[]{:S(2)}, u32[]{:S(2)}) collective-permute-start(bf16[256,1024]{1,0:T(8,128)(2,1)S(1)} %collective-permute-done.7.refs_9_), channel_id=1, source_target_pairs={{0,16},{8,24},{16,0},{24,8},{1,17},{9,25},{17,1},{25,9},{2,18},{10... | collective-permute-start | bytes 1572872 | tf_op jit(solution)/shard_map/ppermute | solution.py:662
  86.9 17.0 %collective-permute-start.9 = (bf16[256,1024]{1,0:T(8,128)(2,1)S(1)}, bf16[256,1024]{1,0:T(8,128)(2,1)S(1)}, u32[]{:S(2)}, u32[]{:S(2)}) collective-permute-start(bf16[256,1024]{1,0:T(8,128)(2,1)S(1)} %convert_element_type.317.refs_0_.refs_8_), channel_id=1, source_target_pairs={{0,8},{8,0},{16,24},{24,16},{1,9},{9,1},{17,25},{25,17},{2,10},{10... | collective-permute-start | bytes 1572872 | tf_op jit(solution)/shard_map/ppermute | solution.py:662
  87.4 16.5 %collective-permute-start.10 = (bf16[256,1024]{1,0:T(8,128)(2,1)}, bf16[256,1024]{1,0:T(8,128)(2,1)S(1)}, u32[]{:S(2)}, u32[]{:S(2)}) collective-permute-start(bf16[256,1024]{1,0:T(8,128)(2,1)} %copy-done.22), channel_id=1, source_target_pairs={{0,8},{8,0},{16,24},{24,16},{1,9},{9,1},{17,25},{25,17},{2,10},{10... | collective-permute-start | bytes 1572872 | tf_op jit(solution)/shard_map/ppermute | solution.py:662
  115.3 48.3 %collective-permute-start.20 = (bf16[512,1024]{1,0:T(8,128)(2,1)S(1)}, bf16[512,1024]{1,0:T(8,128)(2,1)S(1)}, u32[]{:S(2)}, u32[]{:S(2)}) collective-permute-start(bf16[512,1024]{1,0:T(8,128)(2,1)S(1)} %get-tuple-element.110), channel_id=1, source_target_pairs={{0,16},{8,24},{16,0},{24,8},{1,17},{9,25},{17,1},{25,9},{2,18},{10... | collective-permute-start | bytes 3145736 | tf_op jit(solution)/shard_map/ppermute | solution.py:662
  115.3 52.0 %collective-permute-start.22 = (bf16[2,256,1024]{2,1,0:T(8,128)(2,1)S(1)}, bf16[2,256,1024]{2,1,0:T(8,128)(2,1)S(1)}, u32[]{:S(2)}, u32[]{:S(2)}) collective-permute-start(bf16[2,256,1024]{2,1,0:T(8,128)(2,1)S(1)} %copy-done.59), channel_id=1, source_target_pairs={{0,8},{8,0},{16,24},{24,16},{1,9},{9,1},{17,25},{25,17},{2,10},{10... | collective-permute-start | bytes 3145736 | tf_op jit(solution)/shard_map/ppermute | solution.py:662
  205.8 8.0 %collective-permute-start.25 = (bf16[512,1024]{1,0:T(8,128)(2,1)}, bf16[512,1024]{1,0:T(8,128)(2,1)S(1)}, u32[]{:S(2)}, u32[]{:S(2)}) collective-permute-start(bf16[512,1024]{1,0:T(8,128)(2,1)} %get-tuple-element.120), channel_id=1, source_target_pairs={{0,8},{8,0},{16,24},{24,16},{1,9},{9,1},{17,25},{25,17},{2,10},{10... | collective-permute-start | bytes 3145736 | tf_op jit(solution)/shard_map/ppermute | solution.py:662
  212.3 36.8 %collective-permute-start.27 = (bf16[2,384,1024]{2,1,0:T(8,128)(2,1)S(1)}, bf16[2,384,1024]{2,1,0:T(8,128)(2,1)S(1)}, u32[]{:S(2)}, u32[]{:S(2)}) collective-permute-start(bf16[2,384,1024]{2,1,0:T(8,128)(2,1)S(1)} %dynamic-slice_bitcast_fusion.3), channel_id=1, source_target_pairs={{0,4},{4,0},{1,5},{5,1},{2,6},{6,2},{3,7},{7,3},{8,12},{12,8},{9,1... | collective-permute-start | bytes 4718600 | tf_op jit(solution)/shard_map/ppermute | solution.py:671
  218.9 25.1 %collective-permute-start.26 = (bf16[512,1024]{1,0:T(8,128)(2,1)S(1)}, bf16[512,1024]{1,0:T(8,128)(2,1)S(1)}, u32[]{:S(2)}, u32[]{:S(2)}) collective-permute-start(bf16[512,1024]{1,0:T(8,128)(2,1)S(1)} %fusion.61), channel_id=1, source_target_pairs={{0,16},{8,24},{16,0},{24,8},{1,17},{9,25},{17,1},{25,9},{2,18},{10... | collective-permute-start | bytes 3145736 | tf_op jit(solution)/shard_map/ppermute | solution.py:662
  245.2 53.7 %collective-permute-start.29 = (bf16[2,128,3072]{2,1,0:T(8,128)(2,1)}, bf16[2,128,3072]{2,1,0:T(8,128)(2,1)}, u32[]{:S(2)}, u32[]{:S(2)}) collective-permute-start(bf16[2,128,3072]{2,1,0:T(8,128)(2,1)} %dynamic-slice_bitcast_fusion.1), channel_id=1, source_target_pairs={{0,16},{8,24},{16,0},{24,8},{1,17},{9,25},{17,1},{25,9},{2,18},{10... | collective-permute-start | bytes 4718600 | tf_op jit(solution)/shard_map/ppermute | solution.py:662
  247.0 55.5 %collective-permute-start.28 = (bf16[2,128,3072]{2,1,0:T(8,128)(2,1)}, bf16[2,128,3072]{2,1,0:T(8,128)(2,1)}, u32[]{:S(2)}, u32[]{:S(2)}) collective-permute-start(bf16[2,128,3072]{2,1,0:T(8,128)(2,1)} %dynamic-slice_bitcast_fusion.2), channel_id=1, source_target_pairs={{0,4},{4,0},{1,5},{5,1},{2,6},{6,2},{3,7},{7,3},{8,12},{12,8},{9,1... | collective-permute-start | bytes 4718600 | tf_op jit(solution)/shard_map/ppermute | solution.py:671
  249.8 47.9 %collective-permute-start.30 = (bf16[384,1024]{1,0:T(8,128)(2,1)S(1)}, bf16[384,1024]{1,0:T(8,128)(2,1)S(1)}, u32[]{:S(2)}, u32[]{:S(2)}) collective-permute-start(bf16[384,1024]{1,0:T(8,128)(2,1)S(1)} %get-tuple-element.199), channel_id=1, source_target_pairs={{0,16},{8,24},{16,0},{24,8},{1,17},{9,25},{17,1},{25,9},{2,18},{10... | collective-permute-start | bytes 2359304 | tf_op jit(solution)/shard_map/ppermute | solution.py:662
  316.8 9.6 %collective-permute-start.31 = (bf16[2,2,128,2048]{3,2,0,1:T(8,128)(2,1)}, bf16[2,2,128,2048]{3,2,0,1:T(8,128)(2,1)}, u32[]{:S(2)}, u32[]{:S(2)}) collective-permute-start(bf16[2,2,128,2048]{3,2,0,1:T(8,128)(2,1)} %copy_bitcast_fusion), channel_id=1, source_target_pairs={{0,8},{8,0},{16,24},{24,16},{1,9},{9,1},{17,25},{25,17},{2,10},{10... | collective-permute-start | bytes 6291464 | tf_op jit(solution)/shard_map/ppermute | solution.py:662
  318.3 20.7 %collective-permute-start.34 = (bf16[128,3072]{1,0:T(8,128)(2,1)}, bf16[128,3072]{1,0:T(8,128)(2,1)}, u32[]{:S(2)}, u32[]{:S(2)}) collective-permute-start(bf16[128,3072]{1,0:T(8,128)(2,1)} %get-tuple-element.195), channel_id=1, source_target_pairs={{0,4},{4,0},{1,5},{5,1},{2,6},{6,2},{3,7},{7,3},{8,12},{12,8},{9,1... | collective-permute-start | bytes 2359304 | tf_op jit(solution)/shard_map/ppermute | solution.py:671
  319.9 21.5 %collective-permute-start.35 = (bf16[128,3072]{1,0:T(8,128)(2,1)}, bf16[128,3072]{1,0:T(8,128)(2,1)}, u32[]{:S(2)}, u32[]{:S(2)}) collective-permute-start(bf16[128,3072]{1,0:T(8,128)(2,1)} %get-tuple-element.193), channel_id=1, source_target_pairs={{0,16},{8,24},{16,0},{24,8},{1,17},{9,25},{17,1},{25,9},{2,18},{10... | collective-permute-start | bytes 2359304 | tf_op jit(solution)/shard_map/ppermute | solution.py:662
  320.5 144.9 %all-reduce.11.cloned.1.call-start = ((), (), s32[]{:S(2)}) async-start(), calls=%async_computation.4 | async-start | bytes 4194304 | tf_op jit(solution)/shard_map/psum | solution.py:882
  324.7 25.5 %collective-permute-start.37 = (bf16[256,1024]{1,0:T(8,128)(2,1)S(1)}, bf16[256,1024]{1,0:T(8,128)(2,1)S(1)}, u32[]{:S(2)}, u32[]{:S(2)}) collective-permute-start(bf16[256,1024]{1,0:T(8,128)(2,1)S(1)} %get-tuple-element.201), channel_id=1, source_target_pairs={{0,4},{4,0},{1,5},{5,1},{2,6},{6,2},{3,7},{7,3},{8,12},{12,8},{9,1... | collective-permute-start | bytes 1572872 | tf_op jit(solution)/shard_map/ppermute | solution.py:671
  330.8 41.0 %collective-permute-start.33 = (bf16[2,128,2048]{2,1,0:T(8,128)(2,1)}, bf16[2,128,2048]{2,1,0:T(8,128)(2,1)}, u32[]{:S(2)}, u32[]{:S(2)}) collective-permute-start(bf16[2,128,2048]{2,1,0:T(8,128)(2,1)} %get-tuple-element.198), channel_id=1, source_target_pairs={{0,4},{4,0},{1,5},{5,1},{2,6},{6,2},{3,7},{7,3},{8,12},{12,8},{9,1... | collective-permute-start | bytes 3145736 | tf_op jit(solution)/shard_map/ppermute | solution.py:671
  343.6 20.7 %collective-permute-start.36 = (bf16[128,3072]{1,0:T(8,128)(2,1)}, bf16[128,3072]{1,0:T(8,128)(2,1)}, u32[]{:S(2)}, u32[]{:S(2)}) collective-permute-start(bf16[128,3072]{1,0:T(8,128)(2,1)} %add_convert_fusion.1), channel_id=1, source_target_pairs={{0,8},{8,0},{16,24},{24,16},{1,9},{9,1},{17,25},{25,17},{2,10},{10... | collective-permute-start | bytes 2359304 | tf_op jit(solution)/shard_map/ppermute | solution.py:662
  374.7 26.4 %collective-permute-start.38 = (bf16[512,1024]{1,0:T(8,128)(2,1)}, bf16[512,1024]{1,0:T(8,128)(2,1)}, u32[]{:S(2)}, u32[]{:S(2)}) collective-permute-start(bf16[512,1024]{1,0:T(8,128)(2,1)} %slice.65), channel_id=1, source_target_pairs={{0,16},{8,24},{16,0},{24,8},{1,17},{9,25},{17,1},{25,9},{2,18},{10... | collective-permute-start | bytes 3145736 | tf_op jit(solution)/shard_map/ppermute | solution.py:662
  375.2 30.6 %collective-permute-start.23 = (bf16[512,1024]{1,0:T(8,128)(2,1)}, bf16[512,1024]{1,0:T(8,128)(2,1)}, u32[]{:S(2)}, u32[]{:S(2)}) collective-permute-start(bf16[512,1024]{1,0:T(8,128)(2,1)} %get-tuple-element.115), channel_id=1, source_target_pairs={{0,8},{8,0},{16,24},{24,16},{1,9},{9,1},{17,25},{25,17},{2,10},{10... | collective-permute-start | bytes 3145736 | tf_op jit(solution)/shard_map/ppermute | solution.py:662
  376.0 46.1 %collective-permute-start.40 = (bf16[128,2048]{1,0:T(8,128)(2,1)}, bf16[128,2048]{1,0:T(8,128)(2,1)}, u32[]{:S(2)}, u32[]{:S(2)}) collective-permute-start(bf16[128,2048]{1,0:T(8,128)(2,1)} %get-tuple-element.205), channel_id=1, source_target_pairs={{0,16},{8,24},{16,0},{24,8},{1,17},{9,25},{17,1},{25,9},{2,18},{10... | collective-permute-start | bytes 1572872 | tf_op jit(solution)/shard_map/ppermute | solution.py:662
  377.5 142.0 %all-reduce.9.cloned.1.call-start = ((), (), s32[]{:S(2)}) async-start(), calls=%async_computation.3 | async-start | bytes 2097152 | tf_op jit(solution)/shard_map/psum | solution.py:891
  403.6 8.1 %collective-permute-start.41 = (f32[1,288]{1,0:T(1,128)S(1)}, f32[1,288]{1,0:T(1,128)S(1)}, u32[]{:S(2)}, u32[]{:S(2)}) collective-permute-start(f32[1,288]{1,0:T(1,128)S(1)} %get-tuple-element.230), channel_id=1, source_target_pairs={{0,4},{4,0},{8,12},{12,8},{16,20},{20,16},{24,28},{28,24},{1,5},{5... | collective-permute-start | bytes 3464 | tf_op jit(solution)/shard_map/ppermute | solution.py:687
  405.3 9.0 %collective-permute-start.42 = (f32[1,288]{1,0:T(1,128)S(1)}, f32[1,288]{1,0:T(1,128)S(1)}, u32[]{:S(2)}, u32[]{:S(2)}) collective-permute-start(f32[1,288]{1,0:T(1,128)S(1)} %get-tuple-element.229), channel_id=1, source_target_pairs={{0,8},{4,12},{8,0},{12,4},{16,24},{20,28},{24,16},{28,20},{1,9},{5... | collective-permute-start | bytes 3464 | tf_op jit(solution)/shard_map/ppermute | solution.py:687
  405.3 9.0 %collective-permute-start.43 = (f32[1,288]{1,0:T(1,128)S(1)}, f32[1,288]{1,0:T(1,128)S(1)}, u32[]{:S(2)}, u32[]{:S(2)}) collective-permute-start(f32[1,288]{1,0:T(1,128)S(1)} %get-tuple-element.228), channel_id=1, source_target_pairs={{0,12},{4,8},{8,4},{12,0},{16,28},{20,24},{24,20},{28,16},{1,13},{... | collective-permute-start | bytes 3464 | tf_op jit(solution)/shard_map/ppermute | solution.py:687
  405.8 11.1 %collective-permute-start.44 = (f32[1,288]{1,0:T(1,128)S(1)}, f32[1,288]{1,0:T(1,128)S(1)}, u32[]{:S(2)}, u32[]{:S(2)}) collective-permute-start(f32[1,288]{1,0:T(1,128)S(1)} %get-tuple-element.227), channel_id=1, source_target_pairs={{0,16},{4,20},{8,24},{12,28},{16,0},{20,4},{24,8},{28,12},{1,17},{... | collective-permute-start | bytes 3464 | tf_op jit(solution)/shard_map/ppermute | solution.py:687
  416.9 54.4 %collective-permute-start.39 = (bf16[256,1024]{1,0:T(8,128)(2,1)}, bf16[256,1024]{1,0:T(8,128)(2,1)}, u32[]{:S(2)}, u32[]{:S(2)}) collective-permute-start(bf16[256,1024]{1,0:T(8,128)(2,1)} %get-tuple-element.220), channel_id=1, source_target_pairs={{0,8},{8,0},{16,24},{24,16},{1,9},{9,1},{17,25},{25,17},{2,10},{10... | collective-permute-start | bytes 1572872 | tf_op jit(solution)/shard_map/ppermute | solution.py:662
  416.9 56.9 %collective-permute-start.24 = (bf16[256,1024]{1,0:T(8,128)(2,1)}, bf16[256,1024]{1,0:T(8,128)(2,1)}, u32[]{:S(2)}, u32[]{:S(2)}) collective-permute-start(bf16[256,1024]{1,0:T(8,128)(2,1)} %get-tuple-element.223), channel_id=1, source_target_pairs={{0,8},{8,0},{16,24},{24,16},{1,9},{9,1},{17,25},{25,17},{2,10},{10... | collective-permute-start | bytes 1572872 | tf_op jit(solution)/shard_map/ppermute | solution.py:662
  418.2 52.4 %collective-permute-start.48 = (f32[1,288]{1,0:T(1,128)S(1)}, f32[1,288]{1,0:T(1,128)S(1)}, u32[]{:S(2)}, u32[]{:S(2)}) collective-permute-start(f32[1,288]{1,0:T(1,128)S(1)} %add_add_fusion), channel_id=1, source_target_pairs={{0,1},{1,0},{2,3},{3,2},{4,5},{5,4},{6,7},{7,6},{8,9},{9,8},{10,11... | collective-permute-start | bytes 3464 | tf_op jit(solution)/shard_map/ppermute | solution.py:907
  419.7 50.9 %collective-permute-start.49 = (f32[1,288]{1,0:T(1,128)S(1)}, f32[1,288]{1,0:T(1,128)S(1)}, u32[]{:S(2)}, u32[]{:S(2)}) collective-permute-start(f32[1,288]{1,0:T(1,128)S(1)} %add_add_fusion), channel_id=1, source_target_pairs={{0,2},{1,3},{2,0},{3,1},{4,6},{5,7},{6,4},{7,5},{8,10},{9,11},{10,... | collective-permute-start | bytes 3464 | tf_op jit(solution)/shard_map/ppermute | solution.py:907
  422.1 48.5 %collective-permute-start.50 = (f32[1,288]{1,0:T(1,128)S(1)}, f32[1,288]{1,0:T(1,128)S(1)}, u32[]{:S(2)}, u32[]{:S(2)}) collective-permute-start(f32[1,288]{1,0:T(1,128)S(1)} %add_add_fusion), channel_id=1, source_target_pairs={{0,3},{1,2},{2,1},{3,0},{4,7},{5,6},{6,5},{7,4},{8,11},{9,10},{10,... | collective-permute-start | bytes 3464 | tf_op jit(solution)/shard_map/ppermute | solution.py:907
  (74 other events, 822.5 us)
Sparse Core Ops, SparseCore 0:
  10.5 67.0 all-gather.4
  80.1 94.0 all-gather.2
  320.6 43.6 all-reduce.6
  377.6 87.7 all-reduce.10
  468.3 51.1 all-reduce.8

commit v6 on v5

--- a/solution.py
+++ b/solution.py
@@ -396,7 +396,7 @@
     )(place, *[expand] * (2 * chips), *[shrink] * chips, own, other, c, c_other)
 
 
-def back_kernel(n, inner, place_ref, *refs):
+def back_kernel(n, inner, half, place_ref, *refs):
     qkv_parts = refs[: n * inner]
     out_parts = refs[n * inner : (n + 2) * inner]
     refs = refs[(n + 2) * inner :]
@@ -415,14 +415,13 @@
         gain_q_ref,
         gain_k_ref,
     ) = refs[:13]
-    grad_ref, share_ref, gains_ref, qkv, out, key_sum, value_sum, share_sum = refs[13:]
+    refs = refs[13:]
+    if half:
+        base_ref, refs = refs[0], refs[2:]
+    grad_ref, share_ref, gains_ref, qkv, out, key_sum, value_sum = refs
     block = q_ref.shape[0]
     heads = k_ref.shape[1] // HEAD_SIZE
-    half, step = pl.program_id(0), pl.program_id(1)
-
-    @pl.when((half == 0) & (step == 0))
-    def _():
-        gains_ref[...] = jnp.zeros_like(gains_ref)
+    step = pl.program_id(0)
 
     @pl.when(step == 0)
     def _():
@@ -437,6 +436,7 @@
 
         key_sum[...] = jnp.zeros_like(key_sum)
         value_sum[...] = jnp.zeros_like(value_sum)
+        gains_ref[...] = jnp.zeros_like(gains_ref)
 
     def work(j):
         size = (j + 1) * block
@@ -500,17 +500,9 @@
         grad_ref[...] = grad
         share = dot_nt(grad, qkv[...])
 
-        @pl.when(half == 0)
-        def _():
-            share_sum[j] = share
-
-        @pl.when((half > 0) & (half < HALVES - 1))
-        def _():
-            share_sum[j] += share
-
-        @pl.when(half == HALVES - 1)
-        def _():
-            share_ref[...] = (share_sum[j] + share).astype(LOW)
+        if half:
+            share = share + base_ref[...].astype(FULL)
+        share_ref[...] = share.astype(LOW)
 
     for j in range(n):
         pl.when(step == n - 1 - j)(functools.partial(work, j))
@@ -518,7 +510,7 @@
 
 def back(
     place, qkv_parts, out_parts, hidden_grad, attended, totals, q, k, v, raw, cos, sin, seg_col,
-    seg_row, gain_q, gain_k,
+    seg_row, gain_q, gain_k, half, base,
 ):
     inner = len(out_parts) // 2
     n = len(qkv_parts) // inner
@@ -526,15 +518,15 @@
     q_width, k_width = q.shape[1] // HALVES, k.shape[1] // HALVES
     block = length // n
     width = q_width + 2 * k_width
-    whole = lambda h, i, p: (0, 0)
-    natural = lambda h, i, p: (n - 1 - i, 0)
-    slot = lambda h, i, p: (p[0] ^ (n - 1 - i), 0)
-    last_slot = lambda h, i, p: (p[0] ^ (n - 1 - jnp.where(h == HALVES - 1, i, 0)), 0)
-    of_half = lambda h, i, p: (0, h)
-    natural_half = lambda h, i, p: (n - 1 - i, h)
-    slot_half = lambda h, i, p: (p[0] ^ (n - 1 - i), h)
+    whole = lambda i, p: (0, 0)
+    natural = lambda i, p: (n - 1 - i, 0)
+    slot = lambda i, p: (p[0] ^ (n - 1 - i), 0)
+    natural_half = lambda i, p: (n - 1 - i, half)
+    slot_half = lambda i, p: (p[0] ^ (n - 1 - i), half)
+    base = list(base or ())
+    before = 1 + len(qkv_parts) + len(out_parts) + 13
     return pl.pallas_call(
-        functools.partial(back_kernel, n, inner),
+        functools.partial(back_kernel, n, inner, half),
         out_shape=(
             jax.ShapeDtypeStruct((length, HALVES * width), LOW),
             jax.ShapeDtypeStruct((length, D), LOW),
@@ -542,16 +534,16 @@
         ),
         grid_spec=pltpu.PrefetchScalarGridSpec(
             num_scalar_prefetch=1,
-            grid=(HALVES, n),
-            in_specs=[pl.BlockSpec((p.shape[0], width), of_half) for p in qkv_parts]
+            grid=(n,),
+            in_specs=[resident((p.shape[0], width), half) for p in qkv_parts]
             + [resident(p.shape) for p in out_parts]
             + [
                 pl.BlockSpec((block, D), slot),
                 pl.BlockSpec((block, q_width), slot_half),
                 pl.BlockSpec((block, HEAD_SIZE), slot_half),
                 pl.BlockSpec((block, q_width), natural_half),
-                pl.BlockSpec((length, k_width), of_half),
-                pl.BlockSpec((length, k_width), of_half),
+                resident((length, k_width), half),
+                resident((length, k_width), half),
                 pl.BlockSpec((block, q_width + k_width), natural_half),
                 pl.BlockSpec((block, HEAD_SIZE), natural),
                 pl.BlockSpec((block, HEAD_SIZE), natural),
@@ -559,10 +551,11 @@
                 pl.BlockSpec((1, length), whole),
                 pl.BlockSpec((1, HEAD_SIZE), whole),
                 pl.BlockSpec((1, HEAD_SIZE), whole),
-            ],
+            ]
+            + [pl.BlockSpec((block, D), slot), ANYWHERE][: len(base)],
             out_specs=(
                 pl.BlockSpec((block, width), natural_half),
-                pl.BlockSpec((block, D), last_slot),
+                pl.BlockSpec((block, D), slot),
                 pl.BlockSpec((8, HEAD_SIZE), whole),
             ),
             scratch_shapes=[
@@ -570,9 +563,9 @@
                 pltpu.VMEM((q_width, D), LOW),
                 pltpu.VMEM((length, k_width), FULL),
                 pltpu.VMEM((length, k_width), FULL),
-                pltpu.VMEM((n, block, D), FULL),
             ],
         ),
+        input_output_aliases={before + 1: 0} if base else {},
         compiler_params=pltpu.CompilerParams(vmem_limit_bytes=56 * MIB),
         cost_estimate=pl.CostEstimate(
             flops=2 * length * D * (q_width + width) + 5 * length * length * q_width,
@@ -582,7 +575,7 @@
         name="back",
     )(
         place, *qkv_parts, *out_parts, hidden_grad, attended, totals, q, k, v, raw, cos, sin,
-        seg_col, seg_row, gain_q, gain_k,
+        seg_col, seg_row, gain_q, gain_k, *base,
     )
 
 
@@ -849,46 +842,60 @@
         other_rows = pick(expand_cuts, 1, core ^ 1)
         other_sent = [swap_grp(pick(other_rows, 1, mine ^ t), t) for t in range(1, inner)]
         own_rows = pick(expand_cuts, 1, core)
-        late_rows = after(own_rows, grad_slots[-1])
-        own_sent = [swap_chip(pick(late_rows, 0, chip ^ s), s) for s in range(1, chips)]
+
+        def first_over_x(t, *gates):
+            cut = after(own_rows, *gates)
+            sent = [swap_chip(pick(pick(cut, 0, chip ^ s), 0, mine ^ t), s) for s in range(1, chips)]
+            return pick(pick(own_rows, 0, chip), 0, mine ^ t), sent
+
+        def back_part(half, attended, base):
+            return back(
+                place, qkv_parts, out_parts, grad_all, attended, totals, q, k, v, raw, cos, sin, seg_col,
+                seg_row, gain_query, gain_key, half, base,
+            )
+
+        own_far = [first_over_x(t, *grad_slots) for t in range(1, inner)]
         line[:] = [grad_expand]
         shrink_cut = send_x(next_cut(pick(shrink_cuts, 1, mine), shrink_sent, 0, chip, chips))
         grad_slots = lax.optimization_barrier((*grad_slots, *line))[:chips]
         grad_all = jnp.concatenate(grad_slots)
-        grad, back_all, head_gains = back(
-            place, qkv_parts, out_parts, grad_all, attended, totals, q, k, v, raw, cos, sin, seg_col,
-            seg_row, gain_query, gain_key,
-        )
-
-        line[:] = [head_gains]
+        grad, back_all, gains_first_part = back_part(0, attended, None)
+
+        line[:] = [gains_first_part]
         shrink_cut = next_sum(*shrink_cut)
         total_shrink = lax.psum(shrink_cut, "rep")
-        own_cut = send_y(next_cut(pick(own_rows, 0, chip), own_sent, 0, mine, inner))
+        own_near = first_over_x(0, *line)
+        own_sent = [swap_grp(next_sum(*own_far[t - 1]), t) for t in range(1, inner)]
         other_cut = send_x(next_cut(pick(other_rows, 1, mine), other_sent, 0, chip, chips))
+        attended, back_all, grad = lax.optimization_barrier((attended, back_all, grad, *line))[:3]
+        grad, back_all, head_gains = back_part(1, attended, (back_all, grad))
+
+        line[:] = [head_gains]
+        head_gains = head_gains + gains_first_part
+        own_cut = next_sum(next_sum(*own_near), own_sent)
+        other_cut = swap_core(next_sum(*other_cut))
+        qkv_cuts, qkv_sent = cut_qkv(after(grad, *line))
+        own_cut, other_cut, total_shrink = lax.optimization_barrier(
+            (own_cut, other_cut, total_shrink, qkv_cuts, *line)
+        )[:3]
+        line[:] = [own_cut]
+        own_cut, other_cut = lax.psum((own_cut, other_cut), "rep")
         grad_out = dot_tn(after(attended, *line), grad_all).astype(LOW)
         out_cuts = grad_out.reshape(2, inner, out_weight.shape[0], D)
         out_sent = [swap_core(pick(out_cuts, 0, core ^ 1))]
         line[:] = [grad_out]
-        qkv_cuts, qkv_sent = cut_qkv(after(grad, *line))
         out_cut = send_y(next_cut(pick(out_cuts, 0, core), out_sent, 0, mine, inner))
         qkv_cut = send_y(next_cut(qkv_cuts, qkv_sent, 1, mine, inner))
-        own_cut = next_sum(*own_cut)
-        other_cut = swap_core(next_sum(*other_cut))
         out_cut = next_sum(*out_cut)
-        own_cut, other_cut, out_cut, total_shrink = lax.optimization_barrier(
-            (own_cut, other_cut, out_cut, total_shrink, *line)
-        )[:4]
-        line[:] = [out_cut]
-        own_cut, other_cut, total_out = lax.psum((own_cut, other_cut, out_cut), "rep")
         kept, sent = send_x(next_cut(*qkv_cut, 0, chip, chips))
         shares = []
         for s in range(1, chips):
             share = after(back_all[2 * s * block : 2 * (s + 1) * block], kept)
             shares.append(swap_chip(share, s))
-        *qkv_cuts, own_cut, other_cut, total_out = lax.optimization_barrier(
-            (kept, *sent, own_cut, other_cut, total_out, *line)
+        *qkv_cuts, out_cut, own_cut, other_cut = lax.optimization_barrier(
+            (kept, *sent, out_cut, own_cut, other_cut, *line)
         )[: 3 + chips]
-        qkv_cuts = lax.psum(tuple(qkv_cuts), "rep")
+        total_out, *qkv_cuts = lax.psum((out_cut, *qkv_cuts), "rep")
 
         shares = [back_all[: 2 * block]] + [after(value, *line) for value in shares]
         input_part, gain_part = norm_back(inputs, gain_one, sum_of(shares))

time: 546 us -> 522 us (0.956)
  waiting for transfers between devices: 243 us -> 219 us
    ppermute x26 -> x27, waiting for transfers between devices: 99.3 us -> 67.2 us  [swap_ctx(): return lax.ppermute(value, 'ctx', [(i, i ^ s) for i in range(n)])]
    ppermute x8, waiting for transfers between devices: 48 us -> 78.7 us  [swap_grp(): return lax.ppermute(value, 'grp', [(i, i ^ t) for i in range(inner)])]
    psum x2, waiting for transfers between devices: 77.1 us -> 65.5 us  [the longest x1 43.8 us: on_device(): total_out, *qkv_cuts = lax.psum((out_cut, *qkv_cuts), 'rep')]
    psum x1, waiting for transfers between devices: 13.1 us -> 1.68 us  [on_device(): total_shrink = lax.psum(shrink_cut, 'rep')]
    convert_element_type x6 -> x5, other arithmetic: 17.3 us -> 10.7 us  [next_cut(): sum_of([pick(value, axis, place ^ s) for value in (kept, *sent)])]
    pallas_call x1 -> x2, Pallas kernels: 43 us -> 47.5 us  [back(): pl.pallas_call(functools.partial(back_kernel, n, inner, half), out_shape=...]
    unnamed x144 -> x136, local copies, waits for them, and re-layouts: 21.1 us -> 17.1 us
    ppermute x26 -> x27, starting transfers between devices: 10.6 us -> 11.9 us  [swap_ctx(): return lax.ppermute(value, 'ctx', [(i, i ^ s) for i in range(n)])]
  transfers between devices with their start and end apart: 56 -> 57, of which waited for: 19 -> 17; matrix products, arithmetic and copies ran while one was open for 16% -> 18% of each run, Pallas kernels for 15% -> 17%
where the time goes in v6:
time: 522 us; the launch traced here: 515 us
  waiting for transfers between devices  219 us (42%)
  Pallas kernels  126 us (24%)
  other arithmetic  57.7 us (11%)
  starting transfers between devices  39.9 us (8%)
  local copies, waits for them, and re-layouts  33.3 us (6%)
  matrix products  22.9 us (4%)
  between operations  15.3 us (3%)
    ppermute x8, waiting for transfers between devices, swap_grp(): return lax.ppermute(value, 'grp', [(i, i ^ t) for i in range(inner)])  78.7 us
    ppermute x27, waiting for transfers between devices, swap_ctx(): return lax.ppermute(value, 'ctx', [(i, i ^ s) for i in range(n)])  67.2 us
    pallas_call x2, Pallas kernels, back(): pl.pallas_call(functools.partial(back_kernel, n, inner, half), out_shape=...  47.5 us
    psum x1, waiting for transfers between devices, on_device(): total_out, *qkv_cuts = lax.psum((out_cut, *qkv_cuts), 'rep')  43.8 us
    pallas_call x1, Pallas kernels, feed(): pl.pallas_call(functools.partial(feed_kernel, chips), out_shape=(wide(D),...  31.6 us
    pallas_call x2, Pallas kernels, attend(): pl.pallas_call(functools.partial(attend_kernel, n, inner, first, bool(bas...  23.1 us
    dot_general x4, matrix products, dot_tn(): lax.dot_general(a, b, (((0,), (0,)), ((), ())), preferred_element_type=FULL)  22.9 us
    psum x1, waiting for transfers between devices, on_device(): own_cut, other_cut = lax.psum((own_cut, other_cut), 'rep')  21.7 us
  transfers between devices with their start and end apart: 57, of which 17 were waited for; matrix products, arithmetic and copies ran while one was open for 18% of the time, Pallas kernels for 17%

profile of v6, /device:TPU:0, one launch (start us, length us, event | category | flops | bytes accessed | tf_op | source)
XLA Modules:
  0.0 514.9 jit_solution(13851777678830570123)
XLA Ops:
  7.3 2.5 convert_element_type.316
  9.9 3.4 convert_element_type.315
  13.4 3.0 collective-permute-start
  16.7 1.9 collective-permute-start.3
  27.7 2.0 collective-permute-start.8
  32.1 15.8 %collective-permute-done.14.refs_4_ = bf16[128,2048]{1,0:T(8,128)(2,1)} collective-permute-done((bf16[128,2048]{1,0:T(8,128)(2,1)}, bf16[128,2048]{1,0:T(8,128)(2,1)}, u32[]{:S(2)}, u32[]{:S(2)}) %collective-permute-start.14) | collective-permute-done | bytes 524320 | tf_op jit(solution)/shard_map/ppermute | solution.py:655
  48.7 2.0 copy.41
  50.8 2.5 gather_fusion.1
  53.7 14.7 %collective-permute-done.11.refs_1_ = bf16[128,2048]{1,0:T(8,128)(2,1)} collective-permute-done((bf16[128,2048]{1,0:T(8,128)(2,1)}, bf16[128,2048]{1,0:T(8,128)(2,1)}, u32[]{:S(2)}, u32[]{:S(2)}) %collective-permute-start.11) | collective-permute-done | bytes 524320 | tf_op jit(solution)/shard_map/ppermute | solution.py:664
  69.4 1.8 collective-permute-start.19
  71.2 11.8 %collective-permute-done.15.refs_5_ = bf16[128,2048]{1,0:T(8,128)(2,1)S(1)} collective-permute-done((bf16[128,2048]{1,0:T(8,128)(2,1)}, bf16[128,2048]{1,0:T(8,128)(2,1)S(1)}, u32[]{:S(2)}, u32[]{:S(2)}) %collective-permute-start.15) | collective-permute-done | bytes 524320 | tf_op jit(solution)/shard_map/ppermute | solution.py:664
  84.2 1.9 fusion.26
  89.7 10.6 %project.1 = (bf16[1024,1024]{1,0:T(8,128)(2,1)S(1)}, bf16[1024,1024]{1,0:T(8,128)(2,1)S(1)}, bf16[1024,512]{1,0:T(8,128)(2,1)S(1)}, bf16[1024,512]{1,0:T(8,128)(2,1)S(1)}, bf16[1024,1536]{1,0:T(8,128)(2,1)}) custom-call(s32[2]{0:T(128)S(1)} %pad_add_fusion.place_ref, bf16[128,2048]{1,0:T(8,128)(2,1)} %get-tuple-element.104.refs_0_, ...), custom_call_target="tpu_custom_call" | custom-call | flops 4294967296 | bytes 16777216 | tf_op jit(solution)/shard_map/project/pallas_call | solution.py:150
  104.0 11.3 %attend.2 = (bf16[1024,1024]{1,0:T(8,128)(2,1)}, f32[1024,256]{1,0:T(8,128)S(1)}, bf16[512,1024]{1,0:T(8,128)(2,1)S(1)}) custom-call(s32[2]{0:T(128)S(1)} %pad_add_fusion.place_ref, bf16[256,1024]{1,0:T(8,128)(2,1)S(1)} %convert_element_type.311.refs_0_.refs_8_, bf16[256,1024]{1,0:T(8,128)(2,1)S(1)} %copy-done.20, ...), custom_call_target="tpu_custom_call" | custom-call | flops 3221225472 | bytes 8388608 | tf_op jit(solution)/shard_map/attend/pallas_call | solution.py:258
  115.8 11.8 %attend.3 = (bf16[1024,1024]{1,0:T(8,128)(2,1)}, f32[1024,256]{1,0:T(8,128)S(1)}, bf16[512,1024]{1,0:T(8,128)(2,1)S(1)}) custom-call(s32[2]{0:T(128)S(1)} %pad_add_fusion.place_ref, bf16[256,1024]{1,0:T(8,128)(2,1)S(1)} %convert_element_type.311.refs_0_.refs_8_, bf16[256,1024]{1,0:T(8,128)(2,1)S(1)} %copy-done.20, ...), custom_call_target="tpu_custom_call", output_to_operand_aliasing={{0}: (10, {}), {1}: (11, {})} | custom-call | flops 3221225472 | bytes 8388608 | tf_op jit(solution)/shard_map/attend/pallas_call | solution.py:258
  127.6 35.9 %collective-permute-done.20 = bf16[512,1024]{1,0:T(8,128)(2,1)S(1)} collective-permute-done((bf16[512,1024]{1,0:T(8,128)(2,1)S(1)}, bf16[512,1024]{1,0:T(8,128)(2,1)S(1)}, u32[]{:S(2)}, u32[]{:S(2)}) %collective-permute-start.20) | collective-permute-done | bytes 1048608 | tf_op jit(solution)/shard_map/ppermute | solution.py:655
  165.3 1.8 multiply_convert_fusion.refs_6_
  169.9 4.3 all-gather.3.cloned.1.call-done.refs_0_.refs_1_.refs_2_.refs_3_
  174.2 31.6 %feed.1 = (bf16[1024,1024]{1,0:T(8,128)(2,1)}, bf16[1024,1024]{1,0:T(8,128)(2,1)}, bf16[1024,1536]{1,0:T(8,128)(2,1)}, bf16[1024,3072]{1,0:T(8,128)(2,1)}, bf16[...) custom-call(s32[2]{0:T(128)} %copy-done.30, ...), custom_call_target="tpu_custom_call" | custom-call | flops 19327352832 | bytes 31457280 | tf_op jit(solution)/shard_map/feed/pallas_call | solution.py:364
  206.1 6.0 %convolution_convert_fusion.1 = bf16[1536,1024]{1,0:T(8,128)(2,1)S(1)} fusion(bf16[1024,1536]{1,0:T(8,128)(2,1)} %get-tuple-element.124, bf16[1024,1024]{1,0:T(8,128)(2,1)} %get-tuple-element.125), kind=kOutput, calls=%fused_computation.3 | convolution fusion | flops 3222798336 | bytes 8388608 | tf_op jit(solution)/shard_map/dot_general | solution.py:51
  213.8 2.5 multiply_reduce_fusion
  216.3 2.5 fusion.61
  219.7 7.3 %convolution_convert_fusion = bf16[1024,3072]{1,0:T(8,128)(2,1)S(1)} fusion(bf16[1024,1024]{1,0:T(8,128)(2,1)S(1)} %copy-done.61, bf16[1024,3072]{1,0:T(8,128)(2,1)S(1)} %copy-done.60), kind=kOutput, calls=%fused_computation.2 | convolution fusion | flops 6445596672 | bytes 14680064 | tf_op jit(solution)/shard_map/dot_general | solution.py:51
  229.6 19.9 %collective-permute-done.27 = bf16[2,384,1024]{2,1,0:T(8,128)(2,1)S(1)} collective-permute-done((bf16[2,384,1024]{2,1,0:T(8,128)(2,1)S(1)}, bf16[2,384,1024]{2,1,0:T(8,128)(2,1)S(1)}, u32[]{:S(2)}, u32[]{:S(2)}) %collective-permute-start.27) | collective-permute-done | bytes 1572896 | tf_op jit(solution)/shard_map/ppermute | solution.py:664
  254.7 23.7 %back.2 = (bf16[1024,2048]{1,0:T(8,128)(2,1)}, bf16[1024,1024]{1,0:T(8,128)(2,1)}, f32[8,128]{1,0:T(8,128)}) custom-call(s32[2]{0:T(128)} %copy-done.30, bf16[128,2048]{1,0:T(8,128)(2,1)} %get-tuple-element.104.refs_0_, bf16[128,2048]{1,0:T(8,128)(2,1)} %collective-permute-done.11.refs_1_, bf16[128,2048]{1,0:T(8,128)(2,1)} %copy-done.23, ...), custom_call_target="tpu_custom_call" | custom-call | flops 5905580032 | bytes 31457280 | tf_op jit(solution)/shard_map/back/pallas_call | solution.py:528
  278.4 2.3 add_convert_fusion.3
  280.7 2.1 dynamic-slice_bitcast_fusion.4
  283.1 4.0 collective-permute-done.29
  290.3 2.4 fusion.17
  293.3 23.8 %back.3 = (bf16[1024,2048]{1,0:T(8,128)(2,1)}, bf16[1024,1024]{1,0:T(8,128)(2,1)}, f32[8,128]{1,0:T(8,128)}) custom-call(s32[2]{0:T(128)} %copy-done.30, bf16[128,2048]{1,0:T(8,128)(2,1)} %get-tuple-element.104.refs_0_, bf16[128,2048]{1,0:T(8,128)(2,1)} %collective-permute-done.11.refs_1_, ...), custom_call_target="tpu_custom_call", output_to_operand_aliasing={{0}: (27, {})} | custom-call | flops 5905580032 | bytes 31457280 | tf_op jit(solution)/shard_map/back/pallas_call | solution.py:528
  321.1 4.9 convolution_convert_fusion.2
  330.9 4.6 convolution_convert_fusion.3
  335.7 2.6 collective-permute-done.36
  339.7 3.7 fusion.11
  345.5 2.4 slice.65
  347.9 32.2 %collective-permute-done.38 = bf16[256,1024]{1,0:T(8,128)(2,1)} collective-permute-done((bf16[256,1024]{1,0:T(8,128)(2,1)}, bf16[256,1024]{1,0:T(8,128)(2,1)}, u32[]{:S(2)}, u32[]{:S(2)}) %collective-permute-start.38) | collective-permute-done | bytes 524320 | tf_op jit(solution)/shard_map/ppermute | solution.py:664
  380.1 2.0 add_convert_fusion.6
  382.2 2.6 fusion.28
  386.9 5.8 %multiply_subtract_fusion = (f32[384,1024]{1,0:T(8,128)}, f32[384,1024]{1,0:T(8,128)}, f32[384,1024]{1,0:T(8,128)}) fusion(f32[384,1024]{1,0:T(8,128)} %param.32, bf16[384,1024]{1,0:T(8,128)(2,1)} %all-reduce.7.cloned.1.call-done, f32[384,1024]{1,0:T(8,128)} %param.34, f32[384,1024]{1,0:T(8,128)} %param.33), kind=kLoop, calls=%fused_computation.51 | loop fusion | flops 6291456 | bytes 10223616 | tf_op jit(solution)/shard_map/sub | solution.py:72
  392.7 21.7 %all-reduce.11.cloned.1.call-done = (bf16[128,3072]{1,0:T(8,128)(2,1)}, bf16[128,3072]{1,0:T(8,128)(2,1)}) async-done(((bf16[128,3072]{1,0:T(8,128)(2,1)}, bf16[128,3072]{1,0:T(8,128)(2,1)}), (bf16[128,3072]{1,0:T(8,128)(2,1)}, bf16[128,3072]{1,0:T(8,128)(2,1)})) %all-reduce.11.cloned.1.call-update) | async-done | bytes 1572880 | tf_op jit(solution)/shard_map/psum | solution.py:882
  414.4 6.3 %collective-permute-done.41 = bf16[128,2048]{1,0:T(8,128)(2,1)} collective-permute-done((bf16[128,2048]{1,0:T(8,128)(2,1)}, bf16[128,2048]{1,0:T(8,128)(2,1)}, u32[]{:S(2)}, u32[]{:S(2)}) %collective-permute-start.41) | collective-permute-done | bytes 524320 | tf_op jit(solution)/shard_map/ppermute | solution.py:655
  420.7 2.4 fusion.8
  428.5 4.9 fusion.7
  440.1 2.1 collective-permute-start.51
  442.3 6.5 %adam_pair.1 = (f32[128,6144]{1,0:T(8,128)}, f32[128,6144]{1,0:T(8,128)}, f32[128,6144]{1,0:T(8,128)}) custom-call(s32[2]{0:T(128)S(1)} %copy-done.31, bf16[128,3072]{1,0:T(8,128)(2,1)S(1)} %copy-done.17, bf16[128,3072]{1,0:T(8,128)(2,1)S(1)} %copy-done.18, f32[128,6144]{1,0:T(8,128)S(1)} %copy-done.2, f32[128,6144]{1,0:T(8,128)S(1)} %copy-done.5, ...), custom_call_target="tpu_custom_call" | custom-call | flops 15728640 | bytes 20447232 | tf_op jit(solution)/shard_map/adam_pair/pallas_call | solution.py:630
  451.7 43.8 %all-reduce.9.cloned.1.call-done = (bf16[128,2048]{1,0:T(8,128)(2,1)}, bf16[128,2048]{1,0:T(8,128)(2,1)}, bf16[256,1024]{1,0:T(8,128)(2,1)}) async-done(((bf16[128,2048]{1,0:T(8,128)(2,1)}, bf16[128,2048]{1,0:T(8,128)(2,1)}, bf16[256,1024]{1,0:T(8,128)(2,1)}), (bf16[128,2048]{1,0:T(8,128)(2,1)}, bf16[128,2048]{1,0:T(8,128)(2,1)}, bf16[256,1024]{1,0:T(8,128)(2,1)})) %all-reduce.9.cloned.1.call-update) | async-done | bytes 1572880 | tf_op jit(solution)/shard_map/psum | solution.py:898
  495.5 3.4 multiply_subtract_fusion.1
  500.7 7.2 %adam_cuts.1 = (f32[128,4096]{1,0:T(8,128)}, f32[128,4096]{1,0:T(8,128)}, f32[128,4096]{1,0:T(8,128)}) custom-call(s32[1]{0:T(128)} %bitcast.55.key_ref, bf16[128,2048]{1,0:T(8,128)(2,1)S(1)} %copy-done.27, bf16[128,2048]{1,0:T(8,128)(2,1)S(1)} %copy-done.28, f32[128,4096]{1,0:T(8,128)S(1)} %copy-done.4, f32[128,4096]{1,0:T(8,128)S(1)} %copy-done.12, ...), custom_call_target="tpu_custom_call" | custom-call | flops 10485760 | bytes 13631488 | tf_op jit(solution)/shard_map/adam_cuts/pallas_call | solution.py:600
  (293 shorter events, 73.4 us)
Async XLA Ops:
  7.2 162.7 %all-gather.5.cloned.1.call-start = ((), (), s32[]{:S(2)}) async-start(), calls=%async_computation.1 | async-start | bytes 7077888 | tf_op jit(solution)/shard_map/all_gather | solution.py:766
  9.8 164.4 %all-gather.3.cloned.1.call-start = ((), (), s32[]{:S(2)}) async-start(), calls=%async_computation | async-start | bytes 14155776 | tf_op jit(solution)/shard_map/all_gather | solution.py:766
  13.3 317.7 %all-reduce.7.cloned.1.call-start = ((), (), s32[]{:S(2)}) async-start(), calls=%async_computation.2 | async-start | bytes 1572864 | tf_op jit(solution)/shard_map/psum | solution.py:866
  13.4 11.0 %collective-permute-start = (f32[1,1312]{1,0:T(1,128)S(1)}, f32[1,1312]{1,0:T(1,128)S(1)}, u32[]{:S(2)}, u32[]{:S(2)}) collective-permute-start(f32[1,1312]{1,0:T(1,128)S(1)} %reshape.234), channel_id=1, source_target_pairs={{0,4},{4,0},{8,12},{12,8},{16,20},{20,16},{24,28},{28,24},{1,5},{5... | collective-permute-start | bytes 15752 | tf_op jit(solution)/shard_map/ppermute | solution.py:680
  16.4 11.2 %collective-permute-start.2 = (f32[1,1312]{1,0:T(1,128)S(1)}, f32[1,1312]{1,0:T(1,128)S(1)}, u32[]{:S(2)}, u32[]{:S(2)}) collective-permute-start(f32[1,1312]{1,0:T(1,128)S(1)} %reshape.234), channel_id=1, source_target_pairs={{0,12},{4,8},{8,4},{12,0},{16,28},{20,24},{24,20},{28,16},{1,13},{... | collective-permute-start | bytes 15752 | tf_op jit(solution)/shard_map/ppermute | solution.py:680
  16.7 13.0 %collective-permute-start.3 = (f32[1,1312]{1,0:T(1,128)S(1)}, f32[1,1312]{1,0:T(1,128)S(1)}, u32[]{:S(2)}, u32[]{:S(2)}) collective-permute-start(f32[1,1312]{1,0:T(1,128)S(1)} %reshape.234), channel_id=1, source_target_pairs={{0,16},{4,20},{8,24},{12,28},{16,0},{20,4},{24,8},{28,12},{1,17},{... | collective-permute-start | bytes 15752 | tf_op jit(solution)/shard_map/ppermute | solution.py:680
  18.6 11.1 %collective-permute-start.4 = (f32[1,1312]{1,0:T(1,128)S(1)}, f32[1,1312]{1,0:T(1,128)S(1)}, u32[]{:S(2)}, u32[]{:S(2)}) collective-permute-start(f32[1,1312]{1,0:T(1,128)S(1)} %reshape.234), channel_id=1, source_target_pairs={{0,20},{4,16},{8,28},{12,24},{16,4},{20,0},{24,12},{28,8},{1,21},{... | collective-permute-start | bytes 15752 | tf_op jit(solution)/shard_map/ppermute | solution.py:680
  27.7 26.0 %collective-permute-start.8 = (bf16[256,1024]{1,0:T(8,128)(2,1)S(1)}, bf16[256,1024]{1,0:T(8,128)(2,1)S(1)}, u32[]{:S(2)}, u32[]{:S(2)}) collective-permute-start(bf16[256,1024]{1,0:T(8,128)(2,1)S(1)} %convert_element_type.311.refs_0_.refs_8_), channel_id=1, source_target_pairs={{0,4},{4,0},{1,5},{5,1},{2,6},{6,2},{3,7},{7,3},{8,12},{12,8},{9,1... | collective-permute-start | bytes 1572872 | tf_op jit(solution)/shard_map/ppermute | solution.py:664
  29.7 18.2 %collective-permute-start.14 = (bf16[128,2048]{1,0:T(8,128)(2,1)}, bf16[128,2048]{1,0:T(8,128)(2,1)}, u32[]{:S(2)}, u32[]{:S(2)}) collective-permute-start(bf16[128,2048]{1,0:T(8,128)(2,1)} %get-tuple-element.105), channel_id=1, source_target_pairs={{0,16},{8,24},{16,0},{24,8},{1,17},{9,25},{17,1},{25,9},{2,18},{10... | collective-permute-start | bytes 1572872 | tf_op jit(solution)/shard_map/ppermute | solution.py:655
  31.3 37.1 %collective-permute-start.11 = (bf16[128,2048]{1,0:T(8,128)(2,1)}, bf16[128,2048]{1,0:T(8,128)(2,1)}, u32[]{:S(2)}, u32[]{:S(2)}) collective-permute-start(bf16[128,2048]{1,0:T(8,128)(2,1)} %get-tuple-element.104.refs_0_), channel_id=1, source_target_pairs={{0,4},{4,0},{1,5},{5,1},{2,6},{6,2},{3,7},{7,3},{8,12},{12,8},{9,1... | collective-permute-start | bytes 1572872 | tf_op jit(solution)/shard_map/ppermute | solution.py:664
  31.9 37.5 %collective-permute-start.18 = (bf16[256,1024]{1,0:T(8,128)(2,1)S(1)}, bf16[256,1024]{1,0:T(8,128)(2,1)}, u32[]{:S(2)}, u32[]{:S(2)}) collective-permute-start(bf16[256,1024]{1,0:T(8,128)(2,1)S(1)} %dynamic-slice_bitcast_fusion.6.refs_8_), channel_id=1, source_target_pairs={{0,16},{8,24},{16,0},{24,8},{1,17},{9,25},{17,1},{25,9},{2,18},{10... | collective-permute-start | bytes 1572872 | tf_op jit(solution)/shard_map/ppermute | solution.py:655
  32.1 37.3 %collective-permute-start.7 = (bf16[256,1024]{1,0:T(8,128)(2,1)}, bf16[256,1024]{1,0:T(8,128)(2,1)S(1)}, u32[]{:S(2)}, u32[]{:S(2)}) collective-permute-start(bf16[256,1024]{1,0:T(8,128)(2,1)} %dynamic-slice_bitcast_fusion.7), channel_id=1, source_target_pairs={{0,8},{8,0},{16,24},{24,16},{1,9},{9,1},{17,25},{25,17},{2,10},{10... | collective-permute-start | bytes 1572872 | tf_op jit(solution)/shard_map/ppermute | solution.py:655
  47.9 35.1 %collective-permute-start.15 = (bf16[128,2048]{1,0:T(8,128)(2,1)}, bf16[128,2048]{1,0:T(8,128)(2,1)S(1)}, u32[]{:S(2)}, u32[]{:S(2)}) collective-permute-start(bf16[128,2048]{1,0:T(8,128)(2,1)} %collective-permute-done.14.refs_4_), channel_id=1, source_target_pairs={{0,4},{4,0},{1,5},{5,1},{2,6},{6,2},{3,7},{7,3},{8,12},{12,8},{9,1... | collective-permute-start | bytes 1572872 | tf_op jit(solution)/shard_map/ppermute | solution.py:664
  53.7 32.4 %collective-permute-start.12 = (bf16[128,2048]{1,0:T(8,128)(2,1)}, bf16[128,2048]{1,0:T(8,128)(2,1)S(1)}, u32[]{:S(2)}, u32[]{:S(2)}) collective-permute-start(bf16[128,2048]{1,0:T(8,128)(2,1)} %get-tuple-element.104.refs_0_), channel_id=1, source_target_pairs={{0,8},{8,0},{16,24},{24,16},{1,9},{9,1},{17,25},{25,17},{2,10},{10... | collective-permute-start | bytes 1572872 | tf_op jit(solution)/shard_map/ppermute | solution.py:655
  68.4 19.0 %collective-permute-start.13 = (bf16[128,2048]{1,0:T(8,128)(2,1)}, bf16[128,2048]{1,0:T(8,128)(2,1)}, u32[]{:S(2)}, u32[]{:S(2)}) collective-permute-start(bf16[128,2048]{1,0:T(8,128)(2,1)} %collective-permute-done.11.refs_1_), channel_id=1, source_target_pairs={{0,8},{8,0},{16,24},{24,16},{1,9},{9,1},{17,25},{25,17},{2,10},{10... | collective-permute-start | bytes 1572872 | tf_op jit(solution)/shard_map/ppermute | solution.py:655
  69.4 18.1 %collective-permute-start.16 = (bf16[128,2048]{1,0:T(8,128)(2,1)}, bf16[128,2048]{1,0:T(8,128)(2,1)}, u32[]{:S(2)}, u32[]{:S(2)}) collective-permute-start(bf16[128,2048]{1,0:T(8,128)(2,1)} %collective-permute-done.14.refs_4_), channel_id=1, source_target_pairs={{0,8},{8,0},{16,24},{24,16},{1,9},{9,1},{17,25},{25,17},{2,10},{10... | collective-permute-start | bytes 1572872 | tf_op jit(solution)/shard_map/ppermute | solution.py:655
  69.4 18.1 %collective-permute-start.19 = (bf16[256,1024]{1,0:T(8,128)(2,1)S(1)}, bf16[256,1024]{1,0:T(8,128)(2,1)}, u32[]{:S(2)}, u32[]{:S(2)}) collective-permute-start(bf16[256,1024]{1,0:T(8,128)(2,1)S(1)} %collective-permute-done.7.refs_9_), channel_id=1, source_target_pairs={{0,16},{8,24},{16,0},{24,8},{1,17},{9,25},{17,1},{25,9},{2,18},{10... | collective-permute-start | bytes 1572872 | tf_op jit(solution)/shard_map/ppermute | solution.py:655
  86.9 17.0 %collective-permute-start.9 = (bf16[256,1024]{1,0:T(8,128)(2,1)S(1)}, bf16[256,1024]{1,0:T(8,128)(2,1)S(1)}, u32[]{:S(2)}, u32[]{:S(2)}) collective-permute-start(bf16[256,1024]{1,0:T(8,128)(2,1)S(1)} %convert_element_type.311.refs_0_.refs_8_), channel_id=1, source_target_pairs={{0,8},{8,0},{16,24},{24,16},{1,9},{9,1},{17,25},{25,17},{2,10},{10... | collective-permute-start | bytes 1572872 | tf_op jit(solution)/shard_map/ppermute | solution.py:655
  87.4 16.5 %collective-permute-start.10 = (bf16[256,1024]{1,0:T(8,128)(2,1)}, bf16[256,1024]{1,0:T(8,128)(2,1)S(1)}, u32[]{:S(2)}, u32[]{:S(2)}) collective-permute-start(bf16[256,1024]{1,0:T(8,128)(2,1)} %copy-done.19), channel_id=1, source_target_pairs={{0,8},{8,0},{16,24},{24,16},{1,9},{9,1},{17,25},{25,17},{2,10},{10... | collective-permute-start | bytes 1572872 | tf_op jit(solution)/shard_map/ppermute | solution.py:655
  115.2 48.3 %collective-permute-start.20 = (bf16[512,1024]{1,0:T(8,128)(2,1)S(1)}, bf16[512,1024]{1,0:T(8,128)(2,1)S(1)}, u32[]{:S(2)}, u32[]{:S(2)}) collective-permute-start(bf16[512,1024]{1,0:T(8,128)(2,1)S(1)} %get-tuple-element.117), channel_id=1, source_target_pairs={{0,16},{8,24},{16,0},{24,8},{1,17},{9,25},{17,1},{25,9},{2,18},{10... | collective-permute-start | bytes 3145736 | tf_op jit(solution)/shard_map/ppermute | solution.py:655
  115.2 52.0 %collective-permute-start.22 = (bf16[2,256,1024]{2,1,0:T(8,128)(2,1)S(1)}, bf16[2,256,1024]{2,1,0:T(8,128)(2,1)S(1)}, u32[]{:S(2)}, u32[]{:S(2)}) collective-permute-start(bf16[2,256,1024]{2,1,0:T(8,128)(2,1)S(1)} %copy-done.57), channel_id=1, source_target_pairs={{0,8},{8,0},{16,24},{24,16},{1,9},{9,1},{17,25},{25,17},{2,10},{10... | collective-permute-start | bytes 3145736 | tf_op jit(solution)/shard_map/ppermute | solution.py:655
  212.2 37.3 %collective-permute-start.27 = (bf16[2,384,1024]{2,1,0:T(8,128)(2,1)S(1)}, bf16[2,384,1024]{2,1,0:T(8,128)(2,1)S(1)}, u32[]{:S(2)}, u32[]{:S(2)}) collective-permute-start(bf16[2,384,1024]{2,1,0:T(8,128)(2,1)S(1)} %dynamic-slice_bitcast_fusion.2), channel_id=1, source_target_pairs={{0,4},{4,0},{1,5},{5,1},{2,6},{6,2},{3,7},{7,3},{8,12},{12,8},{9,1... | collective-permute-start | bytes 4718600 | tf_op jit(solution)/shard_map/ppermute | solution.py:664
  218.8 31.8 %collective-permute-start.26 = (bf16[512,1024]{1,0:T(8,128)(2,1)S(1)}, bf16[512,1024]{1,0:T(8,128)(2,1)S(1)}, u32[]{:S(2)}, u32[]{:S(2)}) collective-permute-start(bf16[512,1024]{1,0:T(8,128)(2,1)S(1)} %fusion.61), channel_id=1, source_target_pairs={{0,16},{8,24},{16,0},{24,8},{1,17},{9,25},{17,1},{25,9},{2,18},{10... | collective-permute-start | bytes 3145736 | tf_op jit(solution)/shard_map/ppermute | solution.py:655
  228.4 61.9 %collective-permute-start.28 = (bf16[2,128,3072]{2,1,0:T(8,128)(2,1)}, bf16[2,128,3072]{2,1,0:T(8,128)(2,1)}, u32[]{:S(2)}, u32[]{:S(2)}) collective-permute-start(bf16[2,128,3072]{2,1,0:T(8,128)(2,1)} %dynamic-slice_bitcast_fusion.1), channel_id=1, source_target_pairs={{0,4},{4,0},{1,5},{5,1},{2,6},{6,2},{3,7},{7,3},{8,12},{12,8},{9,1... | collective-permute-start | bytes 4718600 | tf_op jit(solution)/shard_map/ppermute | solution.py:664
  250.2 28.2 %collective-permute-start.30 = (bf16[384,1024]{1,0:T(8,128)(2,1)S(1)}, bf16[384,1024]{1,0:T(8,128)(2,1)}, u32[]{:S(2)}, u32[]{:S(2)}) collective-permute-start(bf16[384,1024]{1,0:T(8,128)(2,1)S(1)} %get-tuple-element.211), channel_id=1, source_target_pairs={{0,16},{8,24},{16,0},{24,8},{1,17},{9,25},{17,1},{25,9},{2,18},{10... | collective-permute-start | bytes 2359304 | tf_op jit(solution)/shard_map/ppermute | solution.py:655
  251.6 35.5 %collective-permute-start.29 = (bf16[128,3072]{1,0:T(8,128)(2,1)}, bf16[128,3072]{1,0:T(8,128)(2,1)}, u32[]{:S(2)}, u32[]{:S(2)}) collective-permute-start(bf16[128,3072]{1,0:T(8,128)(2,1)} %dynamic-slice_bitcast_fusion.5), channel_id=1, source_target_pairs={{0,16},{8,24},{16,0},{24,8},{1,17},{9,25},{17,1},{25,9},{2,18},{10... | collective-permute-start | bytes 2359304 | tf_op jit(solution)/shard_map/ppermute | solution.py:655
  282.8 34.3 %collective-permute-start.32 = (bf16[128,3072]{1,0:T(8,128)(2,1)}, bf16[128,3072]{1,0:T(8,128)(2,1)}, u32[]{:S(2)}, u32[]{:S(2)}) collective-permute-start(bf16[128,3072]{1,0:T(8,128)(2,1)} %dynamic-slice_bitcast_fusion.4), channel_id=1, source_target_pairs={{0,16},{8,24},{16,0},{24,8},{1,17},{9,25},{17,1},{25,9},{2,18},{10... | collective-permute-start | bytes 2359304 | tf_op jit(solution)/shard_map/ppermute | solution.py:655
  287.1 127.3 %all-reduce.11.cloned.1.call-start = ((), (), s32[]{:S(2)}) async-start(), calls=%async_computation.4 | async-start | bytes 3145728 | tf_op jit(solution)/shard_map/psum | solution.py:882
  288.7 30.2 %collective-permute-start.33 = (bf16[128,3072]{1,0:T(8,128)(2,1)S(1)}, bf16[128,3072]{1,0:T(8,128)(2,1)S(1)}, u32[]{:S(2)}, u32[]{:S(2)}) collective-permute-start(bf16[128,3072]{1,0:T(8,128)(2,1)S(1)} %fusion.19), channel_id=1, source_target_pairs={{0,4},{4,0},{1,5},{5,1},{2,6},{6,2},{3,7},{7,3},{8,12},{12,8},{9,1... | collective-permute-start | bytes 2359304 | tf_op jit(solution)/shard_map/ppermute | solution.py:664
  292.7 27.3 %collective-permute-start.31 = (bf16[128,3072]{1,0:T(8,128)(2,1)S(1)}, bf16[128,3072]{1,0:T(8,128)(2,1)S(1)}, u32[]{:S(2)}, u32[]{:S(2)}) collective-permute-start(bf16[128,3072]{1,0:T(8,128)(2,1)S(1)} %get-tuple-element.207), channel_id=1, source_target_pairs={{0,16},{8,24},{16,0},{24,8},{1,17},{9,25},{17,1},{25,9},{2,18},{10... | collective-permute-start | bytes 2359304 | tf_op jit(solution)/shard_map/ppermute | solution.py:655
  321.0 9.9 %collective-permute-start.35 = (bf16[128,3072]{1,0:T(8,128)(2,1)}, bf16[128,3072]{1,0:T(8,128)(2,1)}, u32[]{:S(2)}, u32[]{:S(2)}) collective-permute-start(bf16[128,3072]{1,0:T(8,128)(2,1)} %add_convert_fusion.1), channel_id=1, source_target_pairs={{0,8},{8,0},{16,24},{24,16},{1,9},{9,1},{17,25},{25,17},{2,10},{10... | collective-permute-start | bytes 2359304 | tf_op jit(solution)/shard_map/ppermute | solution.py:655
  328.7 11.0 %collective-permute-start.34 = (bf16[2,2,128,2048]{3,2,0,1:T(8,128)(2,1)}, bf16[2,2,128,2048]{3,2,0,1:T(8,128)(2,1)}, u32[]{:S(2)}, u32[]{:S(2)}) collective-permute-start(bf16[2,2,128,2048]{3,2,0,1:T(8,128)(2,1)} %copy_bitcast_fusion), channel_id=1, source_target_pairs={{0,8},{8,0},{16,24},{24,16},{1,9},{9,1},{17,25},{25,17},{2,10},{10... | collective-permute-start | bytes 6291464 | tf_op jit(solution)/shard_map/ppermute | solution.py:655
  343.4 38.8 %collective-permute-start.37 = (bf16[2,128,2048]{2,1,0:T(8,128)(2,1)}, bf16[2,128,2048]{2,1,0:T(8,128)(2,1)}, u32[]{:S(2)}, u32[]{:S(2)}) collective-permute-start(bf16[2,128,2048]{2,1,0:T(8,128)(2,1)} %get-tuple-element.210), channel_id=1, source_target_pairs={{0,4},{4,0},{1,5},{5,1},{2,6},{6,2},{3,7},{7,3},{8,12},{12,8},{9,1... | collective-permute-start | bytes 3145736 | tf_op jit(solution)/shard_map/ppermute | solution.py:664
  344.9 35.3 %collective-permute-start.38 = (bf16[256,1024]{1,0:T(8,128)(2,1)}, bf16[256,1024]{1,0:T(8,128)(2,1)}, u32[]{:S(2)}, u32[]{:S(2)}) collective-permute-start(bf16[256,1024]{1,0:T(8,128)(2,1)} %get-tuple-element.213), channel_id=1, source_target_pairs={{0,4},{4,0},{1,5},{5,1},{2,6},{6,2},{3,7},{7,3},{8,12},{12,8},{9,1... | collective-permute-start | bytes 1572872 | tf_op jit(solution)/shard_map/ppermute | solution.py:664
  345.4 150.0 %all-reduce.9.cloned.1.call-start = ((), (), s32[]{:S(2)}) async-start(), calls=%async_computation.3 | async-start | bytes 3145728 | tf_op jit(solution)/shard_map/psum | solution.py:898
  384.8 35.9 %collective-permute-start.39 = (bf16[512,1024]{1,0:T(8,128)(2,1)}, bf16[512,1024]{1,0:T(8,128)(2,1)}, u32[]{:S(2)}, u32[]{:S(2)}) collective-permute-start(bf16[512,1024]{1,0:T(8,128)(2,1)} %slice.65), channel_id=1, source_target_pairs={{0,16},{8,24},{16,0},{24,8},{1,17},{9,25},{17,1},{25,9},{2,18},{10... | collective-permute-start | bytes 3145736 | tf_op jit(solution)/shard_map/ppermute | solution.py:655
  386.3 40.7 %collective-permute-start.23 = (bf16[512,1024]{1,0:T(8,128)(2,1)}, bf16[512,1024]{1,0:T(8,128)(2,1)}, u32[]{:S(2)}, u32[]{:S(2)}) collective-permute-start(bf16[512,1024]{1,0:T(8,128)(2,1)} %get-tuple-element.122), channel_id=1, source_target_pairs={{0,8},{8,0},{16,24},{24,16},{1,9},{9,1},{17,25},{25,17},{2,10},{10... | collective-permute-start | bytes 3145736 | tf_op jit(solution)/shard_map/ppermute | solution.py:655
  386.3 34.4 %collective-permute-start.41 = (bf16[128,2048]{1,0:T(8,128)(2,1)}, bf16[128,2048]{1,0:T(8,128)(2,1)}, u32[]{:S(2)}, u32[]{:S(2)}) collective-permute-start(bf16[128,2048]{1,0:T(8,128)(2,1)} %get-tuple-element.217), channel_id=1, source_target_pairs={{0,16},{8,24},{16,0},{24,8},{1,17},{9,25},{17,1},{25,9},{2,18},{10... | collective-permute-start | bytes 1572872 | tf_op jit(solution)/shard_map/ppermute | solution.py:655
  423.2 10.3 %collective-permute-start.42 = (f32[1,288]{1,0:T(1,128)S(1)}, f32[1,288]{1,0:T(1,128)S(1)}, u32[]{:S(2)}, u32[]{:S(2)}) collective-permute-start(f32[1,288]{1,0:T(1,128)S(1)} %get-tuple-element.242), channel_id=1, source_target_pairs={{0,4},{4,0},{8,12},{12,8},{16,20},{20,16},{24,28},{28,24},{1,5},{5... | collective-permute-start | bytes 3464 | tf_op jit(solution)/shard_map/ppermute | solution.py:680
  424.7 9.1 %collective-permute-start.43 = (f32[1,288]{1,0:T(1,128)S(1)}, f32[1,288]{1,0:T(1,128)S(1)}, u32[]{:S(2)}, u32[]{:S(2)}) collective-permute-start(f32[1,288]{1,0:T(1,128)S(1)} %get-tuple-element.241), channel_id=1, source_target_pairs={{0,8},{4,12},{8,0},{12,4},{16,24},{20,28},{24,16},{28,20},{1,9},{5... | collective-permute-start | bytes 3464 | tf_op jit(solution)/shard_map/ppermute | solution.py:680
  424.8 10.4 %collective-permute-start.44 = (f32[1,288]{1,0:T(1,128)S(1)}, f32[1,288]{1,0:T(1,128)S(1)}, u32[]{:S(2)}, u32[]{:S(2)}) collective-permute-start(f32[1,288]{1,0:T(1,128)S(1)} %get-tuple-element.240), channel_id=1, source_target_pairs={{0,12},{4,8},{8,4},{12,0},{16,28},{20,24},{24,20},{28,16},{1,13},{... | collective-permute-start | bytes 3464 | tf_op jit(solution)/shard_map/ppermute | solution.py:680
  425.4 9.9 %collective-permute-start.45 = (f32[1,288]{1,0:T(1,128)S(1)}, f32[1,288]{1,0:T(1,128)S(1)}, u32[]{:S(2)}, u32[]{:S(2)}) collective-permute-start(f32[1,288]{1,0:T(1,128)S(1)} %get-tuple-element.239), channel_id=1, source_target_pairs={{0,16},{4,20},{8,24},{12,28},{16,0},{20,4},{24,8},{28,12},{1,17},{... | collective-permute-start | bytes 3464 | tf_op jit(solution)/shard_map/ppermute | solution.py:680
  426.9 8.8 %collective-permute-start.46 = (f32[1,288]{1,0:T(1,128)S(1)}, f32[1,288]{1,0:T(1,128)S(1)}, u32[]{:S(2)}, u32[]{:S(2)}) collective-permute-start(f32[1,288]{1,0:T(1,128)S(1)} %get-tuple-element.238), channel_id=1, source_target_pairs={{0,20},{4,16},{8,28},{12,24},{16,4},{20,0},{24,12},{28,8},{1,21},{... | collective-permute-start | bytes 3464 | tf_op jit(solution)/shard_map/ppermute | solution.py:680
  435.1 14.3 %collective-permute-start.40 = (bf16[256,1024]{1,0:T(8,128)(2,1)S(1)}, bf16[256,1024]{1,0:T(8,128)(2,1)S(1)}, u32[]{:S(2)}, u32[]{:S(2)}) collective-permute-start(bf16[256,1024]{1,0:T(8,128)(2,1)S(1)} %get-tuple-element.232), channel_id=1, source_target_pairs={{0,8},{8,0},{16,24},{24,16},{1,9},{9,1},{17,25},{25,17},{2,10},{10... | collective-permute-start | bytes 1572872 | tf_op jit(solution)/shard_map/ppermute | solution.py:655
  435.3 15.3 %collective-permute-start.24 = (bf16[256,1024]{1,0:T(8,128)(2,1)S(1)}, bf16[256,1024]{1,0:T(8,128)(2,1)S(1)}, u32[]{:S(2)}, u32[]{:S(2)}) collective-permute-start(bf16[256,1024]{1,0:T(8,128)(2,1)S(1)} %get-tuple-element.235), channel_id=1, source_target_pairs={{0,8},{8,0},{16,24},{24,16},{1,9},{9,1},{17,25},{25,17},{2,10},{10... | collective-permute-start | bytes 1572872 | tf_op jit(solution)/shard_map/ppermute | solution.py:655
  437.8 11.0 %collective-permute-start.49 = (f32[1,288]{1,0:T(1,128)S(1)}, f32[1,288]{1,0:T(1,128)S(1)}, u32[]{:S(2)}, u32[]{:S(2)}) collective-permute-start(f32[1,288]{1,0:T(1,128)S(1)} %add_add_fusion), channel_id=1, source_target_pairs={{0,1},{1,0},{2,3},{3,2},{4,5},{5,4},{6,7},{7,6},{8,9},{9,8},{10,11... | collective-permute-start | bytes 3464 | tf_op jit(solution)/shard_map/ppermute | solution.py:914
  439.0 9.8 %collective-permute-start.50 = (f32[1,288]{1,0:T(1,128)S(1)}, f32[1,288]{1,0:T(1,128)S(1)}, u32[]{:S(2)}, u32[]{:S(2)}) collective-permute-start(f32[1,288]{1,0:T(1,128)S(1)} %add_add_fusion), channel_id=1, source_target_pairs={{0,2},{1,3},{2,0},{3,1},{4,6},{5,7},{6,4},{7,5},{8,10},{9,11},{10,... | collective-permute-start | bytes 3464 | tf_op jit(solution)/shard_map/ppermute | solution.py:914
  440.1 8.6 %collective-permute-start.51 = (f32[1,288]{1,0:T(1,128)S(1)}, f32[1,288]{1,0:T(1,128)S(1)}, u32[]{:S(2)}, u32[]{:S(2)}) collective-permute-start(f32[1,288]{1,0:T(1,128)S(1)} %add_add_fusion), channel_id=1, source_target_pairs={{0,3},{1,2},{2,1},{3,0},{4,7},{5,6},{6,5},{7,4},{8,11},{9,10},{10,... | collective-permute-start | bytes 3464 | tf_op jit(solution)/shard_map/ppermute | solution.py:914
  (71 other events, 899.7 us)
Sparse Core Ops, SparseCore 0:
  10.5 67.0 all-gather.4
  80.0 94.0 all-gather.2
  287.2 43.6 all-reduce.6
  345.6 68.8 all-reduce.10
  427.0 68.3 all-reduce.8

commit v7 on v6

--- a/solution.py
+++ b/solution.py
@@ -584,7 +584,7 @@
     weight_ref, first_ref, second_ref, new_first, new_second, new_weight, grad = refs[-7:]
     for s, cut in enumerate(cuts):
 
-        @pl.when((pl.program_id(1) ^ key_ref[0]) == s)
+        @pl.when((pl.program_id(1) ^ key_ref[0]) % len(cuts) == s)
         def _():
             grad[...] = cut[...].astype(FULL)
 
@@ -859,6 +859,10 @@
         shrink_cut = send_x(next_cut(pick(shrink_cuts, 1, mine), shrink_sent, 0, chip, chips))
         grad_slots = lax.optimization_barrier((*grad_slots, *line))[:chips]
         grad_all = jnp.concatenate(grad_slots)
+        grad_out = dot_tn(attended, grad_all).astype(LOW)
+        out_cuts = grad_out.reshape(2, inner, out_weight.shape[0], D)
+        out_sent = [swap_core(pick(out_cuts, 0, core ^ 1))]
+        attended = after(attended, out_cuts)
         grad, back_all, gains_first_part = back_part(0, attended, None)
 
         line[:] = [gains_first_part]
@@ -867,6 +871,7 @@
         own_near = first_over_x(0, *line)
         own_sent = [swap_grp(next_sum(*own_far[t - 1]), t) for t in range(1, inner)]
         other_cut = send_x(next_cut(pick(other_rows, 1, mine), other_sent, 0, chip, chips))
+        out_cut = send_y(next_cut(pick(out_cuts, 0, core), out_sent, 0, mine, inner))
         attended, back_all, grad = lax.optimization_barrier((attended, back_all, grad, *line))[:3]
         grad, back_all, head_gains = back_part(1, attended, (back_all, grad))
 
@@ -874,30 +879,22 @@
         head_gains = head_gains + gains_first_part
         own_cut = next_sum(next_sum(*own_near), own_sent)
         other_cut = swap_core(next_sum(*other_cut))
-        qkv_cuts, qkv_sent = cut_qkv(after(grad, *line))
-        own_cut, other_cut, total_shrink = lax.optimization_barrier(
-            (own_cut, other_cut, total_shrink, qkv_cuts, *line)
-        )[:3]
+        own_cut, other_cut, total_shrink, grad, back_all = lax.optimization_barrier(
+            (own_cut, other_cut, total_shrink, grad, back_all, *line)
+        )[:5]
         line[:] = [own_cut]
         own_cut, other_cut = lax.psum((own_cut, other_cut), "rep")
-        grad_out = dot_tn(after(attended, *line), grad_all).astype(LOW)
-        out_cuts = grad_out.reshape(2, inner, out_weight.shape[0], D)
-        out_sent = [swap_core(pick(out_cuts, 0, core ^ 1))]
-        line[:] = [grad_out]
-        out_cut = send_y(next_cut(pick(out_cuts, 0, core), out_sent, 0, mine, inner))
+        qkv_cuts, qkv_sent = cut_qkv(grad)
         qkv_cut = send_y(next_cut(qkv_cuts, qkv_sent, 1, mine, inner))
         out_cut = next_sum(*out_cut)
         kept, sent = send_x(next_cut(*qkv_cut, 0, chip, chips))
-        shares = []
+        *qkv_cuts, out_cut, own_cut, other_cut, back_all = lax.optimization_barrier(
+            (kept, *sent, out_cut, own_cut, other_cut, back_all, *line)
+        )[: 4 + chips]
+        total_out, *qkv_cuts = lax.psum((out_cut, *qkv_cuts), "rep")
+        shares = [back_all[: 2 * block]]
         for s in range(1, chips):
-            share = after(back_all[2 * s * block : 2 * (s + 1) * block], kept)
-            shares.append(swap_chip(share, s))
-        *qkv_cuts, out_cut, own_cut, other_cut = lax.optimization_barrier(
-            (kept, *sent, out_cut, own_cut, other_cut, *line)
-        )[: 3 + chips]
-        total_out, *qkv_cuts = lax.psum((out_cut, *qkv_cuts), "rep")
-
-        shares = [back_all[: 2 * block]] + [after(value, *line) for value in shares]
+            shares.append(swap_chip(back_all[2 * s * block : 2 * (s + 1) * block], s))
         input_part, gain_part = norm_back(inputs, gain_one, sum_of(shares))
         gain_one_grad = jnp.sum(gain_part, axis=0)
         input_grad = (input_part + hidden_grad).astype(LOW)
@@ -933,13 +930,16 @@
             *adam_cuts(
                 key, qkv_cuts, qkv_weight, qkv_first, qkv_second, RATE_QKV, size, qkv_column
             ),
-            *adam_step(out_weight, out_first, out_second, total_out.astype(FULL), RATE_OUT),
+            *adam_cuts(
+                key, [total_out], out_weight, out_first, out_second, RATE_OUT, D // 4, lambda i, s: i
+            ),
             *adam_pair(
                 place, own_cut, other_cut, expand_weight, expand_first, expand_second, RATE_EXPAND,
                 FF // n,
             ),
-            *adam_step(
-                shrink_weight, shrink_first, shrink_second, total_shrink.astype(FULL), RATE_SHRINK
+            *adam_cuts(
+                key, [total_shrink], shrink_weight, shrink_first, shrink_second, RATE_SHRINK, D // 4,
+                lambda i, s: i,
             ),
             *adam_step(norm_gains, gains_first, gains_second, total_gains, RATE_GAINS),
         )

time: 522 us -> 526 us (level)
  other arithmetic: 57.7 us -> 38.2 us
  local copies, waits for them, and re-layouts: 33.3 us -> 49.5 us
  Pallas kernels: 126 us -> 134 us
    psum x1, waiting for transfers between devices: 43.8 us -> 21 us  [on_device(): total_out, *qkv_cuts = lax.psum((out_cut, *qkv_cuts), 'rep')]
    ppermute x27, waiting for transfers between devices: 67.2 us -> 88.2 us  [swap_ctx(): return lax.ppermute(value, 'ctx', [(i, i ^ s) for i in range(n)])]
    unnamed x136 -> x154, local copies, waits for them, and re-layouts: 17.1 us -> 32.8 us
    sub x3 -> x1, other arithmetic: 9.78 us -> 0.6 us  [adam_step(): weight - step_rate * (step_dir + WEIGHT_DECAY * weight)]
    pallas_call x1 -> x3, Pallas kernels: 7.22 us -> 13.4 us  [adam_cuts(): pl.pallas_call(functools.partial(adam_kernel, rate), out_shape=(shape, sh...]
    psum x1, waiting for transfers between devices: 1.68 us -> 7.84 us  [on_device(): total_shrink = lax.psum(shrink_cut, 'rep')]
    psum x1, waiting for transfers between devices: 21.7 us -> 27.7 us  [on_device(): own_cut, other_cut = lax.psum((own_cut, other_cut), 'rep')]
    ppermute x8, waiting for transfers between devices: 78.7 us -> 73.3 us  [swap_grp(): return lax.ppermute(value, 'grp', [(i, i ^ t) for i in range(inner)])]
  transfers between devices with their start and end apart: 57 -> 57, of which waited for: 17 -> 18; matrix products, arithmetic and copies ran while one was open for 18% -> 14% of each run, Pallas kernels for 17% -> 18%
where the time goes in v7:
time: 526 us; the launch traced here: 519 us
  waiting for transfers between devices  221 us (42%)
  Pallas kernels  134 us (25%)
  local copies, waits for them, and re-layouts  49.5 us (9%)
  starting transfers between devices  38.2 us (7%)
  other arithmetic  38.2 us (7%)
  matrix products  23.4 us (4%)
  between operations  15.3 us (3%)
    ppermute x27, waiting for transfers between devices, swap_ctx(): return lax.ppermute(value, 'ctx', [(i, i ^ s) for i in range(n)])  88.2 us
    ppermute x8, waiting for transfers between devices, swap_grp(): return lax.ppermute(value, 'grp', [(i, i ^ t) for i in range(inner)])  73.3 us
    pallas_call x2, Pallas kernels, back(): pl.pallas_call(functools.partial(back_kernel, n, inner, half), out_shape=...  47.5 us
    unnamed x154, local copies, waits for them, and re-layouts  32.8 us
    pallas_call x1, Pallas kernels, feed(): pl.pallas_call(functools.partial(feed_kernel, chips), out_shape=(wide(D),...  31.6 us
    psum x1, waiting for transfers between devices, on_device(): own_cut, other_cut = lax.psum((own_cut, other_cut), 'rep')  27.7 us
    pallas_call x2, Pallas kernels, attend(): pl.pallas_call(functools.partial(attend_kernel, n, inner, first, bool(bas...  24.6 us
    dot_general x4, matrix products, dot_tn(): lax.dot_general(a, b, (((0,), (0,)), ((), ())), preferred_element_type=FULL)  23.4 us
  transfers between devices with their start and end apart: 57, of which 18 were waited for; matrix products, arithmetic and copies ran while one was open for 14% of the time, Pallas kernels for 18%

profile of v7, /device:TPU:0, one launch (start us, length us, event | category | flops | bytes accessed | tf_op | source)
XLA Modules:
  0.0 519.2 jit_solution(8721159436084366986)
XLA Ops:
  7.3 2.5 convert_element_type.310
  9.9 3.2 convert_element_type.309
  13.3 3.0 collective-permute-start
  16.5 1.9 collective-permute-start.3
  19.9 1.8 fusion.27
  25.1 1.8 fusion.28
  32.3 2.0 collective-permute-start.8
  36.8 22.4 %collective-permute-done.14.refs_4_ = bf16[128,2048]{1,0:T(8,128)(2,1)S(1)} collective-permute-done((bf16[128,2048]{1,0:T(8,128)(2,1)}, bf16[128,2048]{1,0:T(8,128)(2,1)S(1)}, u32[]{:S(2)}, u32[]{:S(2)}) %collective-permute-start.14) | collective-permute-done | bytes 524320 | tf_op jit(solution)/shard_map/ppermute | solution.py:655
  60.0 2.0 copy.41
  62.0 2.5 gather_fusion.1
  65.0 10.4 %collective-permute-done.11.refs_1_ = bf16[128,2048]{1,0:T(8,128)(2,1)} collective-permute-done((bf16[128,2048]{1,0:T(8,128)(2,1)}, bf16[128,2048]{1,0:T(8,128)(2,1)}, u32[]{:S(2)}, u32[]{:S(2)}) %collective-permute-start.11) | collective-permute-done | bytes 524320 | tf_op jit(solution)/shard_map/ppermute | solution.py:664
  78.7 7.3 %collective-permute-done.15.refs_5_ = bf16[128,2048]{1,0:T(8,128)(2,1)} collective-permute-done((bf16[128,2048]{1,0:T(8,128)(2,1)S(1)}, bf16[128,2048]{1,0:T(8,128)(2,1)}, u32[]{:S(2)}, u32[]{:S(2)}) %collective-permute-start.15) | collective-permute-done | bytes 524320 | tf_op jit(solution)/shard_map/ppermute | solution.py:664
  87.0 1.9 fusion.22
  89.7 5.8 %collective-permute-done.19.refs_11_ = bf16[256,1024]{1,0:T(8,128)(2,1)} collective-permute-done((bf16[256,1024]{1,0:T(8,128)(2,1)S(1)}, bf16[256,1024]{1,0:T(8,128)(2,1)}, u32[]{:S(2)}, u32[]{:S(2)}) %collective-permute-start.19) | collective-permute-done | bytes 524320 | tf_op jit(solution)/shard_map/ppermute | solution.py:655
  96.5 10.5 %project.1 = (bf16[1024,1024]{1,0:T(8,128)(2,1)S(1)}, bf16[1024,1024]{1,0:T(8,128)(2,1)S(1)}, bf16[1024,512]{1,0:T(8,128)(2,1)S(1)}, bf16[1024,512]{1,0:T(8,128)(2,1)S(1)}, bf16[1024,1536]{1,0:T(8,128)(2,1)}) custom-call(s32[2]{0:T(128)S(1)} %pad_add_fusion.place_ref, bf16[128,2048]{1,0:T(8,128)(2,1)} %get-tuple-element.110.refs_0_, ...), custom_call_target="tpu_custom_call" | custom-call | flops 4294967296 | bytes 16777216 | tf_op jit(solution)/shard_map/project/pallas_call | solution.py:150
  110.7 11.3 %attend.2 = (bf16[1024,1024]{1,0:T(8,128)(2,1)}, f32[1024,256]{1,0:T(8,128)S(1)}, bf16[512,1024]{1,0:T(8,128)(2,1)S(1)}) custom-call(s32[2]{0:T(128)S(1)} %pad_add_fusion.place_ref, bf16[256,1024]{1,0:T(8,128)(2,1)S(1)} %convert_element_type.305.refs_0_.refs_8_, bf16[256,1024]{1,0:T(8,128)(2,1)S(1)} %collective-permute-done.8.refs_1_.refs_9_, ...), custom_call_target="tpu_custom_call" | custom-call | flops 3221225472 | bytes 8388608 | tf_op jit(solution)/shard_map/attend/pallas_call | solution.py:258
  122.1 13.3 %attend.3 = (bf16[1024,1024]{1,0:T(8,128)(2,1)}, f32[1024,256]{1,0:T(8,128)S(1)}, bf16[512,1024]{1,0:T(8,128)(2,1)S(1)}) custom-call(s32[2]{0:T(128)S(1)} %pad_add_fusion.place_ref, bf16[256,1024]{1,0:T(8,128)(2,1)S(1)} %convert_element_type.305.refs_0_.refs_8_, ...), custom_call_target="tpu_custom_call", output_to_operand_aliasing={{0}: (10, {}), {1}: (11, {})} | custom-call | flops 3221225472 | bytes 8388608 | tf_op jit(solution)/shard_map/attend/pallas_call | solution.py:258
  135.5 34.2 %collective-permute-done.20 = bf16[512,1024]{1,0:T(8,128)(2,1)S(1)} collective-permute-done((bf16[512,1024]{1,0:T(8,128)(2,1)S(1)}, bf16[512,1024]{1,0:T(8,128)(2,1)S(1)}, u32[]{:S(2)}, u32[]{:S(2)}) %collective-permute-start.20) | collective-permute-done | bytes 1048608 | tf_op jit(solution)/shard_map/ppermute | solution.py:655
  175.7 31.6 %feed.1 = (bf16[1024,1024]{1,0:T(8,128)(2,1)}, bf16[1024,1024]{1,0:T(8,128)(2,1)}, bf16[1024,1536]{1,0:T(8,128)(2,1)}, bf16[1024,3072]{1,0:T(8,128)(2,1)}, bf16[...) custom-call(s32[2]{0:T(128)} %copy-done.36, ...), custom_call_target="tpu_custom_call" | custom-call | flops 19327352832 | bytes 31457280 | tf_op jit(solution)/shard_map/feed/pallas_call | solution.py:364
  207.4 6.0 %convolution_convert_fusion.1 = bf16[1536,1024]{1,0:T(8,128)(2,1)S(1)} fusion(bf16[1024,1536]{1,0:T(8,128)(2,1)} %get-tuple-element.132, bf16[1024,1024]{1,0:T(8,128)(2,1)} %get-tuple-element.133), kind=kOutput, calls=%fused_computation.3 | convolution fusion | flops 3222798336 | bytes 8388608 | tf_op jit(solution)/shard_map/dot_general | solution.py:51
  217.4 1.8 copy-done.69
  219.2 7.3 %convolution_convert_fusion = bf16[1024,3072]{1,0:T(8,128)(2,1)S(1)} fusion(bf16[1024,1024]{1,0:T(8,128)(2,1)S(1)} %copy-done.70, bf16[1024,3072]{1,0:T(8,128)(2,1)S(1)} %copy-done.69), kind=kOutput, calls=%fused_computation.2 | convolution fusion | flops 6445596672 | bytes 14680064 | tf_op jit(solution)/shard_map/dot_general | solution.py:51
  229.7 21.2 %collective-permute-done.26 = bf16[2,384,1024]{2,1,0:T(8,128)(2,1)S(1)} collective-permute-done((bf16[2,384,1024]{2,1,0:T(8,128)(2,1)S(1)}, bf16[2,384,1024]{2,1,0:T(8,128)(2,1)S(1)}, u32[]{:S(2)}, u32[]{:S(2)}) %collective-permute-start.26) | collective-permute-done | bytes 1572896 | tf_op jit(solution)/shard_map/ppermute | solution.py:664
  252.7 2.2 copy-done.54
  254.9 2.4 convolution_convert_fusion.3
  258.4 1.9 collective-permute-start.32
  261.4 23.6 %back.2 = (bf16[1024,2048]{1,0:T(8,128)(2,1)}, bf16[1024,1024]{1,0:T(8,128)(2,1)}, f32[8,128]{1,0:T(8,128)}) custom-call(s32[2]{0:T(128)} %copy-done.36, bf16[128,2048]{1,0:T(8,128)(2,1)} %get-tuple-element.110.refs_0_, bf16[128,2048]{1,0:T(8,128)(2,1)} %collective-permute-done.11.refs_1_, bf16[128,2048]{1,0:T(8,128)(2,1)} %collective-permute-done.12.refs_2_, ...), custom_call_target="tpu_custom_call" | custom-call | flops 5905580032 | bytes 31457280 | tf_op jit(solution)/shard_map/back/pallas_call | solution.py:528
  285.0 2.3 add_convert_fusion.3
  287.4 2.1 dynamic-slice_bitcast_fusion.5
  292.5 2.4 fusion.14
  297.7 23.9 %back.3 = (bf16[1024,2048]{1,0:T(8,128)(2,1)}, bf16[1024,1024]{1,0:T(8,128)(2,1)}, f32[8,128]{1,0:T(8,128)}) custom-call(s32[2]{0:T(128)} %copy-done.36, bf16[128,2048]{1,0:T(8,128)(2,1)} %get-tuple-element.110.refs_0_, bf16[128,2048]{1,0:T(8,128)(2,1)} %collective-permute-done.11.refs_1_, ...), custom_call_target="tpu_custom_call", output_to_operand_aliasing={{0}: (27, {})} | custom-call | flops 5905580032 | bytes 31457280 | tf_op jit(solution)/shard_map/back/pallas_call | solution.py:528
  324.3 2.2 collective-permute-done.34
  326.7 7.8 %all-reduce.7.cloned.1.call-done.refs_0_ = bf16[384,1024]{1,0:T(8,128)(2,1)} async-done(((bf16[384,1024]{1,0:T(8,128)(2,1)}), bf16[384,1024]{1,0:T(8,128)(2,1)}) %all-reduce.7.cloned.1.call-update) | async-done | bytes 786448 | tf_op jit(solution)/shard_map/psum | solution.py:870
  334.6 7.7 %convolution_convert_fusion.2 = bf16[1024,2048]{1,0:T(8,128)(2,1)S(1)} fusion(bf16[1024,1024]{1,0:T(8,128)(2,1)} %copy-done.42, bf16[1024,2048]{1,0:T(8,128)(2,1)} %get-tuple-element.163), kind=kOutput, calls=%fused_computation.4 | convolution fusion | flops 4297064448 | bytes 10485760 | tf_op jit(solution)/shard_map/dot_general | solution.py:51
  342.5 4.1 collective-permute-done.36
  346.6 2.1 fusion.11
  351.0 34.4 %collective-permute-done.38 = bf16[256,1024]{1,0:T(8,128)(2,1)S(1)} collective-permute-done((bf16[256,1024]{1,0:T(8,128)(2,1)S(1)}, bf16[256,1024]{1,0:T(8,128)(2,1)S(1)}, u32[]{:S(2)}, u32[]{:S(2)}) %collective-permute-start.38) | collective-permute-done | bytes 524320 | tf_op jit(solution)/shard_map/ppermute | solution.py:664
  386.4 2.8 fusion.24
  390.5 27.7 %all-reduce.11.cloned.1.call-done = (bf16[128,3072]{1,0:T(8,128)(2,1)}, bf16[128,3072]{1,0:T(8,128)(2,1)}) async-done(((bf16[128,3072]{1,0:T(8,128)(2,1)}, bf16[128,3072]{1,0:T(8,128)(2,1)}), (bf16[128,3072]{1,0:T(8,128)(2,1)}, bf16[128,3072]{1,0:T(8,128)(2,1)})) %all-reduce.11.cloned.1.call-update) | async-done | bytes 1572880 | tf_op jit(solution)/shard_map/psum | solution.py:886
  418.2 2.3 slice.65
  424.8 3.5 adam_cuts.5
  428.3 16.2 %collective-permute-done.40 = bf16[512,1024]{1,0:T(8,128)(2,1)} collective-permute-done((bf16[512,1024]{1,0:T(8,128)(2,1)}, bf16[512,1024]{1,0:T(8,128)(2,1)}, u32[]{:S(2)}, u32[]{:S(2)}) %collective-permute-start.40) | collective-permute-done | bytes 1048608 | tf_op jit(solution)/shard_map/ppermute | solution.py:655
  444.5 2.5 fusion.8
  452.4 4.7 fusion.7
  466.2 6.5 %adam_pair.1 = (f32[128,6144]{1,0:T(8,128)}, f32[128,6144]{1,0:T(8,128)}, f32[128,6144]{1,0:T(8,128)}) custom-call(s32[2]{0:T(128)S(1)} %copy-done.37, bf16[128,3072]{1,0:T(8,128)(2,1)S(1)} %copy-done.26, bf16[128,3072]{1,0:T(8,128)(2,1)S(1)} %copy-done.27, f32[128,6144]{1,0:T(8,128)S(1)} %copy-done.2, f32[128,6144]{1,0:T(8,128)S(1)} %copy-done.9, ...), custom_call_target="tpu_custom_call" | custom-call | flops 15728640 | bytes 20447232 | tf_op jit(solution)/shard_map/adam_pair/pallas_call | solution.py:630
  475.7 21.0 %all-reduce.9.cloned.1.call-done = (bf16[128,2048]{1,0:T(8,128)(2,1)}, bf16[128,2048]{1,0:T(8,128)(2,1)}, bf16[256,1024]{1,0:T(8,128)(2,1)}) async-done(((bf16[128,2048]{1,0:T(8,128)(2,1)}, bf16[128,2048]{1,0:T(8,128)(2,1)}, bf16[256,1024]{1,0:T(8,128)(2,1)}), (bf16[128,2048]{1,0:T(8,128)(2,1)}, bf16[128,2048]{1,0:T(8,128)(2,1)}, bf16[256,1024]{1,0:T(8,128)(2,1)})) %all-reduce.9.cloned.1.call-update) | async-done | bytes 1572880 | tf_op jit(solution)/shard_map/psum | solution.py:894
  499.1 2.6 adam_cuts.4
  504.9 7.3 %adam_cuts.3 = (f32[128,4096]{1,0:T(8,128)}, f32[128,4096]{1,0:T(8,128)}, f32[128,4096]{1,0:T(8,128)}) custom-call(s32[1]{0:T(128)} %bitcast.55.key_ref, bf16[128,2048]{1,0:T(8,128)(2,1)S(1)} %copy-done.33, bf16[128,2048]{1,0:T(8,128)(2,1)S(1)} %copy-done.34, f32[128,4096]{1,0:T(8,128)S(1)} %copy-done.6, f32[128,4096]{1,0:T(8,128)S(1)} %copy-done.16, ...), custom_call_target="tpu_custom_call" | custom-call | flops 10485760 | bytes 13631488 | tf_op jit(solution)/shard_map/adam_cuts/pallas_call | solution.py:600
  (311 shorter events, 81.9 us)
Async XLA Ops:
  7.2 167.5 %all-gather.5.cloned.1.call-start = ((), (), s32[]{:S(2)}) async-start(), calls=%async_computation.1 | async-start | bytes 7077888 | tf_op jit(solution)/shard_map/all_gather | solution.py:766
  9.8 165.3 %all-gather.3.cloned.1.call-start = ((), (), s32[]{:S(2)}) async-start(), calls=%async_computation | async-start | bytes 14155776 | tf_op jit(solution)/shard_map/all_gather | solution.py:766
  13.1 321.5 %all-reduce.7.cloned.1.call-start = ((), (), s32[]{:S(2)}) async-start(), calls=%async_computation.2 | async-start | bytes 1572864 | tf_op jit(solution)/shard_map/psum | solution.py:870
  13.3 16.1 %collective-permute-start = (f32[1,1312]{1,0:T(1,128)S(1)}, f32[1,1312]{1,0:T(1,128)S(1)}, u32[]{:S(2)}, u32[]{:S(2)}) collective-permute-start(f32[1,1312]{1,0:T(1,128)S(1)} %reshape.234), channel_id=1, source_target_pairs={{0,4},{4,0},{8,12},{12,8},{16,20},{20,16},{24,28},{28,24},{1,5},{5... | collective-permute-start | bytes 15752 | tf_op jit(solution)/shard_map/ppermute | solution.py:680
  16.3 13.5 %collective-permute-start.1 = (f32[1,1312]{1,0:T(1,128)S(1)}, f32[1,1312]{1,0:T(1,128)S(1)}, u32[]{:S(2)}, u32[]{:S(2)}) collective-permute-start(f32[1,1312]{1,0:T(1,128)S(1)} %reshape.234), channel_id=1, source_target_pairs={{0,8},{4,12},{8,0},{12,4},{16,24},{20,28},{24,16},{28,20},{1,9},{5... | collective-permute-start | bytes 15752 | tf_op jit(solution)/shard_map/ppermute | solution.py:680
  16.3 16.0 %collective-permute-start.2 = (f32[1,1312]{1,0:T(1,128)S(1)}, f32[1,1312]{1,0:T(1,128)S(1)}, u32[]{:S(2)}, u32[]{:S(2)}) collective-permute-start(f32[1,1312]{1,0:T(1,128)S(1)} %reshape.234), channel_id=1, source_target_pairs={{0,12},{4,8},{8,4},{12,0},{16,28},{20,24},{24,20},{28,16},{1,13},{... | collective-permute-start | bytes 15752 | tf_op jit(solution)/shard_map/ppermute | solution.py:680
  16.5 17.8 %collective-permute-start.3 = (f32[1,1312]{1,0:T(1,128)S(1)}, f32[1,1312]{1,0:T(1,128)S(1)}, u32[]{:S(2)}, u32[]{:S(2)}) collective-permute-start(f32[1,1312]{1,0:T(1,128)S(1)} %reshape.234), channel_id=1, source_target_pairs={{0,16},{4,20},{8,24},{12,28},{16,0},{20,4},{24,8},{28,12},{1,17},{... | collective-permute-start | bytes 15752 | tf_op jit(solution)/shard_map/ppermute | solution.py:680
  18.4 15.9 %collective-permute-start.4 = (f32[1,1312]{1,0:T(1,128)S(1)}, f32[1,1312]{1,0:T(1,128)S(1)}, u32[]{:S(2)}, u32[]{:S(2)}) collective-permute-start(f32[1,1312]{1,0:T(1,128)S(1)} %reshape.234), channel_id=1, source_target_pairs={{0,20},{4,16},{8,28},{12,24},{16,4},{20,0},{24,12},{28,8},{1,21},{... | collective-permute-start | bytes 15752 | tf_op jit(solution)/shard_map/ppermute | solution.py:680
  32.3 32.6 %collective-permute-start.8 = (bf16[256,1024]{1,0:T(8,128)(2,1)S(1)}, bf16[256,1024]{1,0:T(8,128)(2,1)S(1)}, u32[]{:S(2)}, u32[]{:S(2)}) collective-permute-start(bf16[256,1024]{1,0:T(8,128)(2,1)S(1)} %convert_element_type.305.refs_0_.refs_8_), channel_id=1, source_target_pairs={{0,4},{4,0},{1,5},{5,1},{2,6},{6,2},{3,7},{7,3},{8,12},{12,8},{9,1... | collective-permute-start | bytes 1572872 | tf_op jit(solution)/shard_map/ppermute | solution.py:664
  34.4 24.8 %collective-permute-start.14 = (bf16[128,2048]{1,0:T(8,128)(2,1)}, bf16[128,2048]{1,0:T(8,128)(2,1)S(1)}, u32[]{:S(2)}, u32[]{:S(2)}) collective-permute-start(bf16[128,2048]{1,0:T(8,128)(2,1)} %get-tuple-element.111), channel_id=1, source_target_pairs={{0,16},{8,24},{16,0},{24,8},{1,17},{9,25},{17,1},{25,9},{2,18},{10... | collective-permute-start | bytes 1572872 | tf_op jit(solution)/shard_map/ppermute | solution.py:655
  35.9 39.4 %collective-permute-start.11 = (bf16[128,2048]{1,0:T(8,128)(2,1)}, bf16[128,2048]{1,0:T(8,128)(2,1)}, u32[]{:S(2)}, u32[]{:S(2)}) collective-permute-start(bf16[128,2048]{1,0:T(8,128)(2,1)} %get-tuple-element.110.refs_0_), channel_id=1, source_target_pairs={{0,4},{4,0},{1,5},{5,1},{2,6},{6,2},{3,7},{7,3},{8,12},{12,8},{9,1... | collective-permute-start | bytes 1572872 | tf_op jit(solution)/shard_map/ppermute | solution.py:664
  36.5 40.5 %collective-permute-start.18 = (bf16[256,1024]{1,0:T(8,128)(2,1)S(1)}, bf16[256,1024]{1,0:T(8,128)(2,1)S(1)}, u32[]{:S(2)}, u32[]{:S(2)}) collective-permute-start(bf16[256,1024]{1,0:T(8,128)(2,1)S(1)} %dynamic-slice_bitcast_fusion.6.refs_8_), channel_id=1, source_target_pairs={{0,16},{8,24},{16,0},{24,8},{1,17},{9,25},{17,1},{25,9},{2,18},{10... | collective-permute-start | bytes 1572872 | tf_op jit(solution)/shard_map/ppermute | solution.py:655
  36.8 41.0 %collective-permute-start.7 = (bf16[256,1024]{1,0:T(8,128)(2,1)}, bf16[256,1024]{1,0:T(8,128)(2,1)S(1)}, u32[]{:S(2)}, u32[]{:S(2)}) collective-permute-start(bf16[256,1024]{1,0:T(8,128)(2,1)} %dynamic-slice_bitcast_fusion.7), channel_id=1, source_target_pairs={{0,8},{8,0},{16,24},{24,16},{1,9},{9,1},{17,25},{25,17},{2,10},{10... | collective-permute-start | bytes 1572872 | tf_op jit(solution)/shard_map/ppermute | solution.py:655
  59.2 26.8 %collective-permute-start.15 = (bf16[128,2048]{1,0:T(8,128)(2,1)S(1)}, bf16[128,2048]{1,0:T(8,128)(2,1)}, u32[]{:S(2)}, u32[]{:S(2)}) collective-permute-start(bf16[128,2048]{1,0:T(8,128)(2,1)S(1)} %collective-permute-done.14.refs_4_), channel_id=1, source_target_pairs={{0,4},{4,0},{1,5},{5,1},{2,6},{6,2},{3,7},{7,3},{8,12},{12,8},{9,1... | collective-permute-start | bytes 1572872 | tf_op jit(solution)/shard_map/ppermute | solution.py:664
  64.9 24.1 %collective-permute-start.12 = (bf16[128,2048]{1,0:T(8,128)(2,1)}, bf16[128,2048]{1,0:T(8,128)(2,1)}, u32[]{:S(2)}, u32[]{:S(2)}) collective-permute-start(bf16[128,2048]{1,0:T(8,128)(2,1)} %get-tuple-element.110.refs_0_), channel_id=1, source_target_pairs={{0,8},{8,0},{16,24},{24,16},{1,9},{9,1},{17,25},{25,17},{2,10},{10... | collective-permute-start | bytes 1572872 | tf_op jit(solution)/shard_map/ppermute | solution.py:655
  75.4 14.2 %collective-permute-start.13 = (bf16[128,2048]{1,0:T(8,128)(2,1)}, bf16[128,2048]{1,0:T(8,128)(2,1)}, u32[]{:S(2)}, u32[]{:S(2)}) collective-permute-start(bf16[128,2048]{1,0:T(8,128)(2,1)} %collective-permute-done.11.refs_1_), channel_id=1, source_target_pairs={{0,8},{8,0},{16,24},{24,16},{1,9},{9,1},{17,25},{25,17},{2,10},{10... | collective-permute-start | bytes 1572872 | tf_op jit(solution)/shard_map/ppermute | solution.py:655
  77.8 11.8 %collective-permute-start.16 = (bf16[128,2048]{1,0:T(8,128)(2,1)S(1)}, bf16[128,2048]{1,0:T(8,128)(2,1)}, u32[]{:S(2)}, u32[]{:S(2)}) collective-permute-start(bf16[128,2048]{1,0:T(8,128)(2,1)S(1)} %collective-permute-done.14.refs_4_), channel_id=1, source_target_pairs={{0,8},{8,0},{16,24},{24,16},{1,9},{9,1},{17,25},{25,17},{2,10},{10... | collective-permute-start | bytes 1572872 | tf_op jit(solution)/shard_map/ppermute | solution.py:655
  77.8 17.6 %collective-permute-start.19 = (bf16[256,1024]{1,0:T(8,128)(2,1)S(1)}, bf16[256,1024]{1,0:T(8,128)(2,1)}, u32[]{:S(2)}, u32[]{:S(2)}) collective-permute-start(bf16[256,1024]{1,0:T(8,128)(2,1)S(1)} %collective-permute-done.7.refs_9_), channel_id=1, source_target_pairs={{0,16},{8,24},{16,0},{24,8},{1,17},{9,25},{17,1},{25,9},{2,18},{10... | collective-permute-start | bytes 1572872 | tf_op jit(solution)/shard_map/ppermute | solution.py:655
  86.0 9.4 %collective-permute-start.17 = (bf16[128,2048]{1,0:T(8,128)(2,1)}, bf16[128,2048]{1,0:T(8,128)(2,1)}, u32[]{:S(2)}, u32[]{:S(2)}) collective-permute-start(bf16[128,2048]{1,0:T(8,128)(2,1)} %collective-permute-done.15.refs_5_), channel_id=1, source_target_pairs={{0,8},{8,0},{16,24},{24,16},{1,9},{9,1},{17,25},{25,17},{2,10},{10... | collective-permute-start | bytes 1572872 | tf_op jit(solution)/shard_map/ppermute | solution.py:655
  89.0 21.7 %collective-permute-start.9 = (bf16[256,1024]{1,0:T(8,128)(2,1)S(1)}, bf16[256,1024]{1,0:T(8,128)(2,1)S(1)}, u32[]{:S(2)}, u32[]{:S(2)}) collective-permute-start(bf16[256,1024]{1,0:T(8,128)(2,1)S(1)} %convert_element_type.305.refs_0_.refs_8_), channel_id=1, source_target_pairs={{0,8},{8,0},{16,24},{24,16},{1,9},{9,1},{17,25},{25,17},{2,10},{10... | collective-permute-start | bytes 1572872 | tf_op jit(solution)/shard_map/ppermute | solution.py:655
  89.6 21.1 %collective-permute-start.10 = (bf16[256,1024]{1,0:T(8,128)(2,1)S(1)}, bf16[256,1024]{1,0:T(8,128)(2,1)S(1)}, u32[]{:S(2)}, u32[]{:S(2)}) collective-permute-start(bf16[256,1024]{1,0:T(8,128)(2,1)S(1)} %collective-permute-done.8.refs_1_.refs_9_), channel_id=1, source_target_pairs={{0,8},{8,0},{16,24},{24,16},{1,9},{9,1},{17,25},{25,17},{2,10},{10... | collective-permute-start | bytes 1572872 | tf_op jit(solution)/shard_map/ppermute | solution.py:655
  121.9 47.7 %collective-permute-start.20 = (bf16[512,1024]{1,0:T(8,128)(2,1)S(1)}, bf16[512,1024]{1,0:T(8,128)(2,1)S(1)}, u32[]{:S(2)}, u32[]{:S(2)}) collective-permute-start(bf16[512,1024]{1,0:T(8,128)(2,1)S(1)} %get-tuple-element.123), channel_id=1, source_target_pairs={{0,16},{8,24},{16,0},{24,8},{1,17},{9,25},{17,1},{25,9},{2,18},{10... | collective-permute-start | bytes 3145736 | tf_op jit(solution)/shard_map/ppermute | solution.py:655
  122.0 50.1 %collective-permute-start.22 = (bf16[2,256,1024]{2,1,0:T(8,128)(2,1)S(1)}, bf16[2,256,1024]{2,1,0:T(8,128)(2,1)S(1)}, u32[]{:S(2)}, u32[]{:S(2)}) collective-permute-start(bf16[2,256,1024]{2,1,0:T(8,128)(2,1)S(1)} %copy-done.66), channel_id=1, source_target_pairs={{0,8},{8,0},{16,24},{24,16},{1,9},{9,1},{17,25},{25,17},{2,10},{10... | collective-permute-start | bytes 3145736 | tf_op jit(solution)/shard_map/ppermute | solution.py:655
  213.6 37.3 %collective-permute-start.26 = (bf16[2,384,1024]{2,1,0:T(8,128)(2,1)S(1)}, bf16[2,384,1024]{2,1,0:T(8,128)(2,1)S(1)}, u32[]{:S(2)}, u32[]{:S(2)}) collective-permute-start(bf16[2,384,1024]{2,1,0:T(8,128)(2,1)S(1)} %dynamic-slice_bitcast_fusion.2), channel_id=1, source_target_pairs={{0,4},{4,0},{1,5},{5,1},{2,6},{6,2},{3,7},{7,3},{8,12},{12,8},{9,1... | collective-permute-start | bytes 4718600 | tf_op jit(solution)/shard_map/ppermute | solution.py:664
  217.1 35.5 %collective-permute-start.28 = (bf16[512,1024]{1,0:T(8,128)(2,1)S(1)}, bf16[512,1024]{1,0:T(8,128)(2,1)S(1)}, u32[]{:S(2)}, u32[]{:S(2)}) collective-permute-start(bf16[512,1024]{1,0:T(8,128)(2,1)S(1)} %fusion.57), channel_id=1, source_target_pairs={{0,16},{8,24},{16,0},{24,8},{1,17},{9,25},{17,1},{25,9},{2,18},{10... | collective-permute-start | bytes 3145736 | tf_op jit(solution)/shard_map/ppermute | solution.py:655
  227.9 64.6 %collective-permute-start.31 = (bf16[2,128,3072]{2,1,0:T(8,128)(2,1)}, bf16[2,128,3072]{2,1,0:T(8,128)(2,1)}, u32[]{:S(2)}, u32[]{:S(2)}) collective-permute-start(bf16[2,128,3072]{2,1,0:T(8,128)(2,1)} %dynamic-slice_bitcast_fusion.1), channel_id=1, source_target_pairs={{0,4},{4,0},{1,5},{5,1},{2,6},{6,2},{3,7},{7,3},{8,12},{12,8},{9,1... | collective-permute-start | bytes 4718600 | tf_op jit(solution)/shard_map/ppermute | solution.py:664
  252.5 32.6 %collective-permute-start.27 = (bf16[384,1024]{1,0:T(8,128)(2,1)}, bf16[384,1024]{1,0:T(8,128)(2,1)}, u32[]{:S(2)}, u32[]{:S(2)}) collective-permute-start(bf16[384,1024]{1,0:T(8,128)(2,1)} %get-tuple-element.218), channel_id=1, source_target_pairs={{0,16},{8,24},{16,0},{24,8},{1,17},{9,25},{17,1},{25,9},{2,18},{10... | collective-permute-start | bytes 2359304 | tf_op jit(solution)/shard_map/ppermute | solution.py:655
  258.4 31.2 %collective-permute-start.32 = (bf16[128,3072]{1,0:T(8,128)(2,1)}, bf16[128,3072]{1,0:T(8,128)(2,1)}, u32[]{:S(2)}, u32[]{:S(2)}) collective-permute-start(bf16[128,3072]{1,0:T(8,128)(2,1)} %dynamic-slice_bitcast_fusion.4), channel_id=1, source_target_pairs={{0,16},{8,24},{16,0},{24,8},{1,17},{9,25},{17,1},{25,9},{2,18},{10... | collective-permute-start | bytes 2359304 | tf_op jit(solution)/shard_map/ppermute | solution.py:655
  261.4 35.1 %collective-permute-start.30 = (bf16[2,256,1024]{2,1,0:T(8,128)(2,1)}, bf16[2,256,1024]{2,1,0:T(8,128)(2,1)S(1)}, u32[]{:S(2)}, u32[]{:S(2)}) collective-permute-start(bf16[2,256,1024]{2,1,0:T(8,128)(2,1)} %dynamic-slice_bitcast_fusion.3), channel_id=1, source_target_pairs={{0,8},{8,0},{16,24},{24,16},{1,9},{9,1},{17,25},{25,17},{2,10},{10... | collective-permute-start | bytes 3145736 | tf_op jit(solution)/shard_map/ppermute | solution.py:655
  289.5 32.1 %collective-permute-start.29 = (bf16[128,3072]{1,0:T(8,128)(2,1)}, bf16[128,3072]{1,0:T(8,128)(2,1)}, u32[]{:S(2)}, u32[]{:S(2)}) collective-permute-start(bf16[128,3072]{1,0:T(8,128)(2,1)} %dynamic-slice_bitcast_fusion.5), channel_id=1, source_target_pairs={{0,16},{8,24},{16,0},{24,8},{1,17},{9,25},{17,1},{25,9},{2,18},{10... | collective-permute-start | bytes 2359304 | tf_op jit(solution)/shard_map/ppermute | solution.py:655
  289.6 128.6 %all-reduce.11.cloned.1.call-start = ((), (), s32[]{:S(2)}) async-start(), calls=%async_computation.4 | async-start | bytes 3145728 | tf_op jit(solution)/shard_map/psum | solution.py:886
  291.2 32.0 %collective-permute-start.33 = (bf16[128,3072]{1,0:T(8,128)(2,1)S(1)}, bf16[128,3072]{1,0:T(8,128)(2,1)S(1)}, u32[]{:S(2)}, u32[]{:S(2)}) collective-permute-start(bf16[128,3072]{1,0:T(8,128)(2,1)S(1)} %fusion.16), channel_id=1, source_target_pairs={{0,4},{4,0},{1,5},{5,1},{2,6},{6,2},{3,7},{7,3},{8,12},{12,8},{9,1... | collective-permute-start | bytes 2359304 | tf_op jit(solution)/shard_map/ppermute | solution.py:664
  295.0 31.5 %collective-permute-start.34 = (bf16[128,3072]{1,0:T(8,128)(2,1)S(1)}, bf16[128,3072]{1,0:T(8,128)(2,1)S(1)}, u32[]{:S(2)}, u32[]{:S(2)}) collective-permute-start(bf16[128,3072]{1,0:T(8,128)(2,1)S(1)} %get-tuple-element.213), channel_id=1, source_target_pairs={{0,16},{8,24},{16,0},{24,8},{1,17},{9,25},{17,1},{25,9},{2,18},{10... | collective-permute-start | bytes 2359304 | tf_op jit(solution)/shard_map/ppermute | solution.py:655
  348.7 37.6 %collective-permute-start.37 = (bf16[2,128,2048]{2,1,0:T(8,128)(2,1)}, bf16[2,128,2048]{2,1,0:T(8,128)(2,1)}, u32[]{:S(2)}, u32[]{:S(2)}) collective-permute-start(bf16[2,128,2048]{2,1,0:T(8,128)(2,1)} %get-tuple-element.216), channel_id=1, source_target_pairs={{0,4},{4,0},{1,5},{5,1},{2,6},{6,2},{3,7},{7,3},{8,12},{12,8},{9,1... | collective-permute-start | bytes 3145736 | tf_op jit(solution)/shard_map/ppermute | solution.py:664
  350.2 146.4 %all-reduce.9.cloned.1.call-start = ((), (), s32[]{:S(2)}) async-start(), calls=%async_computation.3 | async-start | bytes 3145728 | tf_op jit(solution)/shard_map/psum | solution.py:894
  350.3 35.1 %collective-permute-start.38 = (bf16[256,1024]{1,0:T(8,128)(2,1)S(1)}, bf16[256,1024]{1,0:T(8,128)(2,1)S(1)}, u32[]{:S(2)}, u32[]{:S(2)}) collective-permute-start(bf16[256,1024]{1,0:T(8,128)(2,1)S(1)} %copy-done.58), channel_id=1, source_target_pairs={{0,4},{4,0},{1,5},{5,1},{2,6},{6,2},{3,7},{7,3},{8,12},{12,8},{9,1... | collective-permute-start | bytes 1572872 | tf_op jit(solution)/shard_map/ppermute | solution.py:664
  389.2 29.0 %collective-permute-start.39 = (bf16[128,2048]{1,0:T(8,128)(2,1)}, bf16[128,2048]{1,0:T(8,128)(2,1)}, u32[]{:S(2)}, u32[]{:S(2)}) collective-permute-start(bf16[128,2048]{1,0:T(8,128)(2,1)} %get-tuple-element.223), channel_id=1, source_target_pairs={{0,16},{8,24},{16,0},{24,8},{1,17},{9,25},{17,1},{25,9},{2,18},{10... | collective-permute-start | bytes 1572872 | tf_op jit(solution)/shard_map/ppermute | solution.py:655
  420.4 24.1 %collective-permute-start.40 = (bf16[512,1024]{1,0:T(8,128)(2,1)}, bf16[512,1024]{1,0:T(8,128)(2,1)}, u32[]{:S(2)}, u32[]{:S(2)}) collective-permute-start(bf16[512,1024]{1,0:T(8,128)(2,1)} %slice.65), channel_id=1, source_target_pairs={{0,16},{8,24},{16,0},{24,8},{1,17},{9,25},{17,1},{25,9},{2,18},{10... | collective-permute-start | bytes 3145736 | tf_op jit(solution)/shard_map/ppermute | solution.py:655
  421.9 29.0 %collective-permute-start.23 = (bf16[512,1024]{1,0:T(8,128)(2,1)}, bf16[512,1024]{1,0:T(8,128)(2,1)}, u32[]{:S(2)}, u32[]{:S(2)}) collective-permute-start(bf16[512,1024]{1,0:T(8,128)(2,1)} %get-tuple-element.128), channel_id=1, source_target_pairs={{0,8},{8,0},{16,24},{24,16},{1,9},{9,1},{17,25},{25,17},{2,10},{10... | collective-permute-start | bytes 3145736 | tf_op jit(solution)/shard_map/ppermute | solution.py:655
  447.2 10.0 %collective-permute-start.42 = (f32[1,288]{1,0:T(1,128)S(1)}, f32[1,288]{1,0:T(1,128)S(1)}, u32[]{:S(2)}, u32[]{:S(2)}) collective-permute-start(f32[1,288]{1,0:T(1,128)S(1)} %get-tuple-element.248), channel_id=1, source_target_pairs={{0,4},{4,0},{8,12},{12,8},{16,20},{20,16},{24,28},{28,24},{1,5},{5... | collective-permute-start | bytes 3464 | tf_op jit(solution)/shard_map/ppermute | solution.py:680
  448.7 9.1 %collective-permute-start.43 = (f32[1,288]{1,0:T(1,128)S(1)}, f32[1,288]{1,0:T(1,128)S(1)}, u32[]{:S(2)}, u32[]{:S(2)}) collective-permute-start(f32[1,288]{1,0:T(1,128)S(1)} %get-tuple-element.247), channel_id=1, source_target_pairs={{0,8},{4,12},{8,0},{12,4},{16,24},{20,28},{24,16},{28,20},{1,9},{5... | collective-permute-start | bytes 3464 | tf_op jit(solution)/shard_map/ppermute | solution.py:680
  448.7 10.3 %collective-permute-start.44 = (f32[1,288]{1,0:T(1,128)S(1)}, f32[1,288]{1,0:T(1,128)S(1)}, u32[]{:S(2)}, u32[]{:S(2)}) collective-permute-start(f32[1,288]{1,0:T(1,128)S(1)} %get-tuple-element.246), channel_id=1, source_target_pairs={{0,12},{4,8},{8,4},{12,0},{16,28},{20,24},{24,20},{28,16},{1,13},{... | collective-permute-start | bytes 3464 | tf_op jit(solution)/shard_map/ppermute | solution.py:680
  449.4 9.7 %collective-permute-start.45 = (f32[1,288]{1,0:T(1,128)S(1)}, f32[1,288]{1,0:T(1,128)S(1)}, u32[]{:S(2)}, u32[]{:S(2)}) collective-permute-start(f32[1,288]{1,0:T(1,128)S(1)} %get-tuple-element.245), channel_id=1, source_target_pairs={{0,16},{4,20},{8,24},{12,28},{16,0},{20,4},{24,8},{28,12},{1,17},{... | collective-permute-start | bytes 3464 | tf_op jit(solution)/shard_map/ppermute | solution.py:680
  450.9 8.8 %collective-permute-start.46 = (f32[1,288]{1,0:T(1,128)S(1)}, f32[1,288]{1,0:T(1,128)S(1)}, u32[]{:S(2)}, u32[]{:S(2)}) collective-permute-start(f32[1,288]{1,0:T(1,128)S(1)} %get-tuple-element.244), channel_id=1, source_target_pairs={{0,20},{4,16},{8,28},{12,24},{16,4},{20,0},{24,12},{28,8},{1,21},{... | collective-permute-start | bytes 3464 | tf_op jit(solution)/shard_map/ppermute | solution.py:680
  459.0 14.4 %collective-permute-start.41 = (bf16[256,1024]{1,0:T(8,128)(2,1)S(1)}, bf16[256,1024]{1,0:T(8,128)(2,1)S(1)}, u32[]{:S(2)}, u32[]{:S(2)}) collective-permute-start(bf16[256,1024]{1,0:T(8,128)(2,1)S(1)} %get-tuple-element.238), channel_id=1, source_target_pairs={{0,8},{8,0},{16,24},{24,16},{1,9},{9,1},{17,25},{25,17},{2,10},{10... | collective-permute-start | bytes 1572872 | tf_op jit(solution)/shard_map/ppermute | solution.py:655
  459.1 15.4 %collective-permute-start.24 = (bf16[256,1024]{1,0:T(8,128)(2,1)S(1)}, bf16[256,1024]{1,0:T(8,128)(2,1)S(1)}, u32[]{:S(2)}, u32[]{:S(2)}) collective-permute-start(bf16[256,1024]{1,0:T(8,128)(2,1)S(1)} %get-tuple-element.241), channel_id=1, source_target_pairs={{0,8},{8,0},{16,24},{24,16},{1,9},{9,1},{17,25},{25,17},{2,10},{10... | collective-permute-start | bytes 1572872 | tf_op jit(solution)/shard_map/ppermute | solution.py:655
  461.7 11.0 %collective-permute-start.49 = (f32[1,288]{1,0:T(1,128)S(1)}, f32[1,288]{1,0:T(1,128)S(1)}, u32[]{:S(2)}, u32[]{:S(2)}) collective-permute-start(f32[1,288]{1,0:T(1,128)S(1)} %add_add_fusion), channel_id=1, source_target_pairs={{0,1},{1,0},{2,3},{3,2},{4,5},{5,4},{6,7},{7,6},{8,9},{9,8},{10,11... | collective-permute-start | bytes 3464 | tf_op jit(solution)/shard_map/ppermute | solution.py:911
  463.3 9.4 %collective-permute-start.50 = (f32[1,288]{1,0:T(1,128)S(1)}, f32[1,288]{1,0:T(1,128)S(1)}, u32[]{:S(2)}, u32[]{:S(2)}) collective-permute-start(f32[1,288]{1,0:T(1,128)S(1)} %add_add_fusion), channel_id=1, source_target_pairs={{0,2},{1,3},{2,0},{3,1},{4,6},{5,7},{6,4},{7,5},{8,10},{9,11},{10,... | collective-permute-start | bytes 3464 | tf_op jit(solution)/shard_map/ppermute | solution.py:911
  (80 other events, 1149.8 us)
Sparse Core Ops, SparseCore 0:
  10.5 65.1 all-gather.4
  78.2 96.8 all-gather.2
  289.7 44.8 all-reduce.6
  350.4 67.7 all-reduce.10
  428.4 68.1 all-reduce.8

commit v8 on v7

--- a/solution.py
+++ b/solution.py
@@ -290,10 +290,11 @@
     )(place, *parts, q, k, v, seg_col, seg_row, *base)
 
 
-def feed_kernel(chips, place_ref, *refs):
-    gates, ups, shrinks = refs[:chips], refs[chips : 2 * chips], refs[2 * chips : 3 * chips]
-    own_ref, other_ref, c_ref, c_other_ref = refs[3 * chips : 3 * chips + 4]
-    refs = refs[3 * chips + 4 :]
+def feed_kernel(chips, inner, place_ref, *refs):
+    gates, ups = refs[:chips], refs[chips : 2 * chips]
+    halves = refs[2 * chips : 2 * chips + 2]
+    own_ref, other_ref, c_ref, c_other_ref = refs[2 * chips + 2 : 2 * chips + 6]
+    refs = refs[2 * chips + 6 :]
     x_out, c_out, active_ref, grad_ref, share_ref, share_other, back_ref, back_other, expand, shrink = refs
     step = pl.program_id(0)
     mine = step < 2
@@ -310,7 +311,17 @@
             here = slice(s * size, (s + 1) * size)
             expand[:, here] = gates[s][...]
             expand[:, half + s * size : half + (s + 1) * size] = ups[s][...]
-            shrink[here, :] = shrinks[s][...]
+
+    rows = half // (2 * chips * inner)
+    for odd in range(2):
+
+        @pl.when((step == 0) & (place_ref[2] == odd))
+        def _():
+            for i in range(chips * inner):
+                source = slice(i * rows, (i + 1) * rows)
+                for part, side in zip(halves, (odd, 1 - odd)):
+                    start = (2 * i + side) * rows
+                    shrink[start : start + rows, :] = part[source, :]
 
     gate_up = dot_nn(x, expand[...])
     grad_active = dot_nt(c, shrink[...]).astype(LOW).astype(FULL)
@@ -337,7 +348,7 @@
         back_other[...] = back
 
 
-def feed(place, n, expand, shrink, own, other, c, c_other):
+def feed(place, n, inner, expand, shrink_halves, own, other, c, c_other):
     chips = n // 2
     rows = own.shape[0]
     size = FF // n
@@ -355,21 +366,17 @@
         pl.BlockSpec((D, size), lambda i, p, s=s: (0, n + 2 * s + (p[0] & 1)), pipeline_mode=once)
         for s in range(chips)
     ]
-    shrinks = [
-        pl.BlockSpec((size, D), lambda i, p, s=s: (2 * s + (p[0] & 1), 0), pipeline_mode=once)
-        for s in range(chips)
-    ]
     wide = lambda w: jax.ShapeDtypeStruct((2 * rows, w), LOW)
     part = jax.ShapeDtypeStruct((rows, D), LOW)
     return pl.pallas_call(
-        functools.partial(feed_kernel, chips),
+        functools.partial(feed_kernel, chips, inner),
         out_shape=(wide(D), wide(D), wide(FF // 2), wide(FF), part, part, part, part),
         grid_spec=pltpu.PrefetchScalarGridSpec(
             num_scalar_prefetch=1,
             grid=(4,),
             in_specs=gates
             + ups
-            + shrinks
+            + [resident(half.shape) for half in shrink_halves]
             + [
                 pl.BlockSpec((block, D), near),
                 pl.BlockSpec((block, D), far),
@@ -393,7 +400,7 @@
             flops=12 * rows * D * FF, bytes_accessed=30 * MIB, transcendentals=0
         ),
         name="feed",
-    )(place, *[expand] * (2 * chips), *[shrink] * chips, own, other, c, c_other)
+    )(place, *[expand] * (2 * chips), *shrink_halves, own, other, c, c_other)
 
 
 def back_kernel(n, inner, half, place_ref, *refs):
@@ -709,14 +716,13 @@
         core = me & 1
         chip = me >> 1
         mine = lax.axis_index("grp")
-        place = jnp.stack([me, mine]).astype(jnp.int32)
+        rep = lax.axis_index("rep")
+        place = jnp.stack([me, mine, rep & 1]).astype(jnp.int32)
         order = me ^ jnp.arange(n)
         q_width = QUERY_FEATURES // chips
         k_width = KEY_FEATURES // chips
         width = q_width + 2 * k_width
         rows = qkv_weight.shape[0]
-
-        rep = lax.axis_index("rep")
 
         def qkv_piece(s):
             to = chip ^ s
@@ -766,7 +772,12 @@
             return lax.all_gather(weight.astype(LOW), ("ctx", "grp"), axis=0, tiled=True)
 
         expand_full = gather_all(expand_weight)
-        shrink_full = gather_all(shrink_weight)
+        odd = rep & 1
+        half_rows = shrink_weight.shape[0] // 2
+        low = lax.dynamic_slice_in_dim(shrink_weight, odd * half_rows, half_rows, 0).astype(LOW)
+        low = lax.all_gather(low, ("ctx", "grp"), axis=0, tiled=True)
+        low = pick(low.reshape(chips, 2, inner * half_rows, D), 1, core).reshape(-1, D)
+        shrink_halves = [low, lax.ppermute(low, "rep", [(i, i ^ 1) for i in range(reps)])]
         other_cotangent = swap_core(cotangent)
 
         ladder = jnp.arange(HEAD_SIZE) % (HEAD_SIZE // 2)
@@ -784,12 +795,13 @@
             *base, share = attend(place, out_parts, q, k, v, seg_col, seg_row, n, s, base)
             shares.append(swap_chip(share, s) if s else share)
         attended, totals = base
+        *shares, shrink_halves[1] = lax.optimization_barrier((*shares, shrink_halves[1]))
         inputs = jnp.concatenate(token_slots[:2]).astype(FULL)
         hidden = inputs + sum_of(shares)
         normed_two = (hidden * inverse_rms(hidden) * gain_two).astype(LOW)
 
         x_all, c_all, active, grad_gate_up, share, share_other, back_share, back_other = feed(
-            place, n, expand_full, shrink_full, normed_two, swap_core(normed_two), cotangent,
+            place, n, inner, expand_full, shrink_halves, normed_two, swap_core(normed_two), cotangent,
             other_cotangent,
         )
         grad_shrink = dot_tn(active, c_all).astype(LOW)
@@ -859,10 +871,6 @@
         shrink_cut = send_x(next_cut(pick(shrink_cuts, 1, mine), shrink_sent, 0, chip, chips))
         grad_slots = lax.optimization_barrier((*grad_slots, *line))[:chips]
         grad_all = jnp.concatenate(grad_slots)
-        grad_out = dot_tn(attended, grad_all).astype(LOW)
-        out_cuts = grad_out.reshape(2, inner, out_weight.shape[0], D)
-        out_sent = [swap_core(pick(out_cuts, 0, core ^ 1))]
-        attended = after(attended, out_cuts)
         grad, back_all, gains_first_part = back_part(0, attended, None)
 
         line[:] = [gains_first_part]
@@ -871,7 +879,11 @@
         own_near = first_over_x(0, *line)
         own_sent = [swap_grp(next_sum(*own_far[t - 1]), t) for t in range(1, inner)]
         other_cut = send_x(next_cut(pick(other_rows, 1, mine), other_sent, 0, chip, chips))
-        out_cut = send_y(next_cut(pick(out_cuts, 0, core), out_sent, 0, mine, inner))
+        grad_out = dot_tn(after(attended, *line), grad_all).astype(LOW)
+        out_cuts = grad_out.reshape(2, inner, out_weight.shape[0], D)
+        out_kept, out_sent = pick(out_cuts, 0, core), pick(out_cuts, 0, core ^ 1)
+        attended, out_kept, out_sent = lax.optimization_barrier((attended, out_kept, out_sent))
+        out_sent = [swap_core(out_sent)]
         attended, back_all, grad = lax.optimization_barrier((attended, back_all, grad, *line))[:3]
         grad, back_all, head_gains = back_part(1, attended, (back_all, grad))
 
@@ -879,13 +891,14 @@
         head_gains = head_gains + gains_first_part
         own_cut = next_sum(next_sum(*own_near), own_sent)
         other_cut = swap_core(next_sum(*other_cut))
-        own_cut, other_cut, total_shrink, grad, back_all = lax.optimization_barrier(
-            (own_cut, other_cut, total_shrink, grad, back_all, *line)
-        )[:5]
+        own_cut, other_cut, total_shrink, grad = lax.optimization_barrier(
+            (own_cut, other_cut, total_shrink, grad, *line)
+        )[:4]
         line[:] = [own_cut]
+        qkv_cuts, qkv_sent = cut_qkv(grad)
         own_cut, other_cut = lax.psum((own_cut, other_cut), "rep")
-        qkv_cuts, qkv_sent = cut_qkv(grad)
         qkv_cut = send_y(next_cut(qkv_cuts, qkv_sent, 1, mine, inner))
+        out_cut = send_y(next_cut(out_kept, out_sent, 0, mine, inner))
         out_cut = next_sum(*out_cut)
         kept, sent = send_x(next_cut(*qkv_cut, 0, chip, chips))
         *qkv_cuts, out_cut, own_cut, other_cut, back_all = lax.optimization_barrier(

time: 526 us -> 519 us (0.987)
  waiting for transfers between devices: 221 us -> 211 us
    unnamed x154 -> x142, local copies, waits for them, and re-layouts: 32.8 us -> 25.5 us
    ppermute x27, waiting for transfers between devices: 88.2 us -> 82.1 us  [swap_ctx(): return lax.ppermute(value, 'ctx', [(i, i ^ s) for i in range(n)])]
  transfers between devices with their start and end apart: 57 -> 58, of which waited for: 18 -> 17; matrix products, arithmetic and copies ran while one was open for 14% -> 15% of each run, Pallas kernels for 18% -> 18%
where the time goes in v8:
time: 519 us; the launch traced here: 512 us
  waiting for transfers between devices  211 us (41%)
  Pallas kernels  133 us (26%)
  local copies, waits for them, and re-layouts  44.3 us (9%)
  starting transfers between devices  42.5 us (8%)
  other arithmetic  42.2 us (8%)
  matrix products  23.2 us (4%)
  between operations  15.3 us (3%)
    ppermute x27, waiting for transfers between devices, swap_ctx(): return lax.ppermute(value, 'ctx', [(i, i ^ s) for i in range(n)])  82.1 us
    ppermute x8, waiting for transfers between devices, swap_grp(): return lax.ppermute(value, 'grp', [(i, i ^ t) for i in range(inner)])  72.9 us
    pallas_call x2, Pallas kernels, back(): pl.pallas_call(functools.partial(back_kernel, n, inner, half), out_shape=...  47.5 us
    pallas_call x1, Pallas kernels, feed(): pl.pallas_call(functools.partial(feed_kernel, chips, inner), out_shape=(w...  31.5 us
    psum x1, waiting for transfers between devices, on_device(): own_cut, other_cut = lax.psum((own_cut, other_cut), 'rep')  28.6 us
    unnamed x142, local copies, waits for them, and re-layouts  25.5 us
    pallas_call x2, Pallas kernels, attend(): pl.pallas_call(functools.partial(attend_kernel, n, inner, first, bool(bas...  23.3 us
    dot_general x4, matrix products, dot_tn(): lax.dot_general(a, b, (((0,), (0,)), ((), ())), preferred_element_type=FULL)  23.2 us
  transfers between devices with their start and end apart: 58, of which 17 were waited for; matrix products, arithmetic and copies ran while one was open for 15% of the time, Pallas kernels for 18%

profile of v8, /device:TPU:0, one launch (start us, length us, event | category | flops | bytes accessed | tf_op | source)
XLA Modules:
  0.0 511.8 jit_solution(16109316660099608581)
XLA Ops:
  7.3 2.0 dynamic-slice_convert_fusion
  9.4 3.4 convert_element_type.308
  12.9 3.0 collective-permute-start
  16.2 1.9 collective-permute-start.3
  27.2 2.0 collective-permute-start.8
  31.6 2.0 copy.42
  33.6 2.6 gather_fusion.1
  37.8 15.0 %collective-permute-done.14.refs_4_ = bf16[128,2048]{1,0:T(8,128)(2,1)} collective-permute-done((bf16[128,2048]{1,0:T(8,128)(2,1)}, bf16[128,2048]{1,0:T(8,128)(2,1)}, u32[]{:S(2)}, u32[]{:S(2)}) %collective-permute-start.14) | collective-permute-done | bytes 524320 | tf_op jit(solution)/shard_map/ppermute | solution.py:662
  53.1 8.7 %collective-permute-done.11.refs_1_ = bf16[128,2048]{1,0:T(8,128)(2,1)} collective-permute-done((bf16[128,2048]{1,0:T(8,128)(2,1)}, bf16[128,2048]{1,0:T(8,128)(2,1)}, u32[]{:S(2)}, u32[]{:S(2)}) %collective-permute-start.11) | collective-permute-done | bytes 524320 | tf_op jit(solution)/shard_map/ppermute | solution.py:671
  66.2 11.5 %collective-permute-done.15.refs_5_ = bf16[128,2048]{1,0:T(8,128)(2,1)} collective-permute-done((bf16[128,2048]{1,0:T(8,128)(2,1)}, bf16[128,2048]{1,0:T(8,128)(2,1)}, u32[]{:S(2)}, u32[]{:S(2)}) %collective-permute-start.15) | collective-permute-done | bytes 524320 | tf_op jit(solution)/shard_map/ppermute | solution.py:671
  77.7 1.9 fusion.20
  83.5 7.0 %collective-permute-done.19.refs_11_ = bf16[256,1024]{1,0:T(8,128)(2,1)} collective-permute-done((bf16[256,1024]{1,0:T(8,128)(2,1)S(1)}, bf16[256,1024]{1,0:T(8,128)(2,1)}, u32[]{:S(2)}, u32[]{:S(2)}) %collective-permute-start.19) | collective-permute-done | bytes 524320 | tf_op jit(solution)/shard_map/ppermute | solution.py:662
  90.5 10.7 %project.1 = (bf16[1024,1024]{1,0:T(8,128)(2,1)S(1)}, bf16[1024,1024]{1,0:T(8,128)(2,1)S(1)}, bf16[1024,512]{1,0:T(8,128)(2,1)S(1)}, bf16[1024,512]{1,0:T(8,128)(2,1)S(1)}, bf16[1024,1536]{1,0:T(8,128)(2,1)}) custom-call(s32[3]{0:T(128)S(1)} %pad_add_fusion.place_ref, bf16[128,2048]{1,0:T(8,128)(2,1)} %get-tuple-element.115.refs_0_, ...), custom_call_target="tpu_custom_call" | custom-call | flops 4294967296 | bytes 16777216 | tf_op jit(solution)/shard_map/project/pallas_call | solution.py:150
  104.9 11.3 %attend.2 = (bf16[1024,1024]{1,0:T(8,128)(2,1)}, f32[1024,256]{1,0:T(8,128)S(1)}, bf16[512,1024]{1,0:T(8,128)(2,1)S(1)}) custom-call(s32[3]{0:T(128)S(1)} %pad_add_fusion.place_ref, bf16[256,1024]{1,0:T(8,128)(2,1)S(1)} %convert_element_type.303.refs_0_.refs_8_, bf16[256,1024]{1,0:T(8,128)(2,1)S(1)} %collective-permute-done.8.refs_1_.refs_9_, ...), custom_call_target="tpu_custom_call" | custom-call | flops 3221225472 | bytes 8388608 | tf_op jit(solution)/shard_map/attend/pallas_call | solution.py:258
  116.4 12.0 %attend.3 = (bf16[1024,1024]{1,0:T(8,128)(2,1)}, f32[1024,256]{1,0:T(8,128)S(1)}, bf16[512,1024]{1,0:T(8,128)(2,1)S(1)}) custom-call(s32[3]{0:T(128)S(1)} %pad_add_fusion.place_ref, bf16[256,1024]{1,0:T(8,128)(2,1)S(1)} %convert_element_type.303.refs_0_.refs_8_, ...), custom_call_target="tpu_custom_call", output_to_operand_aliasing={{0}: (10, {}), {1}: (11, {})} | custom-call | flops 3221225472 | bytes 8388608 | tf_op jit(solution)/shard_map/attend/pallas_call | solution.py:258
  128.4 31.3 %collective-permute-done.20 = bf16[512,1024]{1,0:T(8,128)(2,1)S(1)} collective-permute-done((bf16[512,1024]{1,0:T(8,128)(2,1)S(1)}, bf16[512,1024]{1,0:T(8,128)(2,1)S(1)}, u32[]{:S(2)}, u32[]{:S(2)}) %collective-permute-start.20) | collective-permute-done | bytes 1048608 | tf_op jit(solution)/shard_map/ppermute | solution.py:662
  165.3 31.5 %feed.1 = (bf16[1024,1024]{1,0:T(8,128)(2,1)}, bf16[1024,1024]{1,0:T(8,128)(2,1)}, bf16[1024,1536]{1,0:T(8,128)(2,1)}, bf16[1024,3072]{1,0:T(8,128)(2,1)}, bf16[...) custom-call(s32[3]{0:T(128)} %copy-done.31, ...), custom_call_target="tpu_custom_call" | custom-call | flops 19327352832 | bytes 31457280 | tf_op jit(solution)/shard_map/feed/pallas_call | solution.py:371
  197.0 6.0 %convolution_convert_fusion.1 = bf16[1536,1024]{1,0:T(8,128)(2,1)S(1)} fusion(bf16[1024,1536]{1,0:T(8,128)(2,1)} %get-tuple-element.140, bf16[1024,1024]{1,0:T(8,128)(2,1)} %get-tuple-element.141), kind=kOutput, calls=%fused_computation.3 | convolution fusion | flops 3222798336 | bytes 8388608 | tf_op jit(solution)/shard_map/dot_general | solution.py:51
  204.9 2.2 multiply_reduce_fusion
  207.1 2.2 fusion.57
  210.1 7.3 %convolution_convert_fusion = bf16[1024,3072]{1,0:T(8,128)(2,1)S(1)} fusion(bf16[1024,1024]{1,0:T(8,128)(2,1)S(1)} %copy-done.64, bf16[1024,3072]{1,0:T(8,128)(2,1)S(1)} %copy-done.63), kind=kOutput, calls=%fused_computation.2 | convolution fusion | flops 6445596672 | bytes 14680064 | tf_op jit(solution)/shard_map/dot_general | solution.py:51
  220.6 19.9 %collective-permute-done.27 = bf16[2,384,1024]{2,1,0:T(8,128)(2,1)S(1)} collective-permute-done((bf16[2,384,1024]{2,1,0:T(8,128)(2,1)S(1)}, bf16[2,384,1024]{2,1,0:T(8,128)(2,1)S(1)}, u32[]{:S(2)}, u32[]{:S(2)}) %collective-permute-start.27) | collective-permute-done | bytes 1572896 | tf_op jit(solution)/shard_map/ppermute | solution.py:671
  245.7 23.7 %back.2 = (bf16[1024,2048]{1,0:T(8,128)(2,1)}, bf16[1024,1024]{1,0:T(8,128)(2,1)}, f32[8,128]{1,0:T(8,128)}) custom-call(s32[3]{0:T(128)} %copy-done.31, bf16[128,2048]{1,0:T(8,128)(2,1)} %get-tuple-element.115.refs_0_, bf16[128,2048]{1,0:T(8,128)(2,1)} %collective-permute-done.11.refs_1_, bf16[128,2048]{1,0:T(8,128)(2,1)} %collective-permute-done.12.refs_2_, ...), custom_call_target="tpu_custom_call" | custom-call | flops 5905580032 | bytes 31457280 | tf_op jit(solution)/shard_map/back/pallas_call | solution.py:535
  270.5 2.1 dynamic-slice_bitcast_fusion.6
  272.9 5.8 %collective-permute-done.32 = bf16[128,3072]{1,0:T(8,128)(2,1)} collective-permute-done((bf16[128,3072]{1,0:T(8,128)(2,1)}, bf16[128,3072]{1,0:T(8,128)(2,1)}, u32[]{:S(2)}, u32[]{:S(2)}) %collective-permute-start.32) | collective-permute-done | bytes 786464 | tf_op jit(solution)/shard_map/ppermute | solution.py:662
  278.8 2.4 fusion.16
  282.7 2.5 fusion.14
  285.7 2.4 convolution_convert_fusion.3
  289.3 23.9 %back.3 = (bf16[1024,2048]{1,0:T(8,128)(2,1)}, bf16[1024,1024]{1,0:T(8,128)(2,1)}, f32[8,128]{1,0:T(8,128)}) custom-call(s32[3]{0:T(128)} %copy-done.31, bf16[128,2048]{1,0:T(8,128)(2,1)} %get-tuple-element.115.refs_0_, bf16[128,2048]{1,0:T(8,128)(2,1)} %collective-permute-done.11.refs_1_, ...), custom_call_target="tpu_custom_call", output_to_operand_aliasing={{0}: (27, {})} | custom-call | flops 5905580032 | bytes 31457280 | tf_op jit(solution)/shard_map/back/pallas_call | solution.py:535
  314.8 2.2 add_convert_fusion.2
  317.0 2.2 add_convert_fusion.1
  319.2 3.4 all-reduce.7.cloned.1.call-done.refs_0_
  322.7 7.4 %convolution_convert_fusion.2 = bf16[1024,2048]{1,0:T(8,128)(2,1)S(1)} fusion(bf16[1024,1024]{1,0:T(8,128)(2,1)} %copy-done.37, bf16[1024,2048]{1,0:T(8,128)(2,1)} %get-tuple-element.170), kind=kOutput, calls=%fused_computation.4 | convolution fusion | flops 4297064448 | bytes 10485760 | tf_op jit(solution)/shard_map/dot_general | solution.py:51
  330.8 5.1 %collective-permute-done.36 = bf16[2,2,128,2048]{3,2,0,1:T(8,128)(2,1)S(1)} collective-permute-done((bf16[2,2,128,2048]{3,2,0,1:T(8,128)(2,1)S(1)}, bf16[2,2,128,2048]{3,2,0,1:T(8,128)(2,1)S(1)}, u32[]{:S(2)}, u32[]{:S(2)}) %collective-permute-start.36) | collective-permute-done | bytes 2097184 | tf_op jit(solution)/shard_map/ppermute | solution.py:662
  335.9 2.1 fusion.11
  341.9 32.8 %collective-permute-done.39 = bf16[256,1024]{1,0:T(8,128)(2,1)S(1)} collective-permute-done((bf16[256,1024]{1,0:T(8,128)(2,1)S(1)}, bf16[256,1024]{1,0:T(8,128)(2,1)S(1)}, u32[]{:S(2)}, u32[]{:S(2)}) %collective-permute-start.39) | collective-permute-done | bytes 524320 | tf_op jit(solution)/shard_map/ppermute | solution.py:671
  375.7 2.7 fusion.24
  379.7 28.6 %all-reduce.11.cloned.1.call-done = (bf16[128,3072]{1,0:T(8,128)(2,1)}, bf16[128,3072]{1,0:T(8,128)(2,1)}) async-done(((bf16[128,3072]{1,0:T(8,128)(2,1)}, bf16[128,3072]{1,0:T(8,128)(2,1)}), (bf16[128,3072]{1,0:T(8,128)(2,1)}, bf16[128,3072]{1,0:T(8,128)(2,1)})) %all-reduce.11.cloned.1.call-update) | async-done | bytes 1572880 | tf_op jit(solution)/shard_map/psum | solution.py:899
  408.4 2.5 slice.65
  416.3 3.5 adam_cuts.5
  419.8 15.1 %collective-permute-done.41 = bf16[512,1024]{1,0:T(8,128)(2,1)} collective-permute-done((bf16[512,1024]{1,0:T(8,128)(2,1)}, bf16[512,1024]{1,0:T(8,128)(2,1)}, u32[]{:S(2)}, u32[]{:S(2)}) %collective-permute-start.41) | collective-permute-done | bytes 1048608 | tf_op jit(solution)/shard_map/ppermute | solution.py:662
  434.9 2.4 fusion.8
  442.6 4.7 fusion.7
  453.5 1.8 collective-permute-start.51
  456.4 6.5 %adam_pair.1 = (f32[128,6144]{1,0:T(8,128)}, f32[128,6144]{1,0:T(8,128)}, f32[128,6144]{1,0:T(8,128)}) custom-call(s32[3]{0:T(128)S(1)} %copy-done.32, bf16[128,3072]{1,0:T(8,128)(2,1)S(1)} %copy-done.24, bf16[128,3072]{1,0:T(8,128)(2,1)S(1)} %copy-done.25, f32[128,6144]{1,0:T(8,128)S(1)} %copy-done.2, f32[128,6144]{1,0:T(8,128)S(1)} %copy-done.6, ...), custom_call_target="tpu_custom_call" | custom-call | flops 15728640 | bytes 20447232 | tf_op jit(solution)/shard_map/adam_pair/pallas_call | solution.py:637
  465.8 22.3 %all-reduce.9.cloned.1.call-done = (bf16[128,2048]{1,0:T(8,128)(2,1)}, bf16[128,2048]{1,0:T(8,128)(2,1)}, bf16[256,1024]{1,0:T(8,128)(2,1)}) async-done(((bf16[128,2048]{1,0:T(8,128)(2,1)}, bf16[128,2048]{1,0:T(8,128)(2,1)}, bf16[256,1024]{1,0:T(8,128)(2,1)}), (bf16[128,2048]{1,0:T(8,128)(2,1)}, bf16[128,2048]{1,0:T(8,128)(2,1)}, bf16[256,1024]{1,0:T(8,128)(2,1)})) %all-reduce.9.cloned.1.call-update) | async-done | bytes 1572880 | tf_op jit(solution)/shard_map/psum | solution.py:907
  491.7 2.6 adam_cuts.4
  497.5 7.3 %adam_cuts.3 = (f32[128,4096]{1,0:T(8,128)}, f32[128,4096]{1,0:T(8,128)}, f32[128,4096]{1,0:T(8,128)}) custom-call(s32[1]{0:T(128)} %bitcast.57.key_ref, bf16[128,2048]{1,0:T(8,128)(2,1)S(1)} %copy-done.28, bf16[128,2048]{1,0:T(8,128)(2,1)S(1)} %copy-done.29, f32[128,4096]{1,0:T(8,128)S(1)} %copy-done.4, f32[128,4096]{1,0:T(8,128)S(1)} %copy-done.14, ...), custom_call_target="tpu_custom_call" | custom-call | flops 10485760 | bytes 13631488 | tf_op jit(solution)/shard_map/adam_cuts/pallas_call | solution.py:607
  (302 shorter events, 83.2 us)
Async XLA Ops:
  7.2 73.1 %all-gather.3.cloned.1.call-start = ((), (), s32[]{:S(2)}) async-start(), calls=%async_computation | async-start | bytes 3538944 | tf_op jit(solution)/shard_map/all_gather | solution.py:778
  9.3 155.9 %all-gather.5.cloned.1.call-start = ((), (), s32[]{:S(2)}) async-start(), calls=%async_computation.1 | async-start | bytes 14155776 | tf_op jit(solution)/shard_map/all_gather | solution.py:772
  12.8 309.9 %all-reduce.7.cloned.1.call-start = ((), (), s32[]{:S(2)}) async-start(), calls=%async_computation.2 | async-start | bytes 1572864 | tf_op jit(solution)/shard_map/psum | solution.py:878
  12.9 11.6 %collective-permute-start = (f32[1,1312]{1,0:T(1,128)S(1)}, f32[1,1312]{1,0:T(1,128)S(1)}, u32[]{:S(2)}, u32[]{:S(2)}) collective-permute-start(f32[1,1312]{1,0:T(1,128)S(1)} %reshape.237), channel_id=1, source_target_pairs={{0,4},{4,0},{8,12},{12,8},{16,20},{20,16},{24,28},{28,24},{1,5},{5... | collective-permute-start | bytes 15752 | tf_op jit(solution)/shard_map/ppermute | solution.py:687
  16.0 9.1 %collective-permute-start.1 = (f32[1,1312]{1,0:T(1,128)S(1)}, f32[1,1312]{1,0:T(1,128)S(1)}, u32[]{:S(2)}, u32[]{:S(2)}) collective-permute-start(f32[1,1312]{1,0:T(1,128)S(1)} %reshape.237), channel_id=1, source_target_pairs={{0,8},{4,12},{8,0},{12,4},{16,24},{20,28},{24,16},{28,20},{1,9},{5... | collective-permute-start | bytes 15752 | tf_op jit(solution)/shard_map/ppermute | solution.py:687
  16.0 11.2 %collective-permute-start.2 = (f32[1,1312]{1,0:T(1,128)S(1)}, f32[1,1312]{1,0:T(1,128)S(1)}, u32[]{:S(2)}, u32[]{:S(2)}) collective-permute-start(f32[1,1312]{1,0:T(1,128)S(1)} %reshape.237), channel_id=1, source_target_pairs={{0,12},{4,8},{8,4},{12,0},{16,28},{20,24},{24,20},{28,16},{1,13},{... | collective-permute-start | bytes 15752 | tf_op jit(solution)/shard_map/ppermute | solution.py:687
  16.2 13.0 %collective-permute-start.3 = (f32[1,1312]{1,0:T(1,128)S(1)}, f32[1,1312]{1,0:T(1,128)S(1)}, u32[]{:S(2)}, u32[]{:S(2)}) collective-permute-start(f32[1,1312]{1,0:T(1,128)S(1)} %reshape.237), channel_id=1, source_target_pairs={{0,16},{4,20},{8,24},{12,28},{16,0},{20,4},{24,8},{28,12},{1,17},{... | collective-permute-start | bytes 15752 | tf_op jit(solution)/shard_map/ppermute | solution.py:687
  18.1 11.1 %collective-permute-start.4 = (f32[1,1312]{1,0:T(1,128)S(1)}, f32[1,1312]{1,0:T(1,128)S(1)}, u32[]{:S(2)}, u32[]{:S(2)}) collective-permute-start(f32[1,1312]{1,0:T(1,128)S(1)} %reshape.237), channel_id=1, source_target_pairs={{0,20},{4,16},{8,28},{12,24},{16,4},{20,0},{24,12},{28,8},{1,21},{... | collective-permute-start | bytes 15752 | tf_op jit(solution)/shard_map/ppermute | solution.py:687
  27.2 25.7 %collective-permute-start.8 = (bf16[256,1024]{1,0:T(8,128)(2,1)S(1)}, bf16[256,1024]{1,0:T(8,128)(2,1)S(1)}, u32[]{:S(2)}, u32[]{:S(2)}) collective-permute-start(bf16[256,1024]{1,0:T(8,128)(2,1)S(1)} %convert_element_type.303.refs_0_.refs_8_), channel_id=1, source_target_pairs={{0,4},{4,0},{1,5},{5,1},{2,6},{6,2},{3,7},{7,3},{8,12},{12,8},{9,1... | collective-permute-start | bytes 1572872 | tf_op jit(solution)/shard_map/ppermute | solution.py:671
  29.2 23.6 %collective-permute-start.14 = (bf16[128,2048]{1,0:T(8,128)(2,1)}, bf16[128,2048]{1,0:T(8,128)(2,1)}, u32[]{:S(2)}, u32[]{:S(2)}) collective-permute-start(bf16[128,2048]{1,0:T(8,128)(2,1)} %copy-done.52), channel_id=1, source_target_pairs={{0,16},{8,24},{16,0},{24,8},{1,17},{9,25},{17,1},{25,9},{2,18},{10... | collective-permute-start | bytes 1572872 | tf_op jit(solution)/shard_map/ppermute | solution.py:662
  36.5 25.3 %collective-permute-start.11 = (bf16[128,2048]{1,0:T(8,128)(2,1)}, bf16[128,2048]{1,0:T(8,128)(2,1)}, u32[]{:S(2)}, u32[]{:S(2)}) collective-permute-start(bf16[128,2048]{1,0:T(8,128)(2,1)} %get-tuple-element.115.refs_0_), channel_id=1, source_target_pairs={{0,4},{4,0},{1,5},{5,1},{2,6},{6,2},{3,7},{7,3},{8,12},{12,8},{9,1... | collective-permute-start | bytes 1572872 | tf_op jit(solution)/shard_map/ppermute | solution.py:671
  37.2 26.8 %collective-permute-start.18 = (bf16[256,1024]{1,0:T(8,128)(2,1)S(1)}, bf16[256,1024]{1,0:T(8,128)(2,1)S(1)}, u32[]{:S(2)}, u32[]{:S(2)}) collective-permute-start(bf16[256,1024]{1,0:T(8,128)(2,1)S(1)} %dynamic-slice_bitcast_fusion.7.refs_8_), channel_id=1, source_target_pairs={{0,16},{8,24},{16,0},{24,8},{1,17},{9,25},{17,1},{25,9},{2,18},{10... | collective-permute-start | bytes 1572872 | tf_op jit(solution)/shard_map/ppermute | solution.py:662
  37.6 27.4 %collective-permute-start.7 = (bf16[256,1024]{1,0:T(8,128)(2,1)S(1)}, bf16[256,1024]{1,0:T(8,128)(2,1)S(1)}, u32[]{:S(2)}, u32[]{:S(2)}) collective-permute-start(bf16[256,1024]{1,0:T(8,128)(2,1)S(1)} %dynamic-slice_bitcast_fusion.8), channel_id=1, source_target_pairs={{0,8},{8,0},{16,24},{24,16},{1,9},{9,1},{17,25},{25,17},{2,10},{10... | collective-permute-start | bytes 1572872 | tf_op jit(solution)/shard_map/ppermute | solution.py:662
  52.8 24.9 %collective-permute-start.15 = (bf16[128,2048]{1,0:T(8,128)(2,1)}, bf16[128,2048]{1,0:T(8,128)(2,1)}, u32[]{:S(2)}, u32[]{:S(2)}) collective-permute-start(bf16[128,2048]{1,0:T(8,128)(2,1)} %collective-permute-done.14.refs_4_), channel_id=1, source_target_pairs={{0,4},{4,0},{1,5},{5,1},{2,6},{6,2},{3,7},{7,3},{8,12},{12,8},{9,1... | collective-permute-start | bytes 1572872 | tf_op jit(solution)/shard_map/ppermute | solution.py:671
  52.9 26.7 %collective-permute-start.12 = (bf16[128,2048]{1,0:T(8,128)(2,1)}, bf16[128,2048]{1,0:T(8,128)(2,1)}, u32[]{:S(2)}, u32[]{:S(2)}) collective-permute-start(bf16[128,2048]{1,0:T(8,128)(2,1)} %get-tuple-element.115.refs_0_), channel_id=1, source_target_pairs={{0,8},{8,0},{16,24},{24,16},{1,9},{9,1},{17,25},{25,17},{2,10},{10... | collective-permute-start | bytes 1572872 | tf_op jit(solution)/shard_map/ppermute | solution.py:662
  61.8 18.4 %collective-permute-start.13 = (bf16[128,2048]{1,0:T(8,128)(2,1)}, bf16[128,2048]{1,0:T(8,128)(2,1)}, u32[]{:S(2)}, u32[]{:S(2)}) collective-permute-start(bf16[128,2048]{1,0:T(8,128)(2,1)} %collective-permute-done.11.refs_1_), channel_id=1, source_target_pairs={{0,8},{8,0},{16,24},{24,16},{1,9},{9,1},{17,25},{25,17},{2,10},{10... | collective-permute-start | bytes 1572872 | tf_op jit(solution)/shard_map/ppermute | solution.py:662
  64.7 17.2 %collective-permute-start.16 = (bf16[128,2048]{1,0:T(8,128)(2,1)}, bf16[128,2048]{1,0:T(8,128)(2,1)}, u32[]{:S(2)}, u32[]{:S(2)}) collective-permute-start(bf16[128,2048]{1,0:T(8,128)(2,1)} %collective-permute-done.14.refs_4_), channel_id=1, source_target_pairs={{0,8},{8,0},{16,24},{24,16},{1,9},{9,1},{17,25},{25,17},{2,10},{10... | collective-permute-start | bytes 1572872 | tf_op jit(solution)/shard_map/ppermute | solution.py:662
  65.0 25.5 %collective-permute-start.19 = (bf16[256,1024]{1,0:T(8,128)(2,1)S(1)}, bf16[256,1024]{1,0:T(8,128)(2,1)}, u32[]{:S(2)}, u32[]{:S(2)}) collective-permute-start(bf16[256,1024]{1,0:T(8,128)(2,1)S(1)} %collective-permute-done.7.refs_9_), channel_id=1, source_target_pairs={{0,16},{8,24},{16,0},{24,8},{1,17},{9,25},{17,1},{25,9},{2,18},{10... | collective-permute-start | bytes 1572872 | tf_op jit(solution)/shard_map/ppermute | solution.py:662
  77.7 12.8 %collective-permute-start.17 = (bf16[128,2048]{1,0:T(8,128)(2,1)}, bf16[128,2048]{1,0:T(8,128)(2,1)}, u32[]{:S(2)}, u32[]{:S(2)}) collective-permute-start(bf16[128,2048]{1,0:T(8,128)(2,1)} %collective-permute-done.15.refs_5_), channel_id=1, source_target_pairs={{0,8},{8,0},{16,24},{24,16},{1,9},{9,1},{17,25},{25,17},{2,10},{10... | collective-permute-start | bytes 1572872 | tf_op jit(solution)/shard_map/ppermute | solution.py:662
  79.6 23.9 %collective-permute-start.9 = (bf16[256,1024]{1,0:T(8,128)(2,1)S(1)}, bf16[256,1024]{1,0:T(8,128)(2,1)}, u32[]{:S(2)}, u32[]{:S(2)}) collective-permute-start(bf16[256,1024]{1,0:T(8,128)(2,1)S(1)} %convert_element_type.303.refs_0_.refs_8_), channel_id=1, source_target_pairs={{0,8},{8,0},{16,24},{24,16},{1,9},{9,1},{17,25},{25,17},{2,10},{10... | collective-permute-start | bytes 1572872 | tf_op jit(solution)/shard_map/ppermute | solution.py:662
  80.2 23.4 %collective-permute-start.10 = (bf16[256,1024]{1,0:T(8,128)(2,1)S(1)}, bf16[256,1024]{1,0:T(8,128)(2,1)}, u32[]{:S(2)}, u32[]{:S(2)}) collective-permute-start(bf16[256,1024]{1,0:T(8,128)(2,1)S(1)} %collective-permute-done.8.refs_1_.refs_9_), channel_id=1, source_target_pairs={{0,8},{8,0},{16,24},{24,16},{1,9},{9,1},{17,25},{25,17},{2,10},{10... | collective-permute-start | bytes 1572872 | tf_op jit(solution)/shard_map/ppermute | solution.py:662
  81.9 77.8 %collective-permute-start.21 = (bf16[768,1024]{1,0:T(8,128)(2,1)S(1)}, bf16[768,1024]{1,0:T(8,128)(2,1)S(1)}, u32[]{:S(2)}, u32[]{:S(2)}) collective-permute-start(bf16[768,1024]{1,0:T(8,128)(2,1)S(1)} %bitcast.186), channel_id=1, source_target_pairs={{0,1},{1,0},{2,3},{3,2},{4,5},{5,4},{6,7},{7,6},{8,9},{9,8},{10,11... | collective-permute-start | bytes 4718600 | tf_op jit(solution)/shard_map/ppermute | solution.py:780
  116.2 43.5 %collective-permute-start.20 = (bf16[512,1024]{1,0:T(8,128)(2,1)S(1)}, bf16[512,1024]{1,0:T(8,128)(2,1)S(1)}, u32[]{:S(2)}, u32[]{:S(2)}) collective-permute-start(bf16[512,1024]{1,0:T(8,128)(2,1)S(1)} %get-tuple-element.128), channel_id=1, source_target_pairs={{0,16},{8,24},{16,0},{24,8},{1,17},{9,25},{17,1},{25,9},{2,18},{10... | collective-permute-start | bytes 3145736 | tf_op jit(solution)/shard_map/ppermute | solution.py:662
  116.2 46.2 %collective-permute-start.23 = (bf16[2,256,1024]{2,1,0:T(8,128)(2,1)S(1)}, bf16[2,256,1024]{2,1,0:T(8,128)(2,1)S(1)}, u32[]{:S(2)}, u32[]{:S(2)}) collective-permute-start(bf16[2,256,1024]{2,1,0:T(8,128)(2,1)S(1)} %copy-done.61), channel_id=1, source_target_pairs={{0,8},{8,0},{16,24},{24,16},{1,9},{9,1},{17,25},{25,17},{2,10},{10... | collective-permute-start | bytes 3145736 | tf_op jit(solution)/shard_map/ppermute | solution.py:662
  203.2 37.3 %collective-permute-start.27 = (bf16[2,384,1024]{2,1,0:T(8,128)(2,1)S(1)}, bf16[2,384,1024]{2,1,0:T(8,128)(2,1)S(1)}, u32[]{:S(2)}, u32[]{:S(2)}) collective-permute-start(bf16[2,384,1024]{2,1,0:T(8,128)(2,1)S(1)} %dynamic-slice_bitcast_fusion.2), channel_id=1, source_target_pairs={{0,4},{4,0},{1,5},{5,1},{2,6},{6,2},{3,7},{7,3},{8,12},{12,8},{9,1... | collective-permute-start | bytes 4718600 | tf_op jit(solution)/shard_map/ppermute | solution.py:671
  209.2 32.3 %collective-permute-start.29 = (bf16[512,1024]{1,0:T(8,128)(2,1)S(1)}, bf16[512,1024]{1,0:T(8,128)(2,1)S(1)}, u32[]{:S(2)}, u32[]{:S(2)}) collective-permute-start(bf16[512,1024]{1,0:T(8,128)(2,1)S(1)} %fusion.57), channel_id=1, source_target_pairs={{0,16},{8,24},{16,0},{24,8},{1,17},{9,25},{17,1},{25,9},{2,18},{10... | collective-permute-start | bytes 3145736 | tf_op jit(solution)/shard_map/ppermute | solution.py:662
  218.9 63.8 %collective-permute-start.31 = (bf16[2,128,3072]{2,1,0:T(8,128)(2,1)}, bf16[2,128,3072]{2,1,0:T(8,128)(2,1)}, u32[]{:S(2)}, u32[]{:S(2)}) collective-permute-start(bf16[2,128,3072]{2,1,0:T(8,128)(2,1)} %dynamic-slice_bitcast_fusion.1), channel_id=1, source_target_pairs={{0,4},{4,0},{1,5},{5,1},{2,6},{6,2},{3,7},{7,3},{8,12},{12,8},{9,1... | collective-permute-start | bytes 4718600 | tf_op jit(solution)/shard_map/ppermute | solution.py:671
  241.2 28.2 %collective-permute-start.28 = (bf16[384,1024]{1,0:T(8,128)(2,1)S(1)}, bf16[384,1024]{1,0:T(8,128)(2,1)S(1)}, u32[]{:S(2)}, u32[]{:S(2)}) collective-permute-start(bf16[384,1024]{1,0:T(8,128)(2,1)S(1)} %get-tuple-element.228), channel_id=1, source_target_pairs={{0,16},{8,24},{16,0},{24,8},{1,17},{9,25},{17,1},{25,9},{2,18},{10... | collective-permute-start | bytes 2359304 | tf_op jit(solution)/shard_map/ppermute | solution.py:662
  242.5 36.2 %collective-permute-start.32 = (bf16[128,3072]{1,0:T(8,128)(2,1)}, bf16[128,3072]{1,0:T(8,128)(2,1)}, u32[]{:S(2)}, u32[]{:S(2)}) collective-permute-start(bf16[128,3072]{1,0:T(8,128)(2,1)} %dynamic-slice_bitcast_fusion.5), channel_id=1, source_target_pairs={{0,16},{8,24},{16,0},{24,8},{1,17},{9,25},{17,1},{25,9},{2,18},{10... | collective-permute-start | bytes 2359304 | tf_op jit(solution)/shard_map/ppermute | solution.py:662
  272.6 40.6 %collective-permute-start.30 = (bf16[128,3072]{1,0:T(8,128)(2,1)}, bf16[128,3072]{1,0:T(8,128)(2,1)}, u32[]{:S(2)}, u32[]{:S(2)}) collective-permute-start(bf16[128,3072]{1,0:T(8,128)(2,1)} %dynamic-slice_bitcast_fusion.6), channel_id=1, source_target_pairs={{0,16},{8,24},{16,0},{24,8},{1,17},{9,25},{17,1},{25,9},{2,18},{10... | collective-permute-start | bytes 2359304 | tf_op jit(solution)/shard_map/ppermute | solution.py:662
  278.7 129.7 %all-reduce.11.cloned.1.call-start = ((), (), s32[]{:S(2)}) async-start(), calls=%async_computation.4 | async-start | bytes 3145728 | tf_op jit(solution)/shard_map/psum | solution.py:899
  281.2 33.6 %collective-permute-start.33 = (bf16[128,3072]{1,0:T(8,128)(2,1)}, bf16[128,3072]{1,0:T(8,128)(2,1)}, u32[]{:S(2)}, u32[]{:S(2)}) collective-permute-start(bf16[128,3072]{1,0:T(8,128)(2,1)} %fusion.16), channel_id=1, source_target_pairs={{0,4},{4,0},{1,5},{5,1},{2,6},{6,2},{3,7},{7,3},{8,12},{12,8},{9,1... | collective-permute-start | bytes 2359304 | tf_op jit(solution)/shard_map/ppermute | solution.py:671
  285.2 31.8 %collective-permute-start.34 = (bf16[128,3072]{1,0:T(8,128)(2,1)S(1)}, bf16[128,3072]{1,0:T(8,128)(2,1)}, u32[]{:S(2)}, u32[]{:S(2)}) collective-permute-start(bf16[128,3072]{1,0:T(8,128)(2,1)S(1)} %get-tuple-element.223), channel_id=1, source_target_pairs={{0,16},{8,24},{16,0},{24,8},{1,17},{9,25},{17,1},{25,9},{2,18},{10... | collective-permute-start | bytes 2359304 | tf_op jit(solution)/shard_map/ppermute | solution.py:662
  330.3 9.2 %collective-permute-start.38 = (bf16[2,256,1024]{2,1,0:T(8,128)(2,1)}, bf16[2,256,1024]{2,1,0:T(8,128)(2,1)}, u32[]{:S(2)}, u32[]{:S(2)}) collective-permute-start(bf16[2,256,1024]{2,1,0:T(8,128)(2,1)} %get-tuple-element.174), channel_id=1, source_target_pairs={{0,8},{8,0},{16,24},{24,16},{1,9},{9,1},{17,25},{25,17},{2,10},{10... | collective-permute-start | bytes 3145736 | tf_op jit(solution)/shard_map/ppermute | solution.py:662
  338.0 37.6 %collective-permute-start.37 = (bf16[2,128,2048]{2,1,0:T(8,128)(2,1)}, bf16[2,128,2048]{2,1,0:T(8,128)(2,1)}, u32[]{:S(2)}, u32[]{:S(2)}) collective-permute-start(bf16[2,128,2048]{2,1,0:T(8,128)(2,1)} %get-tuple-element.226), channel_id=1, source_target_pairs={{0,4},{4,0},{1,5},{5,1},{2,6},{6,2},{3,7},{7,3},{8,12},{12,8},{9,1... | collective-permute-start | bytes 3145736 | tf_op jit(solution)/shard_map/ppermute | solution.py:671
  339.4 148.8 %all-reduce.9.cloned.1.call-start = ((), (), s32[]{:S(2)}) async-start(), calls=%async_computation.3 | async-start | bytes 3145728 | tf_op jit(solution)/shard_map/psum | solution.py:907
  341.2 33.5 %collective-permute-start.39 = (bf16[256,1024]{1,0:T(8,128)(2,1)S(1)}, bf16[256,1024]{1,0:T(8,128)(2,1)S(1)}, u32[]{:S(2)}, u32[]{:S(2)}) collective-permute-start(bf16[256,1024]{1,0:T(8,128)(2,1)S(1)} %get-tuple-element.234), channel_id=1, source_target_pairs={{0,4},{4,0},{1,5},{5,1},{2,6},{6,2},{3,7},{7,3},{8,12},{12,8},{9,1... | collective-permute-start | bytes 1572872 | tf_op jit(solution)/shard_map/ppermute | solution.py:671
  378.4 30.0 %collective-permute-start.40 = (bf16[128,2048]{1,0:T(8,128)(2,1)}, bf16[128,2048]{1,0:T(8,128)(2,1)S(1)}, u32[]{:S(2)}, u32[]{:S(2)}) collective-permute-start(bf16[128,2048]{1,0:T(8,128)(2,1)} %get-tuple-element.231), channel_id=1, source_target_pairs={{0,16},{8,24},{16,0},{24,8},{1,17},{9,25},{17,1},{25,9},{2,18},{10... | collective-permute-start | bytes 1572872 | tf_op jit(solution)/shard_map/ppermute | solution.py:662
  410.8 24.1 %collective-permute-start.41 = (bf16[512,1024]{1,0:T(8,128)(2,1)}, bf16[512,1024]{1,0:T(8,128)(2,1)}, u32[]{:S(2)}, u32[]{:S(2)}) collective-permute-start(bf16[512,1024]{1,0:T(8,128)(2,1)} %slice.65), channel_id=1, source_target_pairs={{0,16},{8,24},{16,0},{24,8},{1,17},{9,25},{17,1},{25,9},{2,18},{10... | collective-permute-start | bytes 3145736 | tf_op jit(solution)/shard_map/ppermute | solution.py:662
  412.3 28.8 %collective-permute-start.24 = (bf16[512,1024]{1,0:T(8,128)(2,1)}, bf16[512,1024]{1,0:T(8,128)(2,1)}, u32[]{:S(2)}, u32[]{:S(2)}) collective-permute-start(bf16[512,1024]{1,0:T(8,128)(2,1)} %get-tuple-element.136), channel_id=1, source_target_pairs={{0,8},{8,0},{16,24},{24,16},{1,9},{9,1},{17,25},{25,17},{2,10},{10... | collective-permute-start | bytes 3145736 | tf_op jit(solution)/shard_map/ppermute | solution.py:662
  437.4 10.0 %collective-permute-start.43 = (f32[1,288]{1,0:T(1,128)S(1)}, f32[1,288]{1,0:T(1,128)S(1)}, u32[]{:S(2)}, u32[]{:S(2)}) collective-permute-start(f32[1,288]{1,0:T(1,128)S(1)} %get-tuple-element.260), channel_id=1, source_target_pairs={{0,4},{4,0},{8,12},{12,8},{16,20},{20,16},{24,28},{28,24},{1,5},{5... | collective-permute-start | bytes 3464 | tf_op jit(solution)/shard_map/ppermute | solution.py:687
  438.9 9.0 %collective-permute-start.44 = (f32[1,288]{1,0:T(1,128)S(1)}, f32[1,288]{1,0:T(1,128)S(1)}, u32[]{:S(2)}, u32[]{:S(2)}) collective-permute-start(f32[1,288]{1,0:T(1,128)S(1)} %get-tuple-element.259), channel_id=1, source_target_pairs={{0,8},{4,12},{8,0},{12,4},{16,24},{20,28},{24,16},{28,20},{1,9},{5... | collective-permute-start | bytes 3464 | tf_op jit(solution)/shard_map/ppermute | solution.py:687
  439.0 10.3 %collective-permute-start.45 = (f32[1,288]{1,0:T(1,128)S(1)}, f32[1,288]{1,0:T(1,128)S(1)}, u32[]{:S(2)}, u32[]{:S(2)}) collective-permute-start(f32[1,288]{1,0:T(1,128)S(1)} %get-tuple-element.258), channel_id=1, source_target_pairs={{0,12},{4,8},{8,4},{12,0},{16,28},{20,24},{24,20},{28,16},{1,13},{... | collective-permute-start | bytes 3464 | tf_op jit(solution)/shard_map/ppermute | solution.py:687
  439.6 9.8 %collective-permute-start.46 = (f32[1,288]{1,0:T(1,128)S(1)}, f32[1,288]{1,0:T(1,128)S(1)}, u32[]{:S(2)}, u32[]{:S(2)}) collective-permute-start(f32[1,288]{1,0:T(1,128)S(1)} %get-tuple-element.257), channel_id=1, source_target_pairs={{0,16},{4,20},{8,24},{12,28},{16,0},{20,4},{24,8},{28,12},{1,17},{... | collective-permute-start | bytes 3464 | tf_op jit(solution)/shard_map/ppermute | solution.py:687
  449.3 14.3 %collective-permute-start.42 = (bf16[256,1024]{1,0:T(8,128)(2,1)S(1)}, bf16[256,1024]{1,0:T(8,128)(2,1)S(1)}, u32[]{:S(2)}, u32[]{:S(2)}) collective-permute-start(bf16[256,1024]{1,0:T(8,128)(2,1)S(1)} %get-tuple-element.250), channel_id=1, source_target_pairs={{0,8},{8,0},{16,24},{24,16},{1,9},{9,1},{17,25},{25,17},{2,10},{10... | collective-permute-start | bytes 1572872 | tf_op jit(solution)/shard_map/ppermute | solution.py:662
  449.4 15.3 %collective-permute-start.25 = (bf16[256,1024]{1,0:T(8,128)(2,1)S(1)}, bf16[256,1024]{1,0:T(8,128)(2,1)S(1)}, u32[]{:S(2)}, u32[]{:S(2)}) collective-permute-start(bf16[256,1024]{1,0:T(8,128)(2,1)S(1)} %get-tuple-element.253), channel_id=1, source_target_pairs={{0,8},{8,0},{16,24},{24,16},{1,9},{9,1},{17,25},{25,17},{2,10},{10... | collective-permute-start | bytes 1572872 | tf_op jit(solution)/shard_map/ppermute | solution.py:662
  451.9 11.0 %collective-permute-start.50 = (f32[1,288]{1,0:T(1,128)S(1)}, f32[1,288]{1,0:T(1,128)S(1)}, u32[]{:S(2)}, u32[]{:S(2)}) collective-permute-start(f32[1,288]{1,0:T(1,128)S(1)} %add_add_fusion), channel_id=1, source_target_pairs={{0,1},{1,0},{2,3},{3,2},{4,5},{5,4},{6,7},{7,6},{8,9},{9,8},{10,11... | collective-permute-start | bytes 3464 | tf_op jit(solution)/shard_map/ppermute | solution.py:924
  453.5 9.4 %collective-permute-start.51 = (f32[1,288]{1,0:T(1,128)S(1)}, f32[1,288]{1,0:T(1,128)S(1)}, u32[]{:S(2)}, u32[]{:S(2)}) collective-permute-start(f32[1,288]{1,0:T(1,128)S(1)} %add_add_fusion), channel_id=1, source_target_pairs={{0,2},{1,3},{2,0},{3,1},{4,6},{5,7},{6,4},{7,5},{8,10},{9,11},{10,... | collective-permute-start | bytes 3464 | tf_op jit(solution)/shard_map/ppermute | solution.py:924
  (75 other events, 956.3 us)
Sparse Core Ops, SparseCore 0:
  10.5 43.6 all-gather.2
  56.6 100.6 all-gather.4
  278.8 43.7 all-reduce.6
  339.5 68.7 all-reduce.10
  420.0 68.1 all-reduce.8

commit v9 on v8

--- a/solution.py
+++ b/solution.py
@@ -421,11 +421,12 @@
         seg_row_ref,
         gain_q_ref,
         gain_k_ref,
-    ) = refs[:13]
-    refs = refs[13:]
+        normed_ref,
+    ) = refs[:14]
+    refs = refs[14:]
     if half:
-        base_ref, refs = refs[0], refs[2:]
-    grad_ref, share_ref, gains_ref, qkv, out, key_sum, value_sum = refs
+        base_ref, refs = refs[0], refs[3:]
+    sent_ref, kept_ref, share_ref, gains_ref, qkv, out, key_sum, value_sum, weight_sum = refs
     block = q_ref.shape[0]
     heads = k_ref.shape[1] // HEAD_SIZE
     step = pl.program_id(0)
@@ -444,6 +445,7 @@
         key_sum[...] = jnp.zeros_like(key_sum)
         value_sum[...] = jnp.zeros_like(value_sum)
         gains_ref[...] = jnp.zeros_like(gains_ref)
+        weight_sum[...] = jnp.zeros_like(weight_sum)
 
     def work(j):
         size = (j + 1) * block
@@ -504,7 +506,7 @@
             value_grads.append(value_sum[own_rows, lanes].astype(LOW))
         gains_ref[...] = gains
         grad = jnp.concatenate(query_grads + key_grads + value_grads, axis=1)
-        grad_ref[...] = grad
+        weight_sum[...] += dot_tn(normed_ref[...], grad)
         share = dot_nt(grad, qkv[...])
 
         if half:
@@ -514,10 +516,19 @@
     for j in range(n):
         pl.when(step == n - 1 - j)(functools.partial(work, j))
 
+    @pl.when(step == n - 1)
+    def _():
+        chips, rows, _ = sent_ref.shape
+        core = place_ref[0] & 1
+        for i in range(chips):
+            for ref, side in ((sent_ref, core ^ 1), (kept_ref, core)):
+                start = pl.multiple_of((2 * i + side) * rows, rows)
+                ref[i] = weight_sum[pl.ds(start, rows), :].astype(LOW)
+
 
 def back(
     place, qkv_parts, out_parts, hidden_grad, attended, totals, q, k, v, raw, cos, sin, seg_col,
-    seg_row, gain_q, gain_k, half, base,
+    seg_row, gain_q, gain_k, normed, half, base,
 ):
     inner = len(out_parts) // 2
     n = len(qkv_parts) // inner
@@ -531,11 +542,15 @@
     natural_half = lambda i, p: (n - 1 - i, half)
     slot_half = lambda i, p: (p[0] ^ (n - 1 - i), half)
     base = list(base or ())
-    before = 1 + len(qkv_parts) + len(out_parts) + 13
+    before = 1 + len(qkv_parts) + len(out_parts) + 14
+    chips = n // 2
+    cut = jax.ShapeDtypeStruct((chips, D // n, HALVES * width), LOW)
+    cut_half = pl.BlockSpec((chips, D // n, width), lambda i, p: (0, 0, half))
     return pl.pallas_call(
         functools.partial(back_kernel, n, inner, half),
         out_shape=(
-            jax.ShapeDtypeStruct((length, HALVES * width), LOW),
+            cut,
+            cut,
             jax.ShapeDtypeStruct((length, D), LOW),
             jax.ShapeDtypeStruct((8, HEAD_SIZE), FULL),
         ),
@@ -558,10 +573,12 @@
                 pl.BlockSpec((1, length), whole),
                 pl.BlockSpec((1, HEAD_SIZE), whole),
                 pl.BlockSpec((1, HEAD_SIZE), whole),
+                pl.BlockSpec((block, D), natural),
             ]
-            + [pl.BlockSpec((block, D), slot), ANYWHERE][: len(base)],
+            + [pl.BlockSpec((block, D), slot), ANYWHERE, ANYWHERE][: len(base)],
             out_specs=(
-                pl.BlockSpec((block, width), natural_half),
+                cut_half,
+                cut_half,
                 pl.BlockSpec((block, D), slot),
                 pl.BlockSpec((8, HEAD_SIZE), whole),
             ),
@@ -570,9 +587,10 @@
                 pltpu.VMEM((q_width, D), LOW),
                 pltpu.VMEM((length, k_width), FULL),
                 pltpu.VMEM((length, k_width), FULL),
+                pltpu.VMEM((D, width), FULL),
             ],
         ),
-        input_output_aliases={before + 1: 0} if base else {},
+        input_output_aliases={before + 1: 0, before + 2: 1} if base else {},
         compiler_params=pltpu.CompilerParams(vmem_limit_bytes=56 * MIB),
         cost_estimate=pl.CostEstimate(
             flops=2 * length * D * (q_width + width) + 5 * length * length * q_width,
@@ -582,7 +600,7 @@
         name="back",
     )(
         place, *qkv_parts, *out_parts, hidden_grad, attended, totals, q, k, v, raw, cos, sin,
-        seg_col, seg_row, gain_q, gain_k, *base,
+        seg_col, seg_row, gain_q, gain_k, normed, *base,
     )
 
 
@@ -844,11 +862,6 @@
         def send_y(parts):
             return parts[0], [swap_grp(parts[t], t) for t in range(1, inner)]
 
-        def cut_qkv(grad):
-            grad_qkv = dot_tn(normed, grad).astype(LOW)
-            cuts = grad_qkv.reshape(chips, 2, inner, rows, width)
-            return pick(cuts, 1, core), [swap_core(pick(cuts, 1, core ^ 1))]
-
         grad_expand = dot_tn(after(x_all, hidden_low), grad_gate_up).astype(LOW)
         expand_cuts = grad_expand.reshape(chips, 2, inner, rows, FF)
         other_rows = pick(expand_cuts, 1, core ^ 1)
@@ -863,7 +876,7 @@
         def back_part(half, attended, base):
             return back(
                 place, qkv_parts, out_parts, grad_all, attended, totals, q, k, v, raw, cos, sin, seg_col,
-                seg_row, gain_query, gain_key, half, base,
+                seg_row, gain_query, gain_key, normed, half, base,
             )
 
         own_far = [first_over_x(t, *grad_slots) for t in range(1, inner)]
@@ -871,7 +884,7 @@
         shrink_cut = send_x(next_cut(pick(shrink_cuts, 1, mine), shrink_sent, 0, chip, chips))
         grad_slots = lax.optimization_barrier((*grad_slots, *line))[:chips]
         grad_all = jnp.concatenate(grad_slots)
-        grad, back_all, gains_first_part = back_part(0, attended, None)
+        sent, kept, back_all, gains_first_part = back_part(0, attended, None)
 
         line[:] = [gains_first_part]
         shrink_cut = next_sum(*shrink_cut)
@@ -884,18 +897,19 @@
         out_kept, out_sent = pick(out_cuts, 0, core), pick(out_cuts, 0, core ^ 1)
         attended, out_kept, out_sent = lax.optimization_barrier((attended, out_kept, out_sent))
         out_sent = [swap_core(out_sent)]
-        attended, back_all, grad = lax.optimization_barrier((attended, back_all, grad, *line))[:3]
-        grad, back_all, head_gains = back_part(1, attended, (back_all, grad))
+        attended, back_all, sent, kept = lax.optimization_barrier((attended, back_all, sent, kept, *line))[:4]
+        sent, kept, back_all, head_gains = back_part(1, attended, (back_all, sent, kept))
 
         line[:] = [head_gains]
         head_gains = head_gains + gains_first_part
         own_cut = next_sum(next_sum(*own_near), own_sent)
         other_cut = swap_core(next_sum(*other_cut))
-        own_cut, other_cut, total_shrink, grad = lax.optimization_barrier(
-            (own_cut, other_cut, total_shrink, grad, *line)
-        )[:4]
+        own_cut, other_cut, total_shrink = lax.optimization_barrier(
+            (own_cut, other_cut, total_shrink, *line)
+        )[:3]
         line[:] = [own_cut]
-        qkv_cuts, qkv_sent = cut_qkv(grad)
+        shape = (chips, inner, rows, width)
+        qkv_cuts, qkv_sent = kept.reshape(shape), [swap_core(sent.reshape(shape))]
         own_cut, other_cut = lax.psum((own_cut, other_cut), "rep")
         qkv_cut = send_y(next_cut(qkv_cuts, qkv_sent, 1, mine, inner))
         out_cut = send_y(next_cut(out_kept, out_sent, 0, mine, inner))
@@ -936,6 +950,7 @@
             v_place = k_place + KEY_FEATURES // size
             return jnp.where(i < q_blocks, q_place, jnp.where(i == q_blocks, k_place, v_place))
 
+        total_shrink = after(total_shrink, total_gains)
         key = chip.reshape(1).astype(jnp.int32)
         return (
             output,

time: 519 us -> 506 us (0.975)
  waiting for transfers between devices: 211 us -> 195 us
  Pallas kernels: 133 us -> 143 us
  other arithmetic: 42.2 us -> 50.8 us
  matrix products: 23.2 us -> 15.7 us
  local copies, waits for them, and re-layouts: 44.3 us -> 37.2 us
    psum x1, waiting for transfers between devices: 22.3 us -> 11.6 us  [on_device(): total_out, *qkv_cuts = lax.psum((out_cut, *qkv_cuts), 'rep')]
    pallas_call x2, Pallas kernels: 47.5 us -> 57.1 us  [back(): pl.pallas_call(functools.partial(back_kernel, n, inner, half), out_shape=...]
    unnamed x142 -> x150, local copies, waits for them, and re-layouts: 25.5 us -> 17.9 us
    dot_general x4 -> x3, matrix products: 23.2 us -> 15.7 us  [dot_tn(): lax.dot_general(a, b, (((0,), (0,)), ((), ())), preferred_element_type=FULL)]
  transfers between devices with their start and end apart: 58 -> 58, of which waited for: 17 -> 15; matrix products, arithmetic and copies ran while one was open for 15% -> 17% of each run, Pallas kernels for 18% -> 20%
where the time goes in v9:
time: 506 us; the launch traced here: 499 us
  waiting for transfers between devices  195 us (39%)
  Pallas kernels  143 us (28%)
  other arithmetic  50.8 us (10%)
  starting transfers between devices  42.9 us (8%)
  local copies, waits for them, and re-layouts  37.2 us (7%)
  matrix products  15.7 us (3%)
  between operations  15.3 us (3%)
    ppermute x27, waiting for transfers between devices, swap_ctx(): return lax.ppermute(value, 'ctx', [(i, i ^ s) for i in range(n)])  79.8 us
    ppermute x8, waiting for transfers between devices, swap_grp(): return lax.ppermute(value, 'grp', [(i, i ^ t) for i in range(inner)])  71.6 us
    pallas_call x2, Pallas kernels, back(): pl.pallas_call(functools.partial(back_kernel, n, inner, half), out_shape=...  57.1 us
    pallas_call x1, Pallas kernels, feed(): pl.pallas_call(functools.partial(feed_kernel, chips, inner), out_shape=(w...  31.6 us
    psum x1, waiting for transfers between devices, on_device(): own_cut, other_cut = lax.psum((own_cut, other_cut), 'rep')  29.4 us
    pallas_call x2, Pallas kernels, attend(): pl.pallas_call(functools.partial(attend_kernel, n, inner, first, bool(bas...  24 us
    unnamed x150, local copies, waits for them, and re-layouts  17.9 us
    dot_general x3, matrix products, dot_tn(): lax.dot_general(a, b, (((0,), (0,)), ((), ())), preferred_element_type=FULL)  15.7 us
  transfers between devices with their start and end apart: 58, of which 15 were waited for; matrix products, arithmetic and copies ran while one was open for 17% of the time, Pallas kernels for 20%

profile of v9, /device:TPU:0, one launch (start us, length us, event | category | flops | bytes accessed | tf_op | source)
XLA Modules:
  0.0 499.4 jit_solution(13633718095137474425)
XLA Ops:
  7.3 2.0 dynamic-slice_convert_fusion
  9.4 3.4 convert_element_type.307
  12.9 3.0 collective-permute-start
  16.2 1.9 collective-permute-start.3
  24.3 2.0 collective-permute-start.8
  28.7 2.0 copy.43
  30.8 2.6 gather_fusion.1
  35.1 11.8 %collective-permute-done.14.refs_4_ = bf16[128,2048]{1,0:T(8,128)(2,1)} collective-permute-done((bf16[128,2048]{1,0:T(8,128)(2,1)}, bf16[128,2048]{1,0:T(8,128)(2,1)}, u32[]{:S(2)}, u32[]{:S(2)}) %collective-permute-start.14) | collective-permute-done | bytes 524320 | tf_op jit(solution)/shard_map/ppermute | solution.py:680
  47.1 12.1 %collective-permute-done.11.refs_1_ = bf16[128,2048]{1,0:T(8,128)(2,1)} collective-permute-done((bf16[128,2048]{1,0:T(8,128)(2,1)S(1)}, bf16[128,2048]{1,0:T(8,128)(2,1)}, u32[]{:S(2)}, u32[]{:S(2)}) %collective-permute-start.11) | collective-permute-done | bytes 524320 | tf_op jit(solution)/shard_map/ppermute | solution.py:689
  63.3 8.1 %collective-permute-done.15.refs_5_ = bf16[128,2048]{1,0:T(8,128)(2,1)} collective-permute-done((bf16[128,2048]{1,0:T(8,128)(2,1)}, bf16[128,2048]{1,0:T(8,128)(2,1)}, u32[]{:S(2)}, u32[]{:S(2)}) %collective-permute-start.15) | collective-permute-done | bytes 524320 | tf_op jit(solution)/shard_map/ppermute | solution.py:689
  71.5 1.9 fusion.21
  75.7 1.9 collective-permute-start.21
  77.6 7.2 %collective-permute-done.19.refs_11_ = bf16[256,1024]{1,0:T(8,128)(2,1)} collective-permute-done((bf16[256,1024]{1,0:T(8,128)(2,1)S(1)}, bf16[256,1024]{1,0:T(8,128)(2,1)}, u32[]{:S(2)}, u32[]{:S(2)}) %collective-permute-start.19) | collective-permute-done | bytes 524320 | tf_op jit(solution)/shard_map/ppermute | solution.py:680
  85.8 10.5 %project.1 = (bf16[1024,1024]{1,0:T(8,128)(2,1)S(1)}, bf16[1024,1024]{1,0:T(8,128)(2,1)S(1)}, bf16[1024,512]{1,0:T(8,128)(2,1)S(1)}, bf16[1024,512]{1,0:T(8,128)(2,1)S(1)}, bf16[1024,1536]{1,0:T(8,128)(2,1)}) custom-call(s32[3]{0:T(128)S(1)} %pad_add_fusion.place_ref, bf16[128,2048]{1,0:T(8,128)(2,1)S(1)} %copy-done.21, ...), custom_call_target="tpu_custom_call" | custom-call | flops 4294967296 | bytes 16777216 | tf_op jit(solution)/shard_map/project/pallas_call | solution.py:150
  100.0 12.0 %attend.2 = (bf16[1024,1024]{1,0:T(8,128)(2,1)}, f32[1024,256]{1,0:T(8,128)S(1)}, bf16[512,1024]{1,0:T(8,128)(2,1)S(1)}) custom-call(s32[3]{0:T(128)S(1)} %pad_add_fusion.place_ref, bf16[256,1024]{1,0:T(8,128)(2,1)S(1)} %convert_element_type.302.refs_0_.refs_8_, bf16[256,1024]{1,0:T(8,128)(2,1)S(1)} %copy-done.24, ...), custom_call_target="tpu_custom_call" | custom-call | flops 3221225472 | bytes 8388608 | tf_op jit(solution)/shard_map/attend/pallas_call | solution.py:258
  112.2 12.0 %attend.3 = (bf16[1024,1024]{1,0:T(8,128)(2,1)}, f32[1024,256]{1,0:T(8,128)S(1)}, bf16[512,1024]{1,0:T(8,128)(2,1)S(1)}) custom-call(s32[3]{0:T(128)S(1)} %pad_add_fusion.place_ref, bf16[256,1024]{1,0:T(8,128)(2,1)S(1)} %convert_element_type.302.refs_0_.refs_8_, bf16[256,1024]{1,0:T(8,128)(2,1)S(1)} %copy-done.24, ...), custom_call_target="tpu_custom_call", output_to_operand_aliasing={{0}: (10, {}), {1}: (11, {})} | custom-call | flops 3221225472 | bytes 8388608 | tf_op jit(solution)/shard_map/attend/pallas_call | solution.py:258
  124.2 33.5 %collective-permute-done.20 = bf16[512,1024]{1,0:T(8,128)(2,1)S(1)} collective-permute-done((bf16[512,1024]{1,0:T(8,128)(2,1)S(1)}, bf16[512,1024]{1,0:T(8,128)(2,1)S(1)}, u32[]{:S(2)}, u32[]{:S(2)}) %collective-permute-start.20) | collective-permute-done | bytes 1048608 | tf_op jit(solution)/shard_map/ppermute | solution.py:680
  159.6 1.8 multiply_convert_fusion.refs_6_
  164.3 31.6 %feed.1 = (bf16[1024,1024]{1,0:T(8,128)(2,1)}, bf16[1024,1024]{1,0:T(8,128)(2,1)}, bf16[1024,1536]{1,0:T(8,128)(2,1)}, bf16[1024,3072]{1,0:T(8,128)(2,1)}, bf16[...) custom-call(s32[3]{0:T(128)} %copy-done.38, ...), custom_call_target="tpu_custom_call" | custom-call | flops 19327352832 | bytes 31457280 | tf_op jit(solution)/shard_map/feed/pallas_call | solution.py:371
  196.0 6.0 %convolution_convert_fusion.1 = bf16[1536,1024]{1,0:T(8,128)(2,1)S(1)} fusion(bf16[1024,1536]{1,0:T(8,128)(2,1)} %get-tuple-element.141, bf16[1024,1024]{1,0:T(8,128)(2,1)} %get-tuple-element.142), kind=kOutput, calls=%fused_computation.3 | convolution fusion | flops 3222798336 | bytes 8388608 | tf_op jit(solution)/shard_map/dot_general | solution.py:51
  203.7 2.8 multiply_reduce_fusion
  206.6 2.8 fusion.58
  210.3 7.3 %convolution_convert_fusion = bf16[1024,3072]{1,0:T(8,128)(2,1)S(1)} fusion(bf16[1024,1024]{1,0:T(8,128)(2,1)S(1)} %copy-done.68, bf16[1024,3072]{1,0:T(8,128)(2,1)S(1)} %copy-done.67), kind=kOutput, calls=%fused_computation.2 | convolution fusion | flops 6445596672 | bytes 14680064 | tf_op jit(solution)/shard_map/dot_general | solution.py:51
  220.7 18.7 %collective-permute-done.28 = bf16[2,384,1024]{2,1,0:T(8,128)(2,1)S(1)} collective-permute-done((bf16[2,384,1024]{2,1,0:T(8,128)(2,1)S(1)}, bf16[2,384,1024]{2,1,0:T(8,128)(2,1)S(1)}, u32[]{:S(2)}, u32[]{:S(2)}) %collective-permute-start.28) | collective-permute-done | bytes 1572896 | tf_op jit(solution)/shard_map/ppermute | solution.py:689
  244.7 28.4 %back.2 = (bf16[2,256,2048]{2,1,0:T(8,128)(2,1)}, bf16[2,256,2048]{2,1,0:T(8,128)(2,1)}, bf16[1024,1024]{1,0:T(8,128)(2,1)}, f32[8,128]{1,0:T(8,128)}) custom-call(s32[3]{0:T(128)} %copy-done.38, bf16[128,2048]{1,0:T(8,128)(2,1)} %copy-done.20, bf16[128,2048]{1,0:T(8,128)(2,1)} %collective-permute-done.11.refs_1_, ...), custom_call_target="tpu_custom_call" | custom-call | flops 5905580032 | bytes 31457280 | tf_op jit(solution)/shard_map/back/pallas_call | solution.py:549
  273.1 2.3 add_convert_fusion.5
  275.5 2.1 dynamic-slice_bitcast_fusion.5
  278.0 2.4 fusion.15
  282.1 3.6 fusion.13
  287.2 2.4 convolution_convert_fusion.2
  291.1 28.7 %back.3 = (bf16[2,256,2048]{2,1,0:T(8,128)(2,1)}, bf16[2,256,2048]{2,1,0:T(8,128)(2,1)}, bf16[1024,1024]{1,0:T(8,128)(2,1)}, f32[8,128]{1,0:T(8,128)}) custom-call(s32[3]{0:T(128)} %copy-done.38, bf16[128,2048]{1,0:T(8,128)(2,1)} %copy-done.20, bf16[128,2048]{1,0:T(8,128)(2,1)} %collective-permute-done.11.refs_1_, ...), custom_call_target="tpu_custom_call", output_to_operand_aliasing={{0}: (28, {}), {1}: (29, {})} | custom-call | flops 5905580032 | bytes 31457280 | tf_op jit(solution)/shard_map/back/pallas_call | solution.py:549
  321.5 2.2 add_convert_fusion.4
  323.7 2.2 add_convert_fusion.3
  326.4 2.2 collective-permute-done.36
  328.7 4.4 add_convert_fusion.1
  334.0 2.0 fusion.22
  337.2 32.7 %collective-permute-done.39 = bf16[256,1024]{1,0:T(8,128)(2,1)S(1)} collective-permute-done((bf16[256,1024]{1,0:T(8,128)(2,1)S(1)}, bf16[256,1024]{1,0:T(8,128)(2,1)S(1)}, u32[]{:S(2)}, u32[]{:S(2)}) %collective-permute-start.39) | collective-permute-done | bytes 524320 | tf_op jit(solution)/shard_map/ppermute | solution.py:689
  370.9 2.4 fusion.25
  373.9 29.4 %all-reduce.11.cloned.1.call-done = (bf16[128,3072]{1,0:T(8,128)(2,1)}, bf16[128,3072]{1,0:T(8,128)(2,1)}) async-done(((bf16[128,3072]{1,0:T(8,128)(2,1)}, bf16[128,3072]{1,0:T(8,128)(2,1)}), (bf16[128,3072]{1,0:T(8,128)(2,1)}, bf16[128,3072]{1,0:T(8,128)(2,1)})) %all-reduce.11.cloned.1.call-update) | async-done | bytes 1572880 | tf_op jit(solution)/shard_map/psum | solution.py:913
  403.3 2.5 slice.65
  407.3 22.5 %collective-permute-done.41 = bf16[512,1024]{1,0:T(8,128)(2,1)} collective-permute-done((bf16[512,1024]{1,0:T(8,128)(2,1)}, bf16[512,1024]{1,0:T(8,128)(2,1)}, u32[]{:S(2)}, u32[]{:S(2)}) %collective-permute-start.41) | collective-permute-done | bytes 1048608 | tf_op jit(solution)/shard_map/ppermute | solution.py:680
  429.8 2.4 fusion.8
  437.5 4.7 fusion.7
  451.4 6.5 %adam_pair.1 = (f32[128,6144]{1,0:T(8,128)}, f32[128,6144]{1,0:T(8,128)}, f32[128,6144]{1,0:T(8,128)}) custom-call(s32[3]{0:T(128)S(1)} %copy-done.39, bf16[128,3072]{1,0:T(8,128)(2,1)S(1)} %copy-done.32, bf16[128,3072]{1,0:T(8,128)(2,1)S(1)} %copy-done.33, f32[128,6144]{1,0:T(8,128)S(1)} %copy-done.2, f32[128,6144]{1,0:T(8,128)S(1)} %copy-done.18, ...), custom_call_target="tpu_custom_call" | custom-call | flops 15728640 | bytes 20447232 | tf_op jit(solution)/shard_map/adam_pair/pallas_call | solution.py:655
  458.0 3.3 adam_cuts.5
  464.2 11.6 %all-reduce.9.cloned.1.call-done = (bf16[128,2048]{1,0:T(8,128)(2,1)}, bf16[128,2048]{1,0:T(8,128)(2,1)}, bf16[256,1024]{1,0:T(8,128)(2,1)}) async-done(((bf16[128,2048]{1,0:T(8,128)(2,1)}, bf16[128,2048]{1,0:T(8,128)(2,1)}, bf16[256,1024]{1,0:T(8,128)(2,1)}), (bf16[128,2048]{1,0:T(8,128)(2,1)}, bf16[128,2048]{1,0:T(8,128)(2,1)}, bf16[256,1024]{1,0:T(8,128)(2,1)})) %all-reduce.9.cloned.1.call-update) | async-done | bytes 1572880 | tf_op jit(solution)/shard_map/psum | solution.py:921
  479.3 2.6 adam_cuts.4
  485.1 7.3 %adam_cuts.3 = (f32[128,4096]{1,0:T(8,128)}, f32[128,4096]{1,0:T(8,128)}, f32[128,4096]{1,0:T(8,128)}) custom-call(s32[1]{0:T(128)} %bitcast.56.key_ref, bf16[128,2048]{1,0:T(8,128)(2,1)S(1)} %copy-done.35, bf16[128,2048]{1,0:T(8,128)(2,1)S(1)} %copy-done.36, f32[128,4096]{1,0:T(8,128)S(1)} %copy-done.13, f32[128,4096]{1,0:T(8,128)S(1)} %copy-done.25, ...), custom_call_target="tpu_custom_call" | custom-call | flops 10485760 | bytes 13631488 | tf_op jit(solution)/shard_map/adam_cuts/pallas_call | solution.py:625
  (308 shorter events, 74.3 us)
Async XLA Ops:
  7.2 66.9 %all-gather.3.cloned.1.call-start = ((), (), s32[]{:S(2)}) async-start(), calls=%async_computation | async-start | bytes 3538944 | tf_op jit(solution)/shard_map/all_gather | solution.py:796
  9.3 154.9 %all-gather.5.cloned.1.call-start = ((), (), s32[]{:S(2)}) async-start(), calls=%async_computation.1 | async-start | bytes 14155776 | tf_op jit(solution)/shard_map/all_gather | solution.py:790
  12.8 313.7 %all-reduce.7.cloned.1.call-start = ((), (), s32[]{:S(2)}) async-start(), calls=%async_computation.2 | async-start | bytes 1572864 | tf_op jit(solution)/shard_map/psum | solution.py:891
  12.9 8.7 %collective-permute-start = (f32[1,1312]{1,0:T(1,128)S(1)}, f32[1,1312]{1,0:T(1,128)S(1)}, u32[]{:S(2)}, u32[]{:S(2)}) collective-permute-start(f32[1,1312]{1,0:T(1,128)S(1)} %reshape.242), channel_id=1, source_target_pairs={{0,4},{4,0},{8,12},{12,8},{16,20},{20,16},{24,28},{28,24},{1,5},{5... | collective-permute-start | bytes 15752 | tf_op jit(solution)/shard_map/ppermute | solution.py:705
  16.0 8.3 %collective-permute-start.2 = (f32[1,1312]{1,0:T(1,128)S(1)}, f32[1,1312]{1,0:T(1,128)S(1)}, u32[]{:S(2)}, u32[]{:S(2)}) collective-permute-start(f32[1,1312]{1,0:T(1,128)S(1)} %reshape.242), channel_id=1, source_target_pairs={{0,12},{4,8},{8,4},{12,0},{16,28},{20,24},{24,20},{28,16},{1,13},{... | collective-permute-start | bytes 15752 | tf_op jit(solution)/shard_map/ppermute | solution.py:705
  16.2 10.2 %collective-permute-start.3 = (f32[1,1312]{1,0:T(1,128)S(1)}, f32[1,1312]{1,0:T(1,128)S(1)}, u32[]{:S(2)}, u32[]{:S(2)}) collective-permute-start(f32[1,1312]{1,0:T(1,128)S(1)} %reshape.242), channel_id=1, source_target_pairs={{0,16},{4,20},{8,24},{12,28},{16,0},{20,4},{24,8},{28,12},{1,17},{... | collective-permute-start | bytes 15752 | tf_op jit(solution)/shard_map/ppermute | solution.py:705
  18.1 8.3 %collective-permute-start.4 = (f32[1,1312]{1,0:T(1,128)S(1)}, f32[1,1312]{1,0:T(1,128)S(1)}, u32[]{:S(2)}, u32[]{:S(2)}) collective-permute-start(f32[1,1312]{1,0:T(1,128)S(1)} %reshape.242), channel_id=1, source_target_pairs={{0,20},{4,16},{8,28},{12,24},{16,4},{20,0},{24,12},{28,8},{1,21},{... | collective-permute-start | bytes 15752 | tf_op jit(solution)/shard_map/ppermute | solution.py:705
  24.3 22.6 %collective-permute-start.8 = (bf16[256,1024]{1,0:T(8,128)(2,1)S(1)}, bf16[256,1024]{1,0:T(8,128)(2,1)S(1)}, u32[]{:S(2)}, u32[]{:S(2)}) collective-permute-start(bf16[256,1024]{1,0:T(8,128)(2,1)S(1)} %convert_element_type.302.refs_0_.refs_8_), channel_id=1, source_target_pairs={{0,4},{4,0},{1,5},{5,1},{2,6},{6,2},{3,7},{7,3},{8,12},{12,8},{9,1... | collective-permute-start | bytes 1572872 | tf_op jit(solution)/shard_map/ppermute | solution.py:689
  26.4 20.6 %collective-permute-start.14 = (bf16[128,2048]{1,0:T(8,128)(2,1)}, bf16[128,2048]{1,0:T(8,128)(2,1)}, u32[]{:S(2)}, u32[]{:S(2)}) collective-permute-start(bf16[128,2048]{1,0:T(8,128)(2,1)} %copy-done.56), channel_id=1, source_target_pairs={{0,16},{8,24},{16,0},{24,8},{1,17},{9,25},{17,1},{25,9},{2,18},{10... | collective-permute-start | bytes 1572872 | tf_op jit(solution)/shard_map/ppermute | solution.py:680
  33.6 25.5 %collective-permute-start.11 = (bf16[128,2048]{1,0:T(8,128)(2,1)S(1)}, bf16[128,2048]{1,0:T(8,128)(2,1)}, u32[]{:S(2)}, u32[]{:S(2)}) collective-permute-start(bf16[128,2048]{1,0:T(8,128)(2,1)S(1)} %copy-done.21), channel_id=1, source_target_pairs={{0,4},{4,0},{1,5},{5,1},{2,6},{6,2},{3,7},{7,3},{8,12},{12,8},{9,1... | collective-permute-start | bytes 1572872 | tf_op jit(solution)/shard_map/ppermute | solution.py:689
  34.3 26.7 %collective-permute-start.18 = (bf16[256,1024]{1,0:T(8,128)(2,1)S(1)}, bf16[256,1024]{1,0:T(8,128)(2,1)S(1)}, u32[]{:S(2)}, u32[]{:S(2)}) collective-permute-start(bf16[256,1024]{1,0:T(8,128)(2,1)S(1)} %dynamic-slice_bitcast_fusion.7.refs_8_), channel_id=1, source_target_pairs={{0,16},{8,24},{16,0},{24,8},{1,17},{9,25},{17,1},{25,9},{2,18},{10... | collective-permute-start | bytes 1572872 | tf_op jit(solution)/shard_map/ppermute | solution.py:680
  34.8 27.3 %collective-permute-start.7 = (bf16[256,1024]{1,0:T(8,128)(2,1)}, bf16[256,1024]{1,0:T(8,128)(2,1)S(1)}, u32[]{:S(2)}, u32[]{:S(2)}) collective-permute-start(bf16[256,1024]{1,0:T(8,128)(2,1)} %dynamic-slice_bitcast_fusion.8), channel_id=1, source_target_pairs={{0,8},{8,0},{16,24},{24,16},{1,9},{9,1},{17,25},{25,17},{2,10},{10... | collective-permute-start | bytes 1572872 | tf_op jit(solution)/shard_map/ppermute | solution.py:680
  46.9 24.5 %collective-permute-start.15 = (bf16[128,2048]{1,0:T(8,128)(2,1)}, bf16[128,2048]{1,0:T(8,128)(2,1)}, u32[]{:S(2)}, u32[]{:S(2)}) collective-permute-start(bf16[128,2048]{1,0:T(8,128)(2,1)} %collective-permute-done.14.refs_4_), channel_id=1, source_target_pairs={{0,4},{4,0},{1,5},{5,1},{2,6},{6,2},{3,7},{7,3},{8,12},{12,8},{9,1... | collective-permute-start | bytes 1572872 | tf_op jit(solution)/shard_map/ppermute | solution.py:689
  47.0 26.4 %collective-permute-start.12 = (bf16[128,2048]{1,0:T(8,128)(2,1)S(1)}, bf16[128,2048]{1,0:T(8,128)(2,1)}, u32[]{:S(2)}, u32[]{:S(2)}) collective-permute-start(bf16[128,2048]{1,0:T(8,128)(2,1)S(1)} %copy-done.21), channel_id=1, source_target_pairs={{0,8},{8,0},{16,24},{24,16},{1,9},{9,1},{17,25},{25,17},{2,10},{10... | collective-permute-start | bytes 1572872 | tf_op jit(solution)/shard_map/ppermute | solution.py:680
  59.1 14.9 %collective-permute-start.13 = (bf16[128,2048]{1,0:T(8,128)(2,1)}, bf16[128,2048]{1,0:T(8,128)(2,1)}, u32[]{:S(2)}, u32[]{:S(2)}) collective-permute-start(bf16[128,2048]{1,0:T(8,128)(2,1)} %collective-permute-done.11.refs_1_), channel_id=1, source_target_pairs={{0,8},{8,0},{16,24},{24,16},{1,9},{9,1},{17,25},{25,17},{2,10},{10... | collective-permute-start | bytes 1572872 | tf_op jit(solution)/shard_map/ppermute | solution.py:680
  61.9 13.8 %collective-permute-start.16 = (bf16[128,2048]{1,0:T(8,128)(2,1)}, bf16[128,2048]{1,0:T(8,128)(2,1)}, u32[]{:S(2)}, u32[]{:S(2)}) collective-permute-start(bf16[128,2048]{1,0:T(8,128)(2,1)} %collective-permute-done.14.refs_4_), channel_id=1, source_target_pairs={{0,8},{8,0},{16,24},{24,16},{1,9},{9,1},{17,25},{25,17},{2,10},{10... | collective-permute-start | bytes 1572872 | tf_op jit(solution)/shard_map/ppermute | solution.py:680
  62.1 22.6 %collective-permute-start.19 = (bf16[256,1024]{1,0:T(8,128)(2,1)S(1)}, bf16[256,1024]{1,0:T(8,128)(2,1)}, u32[]{:S(2)}, u32[]{:S(2)}) collective-permute-start(bf16[256,1024]{1,0:T(8,128)(2,1)S(1)} %collective-permute-done.7.refs_9_), channel_id=1, source_target_pairs={{0,16},{8,24},{16,0},{24,8},{1,17},{9,25},{17,1},{25,9},{2,18},{10... | collective-permute-start | bytes 1572872 | tf_op jit(solution)/shard_map/ppermute | solution.py:680
  71.5 13.3 %collective-permute-start.17 = (bf16[128,2048]{1,0:T(8,128)(2,1)}, bf16[128,2048]{1,0:T(8,128)(2,1)}, u32[]{:S(2)}, u32[]{:S(2)}) collective-permute-start(bf16[128,2048]{1,0:T(8,128)(2,1)} %collective-permute-done.15.refs_5_), channel_id=1, source_target_pairs={{0,8},{8,0},{16,24},{24,16},{1,9},{9,1},{17,25},{25,17},{2,10},{10... | collective-permute-start | bytes 1572872 | tf_op jit(solution)/shard_map/ppermute | solution.py:680
  73.4 26.6 %collective-permute-start.9 = (bf16[256,1024]{1,0:T(8,128)(2,1)S(1)}, bf16[256,1024]{1,0:T(8,128)(2,1)}, u32[]{:S(2)}, u32[]{:S(2)}) collective-permute-start(bf16[256,1024]{1,0:T(8,128)(2,1)S(1)} %convert_element_type.302.refs_0_.refs_8_), channel_id=1, source_target_pairs={{0,8},{8,0},{16,24},{24,16},{1,9},{9,1},{17,25},{25,17},{2,10},{10... | collective-permute-start | bytes 1572872 | tf_op jit(solution)/shard_map/ppermute | solution.py:680
  74.0 26.0 %collective-permute-start.10 = (bf16[256,1024]{1,0:T(8,128)(2,1)}, bf16[256,1024]{1,0:T(8,128)(2,1)}, u32[]{:S(2)}, u32[]{:S(2)}) collective-permute-start(bf16[256,1024]{1,0:T(8,128)(2,1)} %copy-done.23), channel_id=1, source_target_pairs={{0,8},{8,0},{16,24},{24,16},{1,9},{9,1},{17,25},{25,17},{2,10},{10... | collective-permute-start | bytes 1572872 | tf_op jit(solution)/shard_map/ppermute | solution.py:680
  75.7 82.0 %collective-permute-start.21 = (bf16[768,1024]{1,0:T(8,128)(2,1)S(1)}, bf16[768,1024]{1,0:T(8,128)(2,1)S(1)}, u32[]{:S(2)}, u32[]{:S(2)}) collective-permute-start(bf16[768,1024]{1,0:T(8,128)(2,1)S(1)} %bitcast.175), channel_id=1, source_target_pairs={{0,1},{1,0},{2,3},{3,2},{4,5},{5,4},{6,7},{7,6},{8,9},{9,8},{10,11... | collective-permute-start | bytes 4718600 | tf_op jit(solution)/shard_map/ppermute | solution.py:798
  112.0 45.7 %collective-permute-start.20 = (bf16[512,1024]{1,0:T(8,128)(2,1)S(1)}, bf16[512,1024]{1,0:T(8,128)(2,1)S(1)}, u32[]{:S(2)}, u32[]{:S(2)}) collective-permute-start(bf16[512,1024]{1,0:T(8,128)(2,1)S(1)} %get-tuple-element.131), channel_id=1, source_target_pairs={{0,16},{8,24},{16,0},{24,8},{1,17},{9,25},{17,1},{25,9},{2,18},{10... | collective-permute-start | bytes 3145736 | tf_op jit(solution)/shard_map/ppermute | solution.py:680
  112.1 49.4 %collective-permute-start.23 = (bf16[2,256,1024]{2,1,0:T(8,128)(2,1)S(1)}, bf16[2,256,1024]{2,1,0:T(8,128)(2,1)S(1)}, u32[]{:S(2)}, u32[]{:S(2)}) collective-permute-start(bf16[2,256,1024]{2,1,0:T(8,128)(2,1)S(1)} %copy-done.65), channel_id=1, source_target_pairs={{0,8},{8,0},{16,24},{24,16},{1,9},{9,1},{17,25},{25,17},{2,10},{10... | collective-permute-start | bytes 3145736 | tf_op jit(solution)/shard_map/ppermute | solution.py:680
  202.2 37.3 %collective-permute-start.28 = (bf16[2,384,1024]{2,1,0:T(8,128)(2,1)S(1)}, bf16[2,384,1024]{2,1,0:T(8,128)(2,1)S(1)}, u32[]{:S(2)}, u32[]{:S(2)}) collective-permute-start(bf16[2,384,1024]{2,1,0:T(8,128)(2,1)S(1)} %dynamic-slice_bitcast_fusion.2), channel_id=1, source_target_pairs={{0,4},{4,0},{1,5},{5,1},{2,6},{6,2},{3,7},{7,3},{8,12},{12,8},{9,1... | collective-permute-start | bytes 4718600 | tf_op jit(solution)/shard_map/ppermute | solution.py:689
  209.3 31.2 %collective-permute-start.27 = (bf16[512,1024]{1,0:T(8,128)(2,1)S(1)}, bf16[512,1024]{1,0:T(8,128)(2,1)S(1)}, u32[]{:S(2)}, u32[]{:S(2)}) collective-permute-start(bf16[512,1024]{1,0:T(8,128)(2,1)S(1)} %fusion.58), channel_id=1, source_target_pairs={{0,16},{8,24},{16,0},{24,8},{1,17},{9,25},{17,1},{25,9},{2,18},{10... | collective-permute-start | bytes 3145736 | tf_op jit(solution)/shard_map/ppermute | solution.py:680
  219.0 63.1 %collective-permute-start.29 = (bf16[2,128,3072]{2,1,0:T(8,128)(2,1)}, bf16[2,128,3072]{2,1,0:T(8,128)(2,1)}, u32[]{:S(2)}, u32[]{:S(2)}) collective-permute-start(bf16[2,128,3072]{2,1,0:T(8,128)(2,1)} %dynamic-slice_bitcast_fusion.1), channel_id=1, source_target_pairs={{0,4},{4,0},{1,5},{5,1},{2,6},{6,2},{3,7},{7,3},{8,12},{12,8},{9,1... | collective-permute-start | bytes 4718600 | tf_op jit(solution)/shard_map/ppermute | solution.py:689
  240.2 33.0 %collective-permute-start.31 = (bf16[384,1024]{1,0:T(8,128)(2,1)S(1)}, bf16[384,1024]{1,0:T(8,128)(2,1)}, u32[]{:S(2)}, u32[]{:S(2)}) collective-permute-start(bf16[384,1024]{1,0:T(8,128)(2,1)S(1)} %get-tuple-element.231), channel_id=1, source_target_pairs={{0,16},{8,24},{16,0},{24,8},{1,17},{9,25},{17,1},{25,9},{2,18},{10... | collective-permute-start | bytes 2359304 | tf_op jit(solution)/shard_map/ppermute | solution.py:680
  241.5 36.4 %collective-permute-start.30 = (bf16[128,3072]{1,0:T(8,128)(2,1)}, bf16[128,3072]{1,0:T(8,128)(2,1)}, u32[]{:S(2)}, u32[]{:S(2)}) collective-permute-start(bf16[128,3072]{1,0:T(8,128)(2,1)} %dynamic-slice_bitcast_fusion.6), channel_id=1, source_target_pairs={{0,16},{8,24},{16,0},{24,8},{1,17},{9,25},{17,1},{25,9},{2,18},{10... | collective-permute-start | bytes 2359304 | tf_op jit(solution)/shard_map/ppermute | solution.py:680
  277.5 42.3 %collective-permute-start.33 = (bf16[128,3072]{1,0:T(8,128)(2,1)}, bf16[128,3072]{1,0:T(8,128)(2,1)}, u32[]{:S(2)}, u32[]{:S(2)}) collective-permute-start(bf16[128,3072]{1,0:T(8,128)(2,1)} %dynamic-slice_bitcast_fusion.5), channel_id=1, source_target_pairs={{0,16},{8,24},{16,0},{24,8},{1,17},{9,25},{17,1},{25,9},{2,18},{10... | collective-permute-start | bytes 2359304 | tf_op jit(solution)/shard_map/ppermute | solution.py:680
  277.9 125.4 %all-reduce.11.cloned.1.call-start = ((), (), s32[]{:S(2)}) async-start(), calls=%async_computation.4 | async-start | bytes 3145728 | tf_op jit(solution)/shard_map/psum | solution.py:913
  280.4 41.1 %collective-permute-start.34 = (bf16[128,3072]{1,0:T(8,128)(2,1)}, bf16[128,3072]{1,0:T(8,128)(2,1)}, u32[]{:S(2)}, u32[]{:S(2)}) collective-permute-start(bf16[128,3072]{1,0:T(8,128)(2,1)} %fusion.15), channel_id=1, source_target_pairs={{0,4},{4,0},{1,5},{5,1},{2,6},{6,2},{3,7},{7,3},{8,12},{12,8},{9,1... | collective-permute-start | bytes 2359304 | tf_op jit(solution)/shard_map/ppermute | solution.py:689
  285.7 38.0 %collective-permute-start.35 = (bf16[128,3072]{1,0:T(8,128)(2,1)}, bf16[128,3072]{1,0:T(8,128)(2,1)}, u32[]{:S(2)}, u32[]{:S(2)}) collective-permute-start(bf16[128,3072]{1,0:T(8,128)(2,1)} %get-tuple-element.229), channel_id=1, source_target_pairs={{0,16},{8,24},{16,0},{24,8},{1,17},{9,25},{17,1},{25,9},{2,18},{10... | collective-permute-start | bytes 2359304 | tf_op jit(solution)/shard_map/ppermute | solution.py:680
  319.8 8.9 %collective-permute-start.32 = (bf16[2,2,128,2048]{3,2,1,0:T(8,128)(2,1)}, bf16[2,2,128,2048]{3,2,1,0:T(8,128)(2,1)}, u32[]{:S(2)}, u32[]{:S(2)}) collective-permute-start(bf16[2,2,128,2048]{3,2,1,0:T(8,128)(2,1)} %bitcast.173), channel_id=1, source_target_pairs={{0,8},{8,0},{16,24},{24,16},{1,9},{9,1},{17,25},{25,17},{2,10},{10... | collective-permute-start | bytes 6291464 | tf_op jit(solution)/shard_map/ppermute | solution.py:680
  333.1 37.9 %collective-permute-start.37 = (bf16[2,128,2048]{2,1,0:T(8,128)(2,1)}, bf16[2,128,2048]{2,1,0:T(8,128)(2,1)}, u32[]{:S(2)}, u32[]{:S(2)}) collective-permute-start(bf16[2,128,2048]{2,1,0:T(8,128)(2,1)} %get-tuple-element.234), channel_id=1, source_target_pairs={{0,4},{4,0},{1,5},{5,1},{2,6},{6,2},{3,7},{7,3},{8,12},{12,8},{9,1... | collective-permute-start | bytes 3145736 | tf_op jit(solution)/shard_map/ppermute | solution.py:689
  333.9 141.9 %all-reduce.9.cloned.1.call-start = ((), (), s32[]{:S(2)}) async-start(), calls=%async_computation.3 | async-start | bytes 3145728 | tf_op jit(solution)/shard_map/psum | solution.py:921
  335.9 34.0 %collective-permute-start.39 = (bf16[256,1024]{1,0:T(8,128)(2,1)S(1)}, bf16[256,1024]{1,0:T(8,128)(2,1)S(1)}, u32[]{:S(2)}, u32[]{:S(2)}) collective-permute-start(bf16[256,1024]{1,0:T(8,128)(2,1)S(1)} %get-tuple-element.240), channel_id=1, source_target_pairs={{0,4},{4,0},{1,5},{5,1},{2,6},{6,2},{3,7},{7,3},{8,12},{12,8},{9,1... | collective-permute-start | bytes 1572872 | tf_op jit(solution)/shard_map/ppermute | solution.py:689
  373.3 30.0 %collective-permute-start.40 = (bf16[128,2048]{1,0:T(8,128)(2,1)S(1)}, bf16[128,2048]{1,0:T(8,128)(2,1)S(1)}, u32[]{:S(2)}, u32[]{:S(2)}) collective-permute-start(bf16[128,2048]{1,0:T(8,128)(2,1)S(1)} %get-tuple-element.237), channel_id=1, source_target_pairs={{0,16},{8,24},{16,0},{24,8},{1,17},{9,25},{17,1},{25,9},{2,18},{10... | collective-permute-start | bytes 1572872 | tf_op jit(solution)/shard_map/ppermute | solution.py:680
  405.7 24.1 %collective-permute-start.41 = (bf16[512,1024]{1,0:T(8,128)(2,1)}, bf16[512,1024]{1,0:T(8,128)(2,1)}, u32[]{:S(2)}, u32[]{:S(2)}) collective-permute-start(bf16[512,1024]{1,0:T(8,128)(2,1)} %slice.65), channel_id=1, source_target_pairs={{0,16},{8,24},{16,0},{24,8},{1,17},{9,25},{17,1},{25,9},{2,18},{10... | collective-permute-start | bytes 3145736 | tf_op jit(solution)/shard_map/ppermute | solution.py:680
  407.2 28.8 %collective-permute-start.24 = (bf16[512,1024]{1,0:T(8,128)(2,1)}, bf16[512,1024]{1,0:T(8,128)(2,1)}, u32[]{:S(2)}, u32[]{:S(2)}) collective-permute-start(bf16[512,1024]{1,0:T(8,128)(2,1)} %get-tuple-element.139), channel_id=1, source_target_pairs={{0,8},{8,0},{16,24},{24,16},{1,9},{9,1},{17,25},{25,17},{2,10},{10... | collective-permute-start | bytes 3145736 | tf_op jit(solution)/shard_map/ppermute | solution.py:680
  432.4 10.0 %collective-permute-start.43 = (f32[1,288]{1,0:T(1,128)S(1)}, f32[1,288]{1,0:T(1,128)S(1)}, u32[]{:S(2)}, u32[]{:S(2)}) collective-permute-start(f32[1,288]{1,0:T(1,128)S(1)} %get-tuple-element.266), channel_id=1, source_target_pairs={{0,4},{4,0},{8,12},{12,8},{16,20},{20,16},{24,28},{28,24},{1,5},{5... | collective-permute-start | bytes 3464 | tf_op jit(solution)/shard_map/ppermute | solution.py:705
  433.9 9.0 %collective-permute-start.44 = (f32[1,288]{1,0:T(1,128)S(1)}, f32[1,288]{1,0:T(1,128)S(1)}, u32[]{:S(2)}, u32[]{:S(2)}) collective-permute-start(f32[1,288]{1,0:T(1,128)S(1)} %get-tuple-element.265), channel_id=1, source_target_pairs={{0,8},{4,12},{8,0},{12,4},{16,24},{20,28},{24,16},{28,20},{1,9},{5... | collective-permute-start | bytes 3464 | tf_op jit(solution)/shard_map/ppermute | solution.py:705
  433.9 10.3 %collective-permute-start.45 = (f32[1,288]{1,0:T(1,128)S(1)}, f32[1,288]{1,0:T(1,128)S(1)}, u32[]{:S(2)}, u32[]{:S(2)}) collective-permute-start(f32[1,288]{1,0:T(1,128)S(1)} %get-tuple-element.264), channel_id=1, source_target_pairs={{0,12},{4,8},{8,4},{12,0},{16,28},{20,24},{24,20},{28,16},{1,13},{... | collective-permute-start | bytes 3464 | tf_op jit(solution)/shard_map/ppermute | solution.py:705
  434.6 9.7 %collective-permute-start.46 = (f32[1,288]{1,0:T(1,128)S(1)}, f32[1,288]{1,0:T(1,128)S(1)}, u32[]{:S(2)}, u32[]{:S(2)}) collective-permute-start(f32[1,288]{1,0:T(1,128)S(1)} %get-tuple-element.263), channel_id=1, source_target_pairs={{0,16},{4,20},{8,24},{12,28},{16,0},{20,4},{24,8},{28,12},{1,17},{... | collective-permute-start | bytes 3464 | tf_op jit(solution)/shard_map/ppermute | solution.py:705
  436.1 8.8 %collective-permute-start.47 = (f32[1,288]{1,0:T(1,128)S(1)}, f32[1,288]{1,0:T(1,128)S(1)}, u32[]{:S(2)}, u32[]{:S(2)}) collective-permute-start(f32[1,288]{1,0:T(1,128)S(1)} %get-tuple-element.262), channel_id=1, source_target_pairs={{0,20},{4,16},{8,28},{12,24},{16,4},{20,0},{24,12},{28,8},{1,21},{... | collective-permute-start | bytes 3464 | tf_op jit(solution)/shard_map/ppermute | solution.py:705
  444.2 17.7 %collective-permute-start.42 = (bf16[256,1024]{1,0:T(8,128)(2,1)S(1)}, bf16[256,1024]{1,0:T(8,128)(2,1)S(1)}, u32[]{:S(2)}, u32[]{:S(2)}) collective-permute-start(bf16[256,1024]{1,0:T(8,128)(2,1)S(1)} %get-tuple-element.256), channel_id=1, source_target_pairs={{0,8},{8,0},{16,24},{24,16},{1,9},{9,1},{17,25},{25,17},{2,10},{10... | collective-permute-start | bytes 1572872 | tf_op jit(solution)/shard_map/ppermute | solution.py:680
  444.3 18.7 %collective-permute-start.25 = (bf16[256,1024]{1,0:T(8,128)(2,1)S(1)}, bf16[256,1024]{1,0:T(8,128)(2,1)S(1)}, u32[]{:S(2)}, u32[]{:S(2)}) collective-permute-start(bf16[256,1024]{1,0:T(8,128)(2,1)S(1)} %get-tuple-element.259), channel_id=1, source_target_pairs={{0,8},{8,0},{16,24},{24,16},{1,9},{9,1},{17,25},{25,17},{2,10},{10... | collective-permute-start | bytes 1572872 | tf_op jit(solution)/shard_map/ppermute | solution.py:680
  446.9 11.0 %collective-permute-start.50 = (f32[1,288]{1,0:T(1,128)S(1)}, f32[1,288]{1,0:T(1,128)S(1)}, u32[]{:S(2)}, u32[]{:S(2)}) collective-permute-start(f32[1,288]{1,0:T(1,128)S(1)} %add_add_fusion), channel_id=1, source_target_pairs={{0,1},{1,0},{2,3},{3,2},{4,5},{5,4},{6,7},{7,6},{8,9},{9,8},{10,11... | collective-permute-start | bytes 3464 | tf_op jit(solution)/shard_map/ppermute | solution.py:938
  448.5 9.4 %collective-permute-start.51 = (f32[1,288]{1,0:T(1,128)S(1)}, f32[1,288]{1,0:T(1,128)S(1)}, u32[]{:S(2)}, u32[]{:S(2)}) collective-permute-start(f32[1,288]{1,0:T(1,128)S(1)} %add_add_fusion), channel_id=1, source_target_pairs={{0,2},{1,3},{2,0},{3,1},{4,6},{5,7},{6,4},{7,5},{8,10},{9,11},{10,... | collective-permute-start | bytes 3464 | tf_op jit(solution)/shard_map/ppermute | solution.py:938
  (79 other events, 955.6 us)
Sparse Core Ops, SparseCore 0:
  10.5 44.1 all-gather.2
  57.2 101.4 all-gather.4
  278.0 44.7 all-reduce.6
  334.0 69.2 all-reduce.10
  407.4 68.3 all-reduce.8
